TPU v7x, 128 devices: a whole 4x4x4 slice. The times are simulated.
128 devices in a mesh: node: 8 (over x_hi, y), local: 16 (over z, x_lo, core).
Axes of the slice: x: 4 (x_hi: 2, x_lo: 2; x = x_hi * 2 + x_lo), y: 4, z: 4, core: 2. Of those that a mesh axis runs over, the one named last changes fastest.
Arguments:
- activations: bfloat16 [49152, 1024], P(('node', 'local')), may hold values from -6 to 6
- cotangent: bfloat16 [49152, 1024], P(('node', 'local')), may hold values from -4 to 4
- gate_up: bfloat16 [3072, 2, 1024], P(('node', 'local')), may hold values from -0.109375 to 0.109375
- down_proj: bfloat16 [3072, 1024], P(('node', 'local')), may hold values from -0.1875 to 0.1875
Outputs:
- grad_input: bfloat16 [49152, 1024], P(('node', 'local'))
- grad_weights: float32 [3072, 3, 1024], P(('node', 'local'))
All inputs are finite; a program needn't handle non-finite values. Where the computation divides by a largest or mean magnitude, that divisor is 1e-20 or more.
Results may differ from a plain program's by a relative error of at most 0.014.
Values may be sent and summed in bfloat16 or wider, within the bound.
No kernel may reach another device: no remote copies, remote signals or barrier semaphores. Data moves between devices by JAX's collectives and lax.ppermute only.
A program may use at most 320 MiB of HBM per device.

v0:
```python
import jax
import jax.numpy as jnp
from jax import lax
from jax.sharding import PartitionSpec as P

EPS = 1e-06


def quantize(values):
    layout = values.shape
    blocks = values.reshape(layout[:-1] + (layout[-1] // 128, 128))
    scales = (jnp.max(jnp.abs(blocks), axis=-1) + EPS).astype(jnp.bfloat16)
    levels = (blocks / scales.astype(jnp.float32)[..., None]).astype(jnp.bfloat16)
    return (levels.reshape(layout), scales)


def restore(levels, scales):
    layout = levels.shape
    blocks = levels.astype(jnp.float32).reshape(layout[:-1] + (layout[-1] // 128, 128))
    return (blocks * scales.astype(jnp.float32)[..., None]).reshape(layout)


def unit_terms(activations, cotangent, gate_rows, up_rows, down_rows):
    gate_value = jnp.dot(activations, gate_rows.T, preferred_element_type=jnp.float32)
    upward = jnp.dot(activations, up_rows.T, preferred_element_type=jnp.float32)
    grad_hidden = jnp.dot(cotangent, down_rows.T, preferred_element_type=jnp.float32)
    sigmoid_gate = jax.nn.sigmoid(gate_value)
    silu_gate = gate_value * sigmoid_gate
    hidden = (silu_gate * upward).astype(jnp.bfloat16)
    silu_slope = sigmoid_gate * (1.0 + gate_value * (1.0 - sigmoid_gate))
    grad_gate = (grad_hidden * upward * silu_slope).astype(jnp.bfloat16)
    grad_up = (grad_hidden * silu_gate).astype(jnp.bfloat16)
    return (hidden, grad_gate, grad_up)


def body(activations, cotangent, gate_up, down_proj):
    width = activations.shape[1]
    shard_rows = gate_up.shape[0]
    node_count = lax.axis_size("node")
    local_count = lax.axis_size("local")
    piece_gate_up = lax.all_gather(gate_up, ("node", "local"), axis=0, tiled=True)
    piece_down = lax.all_gather(down_proj, ("node", "local"), axis=0, tiled=True)
    gate_rows = piece_gate_up[:, 0]
    up_rows = piece_gate_up[:, 1]
    hidden, grad_gate, grad_up = unit_terms(activations, cotangent, gate_rows, up_rows, piece_down)
    input_sum = jnp.dot(grad_gate, gate_rows, preferred_element_type=jnp.float32)
    input_sum = input_sum + jnp.dot(grad_up, up_rows, preferred_element_type=jnp.float32)
    weight_rows = jnp.stack(
        [
            jnp.dot(grad_gate.T, activations, preferred_element_type=jnp.float32),
            jnp.dot(grad_up.T, activations, preferred_element_type=jnp.float32),
            jnp.dot(hidden.T, cotangent, preferred_element_type=jnp.float32),
        ],
        axis=1,
    )
    partial_rows = weight_rows
    carry = (input_sum, partial_rows)
    input_sum, partial_rows = carry
    grad_input = input_sum.astype(jnp.bfloat16)
    grouped = partial_rows.reshape(node_count, local_count, shard_rows, 3, width)
    levels, scales = quantize(grouped)
    got_levels, got_scales = (
        lax.all_to_all(levels, "local", split_axis=1, concat_axis=1, tiled=True),
        lax.all_to_all(scales, "local", split_axis=1, concat_axis=1, tiled=True),
    )
    node_sum = jnp.sum(restore(got_levels, got_scales), axis=1)
    node_levels, node_scales = quantize(node_sum)
    own_levels, own_scales = (
        lax.all_to_all(node_levels, "node", split_axis=0, concat_axis=0, tiled=True),
        lax.all_to_all(node_scales, "node", split_axis=0, concat_axis=0, tiled=True),
    )
    grad_weights = jnp.sum(restore(own_levels, own_scales), axis=0)
    return (grad_input, grad_weights)


def solution(mesh):
    in_specs = (
        P(("node", "local"), None),
        P(("node", "local"), None),
        P(("node", "local"), None, None),
        P(("node", "local"), None),
    )
    out_specs = (P(("node", "local"), None), P(("node", "local"), None, None))
    return jax.shard_map(body, mesh=mesh, in_specs=in_specs, out_specs=out_specs, check_vma=False)
```

profile of v0, /device:TPU:2, one launch (start us, length us, event | category | flops | bytes accessed | tf_op | source)
XLA Modules:
  0.0 934.2 jit_solution(8218839873790255717)
XLA Ops:
  9.5 203.5 %all-gather.3.cloned.1.call-done = bf16[3072,1024]{1,0:T(8,128)(2,1)} async-done(((bf16[24,1024]{1,0:T(8,128)(2,1)}), bf16[3072,1024]{1,0:T(8,128)(2,1)}) %all-gather.3.cloned.1.call-update) | async-done | bytes 6291472 | tf_op jit(solution)/shard_map/all_gather | solution.py:42
  213.0 7.8 fusion.11
  220.8 202.0 %all-gather.5.cloned.1.call-done = bf16[3072,2,1024]{2,0,1:T(8,128)(2,1)} async-done(((bf16[24,2,1024]{2,0,1:T(8,128)(2,1)}), bf16[3072,2,1024]{2,0,1:T(8,128)(2,1)}) %all-gather.5.cloned.1.call-update) | async-done | bytes 12582928 | tf_op jit(solution)/shard_map/all_gather | solution.py:41
  422.8 4.9 fusion.3
  429.2 7.9 multiply_convert_fusion.2
  437.2 10.6 %fusion.7 = f32[3072,1024]{1,0:T(8,128)} fusion(bf16[384,1024]{1,0:T(8,128)(2,1)S(1)} %copy-done.6, f32[384,3072]{1,0:T(8,128)S(1)} %fusion.3, f32[384,3072]{1,0:T(8,128)} %get-tuple-element.4), kind=kOutput, calls=%fused_computation.17 | convolution fusion | flops 2422996992 | bytes 22806528 | tf_op jit(solution)/shard_map/dot_general | solution.py:52
  447.8 6.4 fusion.12
  454.2 6.8 fusion.13
  461.0 12.3 %copy.53 = f32[384,8,8,128]{3,2,1,0:T(8,128)} copy(f32[384,8,8,128]{3,1,2,0:T(8,128)} %bitcast.69) | data formatting | bytes 25165824
  473.3 12.3 %copy.52 = f32[384,8,8,128]{3,2,1,0:T(8,128)} copy(f32[384,8,8,128]{3,1,2,0:T(8,128)} %bitcast.67) | data formatting | bytes 25165824
  485.6 12.2 %copy.54 = f32[384,8,8,128]{3,2,1,0:T(8,128)} copy(f32[384,8,8,128]{3,1,2,0:T(8,128)} %bitcast.71) | data formatting | bytes 25165824
  497.8 55.0 %fusion = f32[8,16,24,3,8]{4,2,1,0,3:T(8,128)} fusion(f32[8,16,24,1,8,128]{5,4,2,1,0,3:T(8,128)} %bitcast.75, f32[8,16,24,1,8,128]{5,4,2,1,0,3:T(8,128)} %bitcast.73, f32[8,16,24,1,8,128]{5,4,2,1,0,3:T(8,128)} %bitcast.74), kind=kLoop, calls=%fused_computation.2 | loop fusion | flops 37675008 | bytes 38043648 | tf_op jit(solution)/shard_map/reduce_max | solution.py:12
  557.9 4.9 all-to-all-start.1
  565.4 15.0 %div.26 = f32[8,16,24,3,8,128]{5,4,2,0,3,1:T(8,128)} broadcast(f32[8,16,24,3,8]{4,2,0,3,1:T(8,128)} %copy.37), dimensions={0,1,2,3,4} | broadcast | bytes 38043648 | tf_op jit(solution)/shard_map/div | solution.py:13
  580.4 39.9 %div.27 = f32[8,16,24,3,1024]{4,2,0,3,1:T(8,128)} reshape(f32[8,16,24,3,8,128]{5,4,2,0,3,1:T(8,128)} %div.26) | data formatting | bytes 75497472 | tf_op jit(solution)/shard_map/div | solution.py:13
  620.3 31.0 %fusion.1 = bf16[8,16,24,3,1024]{4,2,0,3,1:T(8,128)(2,1)} fusion(f32[8,16,24,3,1024]{4,2,0,3,1:T(8,128)} %div.27, f32[8,16,24,1,1024]{4,2,1,0,3:T(8,128)} %bitcast.72, f32[8,16,24,1,1024]{4,2,1,0,3:T(8,128)} %bitcast.70, f32[8,16,24,1,1024]{4,2,1,0,3:T(8,128)} %bitcast.68), kind=kLoop, calls=%fused_computation.4 | loop fusion | flops 37748736 | bytes 94371840 | tf_op jit(solution)/shard_map/convert_element_type | solution.py:13
  651.3 5.7 all-to-all-start
  660.7 15.0 %mul.50 = f32[8,16,24,3,8,128]{5,4,2,0,3,1:T(8,128)} broadcast(f32[8,16,24,3,8]{4,2,0,3,1:T(8,128)} %copy.39), dimensions={0,1,2,3,4} | broadcast | bytes 38043648 | tf_op jit(solution)/shard_map/mul | solution.py:20
  675.7 39.9 %mul.51 = f32[8,16,24,3,1024]{4,2,0,3,1:T(8,128)} reshape(f32[8,16,24,3,8,128]{5,4,2,0,3,1:T(8,128)} %mul.50) | data formatting | bytes 75497472 | tf_op jit(solution)/shard_map/mul | solution.py:20
  715.6 147.9 %all-to-all-done = bf16[8,16,24,3,1024]{4,2,0,3,1:T(8,128)(2,1)} async-done(((bf16[8,16,24,3,1024]{4,2,0,3,1:T(8,128)(2,1)}), bf16[8,16,24,3,1024]{4,2,0,3,1:T(8,128)(2,1)}, u32[]{:S(2)}, u32[]{:S(2)}) %all-to-all-start) | async-done | bytes 18874400 | tf_op jit(solution)/shard_map/all_to_all | solution.py:63
  863.5 18.9 %multiply_reduce_fusion = f32[8,24,3,1024]{3,1,0,2:T(8,128)S(1)} fusion(f32[8,16,24,3,1024]{4,2,0,3,1:T(8,128)} %mul.51, bf16[8,16,24,3,1024]{4,2,0,3,1:T(8,128)(2,1)} %all-to-all-done), kind=kLoop, calls=%fused_computation.5 | loop fusion | flops 27721728 | bytes 58982400 | tf_op jit(solution)/shard_map/reduce_sum | solution.py:66
  900.7 7.2 all-to-all-start.2
  907.9 5.6 fusion.2
  913.4 6.3 add_convert_fusion.1
  (47 shorter events, 40.7 us)
Async XLA Ops:
  7.2 415.6 %copy-start = (bf16[384,1024]{1,0:T(8,128)(2,1)S(1)}, bf16[384,1024]{1,0:T(8,128)(2,1)}, u32[]{:S(2)}) copy-start(bf16[384,1024]{1,0:T(8,128)(2,1)} %param.4) | copy-start | bytes 2359300
  7.2 205.8 %all-gather.3.cloned.1.call-start = ((), (), s32[]{:S(2)}) async-start(), calls=%async_computation.4 | async-start | bytes 6340608 | tf_op jit(solution)/shard_map/all_gather | solution.py:42
  7.9 414.9 %all-gather.5.cloned.1.call-start = ((), (), s32[]{:S(2)}) async-start(), calls=%async_computation.5 | async-start | bytes 12681216 | tf_op jit(solution)/shard_map/all_gather | solution.py:41
  422.8 6.4 copy-start.5
  429.2 8.0 copy-start.6
  437.2 10.6 %copy-start.2 = (bf16[384,3072]{1,0:T(8,128)(2,1)}, bf16[384,3072]{1,0:T(8,128)(2,1)S(1)}, u32[]{:S(2)}) copy-start(bf16[384,3072]{1,0:T(8,128)(2,1)S(1)} %get-tuple-element.2) | copy-start | bytes 7077892
  437.2 17.0 %copy-start.4 = (bf16[384,3072]{1,0:T(8,128)(2,1)}, bf16[384,3072]{1,0:T(8,128)(2,1)S(1)}, u32[]{:S(2)}) copy-start(bf16[384,3072]{1,0:T(8,128)(2,1)S(1)} %get-tuple-element.3) | copy-start | bytes 7077892
  557.9 93.4 %all-to-all-start.1 = ((bf16[16,2,2304]{2,1,0:T(2,128)(2,1)}), bf16[16,2,2304]{2,1,0:T(2,128)(2,1)S(1)}, u32[]{:S(2)}, u32[]{:S(2)}) async-start(bf16[16,2,2304]{2,1,0:T(2,128)(2,1)} %reshape.41), calls=%async_computation.1 | async-start | bytes 294912 | tf_op jit(solution)/shard_map/all_to_all | solution.py:64
  651.3 212.2 %all-to-all-start = ((bf16[8,16,24,3,1024]{4,2,0,3,1:T(8,128)(2,1)}), bf16[8,16,24,3,1024]{4,2,0,3,1:T(8,128)(2,1)}, u32[]{:S(2)}, u32[]{:S(2)}) async-start(bf16[8,16,24,3,1024]{4,2,0,3,1:T(8,128)(2,1)} %fusion.1), calls=%async_computation | async-start | bytes 37748736 | tf_op jit(solution)/shard_map/all_to_all | solution.py:63
  887.9 12.7 %all-to-all-start.3 = ((bf16[8,2,288]{2,1,0:T(2,128)(2,1)}), bf16[8,2,288]{2,1,0:T(2,128)(2,1)S(1)}, u32[]{:S(2)}, u32[]{:S(2)}) async-start(bf16[8,2,288]{2,1,0:T(2,128)(2,1)} %reshape.43), calls=%async_computation.3 | async-start | bytes 24576 | tf_op jit(solution)/shard_map/all_to_all | solution.py:70
  900.7 24.1 %all-to-all-start.2 = ((bf16[8,24,3,1024]{3,1,2,0:T(8,128)(2,1)}), bf16[8,24,3,1024]{3,1,2,0:T(8,128)(2,1)}, u32[]{:S(2)}, u32[]{:S(2)}) async-start(bf16[8,24,3,1024]{3,1,2,0:T(8,128)(2,1)} %copy.45), calls=%async_computation.2 | async-start | bytes 2359296 | tf_op jit(solution)/shard_map/all_to_all | solution.py:69
  907.9 5.6 copy-start.3
  920.0 7.1 copy-start.1
Sparse Core Ops, SparseCore 0:
  9.7 203.2 all-gather.2
  215.2 207.4 all-gather.4
where the time goes:
time: 946 us; the launch traced here: 934 us
  waiting for transfers between devices  555 us (59%)
  local copies, waits for them, and re-layouts  174 us (18%)
  other arithmetic  112 us (12%)
  matrix products  56.3 us (6%)
  starting transfers between devices  22.2 us (2%)
  between operations  14.5 us (2%)
    all_gather x1, waiting for transfers between devices, body(): lax.all_gather(down_proj, ('node', 'local'), axis=0, tiled=True)  203 us
    all_gather x1, waiting for transfers between devices, body(): lax.all_gather(gate_up, ('node', 'local'), axis=0, tiled=True)  202 us
    all_to_all x1, waiting for transfers between devices, body(): lax.all_to_all(levels, 'local', split_axis=1, concat_axis=1, tiled=True)  148 us
    div x4, local copies, waits for them, and re-layouts, quantize(): blocks / scales.astype(jnp.float32)[..., None]  60 us
    mul x4, local copies, waits for them, and re-layouts, restore(): return (blocks * scales.astype(jnp.float32)[..., None]).reshape(layout)  59.1 us
    reduce_max x2, other arithmetic, quantize(): scales = (jnp.max(jnp.abs(blocks), axis=-1) + EPS).astype(jnp.bfloat16)  57.4 us
    unnamed x23, local copies, waits for them, and re-layouts  45.4 us
    convert_element_type x2, other arithmetic, quantize(): (blocks / scales.astype(jnp.float32)[..., None]).astype(jnp.bfloat16)  33.1 us
  transfers between devices with their start and end apart: 6, of which 4 were waited for; matrix products, arithmetic and copies ran while one was open for 19% of the time, Pallas kernels for 0%

commit v1 on v0

v1 whole, which is shorter than its diff:
```python
import jax
import jax.numpy as jnp
from jax import lax
from jax.experimental import pallas as pl
from jax.experimental.pallas import tpu as pltpu
from jax.sharding import PartitionSpec as P

AXES = ("node", "local")
X, Y, Z = 0, 1, 2
RING = 4
DEVICES = 128
TILE = 256
BF16 = jnp.bfloat16
F32 = jnp.float32
NT = (((1,), (1,)), ((), ()))
TN = (((0,), (0,)), ((), ()))


def place(device):
    return [device // 64 * 2 + device // 2 % 2, device // 16 % 4, device // 4 % 4, device % 2]


def index(x, y, z, core):
    return (x // 2) * 64 + y * 16 + z * 4 + (x % 2) * 2 + core


def swap(value, axis, wrap):
    pairs = []
    for device in range(DEVICES):
        there = place(device)
        there[axis] = RING - 1 - there[axis] if wrap(there[3]) else there[axis] ^ 1
        pairs.append((device, index(*there)))
    return lax.ppermute(value, AXES, pairs)


def swap_first(value, axis):
    return swap(value, axis, lambda core: core == 1)


def swap_second(value, axis):
    return swap(value, axis, lambda core: core == 0)


def swap_near(value, axis):
    return swap(value, axis, lambda core: False)


def swap_wrap(value, axis):
    return swap(value, axis, lambda core: True)


def swap_core(value):
    return lax.ppermute(value, AXES, [(d, d ^ 1) for d in range(DEVICES)])


def add(a, b):
    return (a.astype(F32) + b.astype(F32)).astype(BF16)


def join(a, b):
    return jnp.concatenate([a, b], axis=1)


def gather(message, axis, last_axis):
    half = join(message, swap_first(message, axis))
    line = join(half, swap_second(half, axis))
    near = join(line, swap_first(line, last_axis))
    return near, swap_second(near, last_axis)


def reduce(near, back, axis, last_axis):
    near = add(near, back)
    n = near.shape[1] // 2
    line = add(near[:, :n], swap_first(near[:, n:], last_axis))
    n //= 2
    half = add(line[:, :n], swap_second(line[:, n:], axis))
    n //= 2
    return half[:, :n].astype(F32) + swap_first(half[:, n:], axis).astype(F32)


def grads_kernel(*refs):
    xs, cs, ws = refs[:4], refs[4:8], refs[8:10]
    g0, g1, a_ref, x_all, c_all, gu, down, hid, sems = refs[10:]
    group = xs[0].shape[0]
    units = ws[0].shape[1]
    moves = []

    def move(source, target):
        moves.append(pltpu.make_async_copy(source, target, sems.at[len(moves)]))
        moves[-1].start()

    for p, w in enumerate(ws):
        for m in range(2):
            move(w.at[m], gu.at[pl.ds((2 * p + m) * units, units)])
        move(w.at[2], down.at[pl.ds(p * units, units)])
    for i in range(4):
        move(xs[i], x_all.at[pl.ds(i * group, group)])
        move(cs[i], c_all.at[pl.ds(i * group, group)])
    for copy in moves[:10]:
        copy.wait()
    tokens = 4 * group
    for t in range(tokens // TILE):
        if t * TILE == 2 * group:
            for copy in moves[10:]:
                copy.wait()
        rows = slice(t * TILE, (t + 1) * TILE)
        z = lax.dot_general(gu[...], x_all[rows], NT, preferred_element_type=F32)
        gh = lax.dot_general(down[...], c_all[rows], NT, preferred_element_type=F32)
        for p in range(2):
            gate = z[2 * p * units : (2 * p + 1) * units]
            up = z[(2 * p + 1) * units : (2 * p + 2) * units]
            grad = gh[p * units : (p + 1) * units]
            sg = 1.0 / (1.0 + jnp.exp(-gate))
            silu = gate * sg
            hid[p * units : (p + 1) * units, rows] = (silu * up).astype(BF16)
            slope = sg + silu * (1.0 - sg)
            a_ref[2 * p * units : (2 * p + 1) * units, rows] = (grad * up * slope).astype(BF16)
            a_ref[(2 * p + 1) * units : (2 * p + 2) * units, rows] = (grad * silu).astype(BF16)
    width = x_all.shape[1]
    for n in range(width // TILE):
        cols = slice(n * TILE, (n + 1) * TILE)
        d_gu = jnp.dot(a_ref[...], x_all[:, cols], preferred_element_type=F32).astype(BF16)
        d_down = jnp.dot(hid[...], c_all[:, cols], preferred_element_type=F32).astype(BF16)
        for p, g in enumerate((g0, g1)):
            for m in range(2):
                g[m, :, cols] = d_gu[(2 * p + m) * units : (2 * p + m + 1) * units]
            g[2, :, cols] = d_down[p * units : (p + 1) * units]


def grads(xs, cs, ws):
    group, width = xs[0].shape
    units = ws[0].shape[1]
    tokens = 4 * group
    return pl.pallas_call(
        grads_kernel,
        out_shape=[jax.ShapeDtypeStruct(w.shape, BF16) for w in ws]
        + [jax.ShapeDtypeStruct((4 * units, tokens), BF16)],
        in_specs=[pl.BlockSpec(memory_space=pl.ANY)] * 10,
        out_specs=[pl.BlockSpec(memory_space=pltpu.VMEM)] * 3,
        scratch_shapes=[
            pltpu.VMEM((tokens, width), BF16),
            pltpu.VMEM((tokens, width), BF16),
            pltpu.VMEM((4 * units, width), BF16),
            pltpu.VMEM((2 * units, width), BF16),
            pltpu.VMEM((2 * units, tokens), BF16),
            pltpu.SemaphoreType.DMA((14,)),
        ],
        compiler_params=pltpu.CompilerParams(vmem_limit_bytes=32 * 1024 * 1024),
        cost_estimate=pl.CostEstimate(
            flops=12 * tokens * width * 2 * units,
            bytes_accessed=4 * tokens * width + 24 * units * width + 8 * units * tokens,
            transcendentals=4 * tokens * units,
        ),
    )(*xs, *cs, *ws)


def input_kernel(a0, a1, w0, w1, w2, w3, own_ref, z_ref, pair_ref, w_all, sems):
    units = w0.shape[1]
    moves = []
    for p, w in enumerate((w0, w1, w2, w3)):
        for m in range(2):
            moves.append(
                pltpu.make_async_copy(
                    w.at[m], w_all.at[pl.ds((2 * p + m) * units, units)], sems.at[2 * p + m]
                )
            )
            moves[-1].start()
    for copy in moves:
        copy.wait()
    half = 4 * units
    group = own_ref.shape[0]
    for i in range(4):
        cols = slice(i * group, (i + 1) * group)
        total = lax.dot_general(a0[:, cols], w_all[:half], TN, preferred_element_type=F32)
        total = total + lax.dot_general(a1[:, cols], w_all[half:], TN, preferred_element_type=F32)
        if i == 0:
            own_ref[...] = total
        elif i == 2:
            z_ref[...] = total
        else:
            pair_ref[i // 2] = total.astype(BF16)


def input_parts(a0, a1, ws):
    units, width = ws[0].shape[1:]
    group = a0.shape[1] // 4
    vmem = pl.BlockSpec(memory_space=pltpu.VMEM)
    return pl.pallas_call(
        input_kernel,
        out_shape=[
            jax.ShapeDtypeStruct((group, width), F32),
            jax.ShapeDtypeStruct((group, width), F32),
            jax.ShapeDtypeStruct((2, group, width), BF16),
        ],
        in_specs=[vmem] * 2 + [pl.BlockSpec(memory_space=pl.ANY)] * 4,
        out_specs=[vmem] * 3,
        scratch_shapes=[pltpu.VMEM((8 * units, width), BF16), pltpu.SemaphoreType.DMA((8,))],
        compiler_params=pltpu.CompilerParams(vmem_limit_bytes=32 * 1024 * 1024),
        cost_estimate=pl.CostEstimate(
            flops=64 * units * width * group,
            bytes_accessed=16 * units * width + 64 * units * group + 12 * group * width,
            transcendentals=0,
        ),
    )(a0, a1, *ws)


def body(activations, cotangent, gate_up, down_proj):
    x_z, c_z = swap_near(activations, Z), swap_near(cotangent, Z)
    xs = [activations, swap_core(activations), x_z, swap_core(x_z)]
    cs = [cotangent, swap_core(cotangent), c_z, swap_core(c_z)]

    message = jnp.concatenate([gate_up.transpose(1, 0, 2), down_proj[None]], axis=0)
    j0, r0 = gather(message, Y, X)
    j1, r1 = gather(swap_wrap(message, Z), X, Y)

    g_r0, g_r1, a_r = grads(xs, cs, [r0, r1])
    back0, back1 = swap_second(g_r0, X), swap_second(g_r1, Y)
    g_j0, g_j1, a_j = grads(xs, cs, [j0, j1])

    own, z_part, pair = input_parts(a_r, a_j, [r0, r1, j0, j1])
    got = swap_core(pair)
    mine = own + got[0].astype(F32)
    z_part = (z_part + got[1].astype(F32)).astype(BF16)
    grad_input = (mine + swap_near(z_part, Z).astype(F32)).astype(BF16)

    rows0 = reduce(g_j0, back0, Y, X)
    rows1 = reduce(g_j1, back1, X, Y).astype(BF16)
    grad_weights = (rows0 + swap_wrap(rows1, Z).astype(F32)).transpose(1, 0, 2)
    return (grad_input, grad_weights)


def solution(mesh):
    in_specs = (
        P(("node", "local"), None),
        P(("node", "local"), None),
        P(("node", "local"), None, None),
        P(("node", "local"), None),
    )
    out_specs = (P(("node", "local"), None), P(("node", "local"), None, None))
    return jax.shard_map(body, mesh=mesh, in_specs=in_specs, out_specs=out_specs, check_vma=False)
```

time: 946 us -> 129 us (0.14); the launches traced: 934 us -> 127 us
  waiting for transfers between devices: 555 us -> 56.4 us
  local copies, waits for them, and re-layouts: 174 us -> 1.17 us
  other arithmetic: 112 us -> 5.65 us
  matrix products: 56.3 us -> 0 us
  Pallas kernels: 0 us -> 26.8 us
  starting transfers between devices: 22.2 us -> 36.2 us
  between operations: 14.5 us -> 0.92 us
    all_gather x2 -> x0, waiting for transfers between devices: 405 us -> none  [the longest x1 203 us: body(): lax.all_gather(down_proj, ('node', 'local'), axis=0, tiled=True)]
    all_to_all x4 -> x0, waiting for transfers between devices: 148 us -> none  [the longest x1 148 us: body(): lax.all_to_all(levels, 'local', split_axis=1, concat_axis=1, tiled=True)]
    div x4 -> x0, local copies, waits for them, and re-layouts: 60 us -> none  [quantize(): blocks / scales.astype(jnp.float32)[..., None]]
    mul x4 -> x0, local copies, waits for them, and re-layouts: 59.1 us -> none  [restore(): return (blocks * scales.astype(jnp.float32)[..., None]).reshape(layout)]
    reduce_max x2 -> x0, other arithmetic: 57.4 us -> none  [quantize(): scales = (jnp.max(jnp.abs(blocks), axis=-1) + EPS).astype(jnp.bfloat16)]
    ppermute x0 -> x26, waiting for transfers between devices: none -> 56.4 us  [the longest x21 54.1 us: swap(): return lax.ppermute(value, AXES, pairs)]
    dot_general x8 -> x0, matrix products: 56.3 us -> none  [the longest x1 10.6 us: body(): jnp.dot(hidden.T, cotangent, preferred_element_type=jnp.float32)]
    unnamed x23 -> x10, local copies, waits for them, and re-layouts: 45.4 us -> 0.99 us
  transfers between devices with their start and end apart: 6 -> 26, of which waited for: 4 -> 13; matrix products, arithmetic and copies ran while one was open for 19% -> 3% of each run, Pallas kernels for 0% -> 13%
where the time goes in v1:
time: 129 us; the launch traced here: 127 us
  waiting for transfers between devices  56.4 us (44%)
  starting transfers between devices  36.2 us (28%)
  Pallas kernels  26.8 us (21%)
  other arithmetic  5.65 us (4%)
    ppermute x21, waiting for transfers between devices, swap(): return lax.ppermute(value, AXES, pairs)  54.1 us
    ppermute x21, starting transfers between devices, swap(): return lax.ppermute(value, AXES, pairs)  35.6 us
    pallas_call x2, Pallas kernels, grads(): pl.pallas_call(grads_kernel, out_shape=[jax.ShapeDtypeStruct(w.shape, BF1...  20.1 us
    pallas_call x1, Pallas kernels, input_parts(): pl.pallas_call(input_kernel, out_shape=[jax.ShapeDtypeStruct((group, widt...  6.64 us
  transfers between devices with their start and end apart: 26, of which 13 were waited for; matrix products, arithmetic and copies ran while one was open for 3% of the time, Pallas kernels for 13%

profile of v1, /device:TPU:2, one launch (start us, length us, event | category | flops | bytes accessed | tf_op | source)
XLA Modules:
  0.0 127.1 jit_solution(14741312573811806587)
XLA Ops:
  2.4 4.1 %collective-permute-start.10 = (bf16[3,24,1024]{2,1,0:T(8,128)(2,1)S(1)}, bf16[3,24,1024]{2,1,0:T(8,128)(2,1)S(1)}, u32[]{:S(2)}, u32[]{:S(2)}) collective-permute-start(bf16[3,24,1024]{2,1,0:T(8,128)(2,1)S(1)} %pad_maximum_fusion.5), channel_id=1, source_target_pairs={{0,12},{1,13},{2,14},{3,15},{4,8},{5,9},{6,10},{7,11},{8,4},{9,5},... | collective-permute-start | bytes 442376 | tf_op jit(solution)/shard_map/ppermute | solution.py:33
  8.1 2.3 %collective-permute-done.10 = bf16[3,24,1024]{2,1,0:T(8,128)(2,1)S(1)} collective-permute-done((bf16[3,24,1024]{2,1,0:T(8,128)(2,1)S(1)}, bf16[3,24,1024]{2,1,0:T(8,128)(2,1)S(1)}, u32[]{:S(2)}, u32[]{:S(2)}) %collective-permute-start.10) | collective-permute-done | bytes 147488 | tf_op jit(solution)/shard_map/ppermute | solution.py:33
  12.5 3.1 %collective-permute-start.7 = (bf16[3,48,1024]{2,1,0:T(8,128)(2,1)S(1)}, bf16[3,48,1024]{2,1,0:T(8,128)(2,1)S(1)}, u32[]{:S(2)}, u32[]{:S(2)}) collective-permute-start(bf16[3,48,1024]{2,1,0:T(8,128)(2,1)S(1)} %pad_maximum_fusion.3), channel_id=1, source_target_pairs={{0,48},{1,17},{2,50},{3,19},{4,52},{5,21},{6,54},{7,23},{8,56},{9,... | collective-permute-start | bytes 884744 | tf_op jit(solution)/shard_map/ppermute | solution.py:33
  17.2 3.3 %collective-permute-done.7 = bf16[3,48,1024]{2,1,0:T(8,128)(2,1)S(1)} collective-permute-done((bf16[3,48,1024]{2,1,0:T(8,128)(2,1)S(1)}, bf16[3,48,1024]{2,1,0:T(8,128)(2,1)S(1)}, u32[]{:S(2)}, u32[]{:S(2)}) %collective-permute-start.7) | collective-permute-done | bytes 294944 | tf_op jit(solution)/shard_map/ppermute | solution.py:33
  21.3 2.6 %collective-permute-done.12 = bf16[3,48,1024]{2,1,0:T(8,128)(2,1)S(1)} collective-permute-done((bf16[3,48,1024]{2,1,0:T(8,128)(2,1)S(1)}, bf16[3,48,1024]{2,1,0:T(8,128)(2,1)S(1)}, u32[]{:S(2)}, u32[]{:S(2)}) %collective-permute-start.12) | collective-permute-done | bytes 294944 | tf_op jit(solution)/shard_map/ppermute | solution.py:33
  24.0 2.0 %collective-permute-start.13 = (bf16[3,96,1024]{2,1,0:T(8,128)(2,1)S(1)}, bf16[3,96,1024]{2,1,0:T(8,128)(2,1)S(1)}, u32[]{:S(2)}, u32[]{:S(2)}) collective-permute-start(bf16[3,96,1024]{2,1,0:T(8,128)(2,1)S(1)} %pad_maximum_fusion.2), channel_id=1, source_target_pairs={{0,16},{1,49},{2,18},{3,51},{4,20},{5,53},{6,22},{7,55},{8,24},{9,... | collective-permute-start | bytes 1769480 | tf_op jit(solution)/shard_map/ppermute | solution.py:33
  28.1 2.4 %collective-permute-done.8 = bf16[3,96,1024]{2,1,0:T(8,128)(2,1)S(1)} collective-permute-done((bf16[3,96,1024]{2,1,0:T(8,128)(2,1)S(1)}, bf16[3,96,1024]{2,1,0:T(8,128)(2,1)S(1)}, u32[]{:S(2)}, u32[]{:S(2)}) %collective-permute-start.8) | collective-permute-done | bytes 589856 | tf_op jit(solution)/shard_map/ppermute | solution.py:33
  32.2 2.7 %collective-permute-done.13 = bf16[3,96,1024]{2,1,0:T(8,128)(2,1)S(1)} collective-permute-done((bf16[3,96,1024]{2,1,0:T(8,128)(2,1)S(1)}, bf16[3,96,1024]{2,1,0:T(8,128)(2,1)S(1)}, u32[]{:S(2)}, u32[]{:S(2)}) %collective-permute-start.13) | collective-permute-done | bytes 589856 | tf_op jit(solution)/shard_map/ppermute | solution.py:33
  34.9 3.1 %collective-permute-start.14 = (bf16[3,192,1024]{2,1,0:T(8,128)(2,1)S(1)}, bf16[3,192,1024]{2,1,0:T(8,128)(2,1)S(1)}, u32[]{:S(2)}, u32[]{:S(2)}) collective-permute-start(bf16[3,192,1024]{2,1,0:T(8,128)(2,1)S(1)} %constant_dynamic-update-slice_fusion.refs_9_.w3), channel_id=1, source_target_pairs={{0,48},{1,17},{2,50},{3,19},{4,52},{5,21},{6,54},{7,23},{8,56},{9,... | collective-permute-start | bytes 3538952 | tf_op jit(solution)/shard_map/ppermute | solution.py:33
  38.0 8.5 %collective-permute-done.1.refs_2_ = bf16[384,1024]{1,0:T(8,128)(2,1)S(1)} collective-permute-done((bf16[384,1024]{1,0:T(8,128)(2,1)S(1)}, bf16[384,1024]{1,0:T(8,128)(2,1)S(1)}, u32[]{:S(2)}, u32[]{:S(2)}) %collective-permute-start.1) | collective-permute-done | bytes 786464 | tf_op jit(solution)/shard_map/ppermute | solution.py:33
  47.0 11.8 %collective-permute-done.4.refs_6_ = bf16[384,1024]{1,0:T(8,128)(2,1)S(1)} collective-permute-done((bf16[384,1024]{1,0:T(8,128)(2,1)S(1)}, bf16[384,1024]{1,0:T(8,128)(2,1)S(1)}, u32[]{:S(2)}, u32[]{:S(2)}) %collective-permute-start.4) | collective-permute-done | bytes 786464 | tf_op jit(solution)/shard_map/ppermute | solution.py:33
  58.8 2.3 %collective-permute-done.5.refs_7_ = bf16[384,1024]{1,0:T(8,128)(2,1)S(1)} collective-permute-done((bf16[384,1024]{1,0:T(8,128)(2,1)S(1)}, bf16[384,1024]{1,0:T(8,128)(2,1)S(1)}, u32[]{:S(2)}, u32[]{:S(2)}) %collective-permute-start.5) | collective-permute-done | bytes 786464 | tf_op jit(solution)/shard_map/ppermute | solution.py:53
  61.1 10.1 %shard_map.59 = (bf16[3,192,1024]{2,1,0:T(8,128)(2,1)S(1)}, bf16[3,192,1024]{2,1,0:T(8,128)(2,1)S(1)}, bf16[768,1536]{1,0:T(8,128)(2,1)S(1)}) custom-call(bf16[384,1024]{1,0:T(8,128)(2,1)S(1)} %copy-done, bf16[384,1024]{1,0:T(8,128)(2,1)S(1)} %collective-permute-done.refs_1_, bf16[384,1024]{1,0:T(8,128)(2,1)S(1)} %collective-permute-done.1.refs_2_, ...), custom_call_target="tpu_custom_call" | custom-call | flops 7247757312 | bytes 13369344 | tf_op jit(solution)/shard_map/pallas_call | solution.py:134
  71.2 2.4 %collective-permute-start.17 = (bf16[3,192,1024]{2,1,0:T(8,128)(2,1)S(1)}, bf16[3,192,1024]{2,1,0:T(8,128)(2,1)S(1)}, u32[]{:S(2)}, u32[]{:S(2)}) collective-permute-start(bf16[3,192,1024]{2,1,0:T(8,128)(2,1)S(1)} %get-tuple-element.17), channel_id=1, source_target_pairs={{0,66},{1,3},{2,64},{3,1},{4,70},{5,7},{6,68},{7,5},{8,74},{9,11},... | collective-permute-start | bytes 3538952 | tf_op jit(solution)/shard_map/ppermute | solution.py:33
  74.0 10.1 %shard_map.60 = (bf16[3,192,1024]{2,1,0:T(8,128)(2,1)S(1)}, bf16[3,192,1024]{2,1,0:T(8,128)(2,1)S(1)}, bf16[768,1536]{1,0:T(8,128)(2,1)S(1)}) custom-call(bf16[384,1024]{1,0:T(8,128)(2,1)S(1)} %copy-done, bf16[384,1024]{1,0:T(8,128)(2,1)S(1)} %collective-permute-done.refs_1_, bf16[384,1024]{1,0:T(8,128)(2,1)S(1)} %collective-permute-done.1.refs_2_, ...), custom_call_target="tpu_custom_call" | custom-call | flops 7247757312 | bytes 13369344 | tf_op jit(solution)/shard_map/pallas_call | solution.py:134
  84.0 6.6 %shard_map.61 = (f32[384,1024]{1,0:T(8,128)S(1)}, f32[384,1024]{1,0:T(8,128)S(1)}, bf16[2,384,1024]{2,1,0:T(8,128)(2,1)S(1)}) custom-call(bf16[768,1536]{1,0:T(8,128)(2,1)S(1)} %get-tuple-element.11.a0, bf16[768,1536]{1,0:T(8,128)(2,1)S(1)} %get-tuple-element.12.a1, bf16[3,192,1024]{2,1,0:T(8,128)(2,1)S(1)} %collective-permute-done.9.refs_8_.w0, ...), custom_call_target="tpu_custom_call" | custom-call | flops 4831838208 | bytes 12582912 | tf_op jit(solution)/shard_map/pallas_call | solution.py:188
  91.3 2.6 %collective-permute-start.18 = (bf16[3,96,1024]{2,1,0:T(8,128)(2,1)S(1)}, bf16[3,96,1024]{2,1,0:T(8,128)(2,1)S(1)}, u32[]{:S(2)}, u32[]{:S(2)}) collective-permute-start(bf16[3,96,1024]{2,1,0:T(8,128)(2,1)S(1)} %slice.59), channel_id=1, source_target_pairs={{0,2},{1,67},{2,0},{3,65},{4,6},{5,71},{6,4},{7,69},{8,10},{9,75},... | collective-permute-start | bytes 1769480 | tf_op jit(solution)/shard_map/ppermute | solution.py:33
  94.8 7.0 %collective-permute-done.18 = bf16[3,96,1024]{2,1,0:T(8,128)(2,1)S(1)} collective-permute-done((bf16[3,96,1024]{2,1,0:T(8,128)(2,1)S(1)}, bf16[3,96,1024]{2,1,0:T(8,128)(2,1)S(1)}, u32[]{:S(2)}, u32[]{:S(2)}) %collective-permute-start.18) | collective-permute-done | bytes 589856 | tf_op jit(solution)/shard_map/ppermute | solution.py:33
  102.1 2.9 %collective-permute-start.19 = (bf16[3,48,1024]{2,1,0:T(8,128)(2,1)S(1)}, bf16[3,48,1024]{2,1,0:T(8,128)(2,1)S(1)}, u32[]{:S(2)}, u32[]{:S(2)}) collective-permute-start(bf16[3,48,1024]{2,1,0:T(8,128)(2,1)S(1)} %slice.61), channel_id=1, source_target_pairs={{0,48},{1,17},{2,50},{3,19},{4,52},{5,21},{6,54},{7,23},{8,56},{9,... | collective-permute-start | bytes 884744 | tf_op jit(solution)/shard_map/ppermute | solution.py:33
  106.0 6.1 %collective-permute-done.23 = bf16[3,48,1024]{2,1,0:T(8,128)(2,1)S(1)} collective-permute-done((bf16[3,48,1024]{2,1,0:T(8,128)(2,1)S(1)}, bf16[3,48,1024]{2,1,0:T(8,128)(2,1)S(1)}, u32[]{:S(2)}, u32[]{:S(2)}) %collective-permute-start.23) | collective-permute-done | bytes 294944 | tf_op jit(solution)/shard_map/ppermute | solution.py:33
  112.2 3.3 %collective-permute-start.24 = (bf16[3,24,1024]{2,1,0:T(8,128)(2,1)S(1)}, bf16[3,24,1024]{2,1,0:T(8,128)(2,1)S(1)}, u32[]{:S(2)}, u32[]{:S(2)}) collective-permute-start(bf16[3,24,1024]{2,1,0:T(8,128)(2,1)S(1)} %slice.69), channel_id=1, source_target_pairs={{0,2},{1,67},{2,0},{3,65},{4,6},{5,71},{6,4},{7,69},{8,10},{9,75},... | collective-permute-start | bytes 442376 | tf_op jit(solution)/shard_map/ppermute | solution.py:33
  115.7 2.9 %collective-permute-done.24 = bf16[3,24,1024]{2,1,0:T(8,128)(2,1)S(1)} collective-permute-done((bf16[3,24,1024]{2,1,0:T(8,128)(2,1)S(1)}, bf16[3,24,1024]{2,1,0:T(8,128)(2,1)S(1)}, u32[]{:S(2)}, u32[]{:S(2)}) %collective-permute-start.24) | collective-permute-done | bytes 147488 | tf_op jit(solution)/shard_map/ppermute | solution.py:33
  118.6 2.7 %collective-permute-start.25 = (bf16[3,24,1024]{2,1,0:T(8,128)(2,1)S(1)}, bf16[3,24,1024]{2,1,0:T(8,128)(2,1)S(1)}, u32[]{:S(2)}, u32[]{:S(2)}) collective-permute-start(bf16[3,24,1024]{2,1,0:T(8,128)(2,1)S(1)} %add_convert_fusion.6), channel_id=1, source_target_pairs={{0,12},{1,13},{2,14},{3,15},{4,8},{5,9},{6,10},{7,11},{8,4},{9,5},... | collective-permute-start | bytes 442376 | tf_op jit(solution)/shard_map/ppermute | solution.py:33
  121.4 3.7 %collective-permute-done.25 = bf16[3,24,1024]{2,1,0:T(8,128)(2,1)S(1)} collective-permute-done((bf16[3,24,1024]{2,1,0:T(8,128)(2,1)S(1)}, bf16[3,24,1024]{2,1,0:T(8,128)(2,1)S(1)}, u32[]{:S(2)}, u32[]{:S(2)}) %collective-permute-start.25) | collective-permute-done | bytes 147488 | tf_op jit(solution)/shard_map/ppermute | solution.py:33
  (64 shorter events, 17.5 us)
Async XLA Ops:
  2.4 8.0 %collective-permute-start.10 = (bf16[3,24,1024]{2,1,0:T(8,128)(2,1)S(1)}, bf16[3,24,1024]{2,1,0:T(8,128)(2,1)S(1)}, u32[]{:S(2)}, u32[]{:S(2)}) collective-permute-start(bf16[3,24,1024]{2,1,0:T(8,128)(2,1)S(1)} %pad_maximum_fusion.5), channel_id=1, source_target_pairs={{0,12},{1,13},{2,14},{3,15},{4,8},{5,9},{6,10},{7,11},{8,4},{9,5},... | collective-permute-start | bytes 442376 | tf_op jit(solution)/shard_map/ppermute | solution.py:33
  10.4 5.2 %collective-permute-start.11 = (bf16[3,24,1024]{2,1,0:T(8,128)(2,1)S(1)}, bf16[3,24,1024]{2,1,0:T(8,128)(2,1)S(1)}, u32[]{:S(2)}, u32[]{:S(2)}) collective-permute-start(bf16[3,24,1024]{2,1,0:T(8,128)(2,1)S(1)} %collective-permute-done.10), channel_id=1, source_target_pairs={{0,2},{1,67},{2,0},{3,65},{4,6},{5,71},{6,4},{7,69},{8,10},{9,75},... | collective-permute-start | bytes 442376 | tf_op jit(solution)/shard_map/ppermute | solution.py:33
  12.5 8.0 %collective-permute-start.7 = (bf16[3,48,1024]{2,1,0:T(8,128)(2,1)S(1)}, bf16[3,48,1024]{2,1,0:T(8,128)(2,1)S(1)}, u32[]{:S(2)}, u32[]{:S(2)}) collective-permute-start(bf16[3,48,1024]{2,1,0:T(8,128)(2,1)S(1)} %pad_maximum_fusion.3), channel_id=1, source_target_pairs={{0,48},{1,17},{2,50},{3,19},{4,52},{5,21},{6,54},{7,23},{8,56},{9,... | collective-permute-start | bytes 884744 | tf_op jit(solution)/shard_map/ppermute | solution.py:33
  15.6 8.3 %collective-permute-start.12 = (bf16[3,48,1024]{2,1,0:T(8,128)(2,1)S(1)}, bf16[3,48,1024]{2,1,0:T(8,128)(2,1)S(1)}, u32[]{:S(2)}, u32[]{:S(2)}) collective-permute-start(bf16[3,48,1024]{2,1,0:T(8,128)(2,1)S(1)} %pad_maximum_fusion.4), channel_id=1, source_target_pairs={{0,66},{1,3},{2,64},{3,1},{4,70},{5,7},{6,68},{7,5},{8,74},{9,11},... | collective-permute-start | bytes 884744 | tf_op jit(solution)/shard_map/ppermute | solution.py:33
  20.5 10.0 %collective-permute-start.8 = (bf16[3,96,1024]{2,1,0:T(8,128)(2,1)S(1)}, bf16[3,96,1024]{2,1,0:T(8,128)(2,1)S(1)}, u32[]{:S(2)}, u32[]{:S(2)}) collective-permute-start(bf16[3,96,1024]{2,1,0:T(8,128)(2,1)S(1)} %pad_maximum_fusion.1), channel_id=1, source_target_pairs={{0,2},{1,67},{2,0},{3,65},{4,6},{5,71},{6,4},{7,69},{8,10},{9,75},... | collective-permute-start | bytes 1769480 | tf_op jit(solution)/shard_map/ppermute | solution.py:33
  24.0 10.9 %collective-permute-start.13 = (bf16[3,96,1024]{2,1,0:T(8,128)(2,1)S(1)}, bf16[3,96,1024]{2,1,0:T(8,128)(2,1)S(1)}, u32[]{:S(2)}, u32[]{:S(2)}) collective-permute-start(bf16[3,96,1024]{2,1,0:T(8,128)(2,1)S(1)} %pad_maximum_fusion.2), channel_id=1, source_target_pairs={{0,16},{1,49},{2,18},{3,51},{4,20},{5,53},{6,22},{7,55},{8,24},{9,... | collective-permute-start | bytes 1769480 | tf_op jit(solution)/shard_map/ppermute | solution.py:33
  26.0 20.5 %collective-permute-start.1 = (bf16[384,1024]{1,0:T(8,128)(2,1)S(1)}, bf16[384,1024]{1,0:T(8,128)(2,1)S(1)}, u32[]{:S(2)}, u32[]{:S(2)}) collective-permute-start(bf16[384,1024]{1,0:T(8,128)(2,1)S(1)} %copy-done), channel_id=1, source_target_pairs={{0,4},{1,5},{2,6},{3,7},{4,0},{5,1},{6,2},{7,3},{8,12},{9,13},{10,... | collective-permute-start | bytes 2359304 | tf_op jit(solution)/shard_map/ppermute | solution.py:33
  26.0 20.5 %collective-permute-start = (bf16[384,1024]{1,0:T(8,128)(2,1)S(1)}, bf16[384,1024]{1,0:T(8,128)(2,1)S(1)}, u32[]{:S(2)}, u32[]{:S(2)}) collective-permute-start(bf16[384,1024]{1,0:T(8,128)(2,1)S(1)} %copy-done), channel_id=1, source_target_pairs={{0,1},{1,0},{2,3},{3,2},{4,5},{5,4},{6,7},{7,6},{8,9},{9,8},{10,11... | collective-permute-start | bytes 2359304 | tf_op jit(solution)/shard_map/ppermute | solution.py:53
  26.1 32.7 %collective-permute-start.4 = (bf16[384,1024]{1,0:T(8,128)(2,1)S(1)}, bf16[384,1024]{1,0:T(8,128)(2,1)S(1)}, u32[]{:S(2)}, u32[]{:S(2)}) collective-permute-start(bf16[384,1024]{1,0:T(8,128)(2,1)S(1)} %copy-done.1), channel_id=1, source_target_pairs={{0,4},{1,5},{2,6},{3,7},{4,0},{5,1},{6,2},{7,3},{8,12},{9,13},{10,... | collective-permute-start | bytes 2359304 | tf_op jit(solution)/shard_map/ppermute | solution.py:33
  30.6 30.5 %collective-permute-start.9 = (bf16[3,192,1024]{2,1,0:T(8,128)(2,1)S(1)}, bf16[3,192,1024]{2,1,0:T(8,128)(2,1)S(1)}, u32[]{:S(2)}, u32[]{:S(2)}) collective-permute-start(bf16[3,192,1024]{2,1,0:T(8,128)(2,1)S(1)} %pad_maximum_fusion.refs_8_.w2), channel_id=1, source_target_pairs={{0,66},{1,3},{2,64},{3,1},{4,70},{5,7},{6,68},{7,5},{8,74},{9,11},... | collective-permute-start | bytes 3538952 | tf_op jit(solution)/shard_map/ppermute | solution.py:33
  34.9 26.2 %collective-permute-start.14 = (bf16[3,192,1024]{2,1,0:T(8,128)(2,1)S(1)}, bf16[3,192,1024]{2,1,0:T(8,128)(2,1)S(1)}, u32[]{:S(2)}, u32[]{:S(2)}) collective-permute-start(bf16[3,192,1024]{2,1,0:T(8,128)(2,1)S(1)} %constant_dynamic-update-slice_fusion.refs_9_.w3), channel_id=1, source_target_pairs={{0,48},{1,17},{2,50},{3,19},{4,52},{5,21},{6,54},{7,23},{8,56},{9,... | collective-permute-start | bytes 3538952 | tf_op jit(solution)/shard_map/ppermute | solution.py:33
  46.5 12.3 %collective-permute-start.3 = (bf16[384,1024]{1,0:T(8,128)(2,1)S(1)}, bf16[384,1024]{1,0:T(8,128)(2,1)S(1)}, u32[]{:S(2)}, u32[]{:S(2)}) collective-permute-start(bf16[384,1024]{1,0:T(8,128)(2,1)S(1)} %copy-done.1), channel_id=1, source_target_pairs={{0,1},{1,0},{2,3},{3,2},{4,5},{5,4},{6,7},{7,6},{8,9},{9,8},{10,11... | collective-permute-start | bytes 2359304 | tf_op jit(solution)/shard_map/ppermute | solution.py:53
  46.5 12.3 %collective-permute-start.2 = (bf16[384,1024]{1,0:T(8,128)(2,1)S(1)}, bf16[384,1024]{1,0:T(8,128)(2,1)S(1)}, u32[]{:S(2)}, u32[]{:S(2)}) collective-permute-start(bf16[384,1024]{1,0:T(8,128)(2,1)S(1)} %collective-permute-done.1.refs_2_), channel_id=1, source_target_pairs={{0,1},{1,0},{2,3},{3,2},{4,5},{5,4},{6,7},{7,6},{8,9},{9,8},{10,11... | collective-permute-start | bytes 2359304 | tf_op jit(solution)/shard_map/ppermute | solution.py:53
  71.2 19.6 %collective-permute-start.17 = (bf16[3,192,1024]{2,1,0:T(8,128)(2,1)S(1)}, bf16[3,192,1024]{2,1,0:T(8,128)(2,1)S(1)}, u32[]{:S(2)}, u32[]{:S(2)}) collective-permute-start(bf16[3,192,1024]{2,1,0:T(8,128)(2,1)S(1)} %get-tuple-element.17), channel_id=1, source_target_pairs={{0,66},{1,3},{2,64},{3,1},{4,70},{5,7},{6,68},{7,5},{8,74},{9,11},... | collective-permute-start | bytes 3538952 | tf_op jit(solution)/shard_map/ppermute | solution.py:33
  73.6 20.4 %collective-permute-start.21 = (bf16[3,192,1024]{2,1,0:T(8,128)(2,1)S(1)}, bf16[3,192,1024]{2,1,0:T(8,128)(2,1)S(1)}, u32[]{:S(2)}, u32[]{:S(2)}) collective-permute-start(bf16[3,192,1024]{2,1,0:T(8,128)(2,1)S(1)} %get-tuple-element.19), channel_id=1, source_target_pairs={{0,48},{1,17},{2,50},{3,19},{4,52},{5,21},{6,54},{7,23},{8,56},{9,... | collective-permute-start | bytes 3538952 | tf_op jit(solution)/shard_map/ppermute | solution.py:33
  90.7 14.7 %collective-permute-start.15 = (bf16[2,384,1024]{2,1,0:T(8,128)(2,1)S(1)}, bf16[2,384,1024]{2,1,0:T(8,128)(2,1)S(1)}, u32[]{:S(2)}, u32[]{:S(2)}) collective-permute-start(bf16[2,384,1024]{2,1,0:T(8,128)(2,1)S(1)} %get-tuple-element.14), channel_id=1, source_target_pairs={{0,1},{1,0},{2,3},{3,2},{4,5},{5,4},{6,7},{7,6},{8,9},{9,8},{10,11... | collective-permute-start | bytes 4718600 | tf_op jit(solution)/shard_map/ppermute | solution.py:53
  91.3 10.5 %collective-permute-start.18 = (bf16[3,96,1024]{2,1,0:T(8,128)(2,1)S(1)}, bf16[3,96,1024]{2,1,0:T(8,128)(2,1)S(1)}, u32[]{:S(2)}, u32[]{:S(2)}) collective-permute-start(bf16[3,96,1024]{2,1,0:T(8,128)(2,1)S(1)} %slice.59), channel_id=1, source_target_pairs={{0,2},{1,67},{2,0},{3,65},{4,6},{5,71},{6,4},{7,69},{8,10},{9,75},... | collective-permute-start | bytes 1769480 | tf_op jit(solution)/shard_map/ppermute | solution.py:33
  94.5 10.5 %collective-permute-start.22 = (bf16[3,96,1024]{2,1,0:T(8,128)(2,1)S(1)}, bf16[3,96,1024]{2,1,0:T(8,128)(2,1)S(1)}, u32[]{:S(2)}, u32[]{:S(2)}) collective-permute-start(bf16[3,96,1024]{2,1,0:T(8,128)(2,1)S(1)} %slice.65), channel_id=1, source_target_pairs={{0,16},{1,49},{2,18},{3,51},{4,20},{5,53},{6,22},{7,55},{8,24},{9,... | collective-permute-start | bytes 1769480 | tf_op jit(solution)/shard_map/ppermute | solution.py:33
  102.1 13.4 %collective-permute-start.19 = (bf16[3,48,1024]{2,1,0:T(8,128)(2,1)S(1)}, bf16[3,48,1024]{2,1,0:T(8,128)(2,1)S(1)}, u32[]{:S(2)}, u32[]{:S(2)}) collective-permute-start(bf16[3,48,1024]{2,1,0:T(8,128)(2,1)S(1)} %slice.61), channel_id=1, source_target_pairs={{0,48},{1,17},{2,50},{3,19},{4,52},{5,21},{6,54},{7,23},{8,56},{9,... | collective-permute-start | bytes 884744 | tf_op jit(solution)/shard_map/ppermute | solution.py:33
  105.3 6.8 %collective-permute-start.23 = (bf16[3,48,1024]{2,1,0:T(8,128)(2,1)S(1)}, bf16[3,48,1024]{2,1,0:T(8,128)(2,1)S(1)}, u32[]{:S(2)}, u32[]{:S(2)}) collective-permute-start(bf16[3,48,1024]{2,1,0:T(8,128)(2,1)S(1)} %slice.67), channel_id=1, source_target_pairs={{0,66},{1,3},{2,64},{3,1},{4,70},{5,7},{6,68},{7,5},{8,74},{9,11},... | collective-permute-start | bytes 884744 | tf_op jit(solution)/shard_map/ppermute | solution.py:33
  105.6 20.2 %collective-permute-start.16 = (bf16[384,1024]{1,0:T(8,128)(2,1)S(1)}, bf16[384,1024]{1,0:T(8,128)(2,1)S(1)}, u32[]{:S(2)}, u32[]{:S(2)}) collective-permute-start(bf16[384,1024]{1,0:T(8,128)(2,1)S(1)} %fusion), channel_id=1, source_target_pairs={{0,4},{1,5},{2,6},{3,7},{4,0},{5,1},{6,2},{7,3},{8,12},{9,13},{10,... | collective-permute-start | bytes 2359304 | tf_op jit(solution)/shard_map/ppermute | solution.py:33
  112.2 6.4 %collective-permute-start.24 = (bf16[3,24,1024]{2,1,0:T(8,128)(2,1)S(1)}, bf16[3,24,1024]{2,1,0:T(8,128)(2,1)S(1)}, u32[]{:S(2)}, u32[]{:S(2)}) collective-permute-start(bf16[3,24,1024]{2,1,0:T(8,128)(2,1)S(1)} %slice.69), channel_id=1, source_target_pairs={{0,2},{1,67},{2,0},{3,65},{4,6},{5,71},{6,4},{7,69},{8,10},{9,75},... | collective-permute-start | bytes 442376 | tf_op jit(solution)/shard_map/ppermute | solution.py:33
  115.6 5.8 %collective-permute-start.20 = (bf16[3,24,1024]{2,1,0:T(8,128)(2,1)S(1)}, bf16[3,24,1024]{2,1,0:T(8,128)(2,1)S(1)}, u32[]{:S(2)}, u32[]{:S(2)}) collective-permute-start(bf16[3,24,1024]{2,1,0:T(8,128)(2,1)S(1)} %slice.63), channel_id=1, source_target_pairs={{0,16},{1,49},{2,18},{3,51},{4,20},{5,53},{6,22},{7,55},{8,24},{9,... | collective-permute-start | bytes 442376 | tf_op jit(solution)/shard_map/ppermute | solution.py:33
  118.6 6.4 %collective-permute-start.25 = (bf16[3,24,1024]{2,1,0:T(8,128)(2,1)S(1)}, bf16[3,24,1024]{2,1,0:T(8,128)(2,1)S(1)}, u32[]{:S(2)}, u32[]{:S(2)}) collective-permute-start(bf16[3,24,1024]{2,1,0:T(8,128)(2,1)S(1)} %add_convert_fusion.6), channel_id=1, source_target_pairs={{0,12},{1,13},{2,14},{3,15},{4,8},{5,9},{6,10},{7,11},{8,4},{9,5},... | collective-permute-start | bytes 442376 | tf_op jit(solution)/shard_map/ppermute | solution.py:33
  (5 other events, 48.2 us)

commit v2 on v1

v2 whole, which is shorter than its diff:
```python
import jax
import jax.numpy as jnp
from jax import lax
from jax.experimental import pallas as pl
from jax.experimental.pallas import tpu as pltpu
from jax.sharding import PartitionSpec as P

AXES = ("node", "local")
X, Y, Z = 0, 1, 2
RING = 4
DEVICES = 128
TILE = 256
BF16 = jnp.bfloat16
F32 = jnp.float32
NT = (((1,), (1,)), ((), ()))
TN = (((0,), (0,)), ((), ()))


def place(device):
    return [device // 64 * 2 + device // 2 % 2, device // 16 % 4, device // 4 % 4, device % 2]


def index(x, y, z, core):
    return (x // 2) * 64 + y * 16 + z * 4 + (x % 2) * 2 + core


def swap(value, axis, wrap):
    pairs = []
    for device in range(DEVICES):
        there = place(device)
        there[axis] = RING - 1 - there[axis] if wrap(there[3]) else there[axis] ^ 1
        pairs.append((device, index(*there)))
    return lax.ppermute(value, AXES, pairs)


def swap_first(value, axis):
    return swap(value, axis, lambda core: core == 1)


def swap_second(value, axis):
    return swap(value, axis, lambda core: core == 0)


def swap_near(value, axis):
    return swap(value, axis, lambda core: False)


def swap_wrap(value, axis):
    return swap(value, axis, lambda core: True)


def swap_over(value, axis):
    pairs = []
    for device in range(DEVICES):
        there = place(device)
        there[axis] = RING - 1 - there[axis] if there[3] == 1 else there[axis] ^ 1
        there[Z] = RING - 1 - there[Z]
        pairs.append((device, index(*there)))
    return lax.ppermute(value, AXES, pairs)


def swap_core(value):
    return lax.ppermute(value, AXES, [(d, d ^ 1) for d in range(DEVICES)])


def add(a, b):
    return (a.astype(F32) + b.astype(F32)).astype(BF16)


def join(a, b):
    return jnp.concatenate([a, b], axis=1)


def gather(half, swaps):
    for swap_with in swaps[:-1]:
        half = join(half, swap_with(half))
    return half, swaps[-1](half)


def reduce(near, back, swaps):
    near = add(near, back)
    for swap_with in swaps[-2::-1]:
        n = near.shape[1] // 2
        near = add(near[:, :n], swap_with(near[:, n:]))
    return near


def rows_of(refs, start, stop, cols=slice(None)):
    parts = []
    for ref in refs:
        n = ref.shape[0]
        if start < n and stop > 0:
            parts.append(ref[max(start, 0) : min(stop, n), cols])
        start, stop = start - n, stop - n
    return parts[0] if len(parts) == 1 else jnp.concatenate(parts, axis=0)


def grads_kernel(n, *refs):
    xs, cs, ws = refs[:n], refs[n : 2 * n], refs[2 * n : 2 * n + 2]
    g0, g1, a_ref, hid = refs[2 * n + 2 :]
    units, width = ws[0].shape[1:]
    gu = jnp.concatenate([w[m] for w in ws for m in range(2)], axis=0)
    down = jnp.concatenate([w[2] for w in ws], axis=0)
    tokens = hid.shape[1]
    for t in range(tokens // TILE):
        rows = slice(t * TILE, (t + 1) * TILE)
        x = rows_of(xs, t * TILE, (t + 1) * TILE)
        c = rows_of(cs, t * TILE, (t + 1) * TILE)
        z = lax.dot_general(gu, x, NT, preferred_element_type=F32)
        gh = lax.dot_general(down, c, NT, preferred_element_type=F32)
        for p in range(2):
            gate = z[2 * p * units : (2 * p + 1) * units]
            up = z[(2 * p + 1) * units : (2 * p + 2) * units]
            grad = gh[p * units : (p + 1) * units]
            sg = 1.0 / (1.0 + jnp.exp(-gate))
            silu = gate * sg
            hid[p * units : (p + 1) * units, rows] = (silu * up).astype(BF16)
            slope = sg + silu * (1.0 - sg)
            a_ref[2 * p * units : (2 * p + 1) * units, rows] = (grad * up * slope).astype(BF16)
            a_ref[(2 * p + 1) * units : (2 * p + 2) * units, rows] = (grad * silu).astype(BF16)
    for k in range(width // TILE):
        cols = slice(k * TILE, (k + 1) * TILE)
        x = rows_of(xs, 0, tokens, cols)
        c = rows_of(cs, 0, tokens, cols)
        d_gu = jnp.dot(a_ref[...], x, preferred_element_type=F32).astype(BF16)
        d_down = jnp.dot(hid[...], c, preferred_element_type=F32).astype(BF16)
        for p, g in enumerate((g0, g1)):
            for m in range(2):
                g[m, :, cols] = d_gu[(2 * p + m) * units : (2 * p + m + 1) * units]
            g[2, :, cols] = d_down[p * units : (p + 1) * units]


def grads(xs, cs, ws):
    units, width = ws[0].shape[1:]
    tokens = sum(x.shape[0] for x in xs)
    vmem = pl.BlockSpec(memory_space=pltpu.VMEM)

    def kernel(*refs):
        grads_kernel(len(xs), *refs)

    return pl.pallas_call(
        kernel,
        out_shape=[jax.ShapeDtypeStruct(w.shape, BF16) for w in ws]
        + [jax.ShapeDtypeStruct((4 * units, tokens), BF16)],
        in_specs=[vmem] * (2 * len(xs) + 2),
        out_specs=[vmem] * 3,
        scratch_shapes=[pltpu.VMEM((2 * units, tokens), BF16)],
        compiler_params=pltpu.CompilerParams(vmem_limit_bytes=32 * 1024 * 1024),
        cost_estimate=pl.CostEstimate(
            flops=12 * tokens * width * 2 * units,
            bytes_accessed=4 * tokens * width + 24 * units * width + 8 * units * tokens,
            transcendentals=4 * tokens * units,
        ),
    )(*xs, *cs, *ws)


def input_kernel(a0, a1, w0, w1, w2, w3, own_ref, z_ref, pair_ref):
    w_all = jnp.concatenate([w[m] for w in (w0, w1, w2, w3) for m in range(2)], axis=0)
    group = own_ref.shape[0]
    for i in range(4):
        cols = slice(i * group, (i + 1) * group)
        a = jnp.concatenate([a0[:, cols], a1[:, cols]], axis=0)
        total = lax.dot_general(a, w_all, TN, preferred_element_type=F32)
        if i == 0:
            own_ref[...] = total
        elif i == 2:
            z_ref[...] = total
        else:
            pair_ref[i // 2] = total.astype(BF16)


def input_parts(a0, a1, ws):
    units, width = ws[0].shape[1:]
    group = a0.shape[1] // 4
    vmem = pl.BlockSpec(memory_space=pltpu.VMEM)
    return pl.pallas_call(
        input_kernel,
        out_shape=[
            jax.ShapeDtypeStruct((group, width), F32),
            jax.ShapeDtypeStruct((group, width), F32),
            jax.ShapeDtypeStruct((2, group, width), BF16),
        ],
        in_specs=[vmem] * 6,
        out_specs=[vmem] * 3,
        compiler_params=pltpu.CompilerParams(vmem_limit_bytes=32 * 1024 * 1024),
        cost_estimate=pl.CostEstimate(
            flops=64 * units * width * group,
            bytes_accessed=16 * units * width + 64 * units * group + 12 * group * width,
            transcendentals=0,
        ),
    )(a0, a1, *ws)


def body(activations, cotangent, gate_up, down_proj):
    message = jnp.concatenate([gate_up.transpose(1, 0, 2), down_proj[None]], axis=0)
    swaps0 = [lambda v: swap_second(v, Y), lambda v: swap_first(v, X), lambda v: swap_second(v, X)]
    swaps1 = [lambda v: swap_second(v, X), lambda v: swap_first(v, Y), lambda v: swap_second(v, Y)]

    n = activations.shape[0] // 2
    x_a = swap_near(activations[:n], Z)
    half0 = join(message, swap_first(message, Y))
    half1 = join(swap_wrap(message, Z), swap_over(message, X))
    x_core, c_core = swap_core(activations), swap_core(cotangent)

    half0, half1, x_a = lax.optimization_barrier((half0, half1, x_a))
    x_b = swap_near(activations[n:], Z)
    line0 = join(half0, swaps0[0](half0))
    line1 = join(half1, swaps1[0](half1))
    line0, line1, x_b = lax.optimization_barrier((line0, line1, x_b))
    x_z = jnp.concatenate([x_a, x_b], axis=0)
    x_zc = swap_core(x_z)
    c_a = swap_near(cotangent[:n], Z)
    j0 = join(line0, swaps0[1](line0))
    j1 = join(line1, swaps1[1](line1))
    j0, j1, c_a = lax.optimization_barrier((j0, j1, c_a))
    c_b = swap_near(cotangent[n:], Z)
    r0, r1 = swaps0[2](j0), swaps1[2](j1)
    c_z = jnp.concatenate([c_a, c_b], axis=0)
    xs = [activations, x_core, x_z, x_zc]
    cs = [cotangent, c_core, c_z, swap_core(c_z)]

    g_r0, g_r1, a_r = grads(xs, cs, [r0, r1])
    back0, back1 = swaps0[2](g_r0), swaps1[2](g_r1)
    g_j0, g_j1, a_j = grads(xs, cs, [j0, j1])

    own, z_part, pair = input_parts(a_r, a_j, [r0, r1, j0, j1])
    got = swap_core(pair)
    mine = own + got[0].astype(F32)
    z_part = (z_part + got[1].astype(F32)).astype(BF16)
    grad_input = (mine + swap_near(z_part, Z).astype(F32)).astype(BF16)

    half0 = reduce(g_j0, back0, swaps0)
    half1 = reduce(g_j1, back1, swaps1)
    n = half0.shape[1] // 2
    total = half0[:, :n].astype(F32) + swap_first(half0[:, n:], Y).astype(F32)
    total = total + swap_wrap(half1[:, :n], Z).astype(F32) + swap_over(half1[:, n:], X).astype(F32)
    return (grad_input, total.transpose(1, 0, 2))


def solution(mesh):
    in_specs = (
        P(("node", "local"), None),
        P(("node", "local"), None),
        P(("node", "local"), None, None),
        P(("node", "local"), None),
    )
    out_specs = (P(("node", "local"), None), P(("node", "local"), None, None))
    return jax.shard_map(body, mesh=mesh, in_specs=in_specs, out_specs=out_specs, check_vma=False)
```

time: 129 us -> 121 us (0.938)
  Pallas kernels: 26.8 us -> 20.4 us
  waiting for transfers between devices: 56.4 us -> 58.5 us
  other arithmetic: 5.65 us -> 4.12 us
  starting transfers between devices: 36.2 us -> 34.9 us
    ppermute x21, starting transfers between devices: 35.6 us -> 29.8 us  [swap(): return lax.ppermute(value, AXES, pairs)]
    pallas_call x2, Pallas kernels: 20.1 us -> 15.3 us  [grads(): pl.pallas_call(kernel, out_shape=[jax.ShapeDtypeStruct(w.shape, BF16) for...]
    ppermute x0 -> x2, starting transfers between devices: none -> 3.9 us  [swap_over(): return lax.ppermute(value, AXES, pairs)]
    pallas_call x1, Pallas kernels: 6.64 us -> 5.05 us  [input_parts(): pl.pallas_call(input_kernel, out_shape=[jax.ShapeDtypeStruct((group, widt...]
  transfers between devices with their start and end apart: 26 -> 28, of which waited for: 13 -> 19; matrix products, arithmetic and copies ran while one was open for 3% -> 3% of each run, Pallas kernels for 13% -> 11%
where the time goes in v2:
time: 121 us; the launch traced here: 120 us
  waiting for transfers between devices  58.5 us (48%)
  starting transfers between devices  34.9 us (29%)
  Pallas kernels  20.4 us (17%)
  other arithmetic  4.12 us (3%)
  local copies, waits for them, and re-layouts  1.56 us (1%)
    ppermute x21, waiting for transfers between devices, swap(): return lax.ppermute(value, AXES, pairs)  54.5 us
    ppermute x21, starting transfers between devices, swap(): return lax.ppermute(value, AXES, pairs)  29.8 us
    pallas_call x2, Pallas kernels, grads(): pl.pallas_call(kernel, out_shape=[jax.ShapeDtypeStruct(w.shape, BF16) for...  15.3 us
    pallas_call x1, Pallas kernels, input_parts(): pl.pallas_call(input_kernel, out_shape=[jax.ShapeDtypeStruct((group, widt...  5.05 us
    ppermute x2, starting transfers between devices, swap_over(): return lax.ppermute(value, AXES, pairs)  3.9 us
    ppermute x5, waiting for transfers between devices, swap_core(): return lax.ppermute(value, AXES, [(d, d ^ 1) for d in range(DEVICES)])  2.78 us
  transfers between devices with their start and end apart: 28, of which 19 were waited for; matrix products, arithmetic and copies ran while one was open for 3% of the time, Pallas kernels for 11%

profile of v2, /device:TPU:2, one launch (start us, length us, event | category | flops | bytes accessed | tf_op | source)
XLA Modules:
  0.0 120.4 jit_solution(9251682351694070991)
XLA Ops:
  1.9 2.0 %collective-permute-start.4 = (bf16[192,1024]{1,0:T(8,128)(2,1)S(1)}, bf16[192,1024]{1,0:T(8,128)(2,1)S(1)}, u32[]{:S(2)}, u32[]{:S(2)}) collective-permute-start(bf16[192,1024]{1,0:T(8,128)(2,1)S(1)} %get-tuple-element.41), channel_id=1, source_target_pairs={{0,4},{1,5},{2,6},{3,7},{4,0},{5,1},{6,2},{7,3},{8,12},{9,13},{10,... | collective-permute-start | bytes 1179656 | tf_op jit(solution)/shard_map/ppermute | solution.py:33
  3.9 1.7 %collective-permute-start.1 = (bf16[3,24,1024]{2,1,0:T(8,128)(2,1)S(1)}, bf16[3,24,1024]{2,1,0:T(8,128)(2,1)S(1)}, u32[]{:S(2)}, u32[]{:S(2)}) collective-permute-start(bf16[3,24,1024]{2,1,0:T(8,128)(2,1)S(1)} %pad_maximum_fusion.6), channel_id=1, source_target_pairs={{0,16},{1,49},{2,18},{3,51},{4,20},{5,53},{6,22},{7,55},{8,24},{9,... | collective-permute-start | bytes 442376 | tf_op jit(solution)/shard_map/ppermute | solution.py:33
  5.6 2.5 %collective-permute-start.2 = (bf16[3,24,1024]{2,1,0:T(8,128)(2,1)S(1)}, bf16[3,24,1024]{2,1,0:T(8,128)(2,1)S(1)}, u32[]{:S(2)}, u32[]{:S(2)}) collective-permute-start(bf16[3,24,1024]{2,1,0:T(8,128)(2,1)S(1)} %pad_maximum_fusion.6), channel_id=1, source_target_pairs={{0,12},{1,13},{2,14},{3,15},{4,8},{5,9},{6,10},{7,11},{8,4},{9,5},... | collective-permute-start | bytes 442376 | tf_op jit(solution)/shard_map/ppermute | solution.py:33
  9.2 6.1 %collective-permute-done.2 = bf16[3,24,1024]{2,1,0:T(8,128)(2,1)S(1)} collective-permute-done((bf16[3,24,1024]{2,1,0:T(8,128)(2,1)S(1)}, bf16[3,24,1024]{2,1,0:T(8,128)(2,1)S(1)}, u32[]{:S(2)}, u32[]{:S(2)}) %collective-permute-start.2) | collective-permute-done | bytes 147488 | tf_op jit(solution)/shard_map/ppermute | solution.py:33
  19.2 5.2 %collective-permute-done.5 = bf16[3,48,1024]{2,1,0:T(8,128)(2,1)S(1)} collective-permute-done((bf16[3,48,1024]{2,1,0:T(8,128)(2,1)S(1)}, bf16[3,48,1024]{2,1,0:T(8,128)(2,1)S(1)}, u32[]{:S(2)}, u32[]{:S(2)}) %collective-permute-start.5) | collective-permute-done | bytes 294944 | tf_op jit(solution)/shard_map/ppermute | solution.py:33
  24.6 3.7 %collective-permute-done.7 = bf16[192,1024]{1,0:T(8,128)(2,1)S(1)} collective-permute-done((bf16[192,1024]{1,0:T(8,128)(2,1)S(1)}, bf16[192,1024]{1,0:T(8,128)(2,1)S(1)}, u32[]{:S(2)}, u32[]{:S(2)}) %collective-permute-start.7) | collective-permute-done | bytes 393248 | tf_op jit(solution)/shard_map/ppermute | solution.py:33
  32.3 5.8 %collective-permute-done.10 = bf16[3,96,1024]{2,1,0:T(8,128)(2,1)S(1)} collective-permute-done((bf16[3,96,1024]{2,1,0:T(8,128)(2,1)S(1)}, bf16[3,96,1024]{2,1,0:T(8,128)(2,1)S(1)}, u32[]{:S(2)}, u32[]{:S(2)}) %collective-permute-start.10) | collective-permute-done | bytes 589856 | tf_op jit(solution)/shard_map/ppermute | solution.py:33
  39.1 2.0 %collective-permute-done.12 = bf16[192,1024]{1,0:T(8,128)(2,1)S(1)} collective-permute-done((bf16[192,1024]{1,0:T(8,128)(2,1)S(1)}, bf16[192,1024]{1,0:T(8,128)(2,1)S(1)}, u32[]{:S(2)}, u32[]{:S(2)}) %collective-permute-start.12) | collective-permute-done | bytes 393248 | tf_op jit(solution)/shard_map/ppermute | solution.py:33
  41.2 3.2 %collective-permute-start.16 = (bf16[3,192,1024]{2,1,0:T(8,128)(2,1)S(1)}, bf16[3,192,1024]{2,1,0:T(8,128)(2,1)S(1)}, u32[]{:S(2)}, u32[]{:S(2)}) collective-permute-start(bf16[3,192,1024]{2,1,0:T(8,128)(2,1)S(1)} %pad_maximum_fusion.1.refs_9_.w3), channel_id=1, source_target_pairs={{0,48},{1,17},{2,50},{3,19},{4,52},{5,21},{6,54},{7,23},{8,56},{9,... | collective-permute-start | bytes 3538952 | tf_op jit(solution)/shard_map/ppermute | solution.py:33
  44.4 4.2 %collective-permute-done.13 = bf16[192,1024]{1,0:T(8,128)(2,1)S(1)} collective-permute-done((bf16[192,1024]{1,0:T(8,128)(2,1)S(1)}, bf16[192,1024]{1,0:T(8,128)(2,1)S(1)}, u32[]{:S(2)}, u32[]{:S(2)}) %collective-permute-start.13) | collective-permute-done | bytes 393248 | tf_op jit(solution)/shard_map/ppermute | solution.py:33
  52.1 5.3 %collective-permute-done.15.refs_8_.w0 = bf16[3,192,1024]{2,1,0:T(8,128)(2,1)S(1)} collective-permute-done((bf16[3,192,1024]{2,1,0:T(8,128)(2,1)S(1)}, bf16[3,192,1024]{2,1,0:T(8,128)(2,1)S(1)}, u32[]{:S(2)}, u32[]{:S(2)}) %collective-permute-start.15) | collective-permute-done | bytes 1179680 | tf_op jit(solution)/shard_map/ppermute | solution.py:33
  58.6 7.7 %shard_map.59 = (bf16[3,192,1024]{2,1,0:T(8,128)(2,1)S(1)}, bf16[3,192,1024]{2,1,0:T(8,128)(2,1)S(1)}, bf16[768,1536]{1,0:T(8,128)(2,1)S(1)}) custom-call(bf16[384,1024]{1,0:T(8,128)(2,1)S(1)} %copy-done, bf16[384,1024]{1,0:T(8,128)(2,1)S(1)} %collective-permute-done.refs_1_, bf16[384,1024]{1,0:T(8,128)(2,1)S(1)} %constant_dynamic-update-slice_fusion.refs_2_, ...), custom_call_target="tpu_custom_call" | custom-call | flops 7247757312 | bytes 13369344 | tf_op jit(solution)/shard_map/pallas_call | solution.py:141
  66.3 2.3 %collective-permute-start.19 = (bf16[3,192,1024]{2,1,0:T(8,128)(2,1)S(1)}, bf16[3,192,1024]{2,1,0:T(8,128)(2,1)S(1)}, u32[]{:S(2)}, u32[]{:S(2)}) collective-permute-start(bf16[3,192,1024]{2,1,0:T(8,128)(2,1)S(1)} %get-tuple-element.35), channel_id=1, source_target_pairs={{0,66},{1,3},{2,64},{3,1},{4,70},{5,7},{6,68},{7,5},{8,74},{9,11},... | collective-permute-start | bytes 3538952 | tf_op jit(solution)/shard_map/ppermute | solution.py:33
  68.5 1.9 %collective-permute-start.23 = (bf16[3,192,1024]{2,1,0:T(8,128)(2,1)S(1)}, bf16[3,192,1024]{2,1,0:T(8,128)(2,1)S(1)}, u32[]{:S(2)}, u32[]{:S(2)}) collective-permute-start(bf16[3,192,1024]{2,1,0:T(8,128)(2,1)S(1)} %get-tuple-element.37), channel_id=1, source_target_pairs={{0,48},{1,17},{2,50},{3,19},{4,52},{5,21},{6,54},{7,23},{8,56},{9,... | collective-permute-start | bytes 3538952 | tf_op jit(solution)/shard_map/ppermute | solution.py:33
  70.4 7.7 %shard_map.60 = (bf16[3,192,1024]{2,1,0:T(8,128)(2,1)S(1)}, bf16[3,192,1024]{2,1,0:T(8,128)(2,1)S(1)}, bf16[768,1536]{1,0:T(8,128)(2,1)S(1)}) custom-call(bf16[384,1024]{1,0:T(8,128)(2,1)S(1)} %copy-done, bf16[384,1024]{1,0:T(8,128)(2,1)S(1)} %collective-permute-done.refs_1_, bf16[384,1024]{1,0:T(8,128)(2,1)S(1)} %constant_dynamic-update-slice_fusion.refs_2_, ...), custom_call_target="tpu_custom_call" | custom-call | flops 7247757312 | bytes 13369344 | tf_op jit(solution)/shard_map/pallas_call | solution.py:141
  78.1 5.1 %shard_map.61 = (f32[384,1024]{1,0:T(8,128)S(1)}, f32[384,1024]{1,0:T(8,128)S(1)}, bf16[2,384,1024]{2,1,0:T(8,128)(2,1)S(1)}) custom-call(bf16[768,1536]{1,0:T(8,128)(2,1)S(1)} %get-tuple-element.29.a0, bf16[768,1536]{1,0:T(8,128)(2,1)S(1)} %get-tuple-element.30.a1, bf16[3,192,1024]{2,1,0:T(8,128)(2,1)S(1)} %collective-permute-done.15.refs_8_.w0, ...), custom_call_target="tpu_custom_call" | custom-call | flops 4831838208 | bytes 12582912 | tf_op jit(solution)/shard_map/pallas_call | solution.py:176
  83.8 3.2 %collective-permute-start.20 = (bf16[3,96,1024]{2,1,0:T(8,128)(2,1)S(1)}, bf16[3,96,1024]{2,1,0:T(8,128)(2,1)S(1)}, u32[]{:S(2)}, u32[]{:S(2)}) collective-permute-start(bf16[3,96,1024]{2,1,0:T(8,128)(2,1)S(1)} %slice.75), channel_id=1, source_target_pairs={{0,2},{1,67},{2,0},{3,65},{4,6},{5,71},{6,4},{7,69},{8,10},{9,75},... | collective-permute-start | bytes 1769480 | tf_op jit(solution)/shard_map/ppermute | solution.py:33
  88.2 6.7 %collective-permute-done.20 = bf16[3,96,1024]{2,1,0:T(8,128)(2,1)S(1)} collective-permute-done((bf16[3,96,1024]{2,1,0:T(8,128)(2,1)S(1)}, bf16[3,96,1024]{2,1,0:T(8,128)(2,1)S(1)}, u32[]{:S(2)}, u32[]{:S(2)}) %collective-permute-start.20) | collective-permute-done | bytes 589856 | tf_op jit(solution)/shard_map/ppermute | solution.py:33
  95.1 2.7 %collective-permute-start.21 = (bf16[3,48,1024]{2,1,0:T(8,128)(2,1)S(1)}, bf16[3,48,1024]{2,1,0:T(8,128)(2,1)S(1)}, u32[]{:S(2)}, u32[]{:S(2)}) collective-permute-start(bf16[3,48,1024]{2,1,0:T(8,128)(2,1)S(1)} %slice.77), channel_id=1, source_target_pairs={{0,48},{1,17},{2,50},{3,19},{4,52},{5,21},{6,54},{7,23},{8,56},{9,... | collective-permute-start | bytes 884744 | tf_op jit(solution)/shard_map/ppermute | solution.py:33
  101.1 2.0 %collective-permute-done.21 = bf16[3,48,1024]{2,1,0:T(8,128)(2,1)S(1)} collective-permute-done((bf16[3,48,1024]{2,1,0:T(8,128)(2,1)S(1)}, bf16[3,48,1024]{2,1,0:T(8,128)(2,1)S(1)}, u32[]{:S(2)}, u32[]{:S(2)}) %collective-permute-start.21) | collective-permute-done | bytes 294944 | tf_op jit(solution)/shard_map/ppermute | solution.py:33
  103.3 2.8 %collective-permute-done.25 = bf16[3,48,1024]{2,1,0:T(8,128)(2,1)S(1)} collective-permute-done((bf16[3,48,1024]{2,1,0:T(8,128)(2,1)S(1)}, bf16[3,48,1024]{2,1,0:T(8,128)(2,1)S(1)}, u32[]{:S(2)}, u32[]{:S(2)}) %collective-permute-start.25) | collective-permute-done | bytes 294944 | tf_op jit(solution)/shard_map/ppermute | solution.py:33
  107.8 3.2 %collective-permute-start.27 = (bf16[3,24,1024]{2,1,0:T(8,128)(2,1)S(1)}, bf16[3,24,1024]{2,1,0:T(8,128)(2,1)S(1)}, u32[]{:S(2)}, u32[]{:S(2)}) collective-permute-start(bf16[3,24,1024]{2,1,0:T(8,128)(2,1)S(1)} %get-tuple-element.43), channel_id=1, source_target_pairs={{0,14},{1,79},{2,12},{3,77},{4,10},{5,75},{6,8},{7,73},{8,6},{9,71... | collective-permute-start | bytes 442376 | tf_op jit(solution)/shard_map/ppermute | solution.py:59
  111.0 4.6 %collective-permute-done.26 = bf16[3,24,1024]{2,1,0:T(8,128)(2,1)S(1)} collective-permute-done((bf16[3,24,1024]{2,1,0:T(8,128)(2,1)S(1)}, bf16[3,24,1024]{2,1,0:T(8,128)(2,1)S(1)}, u32[]{:S(2)}, u32[]{:S(2)}) %collective-permute-start.26) | collective-permute-done | bytes 147488 | tf_op jit(solution)/shard_map/ppermute | solution.py:33
  116.4 2.7 %collective-permute-done.18 = bf16[384,1024]{1,0:T(8,128)(2,1)S(1)} collective-permute-done((bf16[384,1024]{1,0:T(8,128)(2,1)S(1)}, bf16[384,1024]{1,0:T(8,128)(2,1)S(1)}, u32[]{:S(2)}, u32[]{:S(2)}) %collective-permute-start.18) | collective-permute-done | bytes 786464 | tf_op jit(solution)/shard_map/ppermute | solution.py:33
  (72 shorter events, 25.2 us)
Async XLA Ops:
  1.9 14.6 %collective-permute-start.4 = (bf16[192,1024]{1,0:T(8,128)(2,1)S(1)}, bf16[192,1024]{1,0:T(8,128)(2,1)S(1)}, u32[]{:S(2)}, u32[]{:S(2)}) collective-permute-start(bf16[192,1024]{1,0:T(8,128)(2,1)S(1)} %get-tuple-element.41), channel_id=1, source_target_pairs={{0,4},{1,5},{2,6},{3,7},{4,0},{5,1},{6,2},{7,3},{8,12},{9,13},{10,... | collective-permute-start | bytes 1179656 | tf_op jit(solution)/shard_map/ppermute | solution.py:33
  5.6 9.7 %collective-permute-start.2 = (bf16[3,24,1024]{2,1,0:T(8,128)(2,1)S(1)}, bf16[3,24,1024]{2,1,0:T(8,128)(2,1)S(1)}, u32[]{:S(2)}, u32[]{:S(2)}) collective-permute-start(bf16[3,24,1024]{2,1,0:T(8,128)(2,1)S(1)} %pad_maximum_fusion.6), channel_id=1, source_target_pairs={{0,12},{1,13},{2,14},{3,15},{4,8},{5,9},{6,10},{7,11},{8,4},{9,5},... | collective-permute-start | bytes 442376 | tf_op jit(solution)/shard_map/ppermute | solution.py:33
  8.1 8.3 %collective-permute-start.3 = (bf16[3,24,1024]{2,1,0:T(8,128)(2,1)S(1)}, bf16[3,24,1024]{2,1,0:T(8,128)(2,1)S(1)}, u32[]{:S(2)}, u32[]{:S(2)}) collective-permute-start(bf16[3,24,1024]{2,1,0:T(8,128)(2,1)S(1)} %pad_maximum_fusion.6), channel_id=1, source_target_pairs={{0,14},{1,79},{2,12},{3,77},{4,10},{5,75},{6,8},{7,73},{8,6},{9,71... | collective-permute-start | bytes 442376 | tf_op jit(solution)/shard_map/ppermute | solution.py:59
  16.4 8.0 %collective-permute-start.5 = (bf16[3,48,1024]{2,1,0:T(8,128)(2,1)S(1)}, bf16[3,48,1024]{2,1,0:T(8,128)(2,1)S(1)}, u32[]{:S(2)}, u32[]{:S(2)}) collective-permute-start(bf16[3,48,1024]{2,1,0:T(8,128)(2,1)S(1)} %pad_maximum_fusion.4), channel_id=1, source_target_pairs={{0,48},{1,17},{2,50},{3,19},{4,52},{5,21},{6,54},{7,23},{8,56},{9,... | collective-permute-start | bytes 884744 | tf_op jit(solution)/shard_map/ppermute | solution.py:33
  17.6 6.9 %collective-permute-start.6 = (bf16[3,48,1024]{2,1,0:T(8,128)(2,1)S(1)}, bf16[3,48,1024]{2,1,0:T(8,128)(2,1)S(1)}, u32[]{:S(2)}, u32[]{:S(2)}) collective-permute-start(bf16[3,48,1024]{2,1,0:T(8,128)(2,1)S(1)} %pad_maximum_fusion.5), channel_id=1, source_target_pairs={{0,66},{1,3},{2,64},{3,1},{4,70},{5,7},{6,68},{7,5},{8,74},{9,11},... | collective-permute-start | bytes 884744 | tf_op jit(solution)/shard_map/ppermute | solution.py:33
  19.1 9.2 %collective-permute-start.7 = (bf16[192,1024]{1,0:T(8,128)(2,1)S(1)}, bf16[192,1024]{1,0:T(8,128)(2,1)S(1)}, u32[]{:S(2)}, u32[]{:S(2)}) collective-permute-start(bf16[192,1024]{1,0:T(8,128)(2,1)S(1)} %get-tuple-element.40), channel_id=1, source_target_pairs={{0,4},{1,5},{2,6},{3,7},{4,0},{5,1},{6,2},{7,3},{8,12},{9,13},{10,... | collective-permute-start | bytes 1179656 | tf_op jit(solution)/shard_map/ppermute | solution.py:33
  28.3 9.9 %collective-permute-start.10 = (bf16[3,96,1024]{2,1,0:T(8,128)(2,1)S(1)}, bf16[3,96,1024]{2,1,0:T(8,128)(2,1)S(1)}, u32[]{:S(2)}, u32[]{:S(2)}) collective-permute-start(bf16[3,96,1024]{2,1,0:T(8,128)(2,1)S(1)} %pad_maximum_fusion.2), channel_id=1, source_target_pairs={{0,2},{1,67},{2,0},{3,65},{4,6},{5,71},{6,4},{7,69},{8,10},{9,75},... | collective-permute-start | bytes 1769480 | tf_op jit(solution)/shard_map/ppermute | solution.py:33
  29.2 9.9 %collective-permute-start.11 = (bf16[3,96,1024]{2,1,0:T(8,128)(2,1)S(1)}, bf16[3,96,1024]{2,1,0:T(8,128)(2,1)S(1)}, u32[]{:S(2)}, u32[]{:S(2)}) collective-permute-start(bf16[3,96,1024]{2,1,0:T(8,128)(2,1)S(1)} %pad_maximum_fusion.3), channel_id=1, source_target_pairs={{0,16},{1,49},{2,18},{3,51},{4,20},{5,53},{6,22},{7,55},{8,24},{9,... | collective-permute-start | bytes 1769480 | tf_op jit(solution)/shard_map/ppermute | solution.py:33
  30.4 10.8 %collective-permute-start.12 = (bf16[192,1024]{1,0:T(8,128)(2,1)S(1)}, bf16[192,1024]{1,0:T(8,128)(2,1)S(1)}, u32[]{:S(2)}, u32[]{:S(2)}) collective-permute-start(bf16[192,1024]{1,0:T(8,128)(2,1)S(1)} %get-tuple-element.39), channel_id=1, source_target_pairs={{0,4},{1,5},{2,6},{3,7},{4,0},{5,1},{6,2},{7,3},{8,12},{9,13},{10,... | collective-permute-start | bytes 1179656 | tf_op jit(solution)/shard_map/ppermute | solution.py:33
  31.8 16.9 %collective-permute-start = (bf16[384,1024]{1,0:T(8,128)(2,1)S(1)}, bf16[384,1024]{1,0:T(8,128)(2,1)S(1)}, u32[]{:S(2)}, u32[]{:S(2)}) collective-permute-start(bf16[384,1024]{1,0:T(8,128)(2,1)S(1)} %copy-done), channel_id=1, source_target_pairs={{0,1},{1,0},{2,3},{3,2},{4,5},{5,4},{6,7},{7,6},{8,9},{9,8},{10,11... | collective-permute-start | bytes 2359304 | tf_op jit(solution)/shard_map/ppermute | solution.py:63
  31.8 17.5 %collective-permute-start.9 = (bf16[384,1024]{1,0:T(8,128)(2,1)S(1)}, bf16[384,1024]{1,0:T(8,128)(2,1)S(1)}, u32[]{:S(2)}, u32[]{:S(2)}) collective-permute-start(bf16[384,1024]{1,0:T(8,128)(2,1)S(1)} %copy-done.1), channel_id=1, source_target_pairs={{0,1},{1,0},{2,3},{3,2},{4,5},{5,4},{6,7},{7,6},{8,9},{9,8},{10,11... | collective-permute-start | bytes 2359304 | tf_op jit(solution)/shard_map/ppermute | solution.py:63
  38.2 10.5 %collective-permute-start.13 = (bf16[192,1024]{1,0:T(8,128)(2,1)S(1)}, bf16[192,1024]{1,0:T(8,128)(2,1)S(1)}, u32[]{:S(2)}, u32[]{:S(2)}) collective-permute-start(bf16[192,1024]{1,0:T(8,128)(2,1)S(1)} %get-tuple-element.38), channel_id=1, source_target_pairs={{0,4},{1,5},{2,6},{3,7},{4,0},{5,1},{6,2},{7,3},{8,12},{9,13},{10,... | collective-permute-start | bytes 1179656 | tf_op jit(solution)/shard_map/ppermute | solution.py:33
  41.2 16.2 %collective-permute-start.15 = (bf16[3,192,1024]{2,1,0:T(8,128)(2,1)S(1)}, bf16[3,192,1024]{2,1,0:T(8,128)(2,1)S(1)}, u32[]{:S(2)}, u32[]{:S(2)}) collective-permute-start(bf16[3,192,1024]{2,1,0:T(8,128)(2,1)S(1)} %pad_maximum_fusion.refs_8_.w2), channel_id=1, source_target_pairs={{0,66},{1,3},{2,64},{3,1},{4,70},{5,7},{6,68},{7,5},{8,74},{9,11},... | collective-permute-start | bytes 3538952 | tf_op jit(solution)/shard_map/ppermute | solution.py:33
  41.2 17.4 %collective-permute-start.16 = (bf16[3,192,1024]{2,1,0:T(8,128)(2,1)S(1)}, bf16[3,192,1024]{2,1,0:T(8,128)(2,1)S(1)}, u32[]{:S(2)}, u32[]{:S(2)}) collective-permute-start(bf16[3,192,1024]{2,1,0:T(8,128)(2,1)S(1)} %pad_maximum_fusion.1.refs_9_.w3), channel_id=1, source_target_pairs={{0,48},{1,17},{2,50},{3,19},{4,52},{5,21},{6,54},{7,23},{8,56},{9,... | collective-permute-start | bytes 3538952 | tf_op jit(solution)/shard_map/ppermute | solution.py:33
  66.3 17.0 %collective-permute-start.19 = (bf16[3,192,1024]{2,1,0:T(8,128)(2,1)S(1)}, bf16[3,192,1024]{2,1,0:T(8,128)(2,1)S(1)}, u32[]{:S(2)}, u32[]{:S(2)}) collective-permute-start(bf16[3,192,1024]{2,1,0:T(8,128)(2,1)S(1)} %get-tuple-element.35), channel_id=1, source_target_pairs={{0,66},{1,3},{2,64},{3,1},{4,70},{5,7},{6,68},{7,5},{8,74},{9,11},... | collective-permute-start | bytes 3538952 | tf_op jit(solution)/shard_map/ppermute | solution.py:33
  68.5 18.5 %collective-permute-start.23 = (bf16[3,192,1024]{2,1,0:T(8,128)(2,1)S(1)}, bf16[3,192,1024]{2,1,0:T(8,128)(2,1)S(1)}, u32[]{:S(2)}, u32[]{:S(2)}) collective-permute-start(bf16[3,192,1024]{2,1,0:T(8,128)(2,1)S(1)} %get-tuple-element.37), channel_id=1, source_target_pairs={{0,48},{1,17},{2,50},{3,19},{4,52},{5,21},{6,54},{7,23},{8,56},{9,... | collective-permute-start | bytes 3538952 | tf_op jit(solution)/shard_map/ppermute | solution.py:33
  83.2 16.3 %collective-permute-start.17 = (bf16[2,384,1024]{2,1,0:T(8,128)(2,1)S(1)}, bf16[2,384,1024]{2,1,0:T(8,128)(2,1)S(1)}, u32[]{:S(2)}, u32[]{:S(2)}) collective-permute-start(bf16[2,384,1024]{2,1,0:T(8,128)(2,1)S(1)} %get-tuple-element.32), channel_id=1, source_target_pairs={{0,1},{1,0},{2,3},{3,2},{4,5},{5,4},{6,7},{7,6},{8,9},{9,8},{10,11... | collective-permute-start | bytes 4718600 | tf_op jit(solution)/shard_map/ppermute | solution.py:63
  83.8 11.1 %collective-permute-start.20 = (bf16[3,96,1024]{2,1,0:T(8,128)(2,1)S(1)}, bf16[3,96,1024]{2,1,0:T(8,128)(2,1)S(1)}, u32[]{:S(2)}, u32[]{:S(2)}) collective-permute-start(bf16[3,96,1024]{2,1,0:T(8,128)(2,1)S(1)} %slice.75), channel_id=1, source_target_pairs={{0,2},{1,67},{2,0},{3,65},{4,6},{5,71},{6,4},{7,69},{8,10},{9,75},... | collective-permute-start | bytes 1769480 | tf_op jit(solution)/shard_map/ppermute | solution.py:33
  87.5 11.5 %collective-permute-start.24 = (bf16[3,96,1024]{2,1,0:T(8,128)(2,1)S(1)}, bf16[3,96,1024]{2,1,0:T(8,128)(2,1)S(1)}, u32[]{:S(2)}, u32[]{:S(2)}) collective-permute-start(bf16[3,96,1024]{2,1,0:T(8,128)(2,1)S(1)} %slice.81), channel_id=1, source_target_pairs={{0,16},{1,49},{2,18},{3,51},{4,20},{5,53},{6,22},{7,55},{8,24},{9,... | collective-permute-start | bytes 1769480 | tf_op jit(solution)/shard_map/ppermute | solution.py:33
  95.1 8.0 %collective-permute-start.21 = (bf16[3,48,1024]{2,1,0:T(8,128)(2,1)S(1)}, bf16[3,48,1024]{2,1,0:T(8,128)(2,1)S(1)}, u32[]{:S(2)}, u32[]{:S(2)}) collective-permute-start(bf16[3,48,1024]{2,1,0:T(8,128)(2,1)S(1)} %slice.77), channel_id=1, source_target_pairs={{0,48},{1,17},{2,50},{3,19},{4,52},{5,21},{6,54},{7,23},{8,56},{9,... | collective-permute-start | bytes 884744 | tf_op jit(solution)/shard_map/ppermute | solution.py:33
  99.8 19.4 %collective-permute-start.18 = (bf16[384,1024]{1,0:T(8,128)(2,1)S(1)}, bf16[384,1024]{1,0:T(8,128)(2,1)S(1)}, u32[]{:S(2)}, u32[]{:S(2)}) collective-permute-start(bf16[384,1024]{1,0:T(8,128)(2,1)S(1)} %fusion), channel_id=1, source_target_pairs={{0,4},{1,5},{2,6},{3,7},{4,0},{5,1},{6,2},{7,3},{8,12},{9,13},{10,... | collective-permute-start | bytes 2359304 | tf_op jit(solution)/shard_map/ppermute | solution.py:33
  103.2 7.8 %collective-permute-start.22 = (bf16[3,24,1024]{2,1,0:T(8,128)(2,1)S(1)}, bf16[3,24,1024]{2,1,0:T(8,128)(2,1)S(1)}, u32[]{:S(2)}, u32[]{:S(2)}) collective-permute-start(bf16[3,24,1024]{2,1,0:T(8,128)(2,1)S(1)} %slice.79), channel_id=1, source_target_pairs={{0,16},{1,49},{2,18},{3,51},{4,20},{5,53},{6,22},{7,55},{8,24},{9,... | collective-permute-start | bytes 442376 | tf_op jit(solution)/shard_map/ppermute | solution.py:33
  106.2 9.4 %collective-permute-start.26 = (bf16[3,24,1024]{2,1,0:T(8,128)(2,1)S(1)}, bf16[3,24,1024]{2,1,0:T(8,128)(2,1)S(1)}, u32[]{:S(2)}, u32[]{:S(2)}) collective-permute-start(bf16[3,24,1024]{2,1,0:T(8,128)(2,1)S(1)} %get-tuple-element.42), channel_id=1, source_target_pairs={{0,12},{1,13},{2,14},{3,15},{4,8},{5,9},{6,10},{7,11},{8,4},{9,5},... | collective-permute-start | bytes 442376 | tf_op jit(solution)/shard_map/ppermute | solution.py:33
  107.8 7.9 %collective-permute-start.27 = (bf16[3,24,1024]{2,1,0:T(8,128)(2,1)S(1)}, bf16[3,24,1024]{2,1,0:T(8,128)(2,1)S(1)}, u32[]{:S(2)}, u32[]{:S(2)}) collective-permute-start(bf16[3,24,1024]{2,1,0:T(8,128)(2,1)S(1)} %get-tuple-element.43), channel_id=1, source_target_pairs={{0,14},{1,79},{2,12},{3,77},{4,10},{5,75},{6,8},{7,73},{8,6},{9,71... | collective-permute-start | bytes 442376 | tf_op jit(solution)/shard_map/ppermute | solution.py:59
  (8 other events, 42.7 us)

commit v3 on v2

v3 whole, which is shorter than its diff:
```python
import jax
import jax.numpy as jnp
from jax import lax
from jax.experimental import pallas as pl
from jax.experimental.pallas import tpu as pltpu
from jax.sharding import PartitionSpec as P

AXES = ("x_hi", "y", "z", "x_lo", "core")
SIZES = (2, 4, 4, 2, 2)
X, Y, Z = 0, 1, 2
RING = 4
DEVICES = 128
TILE = 256
BF16 = jnp.bfloat16
F32 = jnp.float32
NT = (((1,), (1,)), ((), ()))
TN = (((0,), (0,)), ((), ()))


def place(device):
    return [device // 64 * 2 + device // 2 % 2, device // 16 % 4, device // 4 % 4, device % 2]


def index(x, y, z, core):
    return (x // 2) * 64 + y * 16 + z * 4 + (x % 2) * 2 + core


def swap(value, axis, wrap):
    pairs = []
    for device in range(DEVICES):
        there = place(device)
        there[axis] = RING - 1 - there[axis] if wrap(there[3]) else there[axis] ^ 1
        pairs.append((device, index(*there)))
    return lax.ppermute(value, AXES, pairs)


def swap_first(value, axis):
    return swap(value, axis, lambda core: core == 1)


def swap_second(value, axis):
    return swap(value, axis, lambda core: core == 0)


def swap_near(value, axis):
    return swap(value, axis, lambda core: False)


def swap_wrap(value, axis):
    return swap(value, axis, lambda core: True)


def swap_over(value, axis):
    pairs = []
    for device in range(DEVICES):
        there = place(device)
        there[axis] = RING - 1 - there[axis] if there[3] == 1 else there[axis] ^ 1
        there[Z] = RING - 1 - there[Z]
        pairs.append((device, index(*there)))
    return lax.ppermute(value, AXES, pairs)


def swap_core(value):
    return lax.ppermute(value, AXES, [(d, d ^ 1) for d in range(DEVICES)])


def add(a, b):
    return (a.astype(F32) + b.astype(F32)).astype(BF16)


def join(a, b):
    return jnp.concatenate([a, b], axis=1)


def rows_of(refs, start, stop, cols=slice(None)):
    parts = []
    for ref in refs:
        n = ref.shape[0]
        if start < n and stop > 0:
            parts.append(ref[max(start, 0) : min(stop, n), cols])
        start, stop = start - n, stop - n
    return parts[0] if len(parts) == 1 else jnp.concatenate(parts, axis=0)


def grads_kernel(n, *refs):
    xs, cs, w = refs[:n], refs[n : 2 * n], refs[2 * n]
    g, a_ref, hid = refs[2 * n + 1 :]
    units, width = w.shape[1:]
    gu = w[:2].reshape(2 * units, width)
    tokens = hid.shape[1]
    for t in range(tokens // TILE):
        rows = slice(t * TILE, (t + 1) * TILE)
        x = rows_of(xs, t * TILE, (t + 1) * TILE)
        c = rows_of(cs, t * TILE, (t + 1) * TILE)
        z = lax.dot_general(gu, x, NT, preferred_element_type=F32)
        grad = lax.dot_general(w[2], c, NT, preferred_element_type=F32)
        gate, up = z[:units], z[units:]
        sg = 1.0 / (1.0 + jnp.exp(-gate))
        silu = gate * sg
        hid[:, rows] = (silu * up).astype(BF16)
        slope = sg + silu * (1.0 - sg)
        a_ref[:units, rows] = (grad * up * slope).astype(BF16)
        a_ref[units:, rows] = (grad * silu).astype(BF16)
    for k in range(width // TILE):
        cols = slice(k * TILE, (k + 1) * TILE)
        x = rows_of(xs, 0, tokens, cols)
        c = rows_of(cs, 0, tokens, cols)
        d_gu = jnp.dot(a_ref[...], x, preferred_element_type=F32).astype(BF16)
        g[0, :, cols] = d_gu[:units]
        g[1, :, cols] = d_gu[units:]
        g[2, :, cols] = jnp.dot(hid[...], c, preferred_element_type=F32).astype(BF16)


def grads(xs, cs, w):
    units, width = w.shape[1:]
    tokens = sum(x.shape[0] for x in xs)
    vmem = pl.BlockSpec(memory_space=pltpu.VMEM)

    def kernel(*refs):
        grads_kernel(len(xs), *refs)

    return pl.pallas_call(
        kernel,
        out_shape=[
            jax.ShapeDtypeStruct(w.shape, BF16),
            jax.ShapeDtypeStruct((2 * units, tokens), BF16),
        ],
        in_specs=[vmem] * (2 * len(xs) + 1),
        out_specs=[vmem] * 2,
        scratch_shapes=[pltpu.VMEM((units, tokens), BF16)],
        compiler_params=pltpu.CompilerParams(vmem_limit_bytes=32 * 1024 * 1024),
        cost_estimate=pl.CostEstimate(
            flops=12 * tokens * width * units,
            bytes_accessed=4 * tokens * width + 12 * units * width + 4 * units * tokens,
            transcendentals=2 * tokens * units,
        ),
    )(*xs, *cs, w)


def input_kernel(a0, a1, w0, w1, own_ref, z_ref, pair_ref):
    w_all = jnp.concatenate([w[m] for w in (w0, w1) for m in range(2)], axis=0)
    group = own_ref.shape[0]
    for i in range(4):
        cols = slice(i * group, (i + 1) * group)
        a = jnp.concatenate([a0[:, cols], a1[:, cols]], axis=0)
        total = lax.dot_general(a, w_all, TN, preferred_element_type=F32)
        if i == 0:
            own_ref[...] = total
        elif i == 2:
            z_ref[...] = total
        else:
            pair_ref[i // 2] = total.astype(BF16)


def input_parts(a0, a1, ws):
    units, width = ws[0].shape[1:]
    group = a0.shape[1] // 4
    vmem = pl.BlockSpec(memory_space=pltpu.VMEM)
    return pl.pallas_call(
        input_kernel,
        out_shape=[
            jax.ShapeDtypeStruct((group, width), F32),
            jax.ShapeDtypeStruct((group, width), F32),
            jax.ShapeDtypeStruct((2, group, width), BF16),
        ],
        in_specs=[vmem] * 4,
        out_specs=[vmem] * 3,
        compiler_params=pltpu.CompilerParams(vmem_limit_bytes=32 * 1024 * 1024),
        cost_estimate=pl.CostEstimate(
            flops=32 * units * width * group,
            bytes_accessed=8 * units * width + 32 * units * group + 12 * group * width,
            transcendentals=0,
        ),
    )(a0, a1, *ws)


def gather(value, axis):
    return lax.all_gather(value, axis, axis=1, tiled=True)


def scatter(value, axis):
    return lax.psum_scatter(value, axis, scatter_dimension=1, tiled=True)


def body(activations, cotangent, gate_up, down_proj):
    message = jnp.concatenate([gate_up.transpose(1, 0, 2), down_proj[None]], axis=0)
    across = ("x_hi", "x_lo")
    x_z = swap_near(activations, Z)
    w0 = gather(message, "y")
    w1 = gather(swap_wrap(message, Z), across)
    x_core, c_core = swap_core(activations), swap_core(cotangent)
    w0, w1, x_z, c_own = lax.optimization_barrier((w0, w1, x_z, cotangent))
    c_z = swap_near(c_own, Z)
    w0 = gather(w0, across)
    w1 = gather(w1, "y")
    xs = [activations, x_core, x_z, swap_core(x_z)]
    cs = [cotangent, c_core, c_z, swap_core(c_z)]

    g0, a0 = grads(xs, cs, w0)
    half0 = scatter(g0, across)
    g1, a1 = grads(xs, cs, w1)
    half1 = scatter(g1, "y")

    own, z_part, pair = input_parts(a0, a1, [w0, w1])
    got = swap_core(pair)
    mine = own + got[0].astype(F32)
    z_part = (z_part + got[1].astype(F32)).astype(BF16)
    grad_input = (mine + swap_near(z_part, Z).astype(F32)).astype(BF16)

    total0 = scatter(half0, "y")
    total1 = swap_wrap(scatter(half1, across), Z)
    total = total0.astype(F32) + total1.astype(F32)
    return (grad_input, total.transpose(1, 0, 2))


def solution(mesh):
    split = jax.sharding.Mesh(mesh.devices.reshape(SIZES), AXES)
    rows = P(AXES, None)
    rows3 = P(AXES, None, None)
    return jax.shard_map(
        body, mesh=split, in_specs=(rows, rows, rows3, rows), out_specs=(rows, rows3), check_vma=False
    )
```

time: 121 us -> 234 us (1.93)
  waiting for transfers between devices: 58.5 us -> 115 us
  local copies, waits for them, and re-layouts: 1.56 us -> 34.1 us
  blocking collectives: 0 us -> 27.9 us
  starting transfers between devices: 34.9 us -> 11.4 us
  between operations: 0.92 us -> 14.2 us
  Pallas kernels: 20.4 us -> 24.6 us
    ppermute x21 -> x5, waiting for transfers between devices: 54.5 us -> 14.2 us  [swap(): return lax.ppermute(value, AXES, pairs)]
    unnamed x0 -> x8, waiting for transfers between devices: none -> 36.3 us
    reduce_scatter x0 -> x2, waiting for transfers between devices: none -> 35 us  [scatter(): return lax.psum_scatter(value, axis, scatter_dimension=1, tiled=True)]
    unnamed x11 -> x52, local copies, waits for them, and re-layouts: 0.09 us -> 34.1 us
    all_gather x0 -> x2, waiting for transfers between devices: none -> 29.2 us  [gather(): return lax.all_gather(value, axis, axis=1, tiled=True)]
    all_gather x0 -> x2, blocking collectives: none -> 27.9 us  [gather(): return lax.all_gather(value, axis, axis=1, tiled=True)]
    ppermute x21 -> x5, starting transfers between devices: 29.8 us -> 10.3 us  [swap(): return lax.ppermute(value, AXES, pairs)]
    ppermute x2 -> x0, starting transfers between devices: 3.9 us -> none  [swap_over(): return lax.ppermute(value, AXES, pairs)]
  transfers between devices with their start and end apart: 28 -> 16, of which waited for: 19 -> 7; matrix products, arithmetic and copies ran while one was open for 3% -> 6% of each run, Pallas kernels for 11% -> 11%
where the time goes in v3:
time: 234 us; the launch traced here: 233 us
  waiting for transfers between devices  115 us (49%)
  local copies, waits for them, and re-layouts  34.1 us (15%)
  blocking collectives  27.9 us (12%)
  Pallas kernels  24.6 us (11%)
  between operations  14.2 us (6%)
  starting transfers between devices  11.4 us (5%)
  other arithmetic  6.25 us (3%)
    unnamed x8, waiting for transfers between devices  36.3 us
    reduce_scatter x2, waiting for transfers between devices, scatter(): return lax.psum_scatter(value, axis, scatter_dimension=1, tiled=True)  35 us
    unnamed x52, local copies, waits for them, and re-layouts  34.1 us
    all_gather x2, waiting for transfers between devices, gather(): return lax.all_gather(value, axis, axis=1, tiled=True)  29.2 us
    all_gather x2, blocking collectives, gather(): return lax.all_gather(value, axis, axis=1, tiled=True)  27.9 us
    pallas_call x2, Pallas kernels, grads(): pl.pallas_call(kernel, out_shape=[jax.ShapeDtypeStruct(w.shape, BF16), ja...  18.4 us
    ppermute x5, waiting for transfers between devices, swap(): return lax.ppermute(value, AXES, pairs)  14.2 us
    ppermute x5, starting transfers between devices, swap(): return lax.ppermute(value, AXES, pairs)  10.3 us
  transfers between devices with their start and end apart: 16, of which 7 were waited for; matrix products, arithmetic and copies ran while one was open for 6% of the time, Pallas kernels for 11%

profile of v3, /device:TPU:2, one launch (start us, length us, event | category | flops | bytes accessed | tf_op | source)
XLA Modules:
  0.0 233.2 jit_solution(5173444607369654668)
XLA Ops:
  7.2 2.0 collective-permute-start.2
  11.0 2.6 %collective-permute-start.1 = (bf16[3,24,1024]{2,1,0:T(8,128)(2,1)S(1)}, bf16[3,24,1024]{2,1,0:T(8,128)(2,1)S(1)}, u32[]{:S(2)}, u32[]{:S(2)}) collective-permute-start(bf16[3,24,1024]{2,1,0:T(8,128)(2,1)S(1)} %pad_maximum_fusion), channel_id=1, source_target_pairs={{0,12},{1,13},{2,14},{3,15},{4,8},{5,9},{6,10},{7,11},{8,4},{9,5},... | collective-permute-start | bytes 442376 | tf_op jit(solution)/shard_map/ppermute | solution.py:34
  13.6 14.2 %all_gather.12 = bf16[3,96,1024]{2,1,0:T(8,128)(2,1)} all-gather(bf16[3,24,1024]{2,1,0:T(8,128)(2,1)S(1)} %pad_maximum_fusion), channel_id=1, replica_groups=mesh['x_hi'=2,'y'=4,'z'=4,'x_lo'=2,'core'=2] {'y'}, dimensions={1}, use_global_device_ids=true | all-gather | bytes 737280 | tf_op jit(solution)/shard_map/all_gather | solution.py:178
  27.7 13.7 %all_gather.13 = bf16[3,96,1024]{2,1,0:T(8,128)(2,1)} all-gather(bf16[3,24,1024]{2,1,0:T(8,128)(2,1)S(1)} %collective-permute-done.1), channel_id=1, replica_groups=mesh['x_hi'=2,'y'=4,'z'=4,'x_lo'=2,'core'=2] {'x_hi','x_lo'}, dimensions={1}, use_global_device_ids=true | all-gather | bytes 737280 | tf_op jit(solution)/shard_map/all_gather | solution.py:178
  43.9 14.1 %collective-permute-done.5.refs_6_ = bf16[384,1024]{1,0:T(8,128)(2,1)S(1)} collective-permute-done((bf16[384,1024]{1,0:T(8,128)(2,1)S(1)}, bf16[384,1024]{1,0:T(8,128)(2,1)S(1)}, u32[]{:S(2)}, u32[]{:S(2)}) %collective-permute-start.5) | collective-permute-done | bytes 786464 | tf_op jit(solution)/shard_map/ppermute | solution.py:34
  61.7 12.4 %all-gather.5.cloned.1.call-done.refs_8_.w1 = bf16[3,384,1024]{2,1,0:T(8,128)(2,1)} async-done(((bf16[3,96,1024]{2,1,0:T(8,128)(2,1)}), bf16[3,384,1024]{2,1,0:T(8,128)(2,1)}) %all-gather.5.cloned.1.call-update) | async-done | bytes 2359312 | tf_op jit(solution)/shard_map/all_gather | solution.py:178
  74.1 1.7 copy-done
  80.3 9.2 %shard_map.60 = (bf16[3,384,1024]{2,1,0:T(8,128)(2,1)}, bf16[768,1536]{1,0:T(8,128)(2,1)S(1)}) custom-call(bf16[384,1024]{1,0:T(8,128)(2,1)S(1)} %copy-done.4, bf16[384,1024]{1,0:T(8,128)(2,1)S(1)} %copy-done.7, bf16[384,1024]{1,0:T(8,128)(2,1)S(1)} %collective-permute-done.2.refs_2_, bf16[384,1024]{1,0:T(8,128)(2,1)S(1)} %copy-done.13, ...), custom_call_target="tpu_custom_call" | custom-call | flops 7247757312 | bytes 13369344 | tf_op jit(solution)/shard_map/pallas_call | solution.py:122
  91.1 16.8 %all-gather.3.cloned.1.call-done.refs_8_.w0 = bf16[3,384,1024]{2,1,0:T(8,128)(2,1)} async-done(((bf16[3,96,1024]{2,1,0:T(8,128)(2,1)}), bf16[3,384,1024]{2,1,0:T(8,128)(2,1)}) %all-gather.3.cloned.1.call-update) | async-done | bytes 2359312 | tf_op jit(solution)/shard_map/all_gather | solution.py:178
  107.9 1.7 copy-done.2
  114.1 9.2 %shard_map.59 = (bf16[3,384,1024]{2,1,0:T(8,128)(2,1)}, bf16[768,1536]{1,0:T(8,128)(2,1)S(1)}) custom-call(bf16[384,1024]{1,0:T(8,128)(2,1)S(1)} %copy-done.4, bf16[384,1024]{1,0:T(8,128)(2,1)S(1)} %copy-done.8, bf16[384,1024]{1,0:T(8,128)(2,1)S(1)} %collective-permute-done.2.refs_2_, bf16[384,1024]{1,0:T(8,128)(2,1)S(1)} %copy-done.14, ...), custom_call_target="tpu_custom_call" | custom-call | flops 7247757312 | bytes 13369344 | tf_op jit(solution)/shard_map/pallas_call | solution.py:122
  124.9 1.7 copy-done.1
  126.5 1.7 copy-done.3
  128.2 1.7 copy-done.19
  129.9 1.7 copy-done.21
  131.6 6.2 %shard_map.61 = (f32[384,1024]{1,0:T(8,128)S(1)}, f32[384,1024]{1,0:T(8,128)S(1)}, bf16[2,384,1024]{2,1,0:T(8,128)(2,1)}) custom-call(bf16[768,1536]{1,0:T(8,128)(2,1)S(1)} %copy-done.21, bf16[768,1536]{1,0:T(8,128)(2,1)S(1)} %copy-done.19, bf16[3,384,1024]{2,1,0:T(8,128)(2,1)S(1)} %copy-done.3, bf16[3,384,1024]{2,1,0:T(8,128)(2,1)S(1)} %copy-done.1), custom_call_target="tpu_custom_call" | custom-call | flops 4831838208 | bytes 12582912 | tf_op jit(solution)/shard_map/pallas_call | solution.py:159
  137.9 5.3 %reduce-scatter.11.cloned.1.call-done = bf16[3,96,1024]{2,1,0:T(8,128)(2,1)} async-done(((bf16[3,384,1024]{2,1,0:T(8,128)(2,1)}), bf16[3,96,1024]{2,1,0:T(8,128)(2,1)}) %reduce-scatter.11.cloned.1.call-update) | async-done | bytes 589840 | tf_op jit(solution)/shard_map/reduce_scatter | solution.py:182
  146.1 29.7 %reduce-scatter.9.cloned.1.call-done = bf16[3,96,1024]{2,1,0:T(8,128)(2,1)} async-done(((bf16[3,384,1024]{2,1,0:T(8,128)(2,1)}), bf16[3,96,1024]{2,1,0:T(8,128)(2,1)}) %reduce-scatter.9.cloned.1.call-update) | async-done | bytes 589840 | tf_op jit(solution)/shard_map/reduce_scatter | solution.py:182
  175.8 1.6 copy.8
  178.4 2.3 fusion
  182.3 16.3 %reduce-scatter.15.cloned.1.call-done = bf16[24,3072]{1,0:T(8,128)(2,1)} async-done(((bf16[96,3072]{1,0:T(8,128)(2,1)}), bf16[24,3072]{1,0:T(8,128)(2,1)}) %reduce-scatter.15.cloned.1.call-update) | async-done | bytes 147472
  199.7 3.0 %collective-permute-start.9 = (bf16[3,24,1024]{2,1,0:T(8,128)(2,1)S(1)}, bf16[3,24,1024]{2,1,0:T(8,128)(2,1)S(1)}, u32[]{:S(2)}, u32[]{:S(2)}) collective-permute-start(bf16[3,24,1024]{2,1,0:T(8,128)(2,1)S(1)} %copy.11), channel_id=1, source_target_pairs={{0,12},{1,13},{2,14},{3,15},{4,8},{5,9},{6,10},{7,11},{8,4},{9,5},... | collective-permute-start | bytes 442376 | tf_op jit(solution)/shard_map/ppermute | solution.py:34
  202.8 2.4 %fusion.2 = bf16[384,1024]{1,0:T(8,128)(2,1)} fusion(f32[384,1024]{1,0:T(8,128)S(1)} %get-tuple-element.19, bf16[384,1024]{1,0:T(8,128)(2,1)S(1)} %collective-permute-done.8, bf16[2,384,1024]{2,1,0:T(8,128)(2,1)} %collective-permute-done.7), kind=kLoop, calls=%fused_computation.4 | loop fusion | flops 1966080 | bytes 3932160 | tf_op jit(solution)/shard_map/convert_element_type | solution.py:208
  205.1 19.2 %reduce-scatter.13.cloned.1.call-done = bf16[24,3072]{1,0:T(8,128)(2,1)} async-done(((bf16[96,3072]{1,0:T(8,128)(2,1)}), bf16[24,3072]{1,0:T(8,128)(2,1)}) %reduce-scatter.13.cloned.1.call-update) | async-done | bytes 147472
  (75 shorter events, 28.6 us)
Async XLA Ops:
  7.2 36.2 %copy-start.4 = (bf16[384,1024]{1,0:T(8,128)(2,1)S(1)}, bf16[384,1024]{1,0:T(8,128)(2,1)}, u32[]{:S(2)}) copy-start(bf16[384,1024]{1,0:T(8,128)(2,1)} %refs_0_.3) | copy-start | bytes 2359300
  7.2 35.1 %copy-start.5 = (bf16[384,1024]{1,0:T(8,128)(2,1)S(1)}, bf16[384,1024]{1,0:T(8,128)(2,1)}, u32[]{:S(2)}) copy-start(bf16[384,1024]{1,0:T(8,128)(2,1)} %refs_4_.3) | copy-start | bytes 2359300
  7.2 66.9 %all-gather.5.cloned.1.call-start = ((), (), s32[]{:S(2)}) async-start(), calls=%async_computation.5 | async-start | bytes 2949120 | tf_op jit(solution)/shard_map/all_gather | solution.py:178
  7.2 34.2 %collective-permute-start.2 = (bf16[384,1024]{1,0:T(8,128)(2,1)}, bf16[384,1024]{1,0:T(8,128)(2,1)S(1)}, u32[]{:S(2)}, u32[]{:S(2)}) collective-permute-start(bf16[384,1024]{1,0:T(8,128)(2,1)} %refs_0_.3), channel_id=1, source_target_pairs={{0,4},{1,5},{2,6},{3,7},{4,0},{5,1},{6,2},{7,3},{8,12},{9,13},{10,... | collective-permute-start | bytes 2359304 | tf_op jit(solution)/shard_map/ppermute | solution.py:34
  11.0 16.8 %collective-permute-start.1 = (bf16[3,24,1024]{2,1,0:T(8,128)(2,1)S(1)}, bf16[3,24,1024]{2,1,0:T(8,128)(2,1)S(1)}, u32[]{:S(2)}, u32[]{:S(2)}) collective-permute-start(bf16[3,24,1024]{2,1,0:T(8,128)(2,1)S(1)} %pad_maximum_fusion), channel_id=1, source_target_pairs={{0,12},{1,13},{2,14},{3,15},{4,8},{5,9},{6,10},{7,11},{8,4},{9,5},... | collective-permute-start | bytes 442376 | tf_op jit(solution)/shard_map/ppermute | solution.py:34
  41.5 66.5 %all-gather.3.cloned.1.call-start = ((), (), s32[]{:S(2)}) async-start(), calls=%async_computation.4 | async-start | bytes 2949120 | tf_op jit(solution)/shard_map/all_gather | solution.py:178
  42.2 101.0 %reduce-scatter.11.cloned.1.call-start = ((), (), s32[]{:S(2)}) async-start(), calls=%async_computation.7 | async-start | bytes 2949120 | tf_op jit(solution)/shard_map/reduce_scatter | solution.py:182
  42.3 15.8 %collective-permute-start.5 = (bf16[384,1024]{1,0:T(8,128)(2,1)S(1)}, bf16[384,1024]{1,0:T(8,128)(2,1)S(1)}, u32[]{:S(2)}, u32[]{:S(2)}) collective-permute-start(bf16[384,1024]{1,0:T(8,128)(2,1)S(1)} %copy-done.5), channel_id=1, source_target_pairs={{0,4},{1,5},{2,6},{3,7},{4,0},{5,1},{6,2},{7,3},{8,12},{9,13},{10,... | collective-permute-start | bytes 2359304 | tf_op jit(solution)/shard_map/ppermute | solution.py:34
  43.4 14.7 %collective-permute-start = (bf16[384,1024]{1,0:T(8,128)(2,1)S(1)}, bf16[384,1024]{1,0:T(8,128)(2,1)S(1)}, u32[]{:S(2)}, u32[]{:S(2)}) collective-permute-start(bf16[384,1024]{1,0:T(8,128)(2,1)S(1)} %copy-done.4), channel_id=1, source_target_pairs={{0,1},{1,0},{2,3},{3,2},{4,5},{5,4},{6,7},{7,6},{8,9},{9,8},{10,11... | collective-permute-start | bytes 2359304 | tf_op jit(solution)/shard_map/ppermute | solution.py:64
  43.4 15.5 %collective-permute-start.4 = (bf16[384,1024]{1,0:T(8,128)(2,1)S(1)}, bf16[384,1024]{1,0:T(8,128)(2,1)S(1)}, u32[]{:S(2)}, u32[]{:S(2)}) collective-permute-start(bf16[384,1024]{1,0:T(8,128)(2,1)S(1)} %copy-done.5), channel_id=1, source_target_pairs={{0,1},{1,0},{2,3},{3,2},{4,5},{5,4},{6,7},{7,6},{8,9},{9,8},{10,11... | collective-permute-start | bytes 2359304 | tf_op jit(solution)/shard_map/ppermute | solution.py:64
  43.9 16.0 %collective-permute-start.3 = (bf16[384,1024]{1,0:T(8,128)(2,1)S(1)}, bf16[384,1024]{1,0:T(8,128)(2,1)S(1)}, u32[]{:S(2)}, u32[]{:S(2)}) collective-permute-start(bf16[384,1024]{1,0:T(8,128)(2,1)S(1)} %collective-permute-done.2.refs_2_), channel_id=1, source_target_pairs={{0,1},{1,0},{2,3},{3,2},{4,5},{5,4},{6,7},{7,6},{8,9},{9,8},{10,11... | collective-permute-start | bytes 2359304 | tf_op jit(solution)/shard_map/ppermute | solution.py:64
  58.0 2.8 %collective-permute-start.6 = (bf16[384,1024]{1,0:T(8,128)(2,1)S(1)}, bf16[384,1024]{1,0:T(8,128)(2,1)S(1)}, u32[]{:S(2)}, u32[]{:S(2)}) collective-permute-start(bf16[384,1024]{1,0:T(8,128)(2,1)S(1)} %collective-permute-done.5.refs_6_), channel_id=1, source_target_pairs={{0,1},{1,0},{2,3},{3,2},{4,5},{5,4},{6,7},{7,6},{8,9},{9,8},{10,11... | collective-permute-start | bytes 2359304 | tf_op jit(solution)/shard_map/ppermute | solution.py:64
  74.1 1.7 copy-start
  90.9 84.9 %reduce-scatter.9.cloned.1.call-start = ((), (), s32[]{:S(2)}) async-start(), calls=%async_computation.6 | async-start | bytes 2949120 | tf_op jit(solution)/shard_map/reduce_scatter | solution.py:182
  107.9 1.7 copy-start.2
  124.8 73.7 %reduce-scatter.15.cloned.1.call-start = ((), (), s32[]{:S(2)}) async-start(), calls=%async_computation.9 | async-start | bytes 737280
  124.9 1.7 copy-start.1
  126.5 1.7 copy-start.3
  128.2 1.7 copy-start.19
  129.9 1.7 copy-start.21
  137.9 40.6 %collective-permute-start.7 = (bf16[2,384,1024]{2,1,0:T(8,128)(2,1)}, bf16[2,384,1024]{2,1,0:T(8,128)(2,1)}, u32[]{:S(2)}, u32[]{:S(2)}) collective-permute-start(bf16[2,384,1024]{2,1,0:T(8,128)(2,1)} %get-tuple-element.20), channel_id=1, source_target_pairs={{0,1},{1,0},{2,3},{3,2},{4,5},{5,4},{6,7},{7,6},{8,9},{9,8},{10,11... | collective-permute-start | bytes 4718600 | tf_op jit(solution)/shard_map/ppermute | solution.py:64
  145.8 78.5 %reduce-scatter.13.cloned.1.call-start = ((), (), s32[]{:S(2)}) async-start(), calls=%async_computation.8 | async-start | bytes 737280
  180.7 22.1 %collective-permute-start.8 = (bf16[384,1024]{1,0:T(8,128)(2,1)}, bf16[384,1024]{1,0:T(8,128)(2,1)S(1)}, u32[]{:S(2)}, u32[]{:S(2)}) collective-permute-start(bf16[384,1024]{1,0:T(8,128)(2,1)} %fusion), channel_id=1, source_target_pairs={{0,4},{1,5},{2,6},{3,7},{4,0},{5,1},{6,2},{7,3},{8,12},{9,13},{10,... | collective-permute-start | bytes 2359304 | tf_op jit(solution)/shard_map/ppermute | solution.py:34
  199.7 25.8 %collective-permute-start.9 = (bf16[3,24,1024]{2,1,0:T(8,128)(2,1)S(1)}, bf16[3,24,1024]{2,1,0:T(8,128)(2,1)S(1)}, u32[]{:S(2)}, u32[]{:S(2)}) collective-permute-start(bf16[3,24,1024]{2,1,0:T(8,128)(2,1)S(1)} %copy.11), channel_id=1, source_target_pairs={{0,12},{1,13},{2,14},{3,15},{4,8},{5,9},{6,10},{7,11},{8,4},{9,5},... | collective-permute-start | bytes 442376 | tf_op jit(solution)/shard_map/ppermute | solution.py:34
  (14 other events, 15.5 us)
Sparse Core Ops, SparseCore 0:
  41.6 32.4 all-gather.4
  75.8 32.1 all-gather.2
  110.3 32.7 reduce-scatter.10
  145.4 30.2 reduce-scatter.8
  178.0 20.4 reduce-scatter.14
  200.8 23.5 reduce-scatter.12

commit v4 on v2

v4 whole, which is shorter than its diff:
```python
import jax
import jax.numpy as jnp
from jax import lax
from jax.experimental import pallas as pl
from jax.experimental.pallas import tpu as pltpu
from jax.sharding import PartitionSpec as P

AXES = ("node", "local")
X, Y, Z = 0, 1, 2
RING = 4
DEVICES = 128
TILE = 256
BF16 = jnp.bfloat16
F32 = jnp.float32
NT = (((1,), (1,)), ((), ()))
TN = (((0,), (0,)), ((), ()))


def place(device):
    return [device // 64 * 2 + device // 2 % 2, device // 16 % 4, device // 4 % 4, device % 2]


def index(x, y, z, core):
    return (x // 2) * 64 + y * 16 + z * 4 + (x % 2) * 2 + core


def swap(value, axis, wrap):
    pairs = []
    for device in range(DEVICES):
        there = place(device)
        there[axis] = RING - 1 - there[axis] if wrap(there[3]) else there[axis] ^ 1
        pairs.append((device, index(*there)))
    return lax.ppermute(value, AXES, pairs)


def swap_first(value, axis):
    return swap(value, axis, lambda core: core == 1)


def swap_second(value, axis):
    return swap(value, axis, lambda core: core == 0)


def swap_near(value, axis):
    return swap(value, axis, lambda core: False)


def swap_wrap(value, axis):
    return swap(value, axis, lambda core: True)


def swap_corner(value):
    pairs = []
    for device in range(DEVICES):
        there = place(device)
        for axis in (X, Y):
            there[axis] = RING - 1 - there[axis] if there[3] == 1 else there[axis] ^ 1
        pairs.append((device, index(*there)))
    return lax.ppermute(value, AXES, pairs)


def swap_core(value):
    return lax.ppermute(value, AXES, [(d, d ^ 1) for d in range(DEVICES)])


def add(a, b):
    return (a.astype(F32) + b.astype(F32)).astype(BF16)


def join(*blocks):
    return jnp.concatenate(blocks, axis=1)


def gather_block(message):
    return join(message, swap_first(message, Y), swap_first(message, X), swap_corner(message))


def reduce_block(block):
    n = block.shape[1] // 4
    own, along_y, along_x, corner = (block[:, i * n : (i + 1) * n] for i in range(4))
    total = own.astype(F32) + swap_first(along_y, Y).astype(F32)
    return total + swap_first(along_x, X).astype(F32) + swap_corner(corner).astype(F32)


def halve(both, axis):
    n = both.shape[1] // 2
    return add(both[:, :n], swap_second(both[:, n:], axis))


def rows_of(refs, start, stop, cols=slice(None)):
    parts = []
    for ref in refs:
        n = ref.shape[0]
        if start < n and stop > 0:
            parts.append(ref[max(start, 0) : min(stop, n), cols])
        start, stop = start - n, stop - n
    return parts[0] if len(parts) == 1 else jnp.concatenate(parts, axis=0)


def grads_kernel(n, *refs):
    xs, cs, refs = refs[:n], refs[n : 2 * n], refs[2 * n :]
    a_ref, hid = refs[-2:]
    parts = len(refs) // 2 - 1
    ws, gs = refs[:parts], refs[parts:-2]
    units, width = ws[0].shape[1:]
    gu = jnp.concatenate([w[m] for w in ws for m in range(2)], axis=0)
    down = jnp.concatenate([w[2] for w in ws], axis=0)
    tokens = hid.shape[1]
    for t in range(tokens // TILE):
        rows = slice(t * TILE, (t + 1) * TILE)
        x = rows_of(xs, t * TILE, (t + 1) * TILE)
        c = rows_of(cs, t * TILE, (t + 1) * TILE)
        z = lax.dot_general(gu, x, NT, preferred_element_type=F32)
        gh = lax.dot_general(down, c, NT, preferred_element_type=F32)
        for p in range(parts):
            gate = z[2 * p * units : (2 * p + 1) * units]
            up = z[(2 * p + 1) * units : (2 * p + 2) * units]
            grad = gh[p * units : (p + 1) * units]
            sg = 1.0 / (1.0 + jnp.exp(-gate))
            silu = gate * sg
            hid[p * units : (p + 1) * units, rows] = (silu * up).astype(BF16)
            slope = sg + silu * (1.0 - sg)
            a_ref[2 * p * units : (2 * p + 1) * units, rows] = (grad * up * slope).astype(BF16)
            a_ref[(2 * p + 1) * units : (2 * p + 2) * units, rows] = (grad * silu).astype(BF16)
    for k in range(width // TILE):
        cols = slice(k * TILE, (k + 1) * TILE)
        x = rows_of(xs, 0, tokens, cols)
        c = rows_of(cs, 0, tokens, cols)
        d_gu = jnp.dot(a_ref[...], x, preferred_element_type=F32).astype(BF16)
        d_down = jnp.dot(hid[...], c, preferred_element_type=F32).astype(BF16)
        for p, g in enumerate(gs):
            for m in range(2):
                g[m, :, cols] = d_gu[(2 * p + m) * units : (2 * p + m + 1) * units]
            g[2, :, cols] = d_down[p * units : (p + 1) * units]


def grads(xs, cs, ws):
    units, width = ws[0].shape[1:]
    tokens = sum(x.shape[0] for x in xs)
    vmem = pl.BlockSpec(memory_space=pltpu.VMEM)

    def kernel(*refs):
        grads_kernel(len(xs), *refs)

    return pl.pallas_call(
        kernel,
        out_shape=[jax.ShapeDtypeStruct(w.shape, BF16) for w in ws]
        + [jax.ShapeDtypeStruct((2 * len(ws) * units, tokens), BF16)],
        in_specs=[vmem] * (2 * len(xs) + len(ws)),
        out_specs=[vmem] * (len(ws) + 1),
        scratch_shapes=[pltpu.VMEM((len(ws) * units, tokens), BF16)],
        compiler_params=pltpu.CompilerParams(vmem_limit_bytes=32 * 1024 * 1024),
        cost_estimate=pl.CostEstimate(
            flops=width, bytes_accessed=width, transcendentals=0
        ),
    )(*xs, *cs, *ws)


def input_kernel(n, *refs):
    parts, ws = refs[:n], refs[n:-3]
    own_ref, z_ref, pair_ref = refs[-3:]
    w_all = jnp.concatenate([w[m] for w in ws for m in range(2)], axis=0)
    group = own_ref.shape[0]
    for i in range(4):
        cols = slice(i * group, (i + 1) * group)
        a = jnp.concatenate([part[:, cols] for part in parts], axis=0)
        total = lax.dot_general(a, w_all, TN, preferred_element_type=F32)
        if i == 0:
            own_ref[...] = total
        elif i == 2:
            z_ref[...] = total
        else:
            pair_ref[i // 2] = total.astype(BF16)


def input_parts(parts, ws):
    units, width = ws[0].shape[1:]
    group = parts[0].shape[1] // 4
    vmem = pl.BlockSpec(memory_space=pltpu.VMEM)

    def kernel(*refs):
        input_kernel(len(parts), *refs)

    return pl.pallas_call(
        kernel,
        out_shape=[
            jax.ShapeDtypeStruct((group, width), F32),
            jax.ShapeDtypeStruct((group, width), F32),
            jax.ShapeDtypeStruct((2, group, width), BF16),
        ],
        in_specs=[vmem] * (len(parts) + len(ws)),
        out_specs=[vmem] * 3,
        compiler_params=pltpu.CompilerParams(vmem_limit_bytes=32 * 1024 * 1024),
        cost_estimate=pl.CostEstimate(
            flops=width, bytes_accessed=width, transcendentals=0
        ),
    )(*parts, *ws)


def body(activations, cotangent, gate_up, down_proj):
    x_z = swap_near(activations, Z)
    message = jnp.concatenate([gate_up.transpose(1, 0, 2), down_proj[None]], axis=0)
    other = swap_wrap(message, Z)
    block0 = gather_block(message)
    block1 = gather_block(other)
    block1, x_z, c_own = lax.optimization_barrier((block1, x_z, cotangent))
    c_z = swap_near(c_own, Z)
    j0 = join(block0, swap_second(block0, Y))
    j1 = join(block1, swap_second(block1, X))
    r0, r1 = swap_second(j0, X), swap_second(j1, Y)
    xs = [activations, swap_core(activations), x_z, swap_core(x_z)]
    cs = [cotangent, swap_core(cotangent), c_z, swap_core(c_z)]

    g_r0, a_r0 = grads(xs, cs, [r0])
    back0 = swap_second(g_r0, X)
    g_r1, a_r1 = grads(xs, cs, [r1])
    back1 = swap_second(g_r1, Y)
    j0, j1, a_r1 = lax.optimization_barrier((j0, j1, a_r1))
    g_j0, g_j1, a_j = grads(xs, cs, [j0, j1])

    own, z_part, pair = input_parts([a_r0, a_r1, a_j], [r0, r1, j0, j1])
    got = swap_core(pair)
    near0, near1 = add(g_j0, back0), add(g_j1, back1)
    near0, near1, z_part = lax.optimization_barrier((near0, near1, z_part))
    mine = own + got[0].astype(F32)
    z_part = swap_near((z_part + got[1].astype(F32)).astype(BF16), Z)

    total1 = reduce_block(halve(near1, X)).astype(BF16)
    total1, z_part = lax.optimization_barrier((total1, z_part))
    grad_input = (mine + z_part.astype(F32)).astype(BF16)
    total0 = reduce_block(halve(near0, Y))
    total = total0 + swap_wrap(total1, Z).astype(F32)
    return (grad_input, total.transpose(1, 0, 2))


def solution(mesh):
    in_specs = (
        P(("node", "local"), None),
        P(("node", "local"), None),
        P(("node", "local"), None, None),
        P(("node", "local"), None),
    )
    out_specs = (P(("node", "local"), None), P(("node", "local"), None, None))
    return jax.shard_map(body, mesh=mesh, in_specs=in_specs, out_specs=out_specs, check_vma=False)
```

time: 121 us -> 103 us (0.85)
  waiting for transfers between devices: 58.5 us -> 24.5 us
  starting transfers between devices: 34.9 us -> 48.1 us
  other arithmetic: 4.12 us -> 5.5 us
    ppermute x21, waiting for transfers between devices: 54.5 us -> 23.2 us  [swap(): return lax.ppermute(value, AXES, pairs)]
    ppermute x21, starting transfers between devices: 29.8 us -> 40.2 us  [swap(): return lax.ppermute(value, AXES, pairs)]
    ppermute x5, waiting for transfers between devices: 2.78 us -> 0.6 us  [swap_core(): return lax.ppermute(value, AXES, [(d, d ^ 1) for d in range(DEVICES)])]
    ppermute x2 -> x4, starting transfers between devices: 3.9 us -> 5.68 us  [swap_corner(): return lax.ppermute(value, AXES, pairs)]
    slice x8 -> x4, local copies, waits for them, and re-layouts: 1.41 us -> 0.14 us  [the longest x2 0.08 us: halve(): return add(both[:, :n], swap_second(both[:, n:], axis))]
    pallas_call x2 -> x3, Pallas kernels: 15.3 us -> 16 us  [grads(): pl.pallas_call(kernel, out_shape=[jax.ShapeDtypeStruct(w.shape, BF16) for...]
  transfers between devices with their start and end apart: 28 -> 30, of which waited for: 19 -> 14; matrix products, arithmetic and copies ran while one was open for 3% -> 6% of each run, Pallas kernels for 11% -> 21%
where the time goes in v4:
time: 103 us; the launch traced here: 101 us
  starting transfers between devices  48.1 us (47%)
  waiting for transfers between devices  24.5 us (24%)
  Pallas kernels  21.1 us (20%)
  other arithmetic  5.5 us (5%)
  local copies, waits for them, and re-layouts  1.21 us (1%)
    ppermute x21, starting transfers between devices, swap(): return lax.ppermute(value, AXES, pairs)  40.2 us
    ppermute x21, waiting for transfers between devices, swap(): return lax.ppermute(value, AXES, pairs)  23.2 us
    pallas_call x3, Pallas kernels, grads(): pl.pallas_call(kernel, out_shape=[jax.ShapeDtypeStruct(w.shape, BF16) for...  16 us
    ppermute x4, starting transfers between devices, swap_corner(): return lax.ppermute(value, AXES, pairs)  5.68 us
    pallas_call x1, Pallas kernels, input_parts(): pl.pallas_call(kernel, out_shape=[jax.ShapeDtypeStruct((group, width), F3...  5.06 us
    ppermute x5, starting transfers between devices, swap_core(): return lax.ppermute(value, AXES, [(d, d ^ 1) for d in range(DEVICES)])  2.24 us
  transfers between devices with their start and end apart: 30, of which 14 were waited for; matrix products, arithmetic and copies ran while one was open for 6% of the time, Pallas kernels for 21%

profile of v4, /device:TPU:2, one launch (start us, length us, event | category | flops | bytes accessed | tf_op | source)
XLA Modules:
  0.0 101.3 jit_solution(7301085718075671134)
XLA Ops:
  0.6 2.0 %collective-permute-start.5 = (bf16[384,1024]{1,0:T(8,128)(2,1)}, bf16[384,1024]{1,0:T(8,128)(2,1)S(1)}, u32[]{:S(2)}, u32[]{:S(2)}) collective-permute-start(bf16[384,1024]{1,0:T(8,128)(2,1)} %refs_0_.5), channel_id=1, source_target_pairs={{0,4},{1,5},{2,6},{3,7},{4,0},{5,1},{6,2},{7,3},{8,12},{9,13},{10,... | collective-permute-start | bytes 2359304 | tf_op jit(solution)/shard_map/ppermute | solution.py:33
  4.4 2.6 %collective-permute-start.1 = (bf16[3,24,1024]{2,1,0:T(8,128)(2,1)S(1)}, bf16[3,24,1024]{2,1,0:T(8,128)(2,1)S(1)}, u32[]{:S(2)}, u32[]{:S(2)}) collective-permute-start(bf16[3,24,1024]{2,1,0:T(8,128)(2,1)S(1)} %get-tuple-element.51), channel_id=1, source_target_pairs={{0,12},{1,13},{2,14},{3,15},{4,8},{5,9},{6,10},{7,11},{8,4},{9,5},... | collective-permute-start | bytes 442376 | tf_op jit(solution)/shard_map/ppermute | solution.py:33
  7.0 1.6 %collective-permute-start.10 = (bf16[3,24,1024]{2,1,0:T(8,128)(2,1)S(1)}, bf16[3,24,1024]{2,1,0:T(8,128)(2,1)S(1)}, u32[]{:S(2)}, u32[]{:S(2)}) collective-permute-start(bf16[3,24,1024]{2,1,0:T(8,128)(2,1)S(1)} %get-tuple-element.51), channel_id=1, source_target_pairs={{0,16},{1,49},{2,18},{3,51},{4,20},{5,53},{6,22},{7,55},{8,24},{9,... | collective-permute-start | bytes 442376 | tf_op jit(solution)/shard_map/ppermute | solution.py:33
  11.0 1.6 %collective-permute-start.2 = (bf16[3,24,1024]{2,1,0:T(8,128)(2,1)S(1)}, bf16[3,24,1024]{2,1,0:T(8,128)(2,1)S(1)}, u32[]{:S(2)}, u32[]{:S(2)}) collective-permute-start(bf16[3,24,1024]{2,1,0:T(8,128)(2,1)S(1)} %collective-permute-done.1), channel_id=1, source_target_pairs={{0,16},{1,49},{2,18},{3,51},{4,20},{5,53},{6,22},{7,55},{8,24},{9,... | collective-permute-start | bytes 442376 | tf_op jit(solution)/shard_map/ppermute | solution.py:33
  16.1 3.1 %collective-permute-start.13 = (bf16[3,96,1024]{2,1,0:T(8,128)(2,1)S(1)}, bf16[3,96,1024]{2,1,0:T(8,128)(2,1)S(1)}, u32[]{:S(2)}, u32[]{:S(2)}) collective-permute-start(bf16[3,96,1024]{2,1,0:T(8,128)(2,1)S(1)} %pad_maximum_fusion.1), channel_id=1, source_target_pairs={{0,48},{1,17},{2,50},{3,19},{4,52},{5,21},{6,54},{7,23},{8,56},{9,... | collective-permute-start | bytes 1769480 | tf_op jit(solution)/shard_map/ppermute | solution.py:33
  21.9 1.7 %collective-permute-start.8 = (bf16[384,1024]{1,0:T(8,128)(2,1)S(1)}, bf16[384,1024]{1,0:T(8,128)(2,1)S(1)}, u32[]{:S(2)}, u32[]{:S(2)}) collective-permute-start(bf16[384,1024]{1,0:T(8,128)(2,1)S(1)} %copy-done.1), channel_id=1, source_target_pairs={{0,4},{1,5},{2,6},{3,7},{4,0},{5,1},{6,2},{7,3},{8,12},{9,13},{10,... | collective-permute-start | bytes 2359304 | tf_op jit(solution)/shard_map/ppermute | solution.py:33
  23.7 3.6 %collective-permute-done.13 = bf16[3,96,1024]{2,1,0:T(8,128)(2,1)S(1)} collective-permute-done((bf16[3,96,1024]{2,1,0:T(8,128)(2,1)S(1)}, bf16[3,96,1024]{2,1,0:T(8,128)(2,1)S(1)}, u32[]{:S(2)}, u32[]{:S(2)}) %collective-permute-start.13) | collective-permute-done | bytes 589856 | tf_op jit(solution)/shard_map/ppermute | solution.py:33
  27.3 2.2 %collective-permute-start.14 = (bf16[3,192,1024]{2,1,0:T(8,128)(2,1)S(1)}, bf16[3,192,1024]{2,1,0:T(8,128)(2,1)S(1)}, u32[]{:S(2)}, u32[]{:S(2)}) collective-permute-start(bf16[3,192,1024]{2,1,0:T(8,128)(2,1)S(1)} %constant_dynamic-update-slice_fusion.refs_8_.refs_5_), channel_id=1, source_target_pairs={{0,66},{1,3},{2,64},{3,1},{4,70},{5,7},{6,68},{7,5},{8,74},{9,11},... | collective-permute-start | bytes 3538952 | tf_op jit(solution)/shard_map/ppermute | solution.py:33
  30.3 3.1 %collective-permute-start.16 = (bf16[3,192,1024]{2,1,0:T(8,128)(2,1)S(1)}, bf16[3,192,1024]{2,1,0:T(8,128)(2,1)S(1)}, u32[]{:S(2)}, u32[]{:S(2)}) collective-permute-start(bf16[3,192,1024]{2,1,0:T(8,128)(2,1)S(1)} %constant_dynamic-update-slice_fusion.5.refs_9_.refs_6_), channel_id=1, source_target_pairs={{0,48},{1,17},{2,50},{3,19},{4,52},{5,21},{6,54},{7,23},{8,56},{9,... | collective-permute-start | bytes 3538952 | tf_op jit(solution)/shard_map/ppermute | solution.py:33
  33.9 6.9 %collective-permute-done.8.refs_6_ = bf16[384,1024]{1,0:T(8,128)(2,1)S(1)} collective-permute-done((bf16[384,1024]{1,0:T(8,128)(2,1)S(1)}, bf16[384,1024]{1,0:T(8,128)(2,1)S(1)}, u32[]{:S(2)}, u32[]{:S(2)}) %collective-permute-start.8) | collective-permute-done | bytes 786464 | tf_op jit(solution)/shard_map/ppermute | solution.py:33
  40.8 1.6 %collective-permute-start.9 = (bf16[384,1024]{1,0:T(8,128)(2,1)S(1)}, bf16[384,1024]{1,0:T(8,128)(2,1)S(1)}, u32[]{:S(2)}, u32[]{:S(2)}) collective-permute-start(bf16[384,1024]{1,0:T(8,128)(2,1)S(1)} %collective-permute-done.8.refs_6_), channel_id=1, source_target_pairs={{0,1},{1,0},{2,3},{3,2},{4,5},{5,4},{6,7},{7,6},{8,9},{9,8},{10,11... | collective-permute-start | bytes 2359304 | tf_op jit(solution)/shard_map/ppermute | solution.py:63
  44.3 4.2 %shard_map.59 = (bf16[3,192,1024]{2,1,0:T(8,128)(2,1)S(1)}, bf16[384,1536]{1,0:T(8,128)(2,1)S(1)}) custom-call(bf16[384,1024]{1,0:T(8,128)(2,1)S(1)} %copy-done, bf16[384,1024]{1,0:T(8,128)(2,1)S(1)} %collective-permute-done.refs_1_, bf16[384,1024]{1,0:T(8,128)(2,1)S(1)} %collective-permute-done.5.refs_2_, ...), custom_call_target="tpu_custom_call" | custom-call | flops 1024 | bytes 1024 | tf_op jit(solution)/shard_map/pallas_call | solution.py:145
  48.5 1.7 %collective-permute-start.18 = (bf16[3,192,1024]{2,1,0:T(8,128)(2,1)S(1)}, bf16[3,192,1024]{2,1,0:T(8,128)(2,1)S(1)}, u32[]{:S(2)}, u32[]{:S(2)}) collective-permute-start(bf16[3,192,1024]{2,1,0:T(8,128)(2,1)S(1)} %get-tuple-element.35), channel_id=1, source_target_pairs={{0,66},{1,3},{2,64},{3,1},{4,70},{5,7},{6,68},{7,5},{8,74},{9,11},... | collective-permute-start | bytes 3538952 | tf_op jit(solution)/shard_map/ppermute | solution.py:33
  50.2 4.2 %shard_map.60 = (bf16[3,192,1024]{2,1,0:T(8,128)(2,1)S(1)}, bf16[384,1536]{1,0:T(8,128)(2,1)S(1)}) custom-call(bf16[384,1024]{1,0:T(8,128)(2,1)S(1)} %copy-done, bf16[384,1024]{1,0:T(8,128)(2,1)S(1)} %collective-permute-done.refs_1_, bf16[384,1024]{1,0:T(8,128)(2,1)S(1)} %collective-permute-done.5.refs_2_, ...), custom_call_target="tpu_custom_call" | custom-call | flops 1024 | bytes 1024 | tf_op jit(solution)/shard_map/pallas_call | solution.py:145
  54.4 2.4 %collective-permute-start.19 = (bf16[3,192,1024]{2,1,0:T(8,128)(2,1)S(1)}, bf16[3,192,1024]{2,1,0:T(8,128)(2,1)S(1)}, u32[]{:S(2)}, u32[]{:S(2)}) collective-permute-start(bf16[3,192,1024]{2,1,0:T(8,128)(2,1)S(1)} %get-tuple-element.37), channel_id=1, source_target_pairs={{0,48},{1,17},{2,50},{3,19},{4,52},{5,21},{6,54},{7,23},{8,56},{9,... | collective-permute-start | bytes 3538952 | tf_op jit(solution)/shard_map/ppermute | solution.py:33
  56.8 7.7 %shard_map.61 = (bf16[3,192,1024]{2,1,0:T(8,128)(2,1)S(1)}, bf16[3,192,1024]{2,1,0:T(8,128)(2,1)S(1)}, bf16[768,1536]{1,0:T(8,128)(2,1)S(1)}) custom-call(bf16[384,1024]{1,0:T(8,128)(2,1)S(1)} %copy-done, bf16[384,1024]{1,0:T(8,128)(2,1)S(1)} %collective-permute-done.refs_1_, bf16[384,1024]{1,0:T(8,128)(2,1)S(1)} %collective-permute-done.5.refs_2_, ...), custom_call_target="tpu_custom_call" | custom-call | flops 1024 | bytes 1024 | tf_op jit(solution)/shard_map/pallas_call | solution.py:145
  64.5 5.1 %shard_map.62 = (f32[384,1024]{1,0:T(8,128)S(1)}, f32[384,1024]{1,0:T(8,128)S(1)}, bf16[2,384,1024]{2,1,0:T(8,128)(2,1)S(1)}) custom-call(bf16[384,1536]{1,0:T(8,128)(2,1)S(1)} %get-tuple-element.25.refs_0_, bf16[384,1536]{1,0:T(8,128)(2,1)S(1)} %get-tuple-element.28.refs_1_, bf16[768,1536]{1,0:T(8,128)(2,1)S(1)} %get-tuple-element.31.refs_2_, ...), custom_call_target="tpu_custom_call" | custom-call | flops 1024 | bytes 1024 | tf_op jit(solution)/shard_map/pallas_call | solution.py:184
  70.1 1.7 %collective-permute-done.19 = bf16[3,192,1024]{2,1,0:T(8,128)(2,1)S(1)} collective-permute-done((bf16[3,192,1024]{2,1,0:T(8,128)(2,1)S(1)}, bf16[3,192,1024]{2,1,0:T(8,128)(2,1)S(1)}, u32[]{:S(2)}, u32[]{:S(2)}) %collective-permute-start.19) | collective-permute-done | bytes 1179680 | tf_op jit(solution)/shard_map/ppermute | solution.py:33
  73.1 2.4 %collective-permute-start.25 = (bf16[3,96,1024]{2,1,0:T(8,128)(2,1)S(1)}, bf16[3,96,1024]{2,1,0:T(8,128)(2,1)S(1)}, u32[]{:S(2)}, u32[]{:S(2)}) collective-permute-start(bf16[3,96,1024]{2,1,0:T(8,128)(2,1)S(1)} %slice.51), channel_id=1, source_target_pairs={{0,48},{1,17},{2,50},{3,19},{4,52},{5,21},{6,54},{7,23},{8,56},{9,... | collective-permute-start | bytes 1769480 | tf_op jit(solution)/shard_map/ppermute | solution.py:33
  77.1 5.3 %collective-permute-done.20 = bf16[3,96,1024]{2,1,0:T(8,128)(2,1)S(1)} collective-permute-done((bf16[3,96,1024]{2,1,0:T(8,128)(2,1)S(1)}, bf16[3,96,1024]{2,1,0:T(8,128)(2,1)S(1)}, u32[]{:S(2)}, u32[]{:S(2)}) %collective-permute-start.20) | collective-permute-done | bytes 589856 | tf_op jit(solution)/shard_map/ppermute | solution.py:33
  82.7 4.6 %collective-permute-start.22 = (bf16[3,24,1024]{2,1,0:T(8,128)(2,1)S(1)}, bf16[3,24,1024]{2,1,0:T(8,128)(2,1)S(1)}, u32[]{:S(2)}, u32[]{:S(2)}) collective-permute-start(bf16[3,24,1024]{2,1,0:T(8,128)(2,1)S(1)} %get-tuple-element.49), channel_id=1, source_target_pairs={{0,2},{1,67},{2,0},{3,65},{4,6},{5,71},{6,4},{7,69},{8,10},{9,75},... | collective-permute-start | bytes 442376 | tf_op jit(solution)/shard_map/ppermute | solution.py:33
  89.6 2.8 %collective-permute-start.27 = (bf16[3,24,1024]{2,1,0:T(8,128)(2,1)S(1)}, bf16[3,24,1024]{2,1,0:T(8,128)(2,1)S(1)}, u32[]{:S(2)}, u32[]{:S(2)}) collective-permute-start(bf16[3,24,1024]{2,1,0:T(8,128)(2,1)S(1)} %get-tuple-element.46), channel_id=1, source_target_pairs={{0,2},{1,67},{2,0},{3,65},{4,6},{5,71},{6,4},{7,69},{8,10},{9,75},... | collective-permute-start | bytes 442376 | tf_op jit(solution)/shard_map/ppermute | solution.py:33
  94.2 3.2 %collective-permute-start.29 = (bf16[3,24,1024]{2,1,0:T(8,128)(2,1)S(1)}, bf16[3,24,1024]{2,1,0:T(8,128)(2,1)S(1)}, u32[]{:S(2)}, u32[]{:S(2)}) collective-permute-start(bf16[3,24,1024]{2,1,0:T(8,128)(2,1)S(1)} %add_convert_fusion.4), channel_id=1, source_target_pairs={{0,12},{1,13},{2,14},{3,15},{4,8},{5,9},{6,10},{7,11},{8,4},{9,5},... | collective-permute-start | bytes 442376 | tf_op jit(solution)/shard_map/ppermute | solution.py:33
  98.6 1.9 %collective-permute-done.29 = bf16[3,24,1024]{2,1,0:T(8,128)(2,1)S(1)} collective-permute-done((bf16[3,24,1024]{2,1,0:T(8,128)(2,1)S(1)}, bf16[3,24,1024]{2,1,0:T(8,128)(2,1)S(1)}, u32[]{:S(2)}, u32[]{:S(2)}) %collective-permute-start.29) | collective-permute-done | bytes 147488 | tf_op jit(solution)/shard_map/ppermute | solution.py:33
  (66 shorter events, 23.5 us)
Async XLA Ops:
  0.6 19.7 %collective-permute-start.5 = (bf16[384,1024]{1,0:T(8,128)(2,1)}, bf16[384,1024]{1,0:T(8,128)(2,1)S(1)}, u32[]{:S(2)}, u32[]{:S(2)}) collective-permute-start(bf16[384,1024]{1,0:T(8,128)(2,1)} %refs_0_.5), channel_id=1, source_target_pairs={{0,4},{1,5},{2,6},{3,7},{4,0},{5,1},{6,2},{7,3},{8,12},{9,13},{10,... | collective-permute-start | bytes 2359304 | tf_op jit(solution)/shard_map/ppermute | solution.py:33
  4.4 6.6 %collective-permute-start.1 = (bf16[3,24,1024]{2,1,0:T(8,128)(2,1)S(1)}, bf16[3,24,1024]{2,1,0:T(8,128)(2,1)S(1)}, u32[]{:S(2)}, u32[]{:S(2)}) collective-permute-start(bf16[3,24,1024]{2,1,0:T(8,128)(2,1)S(1)} %get-tuple-element.51), channel_id=1, source_target_pairs={{0,12},{1,13},{2,14},{3,15},{4,8},{5,9},{6,10},{7,11},{8,4},{9,5},... | collective-permute-start | bytes 442376 | tf_op jit(solution)/shard_map/ppermute | solution.py:33
  11.0 8.2 %collective-permute-start.2 = (bf16[3,24,1024]{2,1,0:T(8,128)(2,1)S(1)}, bf16[3,24,1024]{2,1,0:T(8,128)(2,1)S(1)}, u32[]{:S(2)}, u32[]{:S(2)}) collective-permute-start(bf16[3,24,1024]{2,1,0:T(8,128)(2,1)S(1)} %collective-permute-done.1), channel_id=1, source_target_pairs={{0,16},{1,49},{2,18},{3,51},{4,20},{5,53},{6,22},{7,55},{8,24},{9,... | collective-permute-start | bytes 442376 | tf_op jit(solution)/shard_map/ppermute | solution.py:33
  12.6 6.6 %collective-permute-start.3 = (bf16[3,24,1024]{2,1,0:T(8,128)(2,1)S(1)}, bf16[3,24,1024]{2,1,0:T(8,128)(2,1)S(1)}, u32[]{:S(2)}, u32[]{:S(2)}) collective-permute-start(bf16[3,24,1024]{2,1,0:T(8,128)(2,1)S(1)} %collective-permute-done.1), channel_id=1, source_target_pairs={{0,2},{1,67},{2,0},{3,65},{4,6},{5,71},{6,4},{7,69},{8,10},{9,75},... | collective-permute-start | bytes 442376 | tf_op jit(solution)/shard_map/ppermute | solution.py:33
  16.1 11.2 %collective-permute-start.13 = (bf16[3,96,1024]{2,1,0:T(8,128)(2,1)S(1)}, bf16[3,96,1024]{2,1,0:T(8,128)(2,1)S(1)}, u32[]{:S(2)}, u32[]{:S(2)}) collective-permute-start(bf16[3,96,1024]{2,1,0:T(8,128)(2,1)S(1)} %pad_maximum_fusion.1), channel_id=1, source_target_pairs={{0,48},{1,17},{2,50},{3,19},{4,52},{5,21},{6,54},{7,23},{8,56},{9,... | collective-permute-start | bytes 1769480 | tf_op jit(solution)/shard_map/ppermute | solution.py:33
  19.2 14.2 %collective-permute-start = (bf16[384,1024]{1,0:T(8,128)(2,1)S(1)}, bf16[384,1024]{1,0:T(8,128)(2,1)S(1)}, u32[]{:S(2)}, u32[]{:S(2)}) collective-permute-start(bf16[384,1024]{1,0:T(8,128)(2,1)S(1)} %copy-done), channel_id=1, source_target_pairs={{0,1},{1,0},{2,3},{3,2},{4,5},{5,4},{6,7},{7,6},{8,9},{9,8},{10,11... | collective-permute-start | bytes 2359304 | tf_op jit(solution)/shard_map/ppermute | solution.py:63
  20.4 9.9 %collective-permute-start.15 = (bf16[3,96,1024]{2,1,0:T(8,128)(2,1)S(1)}, bf16[3,96,1024]{2,1,0:T(8,128)(2,1)S(1)}, u32[]{:S(2)}, u32[]{:S(2)}) collective-permute-start(bf16[3,96,1024]{2,1,0:T(8,128)(2,1)S(1)} %pad_maximum_fusion), channel_id=1, source_target_pairs={{0,66},{1,3},{2,64},{3,1},{4,70},{5,7},{6,68},{7,5},{8,74},{9,11},... | collective-permute-start | bytes 1769480 | tf_op jit(solution)/shard_map/ppermute | solution.py:33
  21.9 18.9 %collective-permute-start.8 = (bf16[384,1024]{1,0:T(8,128)(2,1)S(1)}, bf16[384,1024]{1,0:T(8,128)(2,1)S(1)}, u32[]{:S(2)}, u32[]{:S(2)}) collective-permute-start(bf16[384,1024]{1,0:T(8,128)(2,1)S(1)} %copy-done.1), channel_id=1, source_target_pairs={{0,4},{1,5},{2,6},{3,7},{4,0},{5,1},{6,2},{7,3},{8,12},{9,13},{10,... | collective-permute-start | bytes 2359304 | tf_op jit(solution)/shard_map/ppermute | solution.py:33
  27.3 16.4 %collective-permute-start.14 = (bf16[3,192,1024]{2,1,0:T(8,128)(2,1)S(1)}, bf16[3,192,1024]{2,1,0:T(8,128)(2,1)S(1)}, u32[]{:S(2)}, u32[]{:S(2)}) collective-permute-start(bf16[3,192,1024]{2,1,0:T(8,128)(2,1)S(1)} %constant_dynamic-update-slice_fusion.refs_8_.refs_5_), channel_id=1, source_target_pairs={{0,66},{1,3},{2,64},{3,1},{4,70},{5,7},{6,68},{7,5},{8,74},{9,11},... | collective-permute-start | bytes 3538952 | tf_op jit(solution)/shard_map/ppermute | solution.py:33
  30.3 19.9 %collective-permute-start.16 = (bf16[3,192,1024]{2,1,0:T(8,128)(2,1)S(1)}, bf16[3,192,1024]{2,1,0:T(8,128)(2,1)S(1)}, u32[]{:S(2)}, u32[]{:S(2)}) collective-permute-start(bf16[3,192,1024]{2,1,0:T(8,128)(2,1)S(1)} %constant_dynamic-update-slice_fusion.5.refs_9_.refs_6_), channel_id=1, source_target_pairs={{0,48},{1,17},{2,50},{3,19},{4,52},{5,21},{6,54},{7,23},{8,56},{9,... | collective-permute-start | bytes 3538952 | tf_op jit(solution)/shard_map/ppermute | solution.py:33
  33.4 9.0 %collective-permute-start.7 = (bf16[384,1024]{1,0:T(8,128)(2,1)S(1)}, bf16[384,1024]{1,0:T(8,128)(2,1)S(1)}, u32[]{:S(2)}, u32[]{:S(2)}) collective-permute-start(bf16[384,1024]{1,0:T(8,128)(2,1)S(1)} %copy-done.1), channel_id=1, source_target_pairs={{0,1},{1,0},{2,3},{3,2},{4,5},{5,4},{6,7},{7,6},{8,9},{9,8},{10,11... | collective-permute-start | bytes 2359304 | tf_op jit(solution)/shard_map/ppermute | solution.py:63
  33.4 9.0 %collective-permute-start.6 = (bf16[384,1024]{1,0:T(8,128)(2,1)S(1)}, bf16[384,1024]{1,0:T(8,128)(2,1)S(1)}, u32[]{:S(2)}, u32[]{:S(2)}) collective-permute-start(bf16[384,1024]{1,0:T(8,128)(2,1)S(1)} %collective-permute-done.5.refs_2_), channel_id=1, source_target_pairs={{0,1},{1,0},{2,3},{3,2},{4,5},{5,4},{6,7},{7,6},{8,9},{9,8},{10,11... | collective-permute-start | bytes 2359304 | tf_op jit(solution)/shard_map/ppermute | solution.py:63
  48.5 21.1 %collective-permute-start.18 = (bf16[3,192,1024]{2,1,0:T(8,128)(2,1)S(1)}, bf16[3,192,1024]{2,1,0:T(8,128)(2,1)S(1)}, u32[]{:S(2)}, u32[]{:S(2)}) collective-permute-start(bf16[3,192,1024]{2,1,0:T(8,128)(2,1)S(1)} %get-tuple-element.35), channel_id=1, source_target_pairs={{0,66},{1,3},{2,64},{3,1},{4,70},{5,7},{6,68},{7,5},{8,74},{9,11},... | collective-permute-start | bytes 3538952 | tf_op jit(solution)/shard_map/ppermute | solution.py:33
  54.4 17.5 %collective-permute-start.19 = (bf16[3,192,1024]{2,1,0:T(8,128)(2,1)S(1)}, bf16[3,192,1024]{2,1,0:T(8,128)(2,1)S(1)}, u32[]{:S(2)}, u32[]{:S(2)}) collective-permute-start(bf16[3,192,1024]{2,1,0:T(8,128)(2,1)S(1)} %get-tuple-element.37), channel_id=1, source_target_pairs={{0,48},{1,17},{2,50},{3,19},{4,52},{5,21},{6,54},{7,23},{8,56},{9,... | collective-permute-start | bytes 3538952 | tf_op jit(solution)/shard_map/ppermute | solution.py:33
  72.4 10.0 %collective-permute-start.20 = (bf16[3,96,1024]{2,1,0:T(8,128)(2,1)S(1)}, bf16[3,96,1024]{2,1,0:T(8,128)(2,1)S(1)}, u32[]{:S(2)}, u32[]{:S(2)}) collective-permute-start(bf16[3,96,1024]{2,1,0:T(8,128)(2,1)S(1)} %slice.44), channel_id=1, source_target_pairs={{0,66},{1,3},{2,64},{3,1},{4,70},{5,7},{6,68},{7,5},{8,74},{9,11},... | collective-permute-start | bytes 1769480 | tf_op jit(solution)/shard_map/ppermute | solution.py:33
  73.1 15.5 %collective-permute-start.25 = (bf16[3,96,1024]{2,1,0:T(8,128)(2,1)S(1)}, bf16[3,96,1024]{2,1,0:T(8,128)(2,1)S(1)}, u32[]{:S(2)}, u32[]{:S(2)}) collective-permute-start(bf16[3,96,1024]{2,1,0:T(8,128)(2,1)S(1)} %slice.51), channel_id=1, source_target_pairs={{0,48},{1,17},{2,50},{3,19},{4,52},{5,21},{6,54},{7,23},{8,56},{9,... | collective-permute-start | bytes 1769480 | tf_op jit(solution)/shard_map/ppermute | solution.py:33
  75.8 18.4 %collective-permute-start.24 = (bf16[384,1024]{1,0:T(8,128)(2,1)S(1)}, bf16[384,1024]{1,0:T(8,128)(2,1)S(1)}, u32[]{:S(2)}, u32[]{:S(2)}) collective-permute-start(bf16[384,1024]{1,0:T(8,128)(2,1)S(1)} %fusion), channel_id=1, source_target_pairs={{0,4},{1,5},{2,6},{3,7},{4,0},{5,1},{6,2},{7,3},{8,12},{9,13},{10,... | collective-permute-start | bytes 2359304 | tf_op jit(solution)/shard_map/ppermute | solution.py:33
  82.7 6.9 %collective-permute-start.21 = (bf16[3,24,1024]{2,1,0:T(8,128)(2,1)S(1)}, bf16[3,24,1024]{2,1,0:T(8,128)(2,1)S(1)}, u32[]{:S(2)}, u32[]{:S(2)}) collective-permute-start(bf16[3,24,1024]{2,1,0:T(8,128)(2,1)S(1)} %get-tuple-element.47), channel_id=1, source_target_pairs={{0,16},{1,49},{2,18},{3,51},{4,20},{5,53},{6,22},{7,55},{8,24},{9,... | collective-permute-start | bytes 442376 | tf_op jit(solution)/shard_map/ppermute | solution.py:33
  82.7 9.6 %collective-permute-start.22 = (bf16[3,24,1024]{2,1,0:T(8,128)(2,1)S(1)}, bf16[3,24,1024]{2,1,0:T(8,128)(2,1)S(1)}, u32[]{:S(2)}, u32[]{:S(2)}) collective-permute-start(bf16[3,24,1024]{2,1,0:T(8,128)(2,1)S(1)} %get-tuple-element.49), channel_id=1, source_target_pairs={{0,2},{1,67},{2,0},{3,65},{4,6},{5,71},{6,4},{7,69},{8,10},{9,75},... | collective-permute-start | bytes 442376 | tf_op jit(solution)/shard_map/ppermute | solution.py:33
  87.3 6.5 %collective-permute-start.23 = (bf16[3,24,1024]{2,1,0:T(8,128)(2,1)S(1)}, bf16[3,24,1024]{2,1,0:T(8,128)(2,1)S(1)}, u32[]{:S(2)}, u32[]{:S(2)}) collective-permute-start(bf16[3,24,1024]{2,1,0:T(8,128)(2,1)S(1)} %get-tuple-element.48), channel_id=1, source_target_pairs={{0,18},{1,115},{2,16},{3,113},{4,22},{5,119},{6,20},{7,117},{8,26}... | collective-permute-start | bytes 442376 | tf_op jit(solution)/shard_map/ppermute | solution.py:59
  88.9 9.6 %collective-permute-start.26 = (bf16[3,24,1024]{2,1,0:T(8,128)(2,1)S(1)}, bf16[3,24,1024]{2,1,0:T(8,128)(2,1)S(1)}, u32[]{:S(2)}, u32[]{:S(2)}) collective-permute-start(bf16[3,24,1024]{2,1,0:T(8,128)(2,1)S(1)} %get-tuple-element.44), channel_id=1, source_target_pairs={{0,16},{1,49},{2,18},{3,51},{4,20},{5,53},{6,22},{7,55},{8,24},{9,... | collective-permute-start | bytes 442376 | tf_op jit(solution)/shard_map/ppermute | solution.py:33
  89.6 9.0 %collective-permute-start.27 = (bf16[3,24,1024]{2,1,0:T(8,128)(2,1)S(1)}, bf16[3,24,1024]{2,1,0:T(8,128)(2,1)S(1)}, u32[]{:S(2)}, u32[]{:S(2)}) collective-permute-start(bf16[3,24,1024]{2,1,0:T(8,128)(2,1)S(1)} %get-tuple-element.46), channel_id=1, source_target_pairs={{0,2},{1,67},{2,0},{3,65},{4,6},{5,71},{6,4},{7,69},{8,10},{9,75},... | collective-permute-start | bytes 442376 | tf_op jit(solution)/shard_map/ppermute | solution.py:33
  92.4 6.2 %collective-permute-start.28 = (bf16[3,24,1024]{2,1,0:T(8,128)(2,1)S(1)}, bf16[3,24,1024]{2,1,0:T(8,128)(2,1)S(1)}, u32[]{:S(2)}, u32[]{:S(2)}) collective-permute-start(bf16[3,24,1024]{2,1,0:T(8,128)(2,1)S(1)} %get-tuple-element.45), channel_id=1, source_target_pairs={{0,18},{1,115},{2,16},{3,113},{4,22},{5,119},{6,20},{7,117},{8,26}... | collective-permute-start | bytes 442376 | tf_op jit(solution)/shard_map/ppermute | solution.py:59
  94.2 6.4 %collective-permute-start.29 = (bf16[3,24,1024]{2,1,0:T(8,128)(2,1)S(1)}, bf16[3,24,1024]{2,1,0:T(8,128)(2,1)S(1)}, u32[]{:S(2)}, u32[]{:S(2)}) collective-permute-start(bf16[3,24,1024]{2,1,0:T(8,128)(2,1)S(1)} %add_convert_fusion.4), channel_id=1, source_target_pairs={{0,12},{1,13},{2,14},{3,15},{4,8},{5,9},{6,10},{7,11},{8,4},{9,5},... | collective-permute-start | bytes 442376 | tf_op jit(solution)/shard_map/ppermute | solution.py:33
  (8 other events, 68.6 us)

commit v5 on v4

--- a/solution.py
+++ b/solution.py
@@ -82,9 +82,10 @@
     return total + swap_first(along_x, X).astype(F32) + swap_corner(corner).astype(F32)
 
 
-def halve(both, axis):
-    n = both.shape[1] // 2
-    return add(both[:, :n], swap_second(both[:, n:], axis))
+def reduce(near, back, axis):
+    n = near.shape[1] // 2
+    got = swap_second(add(near[:, n:], back[:, n:]), axis)
+    return (near[:, :n].astype(F32) + back[:, :n].astype(F32) + got.astype(F32)).astype(BF16)
 
 
 def rows_of(refs, start, stop, cols=slice(None)):
@@ -200,9 +201,9 @@
 def body(activations, cotangent, gate_up, down_proj):
     x_z = swap_near(activations, Z)
     message = jnp.concatenate([gate_up.transpose(1, 0, 2), down_proj[None]], axis=0)
-    other = swap_wrap(message, Z)
+    message = lax.optimization_barrier(message)
+    block1 = gather_block(swap_wrap(message, Z))
     block0 = gather_block(message)
-    block1 = gather_block(other)
     block1, x_z, c_own = lax.optimization_barrier((block1, x_z, cotangent))
     c_z = swap_near(c_own, Z)
     j0 = join(block0, swap_second(block0, Y))
@@ -211,24 +212,25 @@
     xs = [activations, swap_core(activations), x_z, swap_core(x_z)]
     cs = [cotangent, swap_core(cotangent), c_z, swap_core(c_z)]
 
+    g_j0, a_j0 = grads(xs, cs, [j0])
+    r0, r1, a_j0 = lax.optimization_barrier((r0, r1, a_j0))
+    g_r1, a_r1 = grads(xs, cs, [r1])
+    back1 = swap_second(g_r1, Y)
+    r0, a_r1 = lax.optimization_barrier((r0, a_r1))
     g_r0, a_r0 = grads(xs, cs, [r0])
     back0 = swap_second(g_r0, X)
-    g_r1, a_r1 = grads(xs, cs, [r1])
-    back1 = swap_second(g_r1, Y)
-    j0, j1, a_r1 = lax.optimization_barrier((j0, j1, a_r1))
-    g_j0, g_j1, a_j = grads(xs, cs, [j0, j1])
-
-    own, z_part, pair = input_parts([a_r0, a_r1, a_j], [r0, r1, j0, j1])
+    j1, a_r0 = lax.optimization_barrier((j1, a_r0))
+    g_j1, a_j1 = grads(xs, cs, [j1])
+
+    own, z_part, pair = input_parts([a_r0, a_r1, a_j0, a_j1], [r0, r1, j0, j1])
     got = swap_core(pair)
-    near0, near1 = add(g_j0, back0), add(g_j1, back1)
-    near0, near1, z_part = lax.optimization_barrier((near0, near1, z_part))
+    back0, back1, z_part = lax.optimization_barrier((back0, back1, z_part))
     mine = own + got[0].astype(F32)
     z_part = swap_near((z_part + got[1].astype(F32)).astype(BF16), Z)
-
-    total1 = reduce_block(halve(near1, X)).astype(BF16)
-    total1, z_part = lax.optimization_barrier((total1, z_part))
+    total1 = reduce_block(reduce(g_j1, back1, X)).astype(BF16)
+    total0 = reduce_block(reduce(g_j0, back0, Y))
     grad_input = (mine + z_part.astype(F32)).astype(BF16)
-    total0 = reduce_block(halve(near0, Y))
+    total0, grad_input = lax.optimization_barrier((total0, grad_input))
     total = total0 + swap_wrap(total1, Z).astype(F32)
     return (grad_input, total.transpose(1, 0, 2))
 

time: 103 us -> 111 us (1.078)
  waiting for transfers between devices: 24.5 us -> 33.2 us
  other arithmetic: 5.5 us -> 4.35 us
    ppermute x4, starting transfers between devices: 5.68 us -> 13.8 us  [swap_corner(): return lax.ppermute(value, AXES, pairs)]
    ppermute x21, waiting for transfers between devices: 23.2 us -> 30.8 us  [swap(): return lax.ppermute(value, AXES, pairs)]
    ppermute x21, starting transfers between devices: 40.2 us -> 32.9 us  [swap(): return lax.ppermute(value, AXES, pairs)]
    ppermute x5, waiting for transfers between devices: 0.6 us -> 1.92 us  [swap_core(): return lax.ppermute(value, AXES, [(d, d ^ 1) for d in range(DEVICES)])]
    pallas_call x3 -> x4, Pallas kernels: 16 us -> 16.7 us  [grads(): pl.pallas_call(kernel, out_shape=[jax.ShapeDtypeStruct(w.shape, BF16) for...]
  transfers between devices with their start and end apart: 30 -> 30, of which waited for: 14 -> 14; matrix products, arithmetic and copies ran while one was open for 6% -> 4% of each run, Pallas kernels for 21% -> 16%
where the time goes in v5:
time: 111 us; the launch traced here: 109 us
  starting transfers between devices  47.9 us (43%)
  waiting for transfers between devices  33.2 us (30%)
  Pallas kernels  21.8 us (20%)
  other arithmetic  4.35 us (4%)
  local copies, waits for them, and re-layouts  1.14 us (1%)
    ppermute x21, starting transfers between devices, swap(): return lax.ppermute(value, AXES, pairs)  32.9 us
    ppermute x21, waiting for transfers between devices, swap(): return lax.ppermute(value, AXES, pairs)  30.8 us
    pallas_call x4, Pallas kernels, grads(): pl.pallas_call(kernel, out_shape=[jax.ShapeDtypeStruct(w.shape, BF16) for...  16.7 us
    ppermute x4, starting transfers between devices, swap_corner(): return lax.ppermute(value, AXES, pairs)  13.8 us
    pallas_call x1, Pallas kernels, input_parts(): pl.pallas_call(kernel, out_shape=[jax.ShapeDtypeStruct((group, width), F3...  5.06 us
  transfers between devices with their start and end apart: 30, of which 14 were waited for; matrix products, arithmetic and copies ran while one was open for 4% of the time, Pallas kernels for 16%

profile of v5, /device:TPU:2, one launch (start us, length us, event | category | flops | bytes accessed | tf_op | source)
XLA Modules:
  0.0 109.3 jit_solution(10365039030493362670)
XLA Ops:
  0.6 2.0 %collective-permute-start.5 = (bf16[384,1024]{1,0:T(8,128)(2,1)}, bf16[384,1024]{1,0:T(8,128)(2,1)S(1)}, u32[]{:S(2)}, u32[]{:S(2)}) collective-permute-start(bf16[384,1024]{1,0:T(8,128)(2,1)} %refs_0_.7), channel_id=1, source_target_pairs={{0,4},{1,5},{2,6},{3,7},{4,0},{5,1},{6,2},{7,3},{8,12},{9,13},{10,... | collective-permute-start | bytes 2359304 | tf_op jit(solution)/shard_map/ppermute | solution.py:33
  4.4 2.6 %collective-permute-start.1 = (bf16[3,24,1024]{2,1,0:T(8,128)(2,1)S(1)}, bf16[3,24,1024]{2,1,0:T(8,128)(2,1)S(1)}, u32[]{:S(2)}, u32[]{:S(2)}) collective-permute-start(bf16[3,24,1024]{2,1,0:T(8,128)(2,1)S(1)} %pad_maximum_fusion.2), channel_id=1, source_target_pairs={{0,12},{1,13},{2,14},{3,15},{4,8},{5,9},{6,10},{7,11},{8,4},{9,5},... | collective-permute-start | bytes 442376 | tf_op jit(solution)/shard_map/ppermute | solution.py:33
  7.0 1.5 %collective-permute-start.12 = (bf16[3,24,1024]{2,1,0:T(8,128)(2,1)S(1)}, bf16[3,24,1024]{2,1,0:T(8,128)(2,1)S(1)}, u32[]{:S(2)}, u32[]{:S(2)}) collective-permute-start(bf16[3,24,1024]{2,1,0:T(8,128)(2,1)S(1)} %pad_maximum_fusion.2), channel_id=1, source_target_pairs={{0,18},{1,115},{2,16},{3,113},{4,22},{5,119},{6,20},{7,117},{8,26}... | collective-permute-start | bytes 442376 | tf_op jit(solution)/shard_map/ppermute | solution.py:59
  11.0 1.5 %collective-permute-start.4 = (bf16[3,24,1024]{2,1,0:T(8,128)(2,1)S(1)}, bf16[3,24,1024]{2,1,0:T(8,128)(2,1)S(1)}, u32[]{:S(2)}, u32[]{:S(2)}) collective-permute-start(bf16[3,24,1024]{2,1,0:T(8,128)(2,1)S(1)} %collective-permute-done.1), channel_id=1, source_target_pairs={{0,18},{1,115},{2,16},{3,113},{4,22},{5,119},{6,20},{7,117},{8,26}... | collective-permute-start | bytes 442376 | tf_op jit(solution)/shard_map/ppermute | solution.py:59
  15.3 3.1 %collective-permute-start.13 = (bf16[3,96,1024]{2,1,0:T(8,128)(2,1)S(1)}, bf16[3,96,1024]{2,1,0:T(8,128)(2,1)S(1)}, u32[]{:S(2)}, u32[]{:S(2)}) collective-permute-start(bf16[3,96,1024]{2,1,0:T(8,128)(2,1)S(1)} %pad_maximum_fusion.1), channel_id=1, source_target_pairs={{0,48},{1,17},{2,50},{3,19},{4,52},{5,21},{6,54},{7,23},{8,56},{9,... | collective-permute-start | bytes 1769480 | tf_op jit(solution)/shard_map/ppermute | solution.py:33
  21.9 1.8 %collective-permute-start.8 = (bf16[384,1024]{1,0:T(8,128)(2,1)S(1)}, bf16[384,1024]{1,0:T(8,128)(2,1)S(1)}, u32[]{:S(2)}, u32[]{:S(2)}) collective-permute-start(bf16[384,1024]{1,0:T(8,128)(2,1)S(1)} %copy-done.1), channel_id=1, source_target_pairs={{0,4},{1,5},{2,6},{3,7},{4,0},{5,1},{6,2},{7,3},{8,12},{9,13},{10,... | collective-permute-start | bytes 2359304 | tf_op jit(solution)/shard_map/ppermute | solution.py:33
  23.8 2.7 %collective-permute-done.13 = bf16[3,96,1024]{2,1,0:T(8,128)(2,1)S(1)} collective-permute-done((bf16[3,96,1024]{2,1,0:T(8,128)(2,1)S(1)}, bf16[3,96,1024]{2,1,0:T(8,128)(2,1)S(1)}, u32[]{:S(2)}, u32[]{:S(2)}) %collective-permute-start.13) | collective-permute-done | bytes 589856 | tf_op jit(solution)/shard_map/ppermute | solution.py:33
  26.5 2.2 %collective-permute-start.14 = (bf16[3,192,1024]{2,1,0:T(8,128)(2,1)S(1)}, bf16[3,192,1024]{2,1,0:T(8,128)(2,1)S(1)}, u32[]{:S(2)}, u32[]{:S(2)}) collective-permute-start(bf16[3,192,1024]{2,1,0:T(8,128)(2,1)S(1)} %constant_dynamic-update-slice_fusion.refs_8_.refs_6_), channel_id=1, source_target_pairs={{0,66},{1,3},{2,64},{3,1},{4,70},{5,7},{6,68},{7,5},{8,74},{9,11},... | collective-permute-start | bytes 3538952 | tf_op jit(solution)/shard_map/ppermute | solution.py:33
  28.7 1.5 %collective-permute-done.15 = bf16[3,96,1024]{2,1,0:T(8,128)(2,1)S(1)} collective-permute-done((bf16[3,96,1024]{2,1,0:T(8,128)(2,1)S(1)}, bf16[3,96,1024]{2,1,0:T(8,128)(2,1)S(1)}, u32[]{:S(2)}, u32[]{:S(2)}) %collective-permute-start.15) | collective-permute-done | bytes 589856 | tf_op jit(solution)/shard_map/ppermute | solution.py:33
  30.3 3.4 %collective-permute-start.16 = (bf16[3,192,1024]{2,1,0:T(8,128)(2,1)S(1)}, bf16[3,192,1024]{2,1,0:T(8,128)(2,1)S(1)}, u32[]{:S(2)}, u32[]{:S(2)}) collective-permute-start(bf16[3,192,1024]{2,1,0:T(8,128)(2,1)S(1)} %constant_dynamic-update-slice_fusion.5.refs_8_.refs_7_), channel_id=1, source_target_pairs={{0,48},{1,17},{2,50},{3,19},{4,52},{5,21},{6,54},{7,23},{8,56},{9,... | collective-permute-start | bytes 3538952 | tf_op jit(solution)/shard_map/ppermute | solution.py:33
  34.3 7.7 %collective-permute-done.8.refs_6_ = bf16[384,1024]{1,0:T(8,128)(2,1)S(1)} collective-permute-done((bf16[384,1024]{1,0:T(8,128)(2,1)S(1)}, bf16[384,1024]{1,0:T(8,128)(2,1)S(1)}, u32[]{:S(2)}, u32[]{:S(2)}) %collective-permute-start.8) | collective-permute-done | bytes 786464 | tf_op jit(solution)/shard_map/ppermute | solution.py:33
  42.5 1.9 %collective-permute-done.9.refs_7_ = bf16[384,1024]{1,0:T(8,128)(2,1)S(1)} collective-permute-done((bf16[384,1024]{1,0:T(8,128)(2,1)S(1)}, bf16[384,1024]{1,0:T(8,128)(2,1)S(1)}, u32[]{:S(2)}, u32[]{:S(2)}) %collective-permute-start.9) | collective-permute-done | bytes 786464 | tf_op jit(solution)/shard_map/ppermute | solution.py:63
  44.4 4.2 %shard_map.59 = (bf16[3,192,1024]{2,1,0:T(8,128)(2,1)S(1)}, bf16[384,1536]{1,0:T(8,128)(2,1)S(1)}) custom-call(bf16[384,1024]{1,0:T(8,128)(2,1)S(1)} %copy-done, bf16[384,1024]{1,0:T(8,128)(2,1)S(1)} %collective-permute-done.refs_1_, bf16[384,1024]{1,0:T(8,128)(2,1)S(1)} %collective-permute-done.5.refs_2_, ...), custom_call_target="tpu_custom_call" | custom-call | flops 1024 | bytes 1024 | tf_op jit(solution)/shard_map/pallas_call | solution.py:146
  48.7 4.2 %shard_map.60 = (bf16[3,192,1024]{2,1,0:T(8,128)(2,1)S(1)}, bf16[384,1536]{1,0:T(8,128)(2,1)S(1)}) custom-call(bf16[384,1024]{1,0:T(8,128)(2,1)S(1)} %copy-done, bf16[384,1024]{1,0:T(8,128)(2,1)S(1)} %collective-permute-done.refs_1_, bf16[384,1024]{1,0:T(8,128)(2,1)S(1)} %collective-permute-done.5.refs_2_, ...), custom_call_target="tpu_custom_call" | custom-call | flops 1024 | bytes 1024 | tf_op jit(solution)/shard_map/pallas_call | solution.py:146
  52.9 4.0 %collective-permute-start.18 = (bf16[3,192,1024]{2,1,0:T(8,128)(2,1)S(1)}, bf16[3,192,1024]{2,1,0:T(8,128)(2,1)S(1)}, u32[]{:S(2)}, u32[]{:S(2)}) collective-permute-start(bf16[3,192,1024]{2,1,0:T(8,128)(2,1)S(1)} %get-tuple-element.38), channel_id=1, source_target_pairs={{0,48},{1,17},{2,50},{3,19},{4,52},{5,21},{6,54},{7,23},{8,56},{9,... | collective-permute-start | bytes 3538952 | tf_op jit(solution)/shard_map/ppermute | solution.py:33
  56.8 4.2 %shard_map.61 = (bf16[3,192,1024]{2,1,0:T(8,128)(2,1)S(1)}, bf16[384,1536]{1,0:T(8,128)(2,1)S(1)}) custom-call(bf16[384,1024]{1,0:T(8,128)(2,1)S(1)} %copy-done, bf16[384,1024]{1,0:T(8,128)(2,1)S(1)} %collective-permute-done.refs_1_, bf16[384,1024]{1,0:T(8,128)(2,1)S(1)} %collective-permute-done.5.refs_2_, ...), custom_call_target="tpu_custom_call" | custom-call | flops 1024 | bytes 1024 | tf_op jit(solution)/shard_map/pallas_call | solution.py:146
  61.7 4.2 %shard_map.62 = (bf16[3,192,1024]{2,1,0:T(8,128)(2,1)S(1)}, bf16[384,1536]{1,0:T(8,128)(2,1)S(1)}) custom-call(bf16[384,1024]{1,0:T(8,128)(2,1)S(1)} %copy-done, bf16[384,1024]{1,0:T(8,128)(2,1)S(1)} %collective-permute-done.refs_1_, bf16[384,1024]{1,0:T(8,128)(2,1)S(1)} %collective-permute-done.5.refs_2_, ...), custom_call_target="tpu_custom_call" | custom-call | flops 1024 | bytes 1024 | tf_op jit(solution)/shard_map/pallas_call | solution.py:146
  65.9 5.1 %shard_map.63 = (f32[384,1024]{1,0:T(8,128)S(1)}, f32[384,1024]{1,0:T(8,128)S(1)}, bf16[2,384,1024]{2,1,0:T(8,128)(2,1)S(1)}) custom-call(bf16[384,1536]{1,0:T(8,128)(2,1)S(1)} %get-tuple-element.40.refs_0_, bf16[384,1536]{1,0:T(8,128)(2,1)S(1)} %get-tuple-element.41.refs_1_, bf16[384,1536]{1,0:T(8,128)(2,1)S(1)} %get-tuple-element.42.refs_2_, ...), custom_call_target="tpu_custom_call" | custom-call | flops 1024 | bytes 1024 | tf_op jit(solution)/shard_map/pallas_call | solution.py:185
  71.1 6.4 %collective-permute-done.17 = bf16[3,192,1024]{2,1,0:T(8,128)(2,1)S(1)} collective-permute-done((bf16[3,192,1024]{2,1,0:T(8,128)(2,1)S(1)}, bf16[3,192,1024]{2,1,0:T(8,128)(2,1)S(1)}, u32[]{:S(2)}, u32[]{:S(2)}) %collective-permute-start.17) | collective-permute-done | bytes 1179680 | tf_op jit(solution)/shard_map/ppermute | solution.py:33
  80.2 7.5 %collective-permute-done.25 = bf16[3,96,1024]{2,1,0:T(8,128)(2,1)S(1)} collective-permute-done((bf16[3,96,1024]{2,1,0:T(8,128)(2,1)S(1)}, bf16[3,96,1024]{2,1,0:T(8,128)(2,1)S(1)}, u32[]{:S(2)}, u32[]{:S(2)}) %collective-permute-start.25) | collective-permute-done | bytes 589856 | tf_op jit(solution)/shard_map/ppermute | solution.py:33
  88.1 4.6 %collective-permute-start.28 = (bf16[3,24,1024]{2,1,0:T(8,128)(2,1)S(1)}, bf16[3,24,1024]{2,1,0:T(8,128)(2,1)S(1)}, u32[]{:S(2)}, u32[]{:S(2)}) collective-permute-start(bf16[3,24,1024]{2,1,0:T(8,128)(2,1)S(1)} %get-tuple-element.55), channel_id=1, source_target_pairs={{0,18},{1,115},{2,16},{3,113},{4,22},{5,119},{6,20},{7,117},{8,26}... | collective-permute-start | bytes 442376 | tf_op jit(solution)/shard_map/ppermute | solution.py:59
  93.8 6.1 %collective-permute-start.22 = (bf16[3,24,1024]{2,1,0:T(8,128)(2,1)S(1)}, bf16[3,24,1024]{2,1,0:T(8,128)(2,1)S(1)}, u32[]{:S(2)}, u32[]{:S(2)}) collective-permute-start(bf16[3,24,1024]{2,1,0:T(8,128)(2,1)S(1)} %get-tuple-element.58), channel_id=1, source_target_pairs={{0,18},{1,115},{2,16},{3,113},{4,22},{5,119},{6,20},{7,117},{8,26}... | collective-permute-start | bytes 442376 | tf_op jit(solution)/shard_map/ppermute | solution.py:59
  99.9 5.5 %collective-permute-start.29 = (bf16[3,24,1024]{2,1,0:T(8,128)(2,1)S(1)}, bf16[3,24,1024]{2,1,0:T(8,128)(2,1)S(1)}, u32[]{:S(2)}, u32[]{:S(2)}) collective-permute-start(bf16[3,24,1024]{2,1,0:T(8,128)(2,1)S(1)} %add_convert_fusion.4), channel_id=1, source_target_pairs={{0,12},{1,13},{2,14},{3,15},{4,8},{5,9},{6,10},{7,11},{8,4},{9,5},... | collective-permute-start | bytes 442376 | tf_op jit(solution)/shard_map/ppermute | solution.py:33
  106.8 1.8 %collective-permute-done.29 = bf16[3,24,1024]{2,1,0:T(8,128)(2,1)S(1)} collective-permute-done((bf16[3,24,1024]{2,1,0:T(8,128)(2,1)S(1)}, bf16[3,24,1024]{2,1,0:T(8,128)(2,1)S(1)}, u32[]{:S(2)}, u32[]{:S(2)}) %collective-permute-start.29) | collective-permute-done | bytes 147488 | tf_op jit(solution)/shard_map/ppermute | solution.py:33
  (67 shorter events, 18.7 us)
Async XLA Ops:
  0.6 19.7 %collective-permute-start.5 = (bf16[384,1024]{1,0:T(8,128)(2,1)}, bf16[384,1024]{1,0:T(8,128)(2,1)S(1)}, u32[]{:S(2)}, u32[]{:S(2)}) collective-permute-start(bf16[384,1024]{1,0:T(8,128)(2,1)} %refs_0_.7), channel_id=1, source_target_pairs={{0,4},{1,5},{2,6},{3,7},{4,0},{5,1},{6,2},{7,3},{8,12},{9,13},{10,... | collective-permute-start | bytes 2359304 | tf_op jit(solution)/shard_map/ppermute | solution.py:33
  4.4 6.6 %collective-permute-start.1 = (bf16[3,24,1024]{2,1,0:T(8,128)(2,1)S(1)}, bf16[3,24,1024]{2,1,0:T(8,128)(2,1)S(1)}, u32[]{:S(2)}, u32[]{:S(2)}) collective-permute-start(bf16[3,24,1024]{2,1,0:T(8,128)(2,1)S(1)} %pad_maximum_fusion.2), channel_id=1, source_target_pairs={{0,12},{1,13},{2,14},{3,15},{4,8},{5,9},{6,10},{7,11},{8,4},{9,5},... | collective-permute-start | bytes 442376 | tf_op jit(solution)/shard_map/ppermute | solution.py:33
  7.0 6.0 %collective-permute-start.12 = (bf16[3,24,1024]{2,1,0:T(8,128)(2,1)S(1)}, bf16[3,24,1024]{2,1,0:T(8,128)(2,1)S(1)}, u32[]{:S(2)}, u32[]{:S(2)}) collective-permute-start(bf16[3,24,1024]{2,1,0:T(8,128)(2,1)S(1)} %pad_maximum_fusion.2), channel_id=1, source_target_pairs={{0,18},{1,115},{2,16},{3,113},{4,22},{5,119},{6,20},{7,117},{8,26}... | collective-permute-start | bytes 442376 | tf_op jit(solution)/shard_map/ppermute | solution.py:59
  8.5 6.2 %collective-permute-start.11 = (bf16[3,24,1024]{2,1,0:T(8,128)(2,1)S(1)}, bf16[3,24,1024]{2,1,0:T(8,128)(2,1)S(1)}, u32[]{:S(2)}, u32[]{:S(2)}) collective-permute-start(bf16[3,24,1024]{2,1,0:T(8,128)(2,1)S(1)} %pad_maximum_fusion.2), channel_id=1, source_target_pairs={{0,2},{1,67},{2,0},{3,65},{4,6},{5,71},{6,4},{7,69},{8,10},{9,75},... | collective-permute-start | bytes 442376 | tf_op jit(solution)/shard_map/ppermute | solution.py:33
  11.0 7.4 %collective-permute-start.4 = (bf16[3,24,1024]{2,1,0:T(8,128)(2,1)S(1)}, bf16[3,24,1024]{2,1,0:T(8,128)(2,1)S(1)}, u32[]{:S(2)}, u32[]{:S(2)}) collective-permute-start(bf16[3,24,1024]{2,1,0:T(8,128)(2,1)S(1)} %collective-permute-done.1), channel_id=1, source_target_pairs={{0,18},{1,115},{2,16},{3,113},{4,22},{5,119},{6,20},{7,117},{8,26}... | collective-permute-start | bytes 442376 | tf_op jit(solution)/shard_map/ppermute | solution.py:59
  15.3 11.2 %collective-permute-start.13 = (bf16[3,96,1024]{2,1,0:T(8,128)(2,1)S(1)}, bf16[3,96,1024]{2,1,0:T(8,128)(2,1)S(1)}, u32[]{:S(2)}, u32[]{:S(2)}) collective-permute-start(bf16[3,96,1024]{2,1,0:T(8,128)(2,1)S(1)} %pad_maximum_fusion.1), channel_id=1, source_target_pairs={{0,48},{1,17},{2,50},{3,19},{4,52},{5,21},{6,54},{7,23},{8,56},{9,... | collective-permute-start | bytes 1769480 | tf_op jit(solution)/shard_map/ppermute | solution.py:33
  18.3 15.4 %collective-permute-start = (bf16[384,1024]{1,0:T(8,128)(2,1)S(1)}, bf16[384,1024]{1,0:T(8,128)(2,1)S(1)}, u32[]{:S(2)}, u32[]{:S(2)}) collective-permute-start(bf16[384,1024]{1,0:T(8,128)(2,1)S(1)} %copy-done), channel_id=1, source_target_pairs={{0,1},{1,0},{2,3},{3,2},{4,5},{5,4},{6,7},{7,6},{8,9},{9,8},{10,11... | collective-permute-start | bytes 2359304 | tf_op jit(solution)/shard_map/ppermute | solution.py:63
  20.4 9.9 %collective-permute-start.15 = (bf16[3,96,1024]{2,1,0:T(8,128)(2,1)S(1)}, bf16[3,96,1024]{2,1,0:T(8,128)(2,1)S(1)}, u32[]{:S(2)}, u32[]{:S(2)}) collective-permute-start(bf16[3,96,1024]{2,1,0:T(8,128)(2,1)S(1)} %pad_maximum_fusion), channel_id=1, source_target_pairs={{0,66},{1,3},{2,64},{3,1},{4,70},{5,7},{6,68},{7,5},{8,74},{9,11},... | collective-permute-start | bytes 1769480 | tf_op jit(solution)/shard_map/ppermute | solution.py:33
  21.9 20.1 %collective-permute-start.8 = (bf16[384,1024]{1,0:T(8,128)(2,1)S(1)}, bf16[384,1024]{1,0:T(8,128)(2,1)S(1)}, u32[]{:S(2)}, u32[]{:S(2)}) collective-permute-start(bf16[384,1024]{1,0:T(8,128)(2,1)S(1)} %copy-done.1), channel_id=1, source_target_pairs={{0,4},{1,5},{2,6},{3,7},{4,0},{5,1},{6,2},{7,3},{8,12},{9,13},{10,... | collective-permute-start | bytes 2359304 | tf_op jit(solution)/shard_map/ppermute | solution.py:33
  26.5 22.2 %collective-permute-start.14 = (bf16[3,192,1024]{2,1,0:T(8,128)(2,1)S(1)}, bf16[3,192,1024]{2,1,0:T(8,128)(2,1)S(1)}, u32[]{:S(2)}, u32[]{:S(2)}) collective-permute-start(bf16[3,192,1024]{2,1,0:T(8,128)(2,1)S(1)} %constant_dynamic-update-slice_fusion.refs_8_.refs_6_), channel_id=1, source_target_pairs={{0,66},{1,3},{2,64},{3,1},{4,70},{5,7},{6,68},{7,5},{8,74},{9,11},... | collective-permute-start | bytes 3538952 | tf_op jit(solution)/shard_map/ppermute | solution.py:33
  30.3 18.3 %collective-permute-start.16 = (bf16[3,192,1024]{2,1,0:T(8,128)(2,1)S(1)}, bf16[3,192,1024]{2,1,0:T(8,128)(2,1)S(1)}, u32[]{:S(2)}, u32[]{:S(2)}) collective-permute-start(bf16[3,192,1024]{2,1,0:T(8,128)(2,1)S(1)} %constant_dynamic-update-slice_fusion.5.refs_8_.refs_7_), channel_id=1, source_target_pairs={{0,48},{1,17},{2,50},{3,19},{4,52},{5,21},{6,54},{7,23},{8,56},{9,... | collective-permute-start | bytes 3538952 | tf_op jit(solution)/shard_map/ppermute | solution.py:33
  33.8 8.8 %collective-permute-start.7 = (bf16[384,1024]{1,0:T(8,128)(2,1)S(1)}, bf16[384,1024]{1,0:T(8,128)(2,1)S(1)}, u32[]{:S(2)}, u32[]{:S(2)}) collective-permute-start(bf16[384,1024]{1,0:T(8,128)(2,1)S(1)} %copy-done.1), channel_id=1, source_target_pairs={{0,1},{1,0},{2,3},{3,2},{4,5},{5,4},{6,7},{7,6},{8,9},{9,8},{10,11... | collective-permute-start | bytes 2359304 | tf_op jit(solution)/shard_map/ppermute | solution.py:63
  33.8 8.8 %collective-permute-start.6 = (bf16[384,1024]{1,0:T(8,128)(2,1)S(1)}, bf16[384,1024]{1,0:T(8,128)(2,1)S(1)}, u32[]{:S(2)}, u32[]{:S(2)}) collective-permute-start(bf16[384,1024]{1,0:T(8,128)(2,1)S(1)} %collective-permute-done.5.refs_2_), channel_id=1, source_target_pairs={{0,1},{1,0},{2,3},{3,2},{4,5},{5,4},{6,7},{7,6},{8,9},{9,8},{10,11... | collective-permute-start | bytes 2359304 | tf_op jit(solution)/shard_map/ppermute | solution.py:63
  52.9 18.2 %collective-permute-start.18 = (bf16[3,192,1024]{2,1,0:T(8,128)(2,1)S(1)}, bf16[3,192,1024]{2,1,0:T(8,128)(2,1)S(1)}, u32[]{:S(2)}, u32[]{:S(2)}) collective-permute-start(bf16[3,192,1024]{2,1,0:T(8,128)(2,1)S(1)} %get-tuple-element.38), channel_id=1, source_target_pairs={{0,48},{1,17},{2,50},{3,19},{4,52},{5,21},{6,54},{7,23},{8,56},{9,... | collective-permute-start | bytes 3538952 | tf_op jit(solution)/shard_map/ppermute | solution.py:33
  61.0 16.5 %collective-permute-start.17 = (bf16[3,192,1024]{2,1,0:T(8,128)(2,1)S(1)}, bf16[3,192,1024]{2,1,0:T(8,128)(2,1)S(1)}, u32[]{:S(2)}, u32[]{:S(2)}) collective-permute-start(bf16[3,192,1024]{2,1,0:T(8,128)(2,1)S(1)} %get-tuple-element.37), channel_id=1, source_target_pairs={{0,66},{1,3},{2,64},{3,1},{4,70},{5,7},{6,68},{7,5},{8,74},{9,11},... | collective-permute-start | bytes 3538952 | tf_op jit(solution)/shard_map/ppermute | solution.py:33
  71.0 7.6 %collective-permute-start.23 = (bf16[2,384,1024]{2,1,0:T(8,128)(2,1)S(1)}, bf16[2,384,1024]{2,1,0:T(8,128)(2,1)S(1)}, u32[]{:S(2)}, u32[]{:S(2)}) collective-permute-start(bf16[2,384,1024]{2,1,0:T(8,128)(2,1)S(1)} %get-tuple-element.48), channel_id=1, source_target_pairs={{0,1},{1,0},{2,3},{3,2},{4,5},{5,4},{6,7},{7,6},{8,9},{9,8},{10,11... | collective-permute-start | bytes 4718600 | tf_op jit(solution)/shard_map/ppermute | solution.py:63
  77.7 10.0 %collective-permute-start.25 = (bf16[3,96,1024]{2,1,0:T(8,128)(2,1)S(1)}, bf16[3,96,1024]{2,1,0:T(8,128)(2,1)S(1)}, u32[]{:S(2)}, u32[]{:S(2)}) collective-permute-start(bf16[3,96,1024]{2,1,0:T(8,128)(2,1)S(1)} %add_convert_fusion.1), channel_id=1, source_target_pairs={{0,66},{1,3},{2,64},{3,1},{4,70},{5,7},{6,68},{7,5},{8,74},{9,11},... | collective-permute-start | bytes 1769480 | tf_op jit(solution)/shard_map/ppermute | solution.py:33
  78.5 14.4 %collective-permute-start.19 = (bf16[3,96,1024]{2,1,0:T(8,128)(2,1)S(1)}, bf16[3,96,1024]{2,1,0:T(8,128)(2,1)S(1)}, u32[]{:S(2)}, u32[]{:S(2)}) collective-permute-start(bf16[3,96,1024]{2,1,0:T(8,128)(2,1)S(1)} %add_convert_fusion.3), channel_id=1, source_target_pairs={{0,48},{1,17},{2,50},{3,19},{4,52},{5,21},{6,54},{7,23},{8,56},{9,... | collective-permute-start | bytes 1769480 | tf_op jit(solution)/shard_map/ppermute | solution.py:33
  78.8 26.8 %collective-permute-start.24 = (bf16[384,1024]{1,0:T(8,128)(2,1)S(1)}, bf16[384,1024]{1,0:T(8,128)(2,1)S(1)}, u32[]{:S(2)}, u32[]{:S(2)}) collective-permute-start(bf16[384,1024]{1,0:T(8,128)(2,1)S(1)} %fusion), channel_id=1, source_target_pairs={{0,4},{1,5},{2,6},{3,7},{4,0},{5,1},{6,2},{7,3},{8,12},{9,13},{10,... | collective-permute-start | bytes 2359304 | tf_op jit(solution)/shard_map/ppermute | solution.py:33
  88.1 11.7 %collective-permute-start.28 = (bf16[3,24,1024]{2,1,0:T(8,128)(2,1)S(1)}, bf16[3,24,1024]{2,1,0:T(8,128)(2,1)S(1)}, u32[]{:S(2)}, u32[]{:S(2)}) collective-permute-start(bf16[3,24,1024]{2,1,0:T(8,128)(2,1)S(1)} %get-tuple-element.55), channel_id=1, source_target_pairs={{0,18},{1,115},{2,16},{3,113},{4,22},{5,119},{6,20},{7,117},{8,26}... | collective-permute-start | bytes 442376 | tf_op jit(solution)/shard_map/ppermute | solution.py:59
  92.7 7.1 %collective-permute-start.27 = (bf16[3,24,1024]{2,1,0:T(8,128)(2,1)S(1)}, bf16[3,24,1024]{2,1,0:T(8,128)(2,1)S(1)}, u32[]{:S(2)}, u32[]{:S(2)}) collective-permute-start(bf16[3,24,1024]{2,1,0:T(8,128)(2,1)S(1)} %get-tuple-element.56), channel_id=1, source_target_pairs={{0,2},{1,67},{2,0},{3,65},{4,6},{5,71},{6,4},{7,69},{8,10},{9,75},... | collective-permute-start | bytes 442376 | tf_op jit(solution)/shard_map/ppermute | solution.py:33
  93.2 12.3 %collective-permute-start.20 = (bf16[3,24,1024]{2,1,0:T(8,128)(2,1)S(1)}, bf16[3,24,1024]{2,1,0:T(8,128)(2,1)S(1)}, u32[]{:S(2)}, u32[]{:S(2)}) collective-permute-start(bf16[3,24,1024]{2,1,0:T(8,128)(2,1)S(1)} %get-tuple-element.57), channel_id=1, source_target_pairs={{0,16},{1,49},{2,18},{3,51},{4,20},{5,53},{6,22},{7,55},{8,24},{9,... | collective-permute-start | bytes 442376 | tf_op jit(solution)/shard_map/ppermute | solution.py:33
  93.8 11.7 %collective-permute-start.22 = (bf16[3,24,1024]{2,1,0:T(8,128)(2,1)S(1)}, bf16[3,24,1024]{2,1,0:T(8,128)(2,1)S(1)}, u32[]{:S(2)}, u32[]{:S(2)}) collective-permute-start(bf16[3,24,1024]{2,1,0:T(8,128)(2,1)S(1)} %get-tuple-element.58), channel_id=1, source_target_pairs={{0,18},{1,115},{2,16},{3,113},{4,22},{5,119},{6,20},{7,117},{8,26}... | collective-permute-start | bytes 442376 | tf_op jit(solution)/shard_map/ppermute | solution.py:59
  99.9 8.6 %collective-permute-start.29 = (bf16[3,24,1024]{2,1,0:T(8,128)(2,1)S(1)}, bf16[3,24,1024]{2,1,0:T(8,128)(2,1)S(1)}, u32[]{:S(2)}, u32[]{:S(2)}) collective-permute-start(bf16[3,24,1024]{2,1,0:T(8,128)(2,1)S(1)} %add_convert_fusion.4), channel_id=1, source_target_pairs={{0,12},{1,13},{2,14},{3,15},{4,8},{5,9},{6,10},{7,11},{8,4},{9,5},... | collective-permute-start | bytes 442376 | tf_op jit(solution)/shard_map/ppermute | solution.py:33
  (8 other events, 54.2 us)

commit v6 on v5

--- a/solution.py
+++ b/solution.py
@@ -82,12 +82,6 @@
     return total + swap_first(along_x, X).astype(F32) + swap_corner(corner).astype(F32)
 
 
-def reduce(near, back, axis):
-    n = near.shape[1] // 2
-    got = swap_second(add(near[:, n:], back[:, n:]), axis)
-    return (near[:, :n].astype(F32) + back[:, :n].astype(F32) + got.astype(F32)).astype(BF16)
-
-
 def rows_of(refs, start, stop, cols=slice(None)):
     parts = []
     for ref in refs:
@@ -98,11 +92,10 @@
     return parts[0] if len(parts) == 1 else jnp.concatenate(parts, axis=0)
 
 
-def grads_kernel(n, *refs):
-    xs, cs, refs = refs[:n], refs[n : 2 * n], refs[2 * n :]
+def grads_kernel(n, m, parts, *refs):
+    xs, cs, refs = refs[:n], refs[n : n + m], refs[n + m :]
     a_ref, hid = refs[-2:]
-    parts = len(refs) // 2 - 1
-    ws, gs = refs[:parts], refs[parts:-2]
+    ws, befores, gs = refs[:parts], refs[parts : -2 - parts], refs[-2 - parts : -2]
     units, width = ws[0].shape[1:]
     gu = jnp.concatenate([w[m] for w in ws for m in range(2)], axis=0)
     down = jnp.concatenate([w[2] for w in ws], axis=0)
@@ -127,56 +120,51 @@
         cols = slice(k * TILE, (k + 1) * TILE)
         x = rows_of(xs, 0, tokens, cols)
         c = rows_of(cs, 0, tokens, cols)
-        d_gu = jnp.dot(a_ref[...], x, preferred_element_type=F32).astype(BF16)
-        d_down = jnp.dot(hid[...], c, preferred_element_type=F32).astype(BF16)
+        d_gu = jnp.dot(a_ref[...], x, preferred_element_type=F32)
+        d_down = jnp.dot(hid[...], c, preferred_element_type=F32)
         for p, g in enumerate(gs):
-            for m in range(2):
-                g[m, :, cols] = d_gu[(2 * p + m) * units : (2 * p + m + 1) * units]
-            g[2, :, cols] = d_down[p * units : (p + 1) * units]
-
-
-def grads(xs, cs, ws):
+            for m in range(3):
+                source, row = (d_down, p) if m == 2 else (d_gu, 2 * p + m)
+                sums = source[row * units : (row + 1) * units]
+                if befores:
+                    sums = sums + befores[p][m, :, cols].astype(F32)
+                g[m, :, cols] = sums.astype(BF16)
+
+
+def grads(xs, cs, ws, befores=()):
     units, width = ws[0].shape[1:]
     tokens = sum(x.shape[0] for x in xs)
     vmem = pl.BlockSpec(memory_space=pltpu.VMEM)
 
     def kernel(*refs):
-        grads_kernel(len(xs), *refs)
+        grads_kernel(len(xs), len(cs), len(ws), *refs)
 
     return pl.pallas_call(
         kernel,
         out_shape=[jax.ShapeDtypeStruct(w.shape, BF16) for w in ws]
         + [jax.ShapeDtypeStruct((2 * len(ws) * units, tokens), BF16)],
-        in_specs=[vmem] * (2 * len(xs) + len(ws)),
+        in_specs=[vmem] * (len(xs) + len(cs) + len(ws) + len(befores)),
         out_specs=[vmem] * (len(ws) + 1),
         scratch_shapes=[pltpu.VMEM((len(ws) * units, tokens), BF16)],
         compiler_params=pltpu.CompilerParams(vmem_limit_bytes=32 * 1024 * 1024),
         cost_estimate=pl.CostEstimate(
-            flops=width, bytes_accessed=width, transcendentals=0
+            flops=width if befores else 3 * 10**9, bytes_accessed=width, transcendentals=0
         ),
-    )(*xs, *cs, *ws)
+    )(*xs, *cs, *ws, *befores)
 
 
 def input_kernel(n, *refs):
-    parts, ws = refs[:n], refs[n:-3]
-    own_ref, z_ref, pair_ref = refs[-3:]
+    parts, ws = refs[:n], refs[n:-2]
+    mine_ref, pair_ref = refs[-2:]
     w_all = jnp.concatenate([w[m] for w in ws for m in range(2)], axis=0)
-    group = own_ref.shape[0]
-    for i in range(4):
-        cols = slice(i * group, (i + 1) * group)
-        a = jnp.concatenate([part[:, cols] for part in parts], axis=0)
-        total = lax.dot_general(a, w_all, TN, preferred_element_type=F32)
-        if i == 0:
-            own_ref[...] = total
-        elif i == 2:
-            z_ref[...] = total
-        else:
-            pair_ref[i // 2] = total.astype(BF16)
-
-
-def input_parts(parts, ws):
-    units, width = ws[0].shape[1:]
-    group = parts[0].shape[1] // 4
+    group = mine_ref.shape[0]
+    for i, ref in enumerate((mine_ref, pair_ref)):
+        a = jnp.concatenate([part[:, i * group : (i + 1) * group] for part in parts], axis=0)
+        ref[...] = lax.dot_general(a, w_all, TN, preferred_element_type=F32).astype(ref.dtype)
+
+
+def input_half(parts, ws, group):
+    width = ws[0].shape[2]
     vmem = pl.BlockSpec(memory_space=pltpu.VMEM)
 
     def kernel(*refs):
@@ -186,11 +174,10 @@
         kernel,
         out_shape=[
             jax.ShapeDtypeStruct((group, width), F32),
-            jax.ShapeDtypeStruct((group, width), F32),
-            jax.ShapeDtypeStruct((2, group, width), BF16),
+            jax.ShapeDtypeStruct((group, width), BF16),
         ],
         in_specs=[vmem] * (len(parts) + len(ws)),
-        out_specs=[vmem] * 3,
+        out_specs=[vmem] * 2,
         compiler_params=pltpu.CompilerParams(vmem_limit_bytes=32 * 1024 * 1024),
         cost_estimate=pl.CostEstimate(
             flops=width, bytes_accessed=width, transcendentals=0
@@ -203,34 +190,47 @@
     message = jnp.concatenate([gate_up.transpose(1, 0, 2), down_proj[None]], axis=0)
     message = lax.optimization_barrier(message)
     block1 = gather_block(swap_wrap(message, Z))
-    block0 = gather_block(message)
-    block1, x_z, c_own = lax.optimization_barrier((block1, x_z, cotangent))
+    o0 = gather_block(message)
+    block1, c_own = lax.optimization_barrier((block1, cotangent))
     c_z = swap_near(c_own, Z)
-    j0 = join(block0, swap_second(block0, Y))
-    j1 = join(block1, swap_second(block1, X))
-    r0, r1 = swap_second(j0, X), swap_second(j1, Y)
-    xs = [activations, swap_core(activations), x_z, swap_core(x_z)]
-    cs = [cotangent, swap_core(cotangent), c_z, swap_core(c_z)]
-
-    g_j0, a_j0 = grads(xs, cs, [j0])
-    r0, r1, a_j0 = lax.optimization_barrier((r0, r1, a_j0))
-    g_r1, a_r1 = grads(xs, cs, [r1])
-    back1 = swap_second(g_r1, Y)
-    r0, a_r1 = lax.optimization_barrier((r0, a_r1))
-    g_r0, a_r0 = grads(xs, cs, [r0])
-    back0 = swap_second(g_r0, X)
-    j1, a_r0 = lax.optimization_barrier((j1, a_r0))
-    g_j1, a_j1 = grads(xs, cs, [j1])
-
-    own, z_part, pair = input_parts([a_r0, a_r1, a_j0, a_j1], [r0, r1, j0, j1])
+    o1, x_z = lax.optimization_barrier((block1, x_z))
+    n0, w0 = swap_second(o0, Y), swap_second(o0, X)
+    n0, w0 = lax.optimization_barrier((n0, w0))
+    n1, w1 = swap_second(o1, X), swap_second(o1, Y)
+    n1, w1 = lax.optimization_barrier((n1, w1))
+    f0, f1 = swap_second(n0, X), swap_second(n1, Y)
+    xs, cs = [activations, swap_core(activations)], [cotangent, swap_core(cotangent)]
+    xs_z, cs_z = [x_z, swap_core(x_z)], [c_z, swap_core(c_z)]
+
+    near, far0, far1 = [n1, o1, n0, o0], [f0, w0], [f1, w1]
+    *g_near, a_near = grads(xs, cs, near)
+    *g_far0, a_far0 = grads(xs, cs, far0)
+    f1, a_near, a_far0 = lax.optimization_barrier((f1, a_near, a_far0))
+    *g_far1, a_far1 = grads(xs, cs, [f1, w1])
+    g_f1, g_w1, a_far1_z = grads(xs_z, cs_z, [f1, w1], g_far1)
+    back_f1, back_w1 = swap_second(g_f1, Y), swap_second(g_w1, Y)
+    f0, a_far1_z = lax.optimization_barrier((f0, a_far1_z))
+    g_f0, g_w0, a_far0_z = grads(xs_z, cs_z, [f0, w0], g_far0)
+    back_f0, back_w0 = swap_second(g_f0, X), swap_second(g_w0, X)
+    n1, a_far0_z = lax.optimization_barrier((n1, a_far0_z))
+    g_n1, g_o1, g_n0, g_o0, a_near_z = grads(xs_z, cs_z, [n1, o1, n0, o0], g_near)
+
+    group = activations.shape[0]
+    ws = far1 + far0 + near
+    z_part, z_pair = input_half([a_far1_z, a_far0_z, a_near_z], ws, group)
+    z_got = swap_core(z_pair)
+    mine, pair = input_half([a_far1, a_far0, a_near], ws, group)
     got = swap_core(pair)
-    back0, back1, z_part = lax.optimization_barrier((back0, back1, z_part))
-    mine = own + got[0].astype(F32)
-    z_part = swap_near((z_part + got[1].astype(F32)).astype(BF16), Z)
-    total1 = reduce_block(reduce(g_j1, back1, X)).astype(BF16)
-    total0 = reduce_block(reduce(g_j0, back0, Y))
-    grad_input = (mine + z_part.astype(F32)).astype(BF16)
-    total0, grad_input = lax.optimization_barrier((total0, grad_input))
+    near1 = swap_second(add(g_n1, back_f1), X)
+    near0 = swap_second(add(g_n0, back_f0), Y)
+    z_part = swap_near((z_part + z_got.astype(F32)).astype(BF16), Z)
+
+    def block_sum(own, back, near):
+        return (own.astype(F32) + back.astype(F32) + near.astype(F32)).astype(BF16)
+
+    total1 = reduce_block(block_sum(g_o1, back_w1, near1)).astype(BF16)
+    total0 = reduce_block(block_sum(g_o0, back_w0, near0))
+    grad_input = (mine + got.astype(F32) + z_part.astype(F32)).astype(BF16)
     total = total0 + swap_wrap(total1, Z).astype(F32)
     return (grad_input, total.transpose(1, 0, 2))
 

time: 111 us -> 108 us (0.973)
  waiting for transfers between devices: 33.2 us -> 27.8 us
  starting transfers between devices: 47.9 us -> 51.1 us
    ppermute x21 -> x25, starting transfers between devices: 32.9 us -> 39.3 us  [swap(): return lax.ppermute(value, AXES, pairs)]
    ppermute x4, starting transfers between devices: 13.8 us -> 8.21 us  [swap_corner(): return lax.ppermute(value, AXES, pairs)]
    ppermute x21 -> x25, waiting for transfers between devices: 30.8 us -> 27.3 us  [swap(): return lax.ppermute(value, AXES, pairs)]
    ppermute x5 -> x6, starting transfers between devices: 1.24 us -> 3.62 us  [swap_core(): return lax.ppermute(value, AXES, [(d, d ^ 1) for d in range(DEVICES)])]
    ppermute x5 -> x6, waiting for transfers between devices: 1.92 us -> 0.02 us  [swap_core(): return lax.ppermute(value, AXES, [(d, d ^ 1) for d in range(DEVICES)])]
    pallas_call x4 -> x6, Pallas kernels: 16.7 us -> 17 us  [grads(): pl.pallas_call(kernel, out_shape=[jax.ShapeDtypeStruct(w.shape, BF16) for...]
    pallas_call x1 -> x2, Pallas kernels: 5.06 us -> 5.24 us  [input_half(): pl.pallas_call(kernel, out_shape=[jax.ShapeDtypeStruct((group, width), F3...]
  transfers between devices with their start and end apart: 30 -> 35, of which waited for: 14 -> 16; matrix products, arithmetic and copies ran while one was open for 4% -> 4% of each run, Pallas kernels for 16% -> 19%
where the time goes in v6:
time: 108 us; the launch traced here: 107 us
  starting transfers between devices  51.1 us (47%)
  waiting for transfers between devices  27.8 us (26%)
  Pallas kernels  22.2 us (21%)
  other arithmetic  4.34 us (4%)
    ppermute x25, starting transfers between devices, swap(): return lax.ppermute(value, AXES, pairs)  39.3 us
    ppermute x25, waiting for transfers between devices, swap(): return lax.ppermute(value, AXES, pairs)  27.3 us
    pallas_call x6, Pallas kernels, grads(): pl.pallas_call(kernel, out_shape=[jax.ShapeDtypeStruct(w.shape, BF16) for...  17 us
    ppermute x4, starting transfers between devices, swap_corner(): return lax.ppermute(value, AXES, pairs)  8.21 us
    pallas_call x2, Pallas kernels, input_half(): pl.pallas_call(kernel, out_shape=[jax.ShapeDtypeStruct((group, width), F3...  5.24 us
    ppermute x6, starting transfers between devices, swap_core(): return lax.ppermute(value, AXES, [(d, d ^ 1) for d in range(DEVICES)])  3.62 us
  transfers between devices with their start and end apart: 35, of which 16 were waited for; matrix products, arithmetic and copies ran while one was open for 4% of the time, Pallas kernels for 19%

profile of v6, /device:TPU:2, one launch (start us, length us, event | category | flops | bytes accessed | tf_op | source)
XLA Modules:
  0.0 107.3 jit_solution(13326433399976996164)
XLA Ops:
  4.4 2.6 %collective-permute-start.2 = (bf16[3,24,1024]{2,1,0:T(8,128)(2,1)S(1)}, bf16[3,24,1024]{2,1,0:T(8,128)(2,1)S(1)}, u32[]{:S(2)}, u32[]{:S(2)}) collective-permute-start(bf16[3,24,1024]{2,1,0:T(8,128)(2,1)S(1)} %pad_maximum_fusion.2), channel_id=1, source_target_pairs={{0,12},{1,13},{2,14},{3,15},{4,8},{5,9},{6,10},{7,11},{8,4},{9,5},... | collective-permute-start | bytes 442376 | tf_op jit(solution)/shard_map/ppermute | solution.py:33
  15.3 2.2 %collective-permute-start.14 = (bf16[3,96,1024]{2,1,0:T(8,128)(2,1)S(1)}, bf16[3,96,1024]{2,1,0:T(8,128)(2,1)S(1)}, u32[]{:S(2)}, u32[]{:S(2)}) collective-permute-start(bf16[3,96,1024]{2,1,0:T(8,128)(2,1)S(1)} %pad_maximum_fusion.1.refs_7_.refs_10_), channel_id=1, source_target_pairs={{0,66},{1,3},{2,64},{3,1},{4,70},{5,7},{6,68},{7,5},{8,74},{9,11},... | collective-permute-start | bytes 1769480 | tf_op jit(solution)/shard_map/ppermute | solution.py:33
  17.5 2.7 %collective-permute-start.13 = (bf16[3,96,1024]{2,1,0:T(8,128)(2,1)S(1)}, bf16[3,96,1024]{2,1,0:T(8,128)(2,1)S(1)}, u32[]{:S(2)}, u32[]{:S(2)}) collective-permute-start(bf16[3,96,1024]{2,1,0:T(8,128)(2,1)S(1)} %pad_maximum_fusion.1.refs_7_.refs_10_), channel_id=1, source_target_pairs={{0,48},{1,17},{2,50},{3,19},{4,52},{5,21},{6,54},{7,23},{8,56},{9,... | collective-permute-start | bytes 1769480 | tf_op jit(solution)/shard_map/ppermute | solution.py:33
  20.4 3.0 %collective-permute-start.8 = (bf16[3,96,1024]{2,1,0:T(8,128)(2,1)S(1)}, bf16[3,96,1024]{2,1,0:T(8,128)(2,1)S(1)}, u32[]{:S(2)}, u32[]{:S(2)}) collective-permute-start(bf16[3,96,1024]{2,1,0:T(8,128)(2,1)S(1)} %pad_maximum_fusion.refs_5_.refs_8_), channel_id=1, source_target_pairs={{0,48},{1,17},{2,50},{3,19},{4,52},{5,21},{6,54},{7,23},{8,56},{9,... | collective-permute-start | bytes 1769480 | tf_op jit(solution)/shard_map/ppermute | solution.py:33
  29.8 5.1 %collective-permute-done.8.refs_5_.refs_4_ = bf16[3,96,1024]{2,1,0:T(8,128)(2,1)S(1)} collective-permute-done((bf16[3,96,1024]{2,1,0:T(8,128)(2,1)S(1)}, bf16[3,96,1024]{2,1,0:T(8,128)(2,1)S(1)}, u32[]{:S(2)}, u32[]{:S(2)}) %collective-permute-start.8) | collective-permute-done | bytes 589856 | tf_op jit(solution)/shard_map/ppermute | solution.py:33
  36.1 2.3 %collective-permute-done.7.refs_4_.refs_7_ = bf16[3,96,1024]{2,1,0:T(8,128)(2,1)S(1)} collective-permute-done((bf16[3,96,1024]{2,1,0:T(8,128)(2,1)S(1)}, bf16[3,96,1024]{2,1,0:T(8,128)(2,1)S(1)}, u32[]{:S(2)}, u32[]{:S(2)}) %collective-permute-start.7) | collective-permute-done | bytes 589856 | tf_op jit(solution)/shard_map/ppermute | solution.py:33
  38.5 2.7 %collective-permute-start.9 = (bf16[3,96,1024]{2,1,0:T(8,128)(2,1)S(1)}, bf16[3,96,1024]{2,1,0:T(8,128)(2,1)S(1)}, u32[]{:S(2)}, u32[]{:S(2)}) collective-permute-start(bf16[3,96,1024]{2,1,0:T(8,128)(2,1)S(1)} %collective-permute-done.7.refs_4_.refs_7_), channel_id=1, source_target_pairs={{0,48},{1,17},{2,50},{3,19},{4,52},{5,21},{6,54},{7,23},{8,56},{9,... | collective-permute-start | bytes 1769480 | tf_op jit(solution)/shard_map/ppermute | solution.py:33
  41.2 2.2 %collective-permute-done.18.refs_2_ = bf16[384,1024]{1,0:T(8,128)(2,1)S(1)} collective-permute-done((bf16[384,1024]{1,0:T(8,128)(2,1)S(1)}, bf16[384,1024]{1,0:T(8,128)(2,1)S(1)}, u32[]{:S(2)}, u32[]{:S(2)}) %collective-permute-start.18) | collective-permute-done | bytes 786464 | tf_op jit(solution)/shard_map/ppermute | solution.py:33
  44.8 2.2 %shard_map.60 = (bf16[3,96,1024]{2,1,0:T(8,128)(2,1)S(1)}, bf16[3,96,1024]{2,1,0:T(8,128)(2,1)S(1)}, bf16[384,768]{1,0:T(8,128)(2,1)S(1)}) custom-call(bf16[384,1024]{1,0:T(8,128)(2,1)S(1)} %copy-done, bf16[384,1024]{1,0:T(8,128)(2,1)S(1)} %collective-permute-done.refs_1_, bf16[384,1024]{1,0:T(8,128)(2,1)S(1)} %copy-done.1, ...), custom_call_target="tpu_custom_call" | custom-call | flops 3000000000 | bytes 1024 | tf_op jit(solution)/shard_map/pallas_call | solution.py:142
  47.0 4.1 %shard_map.59 = (bf16[3,96,1024]{2,1,0:T(8,128)(2,1)S(1)}, bf16[3,96,1024]{2,1,0:T(8,128)(2,1)S(1)}, bf16[3,96,1024]{2,1,0:T(8,128)(2,1)S(1)}, bf16[3,96,1024]{2,1,0:T(8,128)(2,1)S(1)}, bf16[768,768]{1,0:T(8,128)(2,1)S(1)}) custom-call(bf16[384,1024]{1,0:T(8,128)(2,1)S(1)} %copy-done, bf16[384,1024]{1,0:T(8,128)(2,1)S(1)} %collective-permute-done.refs_1_, ...), custom_call_target="tpu_custom_call" | custom-call | flops 3000000000 | bytes 1024 | tf_op jit(solution)/shard_map/pallas_call | solution.py:142
  51.1 2.2 %shard_map.61 = (bf16[3,96,1024]{2,1,0:T(8,128)(2,1)S(1)}, bf16[3,96,1024]{2,1,0:T(8,128)(2,1)S(1)}, bf16[384,768]{1,0:T(8,128)(2,1)S(1)}) custom-call(bf16[384,1024]{1,0:T(8,128)(2,1)S(1)} %copy-done, bf16[384,1024]{1,0:T(8,128)(2,1)S(1)} %collective-permute-done.refs_1_, bf16[384,1024]{1,0:T(8,128)(2,1)S(1)} %copy-done.1, ...), custom_call_target="tpu_custom_call" | custom-call | flops 3000000000 | bytes 1024 | tf_op jit(solution)/shard_map/pallas_call | solution.py:142
  53.3 2.2 %shard_map.63 = (bf16[3,96,1024]{2,1,0:T(8,128)(2,1)S(1)}, bf16[3,96,1024]{2,1,0:T(8,128)(2,1)S(1)}, bf16[384,768]{1,0:T(8,128)(2,1)S(1)}) custom-call(bf16[384,1024]{1,0:T(8,128)(2,1)S(1)} %collective-permute-done.6.refs_0_, bf16[384,1024]{1,0:T(8,128)(2,1)S(1)} %collective-permute-done.17.refs_1_, bf16[384,1024]{1,0:T(8,128)(2,1)S(1)} %collective-permute-done.18.refs_2_, ...), custom_call_target="tpu_custom_call" | custom-call | flops 1024 | bytes 1024 | tf_op jit(solution)/shard_map/pallas_call | solution.py:142
  55.5 2.8 %collective-permute-start.29 = (bf16[3,96,1024]{2,1,0:T(8,128)(2,1)S(1)}, bf16[3,96,1024]{2,1,0:T(8,128)(2,1)S(1)}, u32[]{:S(2)}, u32[]{:S(2)}) collective-permute-start(bf16[3,96,1024]{2,1,0:T(8,128)(2,1)S(1)} %get-tuple-element.83), channel_id=1, source_target_pairs={{0,48},{1,17},{2,50},{3,19},{4,52},{5,21},{6,54},{7,23},{8,56},{9,... | collective-permute-start | bytes 1769480 | tf_op jit(solution)/shard_map/ppermute | solution.py:33
  58.3 2.2 %shard_map.64 = (bf16[3,96,1024]{2,1,0:T(8,128)(2,1)S(1)}, bf16[3,96,1024]{2,1,0:T(8,128)(2,1)S(1)}, bf16[384,768]{1,0:T(8,128)(2,1)S(1)}) custom-call(bf16[384,1024]{1,0:T(8,128)(2,1)S(1)} %collective-permute-done.6.refs_0_, bf16[384,1024]{1,0:T(8,128)(2,1)S(1)} %collective-permute-done.17.refs_1_, bf16[384,1024]{1,0:T(8,128)(2,1)S(1)} %collective-permute-done.18.refs_2_, ...), custom_call_target="tpu_custom_call" | custom-call | flops 1024 | bytes 1024 | tf_op jit(solution)/shard_map/pallas_call | solution.py:142
  62.6 4.1 %shard_map.65 = (bf16[3,96,1024]{2,1,0:T(8,128)(2,1)S(1)}, bf16[3,96,1024]{2,1,0:T(8,128)(2,1)S(1)}, bf16[3,96,1024]{2,1,0:T(8,128)(2,1)S(1)}, bf16[3,96,1024]{2,1,0:T(8,128)(2,1)S(1)}, bf16[768,768]{1,0:T(8,128)(2,1)S(1)}) custom-call(bf16[384,1024]{1,0:T(8,128)(2,1)S(1)} %collective-permute-done.6.refs_0_, ...), custom_call_target="tpu_custom_call" | custom-call | flops 1024 | bytes 1024 | tf_op jit(solution)/shard_map/pallas_call | solution.py:142
  66.7 2.6 %shard_map.66 = (f32[384,1024]{1,0:T(8,128)S(1)}, bf16[384,1024]{1,0:T(8,128)(2,1)S(1)}) custom-call(bf16[384,768]{1,0:T(8,128)(2,1)S(1)} %get-tuple-element.62.refs_0_, bf16[384,768]{1,0:T(8,128)(2,1)S(1)} %get-tuple-element.67.refs_1_, bf16[768,768]{1,0:T(8,128)(2,1)S(1)} %get-tuple-element.73.refs_2_, ...), custom_call_target="tpu_custom_call" | custom-call | flops 1024 | bytes 1024 | tf_op jit(solution)/shard_map/pallas_call | solution.py:173
  70.6 2.6 %shard_map.62 = (f32[384,1024]{1,0:T(8,128)S(1)}, bf16[384,1024]{1,0:T(8,128)(2,1)S(1)}) custom-call(bf16[384,768]{1,0:T(8,128)(2,1)S(1)} %get-tuple-element.52.refs_0_, bf16[384,768]{1,0:T(8,128)(2,1)S(1)} %get-tuple-element.53.refs_1_, bf16[768,768]{1,0:T(8,128)(2,1)S(1)} %get-tuple-element.54.refs_2_, ...), custom_call_target="tpu_custom_call" | custom-call | flops 1024 | bytes 1024 | tf_op jit(solution)/shard_map/pallas_call | solution.py:173
  78.4 2.1 %collective-permute-done.28 = bf16[3,96,1024]{2,1,0:T(8,128)(2,1)S(1)} collective-permute-done((bf16[3,96,1024]{2,1,0:T(8,128)(2,1)S(1)}, bf16[3,96,1024]{2,1,0:T(8,128)(2,1)S(1)}, u32[]{:S(2)}, u32[]{:S(2)}) %collective-permute-start.28) | collective-permute-done | bytes 589856 | tf_op jit(solution)/shard_map/ppermute | solution.py:33
  81.2 4.8 %collective-permute-done.22 = bf16[3,96,1024]{2,1,0:T(8,128)(2,1)S(1)} collective-permute-done((bf16[3,96,1024]{2,1,0:T(8,128)(2,1)S(1)}, bf16[3,96,1024]{2,1,0:T(8,128)(2,1)S(1)}, u32[]{:S(2)}, u32[]{:S(2)}) %collective-permute-start.22) | collective-permute-done | bytes 589856 | tf_op jit(solution)/shard_map/ppermute | solution.py:33
  86.0 2.6 %collective-permute-start.33 = (bf16[3,24,1024]{2,1,0:T(8,128)(2,1)S(1)}, bf16[3,24,1024]{2,1,0:T(8,128)(2,1)S(1)}, u32[]{:S(2)}, u32[]{:S(2)}) collective-permute-start(bf16[3,24,1024]{2,1,0:T(8,128)(2,1)S(1)} %get-tuple-element.88), channel_id=1, source_target_pairs={{0,18},{1,115},{2,16},{3,113},{4,22},{5,119},{6,20},{7,117},{8,26}... | collective-permute-start | bytes 442376 | tf_op jit(solution)/shard_map/ppermute | solution.py:59
  89.1 2.6 %collective-permute-start.32 = (bf16[3,24,1024]{2,1,0:T(8,128)(2,1)S(1)}, bf16[3,24,1024]{2,1,0:T(8,128)(2,1)S(1)}, u32[]{:S(2)}, u32[]{:S(2)}) collective-permute-start(bf16[3,24,1024]{2,1,0:T(8,128)(2,1)S(1)} %get-tuple-element.89), channel_id=1, source_target_pairs={{0,2},{1,67},{2,0},{3,65},{4,6},{5,71},{6,4},{7,69},{8,10},{9,75},... | collective-permute-start | bytes 442376 | tf_op jit(solution)/shard_map/ppermute | solution.py:33
  92.2 2.5 %collective-permute-start.27 = (bf16[3,24,1024]{2,1,0:T(8,128)(2,1)S(1)}, bf16[3,24,1024]{2,1,0:T(8,128)(2,1)S(1)}, u32[]{:S(2)}, u32[]{:S(2)}) collective-permute-start(bf16[3,24,1024]{2,1,0:T(8,128)(2,1)S(1)} %get-tuple-element.85), channel_id=1, source_target_pairs={{0,18},{1,115},{2,16},{3,113},{4,22},{5,119},{6,20},{7,117},{8,26}... | collective-permute-start | bytes 442376 | tf_op jit(solution)/shard_map/ppermute | solution.py:59
  98.9 2.9 %collective-permute-start.34 = (bf16[3,24,1024]{2,1,0:T(8,128)(2,1)S(1)}, bf16[3,24,1024]{2,1,0:T(8,128)(2,1)S(1)}, u32[]{:S(2)}, u32[]{:S(2)}) collective-permute-start(bf16[3,24,1024]{2,1,0:T(8,128)(2,1)S(1)} %add_convert_fusion.6), channel_id=1, source_target_pairs={{0,12},{1,13},{2,14},{3,15},{4,8},{5,9},{6,10},{7,11},{8,4},{9,5},... | collective-permute-start | bytes 442376 | tf_op jit(solution)/shard_map/ppermute | solution.py:33
  101.8 3.4 %collective-permute-done.34 = bf16[3,24,1024]{2,1,0:T(8,128)(2,1)S(1)} collective-permute-done((bf16[3,24,1024]{2,1,0:T(8,128)(2,1)S(1)}, bf16[3,24,1024]{2,1,0:T(8,128)(2,1)S(1)}, u32[]{:S(2)}, u32[]{:S(2)}) %collective-permute-start.34) | collective-permute-done | bytes 147488 | tf_op jit(solution)/shard_map/ppermute | solution.py:33
  (72 shorter events, 37.6 us)
Async XLA Ops:
  0.6 19.8 %collective-permute-start.6 = (bf16[384,1024]{1,0:T(8,128)(2,1)}, bf16[384,1024]{1,0:T(8,128)(2,1)S(1)}, u32[]{:S(2)}, u32[]{:S(2)}) collective-permute-start(bf16[384,1024]{1,0:T(8,128)(2,1)} %refs_0_.5), channel_id=1, source_target_pairs={{0,4},{1,5},{2,6},{3,7},{4,0},{5,1},{6,2},{7,3},{8,12},{9,13},{10,... | collective-permute-start | bytes 2359304 | tf_op jit(solution)/shard_map/ppermute | solution.py:33
  13.0 7.2 %collective-permute-start.4 = (bf16[3,24,1024]{2,1,0:T(8,128)(2,1)S(1)}, bf16[3,24,1024]{2,1,0:T(8,128)(2,1)S(1)}, u32[]{:S(2)}, u32[]{:S(2)}) collective-permute-start(bf16[3,24,1024]{2,1,0:T(8,128)(2,1)S(1)} %collective-permute-done.2), channel_id=1, source_target_pairs={{0,2},{1,67},{2,0},{3,65},{4,6},{5,71},{6,4},{7,69},{8,10},{9,75},... | collective-permute-start | bytes 442376 | tf_op jit(solution)/shard_map/ppermute | solution.py:33
  15.3 10.1 %collective-permute-start.14 = (bf16[3,96,1024]{2,1,0:T(8,128)(2,1)S(1)}, bf16[3,96,1024]{2,1,0:T(8,128)(2,1)S(1)}, u32[]{:S(2)}, u32[]{:S(2)}) collective-permute-start(bf16[3,96,1024]{2,1,0:T(8,128)(2,1)S(1)} %pad_maximum_fusion.1.refs_7_.refs_10_), channel_id=1, source_target_pairs={{0,66},{1,3},{2,64},{3,1},{4,70},{5,7},{6,68},{7,5},{8,74},{9,11},... | collective-permute-start | bytes 1769480 | tf_op jit(solution)/shard_map/ppermute | solution.py:33
  17.5 11.1 %collective-permute-start.13 = (bf16[3,96,1024]{2,1,0:T(8,128)(2,1)S(1)}, bf16[3,96,1024]{2,1,0:T(8,128)(2,1)S(1)}, u32[]{:S(2)}, u32[]{:S(2)}) collective-permute-start(bf16[3,96,1024]{2,1,0:T(8,128)(2,1)S(1)} %pad_maximum_fusion.1.refs_7_.refs_10_), channel_id=1, source_target_pairs={{0,48},{1,17},{2,50},{3,19},{4,52},{5,21},{6,54},{7,23},{8,56},{9,... | collective-permute-start | bytes 1769480 | tf_op jit(solution)/shard_map/ppermute | solution.py:33
  20.4 14.5 %collective-permute-start.8 = (bf16[3,96,1024]{2,1,0:T(8,128)(2,1)S(1)}, bf16[3,96,1024]{2,1,0:T(8,128)(2,1)S(1)}, u32[]{:S(2)}, u32[]{:S(2)}) collective-permute-start(bf16[3,96,1024]{2,1,0:T(8,128)(2,1)S(1)} %pad_maximum_fusion.refs_5_.refs_8_), channel_id=1, source_target_pairs={{0,48},{1,17},{2,50},{3,19},{4,52},{5,21},{6,54},{7,23},{8,56},{9,... | collective-permute-start | bytes 1769480 | tf_op jit(solution)/shard_map/ppermute | solution.py:33
  23.4 17.8 %collective-permute-start = (bf16[384,1024]{1,0:T(8,128)(2,1)S(1)}, bf16[384,1024]{1,0:T(8,128)(2,1)S(1)}, u32[]{:S(2)}, u32[]{:S(2)}) collective-permute-start(bf16[384,1024]{1,0:T(8,128)(2,1)S(1)} %copy-done), channel_id=1, source_target_pairs={{0,1},{1,0},{2,3},{3,2},{4,5},{5,4},{6,7},{7,6},{8,9},{9,8},{10,11... | collective-permute-start | bytes 2359304 | tf_op jit(solution)/shard_map/ppermute | solution.py:63
  23.4 20.0 %collective-permute-start.18 = (bf16[384,1024]{1,0:T(8,128)(2,1)S(1)}, bf16[384,1024]{1,0:T(8,128)(2,1)S(1)}, u32[]{:S(2)}, u32[]{:S(2)}) collective-permute-start(bf16[384,1024]{1,0:T(8,128)(2,1)S(1)} %copy-done.1), channel_id=1, source_target_pairs={{0,4},{1,5},{2,6},{3,7},{4,0},{5,1},{6,2},{7,3},{8,12},{9,13},{10,... | collective-permute-start | bytes 2359304 | tf_op jit(solution)/shard_map/ppermute | solution.py:33
  25.4 18.0 %collective-permute-start.1 = (bf16[384,1024]{1,0:T(8,128)(2,1)S(1)}, bf16[384,1024]{1,0:T(8,128)(2,1)S(1)}, u32[]{:S(2)}, u32[]{:S(2)}) collective-permute-start(bf16[384,1024]{1,0:T(8,128)(2,1)S(1)} %copy-done.1), channel_id=1, source_target_pairs={{0,1},{1,0},{2,3},{3,2},{4,5},{5,4},{6,7},{7,6},{8,9},{9,8},{10,11... | collective-permute-start | bytes 2359304 | tf_op jit(solution)/shard_map/ppermute | solution.py:63
  28.6 9.9 %collective-permute-start.7 = (bf16[3,96,1024]{2,1,0:T(8,128)(2,1)S(1)}, bf16[3,96,1024]{2,1,0:T(8,128)(2,1)S(1)}, u32[]{:S(2)}, u32[]{:S(2)}) collective-permute-start(bf16[3,96,1024]{2,1,0:T(8,128)(2,1)S(1)} %pad_maximum_fusion.refs_5_.refs_8_), channel_id=1, source_target_pairs={{0,66},{1,3},{2,64},{3,1},{4,70},{5,7},{6,68},{7,5},{8,74},{9,11},... | collective-permute-start | bytes 1769480 | tf_op jit(solution)/shard_map/ppermute | solution.py:33
  34.9 9.9 %collective-permute-start.15 = (bf16[3,96,1024]{2,1,0:T(8,128)(2,1)S(1)}, bf16[3,96,1024]{2,1,0:T(8,128)(2,1)S(1)}, u32[]{:S(2)}, u32[]{:S(2)}) collective-permute-start(bf16[3,96,1024]{2,1,0:T(8,128)(2,1)S(1)} %collective-permute-done.13.refs_6_.refs_9_), channel_id=1, source_target_pairs={{0,66},{1,3},{2,64},{3,1},{4,70},{5,7},{6,68},{7,5},{8,74},{9,11},... | collective-permute-start | bytes 1769480 | tf_op jit(solution)/shard_map/ppermute | solution.py:33
  38.5 12.6 %collective-permute-start.9 = (bf16[3,96,1024]{2,1,0:T(8,128)(2,1)S(1)}, bf16[3,96,1024]{2,1,0:T(8,128)(2,1)S(1)}, u32[]{:S(2)}, u32[]{:S(2)}) collective-permute-start(bf16[3,96,1024]{2,1,0:T(8,128)(2,1)S(1)} %collective-permute-done.7.refs_4_.refs_7_), channel_id=1, source_target_pairs={{0,48},{1,17},{2,50},{3,19},{4,52},{5,21},{6,54},{7,23},{8,56},{9,... | collective-permute-start | bytes 1769480 | tf_op jit(solution)/shard_map/ppermute | solution.py:33
  41.2 12.1 %collective-permute-start.17 = (bf16[384,1024]{1,0:T(8,128)(2,1)S(1)}, bf16[384,1024]{1,0:T(8,128)(2,1)S(1)}, u32[]{:S(2)}, u32[]{:S(2)}) collective-permute-start(bf16[384,1024]{1,0:T(8,128)(2,1)S(1)} %collective-permute-done.6.refs_0_), channel_id=1, source_target_pairs={{0,1},{1,0},{2,3},{3,2},{4,5},{5,4},{6,7},{7,6},{8,9},{9,8},{10,11... | collective-permute-start | bytes 2359304 | tf_op jit(solution)/shard_map/ppermute | solution.py:63
  43.4 9.9 %collective-permute-start.19 = (bf16[384,1024]{1,0:T(8,128)(2,1)S(1)}, bf16[384,1024]{1,0:T(8,128)(2,1)S(1)}, u32[]{:S(2)}, u32[]{:S(2)}) collective-permute-start(bf16[384,1024]{1,0:T(8,128)(2,1)S(1)} %collective-permute-done.18.refs_2_), channel_id=1, source_target_pairs={{0,1},{1,0},{2,3},{3,2},{4,5},{5,4},{6,7},{7,6},{8,9},{9,8},{10,11... | collective-permute-start | bytes 2359304 | tf_op jit(solution)/shard_map/ppermute | solution.py:63
  55.5 14.0 %collective-permute-start.29 = (bf16[3,96,1024]{2,1,0:T(8,128)(2,1)S(1)}, bf16[3,96,1024]{2,1,0:T(8,128)(2,1)S(1)}, u32[]{:S(2)}, u32[]{:S(2)}) collective-permute-start(bf16[3,96,1024]{2,1,0:T(8,128)(2,1)S(1)} %get-tuple-element.83), channel_id=1, source_target_pairs={{0,48},{1,17},{2,50},{3,19},{4,52},{5,21},{6,54},{7,23},{8,56},{9,... | collective-permute-start | bytes 1769480 | tf_op jit(solution)/shard_map/ppermute | solution.py:33
  60.5 14.7 %collective-permute-start.23 = (bf16[3,96,1024]{2,1,0:T(8,128)(2,1)S(1)}, bf16[3,96,1024]{2,1,0:T(8,128)(2,1)S(1)}, u32[]{:S(2)}, u32[]{:S(2)}) collective-permute-start(bf16[3,96,1024]{2,1,0:T(8,128)(2,1)S(1)} %get-tuple-element.79), channel_id=1, source_target_pairs={{0,66},{1,3},{2,64},{3,1},{4,70},{5,7},{6,68},{7,5},{8,74},{9,11},... | collective-permute-start | bytes 1769480 | tf_op jit(solution)/shard_map/ppermute | solution.py:33
  69.3 7.1 %collective-permute-start.20 = (bf16[384,1024]{1,0:T(8,128)(2,1)S(1)}, bf16[384,1024]{1,0:T(8,128)(2,1)S(1)}, u32[]{:S(2)}, u32[]{:S(2)}) collective-permute-start(bf16[384,1024]{1,0:T(8,128)(2,1)S(1)} %get-tuple-element.75), channel_id=1, source_target_pairs={{0,1},{1,0},{2,3},{3,2},{4,5},{5,4},{6,7},{7,6},{8,9},{9,8},{10,11... | collective-permute-start | bytes 2359304 | tf_op jit(solution)/shard_map/ppermute | solution.py:63
  69.4 11.2 %collective-permute-start.28 = (bf16[3,96,1024]{2,1,0:T(8,128)(2,1)S(1)}, bf16[3,96,1024]{2,1,0:T(8,128)(2,1)S(1)}, u32[]{:S(2)}, u32[]{:S(2)}) collective-permute-start(bf16[3,96,1024]{2,1,0:T(8,128)(2,1)S(1)} %get-tuple-element.81), channel_id=1, source_target_pairs={{0,48},{1,17},{2,50},{3,19},{4,52},{5,21},{6,54},{7,23},{8,56},{9,... | collective-permute-start | bytes 1769480 | tf_op jit(solution)/shard_map/ppermute | solution.py:33
  69.7 11.0 %collective-permute-start.30 = (bf16[3,96,1024]{2,1,0:T(8,128)(2,1)S(1)}, bf16[3,96,1024]{2,1,0:T(8,128)(2,1)S(1)}, u32[]{:S(2)}, u32[]{:S(2)}) collective-permute-start(bf16[3,96,1024]{2,1,0:T(8,128)(2,1)S(1)} %add_convert_fusion.3), channel_id=1, source_target_pairs={{0,66},{1,3},{2,64},{3,1},{4,70},{5,7},{6,68},{7,5},{8,74},{9,11},... | collective-permute-start | bytes 1769480 | tf_op jit(solution)/shard_map/ppermute | solution.py:33
  73.2 32.8 %collective-permute-start.16 = (bf16[384,1024]{1,0:T(8,128)(2,1)S(1)}, bf16[384,1024]{1,0:T(8,128)(2,1)S(1)}, u32[]{:S(2)}, u32[]{:S(2)}) collective-permute-start(bf16[384,1024]{1,0:T(8,128)(2,1)S(1)} %get-tuple-element.56), channel_id=1, source_target_pairs={{0,1},{1,0},{2,3},{3,2},{4,5},{5,4},{6,7},{7,6},{8,9},{9,8},{10,11... | collective-permute-start | bytes 2359304 | tf_op jit(solution)/shard_map/ppermute | solution.py:63
  75.2 10.8 %collective-permute-start.22 = (bf16[3,96,1024]{2,1,0:T(8,128)(2,1)S(1)}, bf16[3,96,1024]{2,1,0:T(8,128)(2,1)S(1)}, u32[]{:S(2)}, u32[]{:S(2)}) collective-permute-start(bf16[3,96,1024]{2,1,0:T(8,128)(2,1)S(1)} %get-tuple-element.77), channel_id=1, source_target_pairs={{0,66},{1,3},{2,64},{3,1},{4,70},{5,7},{6,68},{7,5},{8,74},{9,11},... | collective-permute-start | bytes 1769480 | tf_op jit(solution)/shard_map/ppermute | solution.py:33
  76.4 12.8 %collective-permute-start.24 = (bf16[3,96,1024]{2,1,0:T(8,128)(2,1)S(1)}, bf16[3,96,1024]{2,1,0:T(8,128)(2,1)S(1)}, u32[]{:S(2)}, u32[]{:S(2)}) collective-permute-start(bf16[3,96,1024]{2,1,0:T(8,128)(2,1)S(1)} %add_convert_fusion.5), channel_id=1, source_target_pairs={{0,48},{1,17},{2,50},{3,19},{4,52},{5,21},{6,54},{7,23},{8,56},{9,... | collective-permute-start | bytes 1769480 | tf_op jit(solution)/shard_map/ppermute | solution.py:33
  80.6 25.5 %collective-permute-start.21 = (bf16[384,1024]{1,0:T(8,128)(2,1)S(1)}, bf16[384,1024]{1,0:T(8,128)(2,1)S(1)}, u32[]{:S(2)}, u32[]{:S(2)}) collective-permute-start(bf16[384,1024]{1,0:T(8,128)(2,1)S(1)} %add_convert_fusion.1), channel_id=1, source_target_pairs={{0,4},{1,5},{2,6},{3,7},{4,0},{5,1},{6,2},{7,3},{8,12},{9,13},{10,... | collective-permute-start | bytes 2359304 | tf_op jit(solution)/shard_map/ppermute | solution.py:33
  81.1 11.0 %collective-permute-start.31 = (bf16[3,24,1024]{2,1,0:T(8,128)(2,1)S(1)}, bf16[3,24,1024]{2,1,0:T(8,128)(2,1)S(1)}, u32[]{:S(2)}, u32[]{:S(2)}) collective-permute-start(bf16[3,24,1024]{2,1,0:T(8,128)(2,1)S(1)} %get-tuple-element.87), channel_id=1, source_target_pairs={{0,16},{1,49},{2,18},{3,51},{4,20},{5,53},{6,22},{7,55},{8,24},{9,... | collective-permute-start | bytes 442376 | tf_op jit(solution)/shard_map/ppermute | solution.py:33
  92.2 9.6 %collective-permute-start.27 = (bf16[3,24,1024]{2,1,0:T(8,128)(2,1)S(1)}, bf16[3,24,1024]{2,1,0:T(8,128)(2,1)S(1)}, u32[]{:S(2)}, u32[]{:S(2)}) collective-permute-start(bf16[3,24,1024]{2,1,0:T(8,128)(2,1)S(1)} %get-tuple-element.85), channel_id=1, source_target_pairs={{0,18},{1,115},{2,16},{3,113},{4,22},{5,119},{6,20},{7,117},{8,26}... | collective-permute-start | bytes 442376 | tf_op jit(solution)/shard_map/ppermute | solution.py:59
  (13 other events, 106.0 us)

commit v7 on v6

--- a/solution.py
+++ b/solution.py
@@ -92,10 +92,11 @@
     return parts[0] if len(parts) == 1 else jnp.concatenate(parts, axis=0)
 
 
-def grads_kernel(n, m, parts, *refs):
+def grads_kernel(n, m, parts, joined, *refs):
     xs, cs, refs = refs[:n], refs[n : n + m], refs[n + m :]
     a_ref, hid = refs[-2:]
-    ws, befores, gs = refs[:parts], refs[parts : -2 - parts], refs[-2 - parts : -2]
+    outs = parts // joined
+    ws, befores, gs = refs[:parts], refs[parts : -2 - outs], refs[-2 - outs : -2]
     units, width = ws[0].shape[1:]
     gu = jnp.concatenate([w[m] for w in ws for m in range(2)], axis=0)
     down = jnp.concatenate([w[2] for w in ws], axis=0)
@@ -122,49 +123,55 @@
         c = rows_of(cs, 0, tokens, cols)
         d_gu = jnp.dot(a_ref[...], x, preferred_element_type=F32)
         d_down = jnp.dot(hid[...], c, preferred_element_type=F32)
-        for p, g in enumerate(gs):
+        for p in range(parts):
+            g, before = gs[p // joined], befores[p // joined] if befores else None
+            to = slice(p % joined * units, (p % joined + 1) * units)
             for m in range(3):
                 source, row = (d_down, p) if m == 2 else (d_gu, 2 * p + m)
                 sums = source[row * units : (row + 1) * units]
-                if befores:
-                    sums = sums + befores[p][m, :, cols].astype(F32)
-                g[m, :, cols] = sums.astype(BF16)
-
-
-def grads(xs, cs, ws, befores=()):
+                if before is not None:
+                    sums = sums + before[m, to, cols].astype(F32)
+                g[m, to, cols] = sums.astype(BF16)
+
+
+def grads(xs, cs, ws, befores=(), joined=1, weight=0):
     units, width = ws[0].shape[1:]
     tokens = sum(x.shape[0] for x in xs)
     vmem = pl.BlockSpec(memory_space=pltpu.VMEM)
 
     def kernel(*refs):
-        grads_kernel(len(xs), len(cs), len(ws), *refs)
+        grads_kernel(len(xs), len(cs), len(ws), joined, *refs)
 
     return pl.pallas_call(
         kernel,
-        out_shape=[jax.ShapeDtypeStruct(w.shape, BF16) for w in ws]
+        out_shape=[jax.ShapeDtypeStruct((3, joined * units, width), BF16)] * (len(ws) // joined)
         + [jax.ShapeDtypeStruct((2 * len(ws) * units, tokens), BF16)],
         in_specs=[vmem] * (len(xs) + len(cs) + len(ws) + len(befores)),
-        out_specs=[vmem] * (len(ws) + 1),
+        out_specs=[vmem] * (len(ws) // joined + 1),
         scratch_shapes=[pltpu.VMEM((len(ws) * units, tokens), BF16)],
         compiler_params=pltpu.CompilerParams(vmem_limit_bytes=32 * 1024 * 1024),
         cost_estimate=pl.CostEstimate(
-            flops=width if befores else 3 * 10**9, bytes_accessed=width, transcendentals=0
+            flops=width + weight * 10**9, bytes_accessed=width, transcendentals=0
         ),
     )(*xs, *cs, *ws, *befores)
 
 
 def input_kernel(n, *refs):
-    parts, ws = refs[:n], refs[n:-2]
-    mine_ref, pair_ref = refs[-2:]
+    parts, ws = refs[:n], refs[n:-4]
+    outs = refs[-4:]
     w_all = jnp.concatenate([w[m] for w in ws for m in range(2)], axis=0)
-    group = mine_ref.shape[0]
-    for i, ref in enumerate((mine_ref, pair_ref)):
-        a = jnp.concatenate([part[:, i * group : (i + 1) * group] for part in parts], axis=0)
-        ref[...] = lax.dot_general(a, w_all, TN, preferred_element_type=F32).astype(ref.dtype)
-
-
-def input_half(parts, ws, group):
+    group = outs[0].shape[0]
+    k = len(parts) // 2
+    for i in range(4):
+        half = parts[i // 2 * k : (i // 2 + 1) * k]
+        a = jnp.concatenate([part[:, i % 2 * group : (i % 2 + 1) * group] for part in half], axis=0)
+        total = lax.dot_general(a, w_all, TN, preferred_element_type=F32)
+        outs[i][...] = total.astype(outs[i].dtype)
+
+
+def input_parts(parts, ws):
     width = ws[0].shape[2]
+    group = parts[0].shape[1] // 2
     vmem = pl.BlockSpec(memory_space=pltpu.VMEM)
 
     def kernel(*refs):
@@ -173,11 +180,10 @@
     return pl.pallas_call(
         kernel,
         out_shape=[
-            jax.ShapeDtypeStruct((group, width), F32),
-            jax.ShapeDtypeStruct((group, width), BF16),
+            jax.ShapeDtypeStruct((group, width), kind) for kind in (F32, BF16, F32, BF16)
         ],
         in_specs=[vmem] * (len(parts) + len(ws)),
-        out_specs=[vmem] * 2,
+        out_specs=[vmem] * 4,
         compiler_params=pltpu.CompilerParams(vmem_limit_bytes=32 * 1024 * 1024),
         cost_estimate=pl.CostEstimate(
             flops=width, bytes_accessed=width, transcendentals=0
@@ -189,48 +195,52 @@
     x_z = swap_near(activations, Z)
     message = jnp.concatenate([gate_up.transpose(1, 0, 2), down_proj[None]], axis=0)
     message = lax.optimization_barrier(message)
-    block1 = gather_block(swap_wrap(message, Z))
-    o0 = gather_block(message)
+    other = swap_wrap(message, Z)
+    block1 = gather_block(other)
+    o0, _ = lax.optimization_barrier((gather_block(message), other))
     block1, c_own = lax.optimization_barrier((block1, cotangent))
     c_z = swap_near(c_own, Z)
     o1, x_z = lax.optimization_barrier((block1, x_z))
     n0, w0 = swap_second(o0, Y), swap_second(o0, X)
-    n0, w0 = lax.optimization_barrier((n0, w0))
-    n1, w1 = swap_second(o1, X), swap_second(o1, Y)
-    n1, w1 = lax.optimization_barrier((n1, w1))
+    n1 = swap_second(o1, X)
+    w1 = swap_second(o1, Y)
     f0, f1 = swap_second(n0, X), swap_second(n1, Y)
     xs, cs = [activations, swap_core(activations)], [cotangent, swap_core(cotangent)]
+
+    near = [n1, o1, n0, o0]
+    *g_near, a_near = grads(xs, cs, near, weight=3)
+    x_z, c_z, a_near = lax.optimization_barrier((x_z, c_z, a_near))
     xs_z, cs_z = [x_z, swap_core(x_z)], [c_z, swap_core(c_z)]
-
-    near, far0, far1 = [n1, o1, n0, o0], [f0, w0], [f1, w1]
-    *g_near, a_near = grads(xs, cs, near)
-    *g_far0, a_far0 = grads(xs, cs, far0)
-    f1, a_near, a_far0 = lax.optimization_barrier((f1, a_near, a_far0))
-    *g_far1, a_far1 = grads(xs, cs, [f1, w1])
-    g_f1, g_w1, a_far1_z = grads(xs_z, cs_z, [f1, w1], g_far1)
-    back_f1, back_w1 = swap_second(g_f1, Y), swap_second(g_w1, Y)
-    f0, a_far1_z = lax.optimization_barrier((f0, a_far1_z))
-    g_f0, g_w0, a_far0_z = grads(xs_z, cs_z, [f0, w0], g_far0)
-    back_f0, back_w0 = swap_second(g_f0, X), swap_second(g_w0, X)
-    n1, a_far0_z = lax.optimization_barrier((n1, a_far0_z))
+    f0, w1 = lax.optimization_barrier((f0, w1))
+    g_r0, a_r0 = grads(xs, cs, [w0, f0], joined=2, weight=0)
+    f1, a_r0 = lax.optimization_barrier((f1, a_r0))
+    g_r1, a_r1 = grads(xs, cs, [w1, f1], joined=2, weight=3)
+
+    g_r1, a_r1_z = grads(xs_z, cs_z, [w1, f1], [g_r1], joined=2)
+    back1 = swap_second(g_r1, Y)
+    f0, a_r1_z = lax.optimization_barrier((f0, a_r1_z))
+    g_r0, a_r0_z = grads(xs_z, cs_z, [w0, f0], [g_r0], joined=2)
+    back0 = swap_second(g_r0, X)
+    n1, a_r0_z = lax.optimization_barrier((n1, a_r0_z))
     g_n1, g_o1, g_n0, g_o0, a_near_z = grads(xs_z, cs_z, [n1, o1, n0, o0], g_near)
-
-    group = activations.shape[0]
-    ws = far1 + far0 + near
-    z_part, z_pair = input_half([a_far1_z, a_far0_z, a_near_z], ws, group)
-    z_got = swap_core(z_pair)
-    mine, pair = input_half([a_far1, a_far0, a_near], ws, group)
-    got = swap_core(pair)
-    near1 = swap_second(add(g_n1, back_f1), X)
-    near0 = swap_second(add(g_n0, back_f0), Y)
+    parts = [a_r1, a_r0, a_near, a_r1_z, a_r0_z, a_near_z]
+    own, pair, z_part, z_pair = input_parts(parts, [w1, f1, w0, f0] + near)
+    z_got, got = swap_core(z_pair), swap_core(pair)
+
+    n = g_n1.shape[1]
+    near1 = swap_second(add(g_n1, back1[:, n:]), X)
+    back0, back1 = lax.optimization_barrier((back0, back1))
+    near0 = swap_second(add(g_n0, back0[:, n:]), Y)
+    back0, z_part = lax.optimization_barrier((back0, z_part))
+    mine = own + got.astype(F32)
     z_part = swap_near((z_part + z_got.astype(F32)).astype(BF16), Z)
 
     def block_sum(own, back, near):
         return (own.astype(F32) + back.astype(F32) + near.astype(F32)).astype(BF16)
 
-    total1 = reduce_block(block_sum(g_o1, back_w1, near1)).astype(BF16)
-    total0 = reduce_block(block_sum(g_o0, back_w0, near0))
-    grad_input = (mine + got.astype(F32) + z_part.astype(F32)).astype(BF16)
+    total1 = reduce_block(block_sum(g_o1, back1[:, :n], near1)).astype(BF16)
+    total0 = reduce_block(block_sum(g_o0, back0[:, :n], near0))
+    grad_input = (mine + z_part.astype(F32)).astype(BF16)
     total = total0 + swap_wrap(total1, Z).astype(F32)
     return (grad_input, total.transpose(1, 0, 2))
 

time: 108 us -> 104 us (0.963)
  starting transfers between devices: 51.1 us -> 44.6 us
  waiting for transfers between devices: 27.8 us -> 29.4 us
    ppermute x25 -> x23, starting transfers between devices: 39.3 us -> 33.5 us  [swap(): return lax.ppermute(value, AXES, pairs)]
    ppermute x6, starting transfers between devices: 3.62 us -> 0.6 us  [swap_core(): return lax.ppermute(value, AXES, [(d, d ^ 1) for d in range(DEVICES)])]
    ppermute x4, starting transfers between devices: 8.21 us -> 10.5 us  [swap_corner(): return lax.ppermute(value, AXES, pairs)]
    ppermute x25 -> x23, waiting for transfers between devices: 27.3 us -> 28.9 us  [swap(): return lax.ppermute(value, AXES, pairs)]
    pallas_call x8 -> x7, Pallas kernels: 22.2 us -> 22 us  [the longest x6 17 us: grads(): pl.pallas_call(kernel, out_shape=[jax.ShapeDtypeStruct((3, joined * units...]
  transfers between devices with their start and end apart: 35 -> 33, of which waited for: 16 -> 15; matrix products, arithmetic and copies ran while one was open for 4% -> 4% of each run, Pallas kernels for 19% -> 19%
where the time goes in v7:
time: 104 us; the launch traced here: 102 us
  starting transfers between devices  44.6 us (43%)
  waiting for transfers between devices  29.4 us (28%)
  Pallas kernels  22 us (21%)
  other arithmetic  4.34 us (4%)
    ppermute x23, starting transfers between devices, swap(): return lax.ppermute(value, AXES, pairs)  33.5 us
    ppermute x23, waiting for transfers between devices, swap(): return lax.ppermute(value, AXES, pairs)  28.9 us
    pallas_call x6, Pallas kernels, grads(): pl.pallas_call(kernel, out_shape=[jax.ShapeDtypeStruct((3, joined * units...  17 us
    ppermute x4, starting transfers between devices, swap_corner(): return lax.ppermute(value, AXES, pairs)  10.5 us
    pallas_call x1, Pallas kernels, input_parts(): pl.pallas_call(kernel, out_shape=[jax.ShapeDtypeStruct((group, width), ki...  5.06 us
  transfers between devices with their start and end apart: 33, of which 15 were waited for; matrix products, arithmetic and copies ran while one was open for 4% of the time, Pallas kernels for 19%

profile of v7, /device:TPU:2, one launch (start us, length us, event | category | flops | bytes accessed | tf_op | source)
XLA Modules:
  0.0 102.2 jit_solution(18094531330265879963)
XLA Ops:
  0.6 2.0 %collective-permute-start.11 = (bf16[384,1024]{1,0:T(8,128)(2,1)}, bf16[384,1024]{1,0:T(8,128)(2,1)S(1)}, u32[]{:S(2)}, u32[]{:S(2)}) collective-permute-start(bf16[384,1024]{1,0:T(8,128)(2,1)} %refs_0_.5), channel_id=1, source_target_pairs={{0,4},{1,5},{2,6},{3,7},{4,0},{5,1},{6,2},{7,3},{8,12},{9,13},{10,... | collective-permute-start | bytes 2359304 | tf_op jit(solution)/shard_map/ppermute | solution.py:33
  4.4 2.6 %collective-permute-start.5 = (bf16[3,24,1024]{2,1,0:T(8,128)(2,1)S(1)}, bf16[3,24,1024]{2,1,0:T(8,128)(2,1)S(1)}, u32[]{:S(2)}, u32[]{:S(2)}) collective-permute-start(bf16[3,24,1024]{2,1,0:T(8,128)(2,1)S(1)} %pad_maximum_fusion.2), channel_id=1, source_target_pairs={{0,12},{1,13},{2,14},{3,15},{4,8},{5,9},{6,10},{7,11},{8,4},{9,5},... | collective-permute-start | bytes 442376 | tf_op jit(solution)/shard_map/ppermute | solution.py:33
  15.2 2.5 %collective-permute-start.6 = (bf16[3,96,1024]{2,1,0:T(8,128)(2,1)S(1)}, bf16[3,96,1024]{2,1,0:T(8,128)(2,1)S(1)}, u32[]{:S(2)}, u32[]{:S(2)}) collective-permute-start(bf16[3,96,1024]{2,1,0:T(8,128)(2,1)S(1)} %pad_maximum_fusion.refs_7_.refs_13_), channel_id=1, source_target_pairs={{0,48},{1,17},{2,50},{3,19},{4,52},{5,21},{6,54},{7,23},{8,56},{9,... | collective-permute-start | bytes 1769480 | tf_op jit(solution)/shard_map/ppermute | solution.py:33
  18.7 5.8 %collective-permute-done.8 = bf16[3,24,1024]{2,1,0:T(8,128)(2,1)S(1)} collective-permute-done((bf16[3,24,1024]{2,1,0:T(8,128)(2,1)S(1)}, bf16[3,24,1024]{2,1,0:T(8,128)(2,1)S(1)}, u32[]{:S(2)}, u32[]{:S(2)}) %collective-permute-start.8) | collective-permute-done | bytes 147488 | tf_op jit(solution)/shard_map/ppermute | solution.py:33
  31.6 3.0 %collective-permute-done.13.refs_4_.refs_10_ = bf16[3,96,1024]{2,1,0:T(8,128)(2,1)S(1)} collective-permute-done((bf16[3,96,1024]{2,1,0:T(8,128)(2,1)S(1)}, bf16[3,96,1024]{2,1,0:T(8,128)(2,1)S(1)}, u32[]{:S(2)}, u32[]{:S(2)}) %collective-permute-start.13) | collective-permute-done | bytes 589856 | tf_op jit(solution)/shard_map/ppermute | solution.py:33
  35.3 4.0 %shard_map.61 = (bf16[3,96,1024]{2,1,0:T(8,128)(2,1)S(1)}, bf16[3,96,1024]{2,1,0:T(8,128)(2,1)S(1)}, bf16[3,96,1024]{2,1,0:T(8,128)(2,1)S(1)}, bf16[3,96,1024]{2,1,0:T(8,128)(2,1)S(1)}, bf16[768,768]{1,0:T(8,128)(2,1)S(1)}) custom-call(bf16[384,1024]{1,0:T(8,128)(2,1)S(1)} %copy-done, bf16[384,1024]{1,0:T(8,128)(2,1)S(1)} %collective-permute-done.refs_1_, ...), custom_call_target="tpu_custom_call" | custom-call | flops 3000001024 | bytes 1024 | tf_op jit(solution)/shard_map/pallas_call | solution.py:145
  39.4 4.7 %collective-permute-done.16.refs_2_ = bf16[384,1024]{1,0:T(8,128)(2,1)S(1)} collective-permute-done((bf16[384,1024]{1,0:T(8,128)(2,1)S(1)}, bf16[384,1024]{1,0:T(8,128)(2,1)S(1)}, u32[]{:S(2)}, u32[]{:S(2)}) %collective-permute-start.16) | collective-permute-done | bytes 786464 | tf_op jit(solution)/shard_map/ppermute | solution.py:33
  44.6 2.5 %collective-permute-done.15.refs_4_.refs_8_ = bf16[3,96,1024]{2,1,0:T(8,128)(2,1)S(1)} collective-permute-done((bf16[3,96,1024]{2,1,0:T(8,128)(2,1)S(1)}, bf16[3,96,1024]{2,1,0:T(8,128)(2,1)S(1)}, u32[]{:S(2)}, u32[]{:S(2)}) %collective-permute-start.15) | collective-permute-done | bytes 589856 | tf_op jit(solution)/shard_map/ppermute | solution.py:33
  47.2 2.2 %shard_map.59 = (bf16[3,192,1024]{2,1,0:T(8,128)(2,1)S(1)}, bf16[384,768]{1,0:T(8,128)(2,1)S(1)}) custom-call(bf16[384,1024]{1,0:T(8,128)(2,1)S(1)} %copy-done, bf16[384,1024]{1,0:T(8,128)(2,1)S(1)} %collective-permute-done.refs_1_, bf16[384,1024]{1,0:T(8,128)(2,1)S(1)} %copy-done.1, bf16[384,1024]{1,0:T(8,128)(2,1)S(1)} %collective-permute-done.1.refs_3_, ...), custom_call_target="tpu_custom_call" | custom-call | flops 1024 | bytes 1024 | tf_op jit(solution)/shard_map/pallas_call | solution.py:145
  49.4 2.2 %shard_map.60 = (bf16[3,192,1024]{2,1,0:T(8,128)(2,1)S(1)}, bf16[384,768]{1,0:T(8,128)(2,1)S(1)}) custom-call(bf16[384,1024]{1,0:T(8,128)(2,1)S(1)} %copy-done, bf16[384,1024]{1,0:T(8,128)(2,1)S(1)} %collective-permute-done.refs_1_, bf16[384,1024]{1,0:T(8,128)(2,1)S(1)} %copy-done.1, bf16[384,1024]{1,0:T(8,128)(2,1)S(1)} %collective-permute-done.1.refs_3_, ...), custom_call_target="tpu_custom_call" | custom-call | flops 3000001024 | bytes 1024 | tf_op jit(solution)/shard_map/pallas_call | solution.py:145
  51.7 2.2 %shard_map.62 = (bf16[3,192,1024]{2,1,0:T(8,128)(2,1)S(1)}, bf16[384,768]{1,0:T(8,128)(2,1)S(1)}) custom-call(bf16[384,1024]{1,0:T(8,128)(2,1)S(1)} %collective-permute-done.11.refs_0_, bf16[384,1024]{1,0:T(8,128)(2,1)S(1)} %collective-permute-done.17.refs_1_, bf16[384,1024]{1,0:T(8,128)(2,1)S(1)} %collective-permute-done.16.refs_2_, ...), custom_call_target="tpu_custom_call" | custom-call | flops 1024 | bytes 1024 | tf_op jit(solution)/shard_map/pallas_call | solution.py:145
  54.7 2.2 %shard_map.63 = (bf16[3,192,1024]{2,1,0:T(8,128)(2,1)S(1)}, bf16[384,768]{1,0:T(8,128)(2,1)S(1)}) custom-call(bf16[384,1024]{1,0:T(8,128)(2,1)S(1)} %collective-permute-done.11.refs_0_, bf16[384,1024]{1,0:T(8,128)(2,1)S(1)} %collective-permute-done.17.refs_1_, bf16[384,1024]{1,0:T(8,128)(2,1)S(1)} %collective-permute-done.16.refs_2_, ...), custom_call_target="tpu_custom_call" | custom-call | flops 1024 | bytes 1024 | tf_op jit(solution)/shard_map/pallas_call | solution.py:145
  57.0 1.8 %collective-permute-start.20 = (bf16[3,192,1024]{2,1,0:T(8,128)(2,1)S(1)}, bf16[3,192,1024]{2,1,0:T(8,128)(2,1)S(1)}, u32[]{:S(2)}, u32[]{:S(2)}) collective-permute-start(bf16[3,192,1024]{2,1,0:T(8,128)(2,1)S(1)} %get-tuple-element.74), channel_id=1, source_target_pairs={{0,66},{1,3},{2,64},{3,1},{4,70},{5,7},{6,68},{7,5},{8,74},{9,11},... | collective-permute-start | bytes 3538952 | tf_op jit(solution)/shard_map/ppermute | solution.py:33
  58.8 4.1 %shard_map.64 = (bf16[3,96,1024]{2,1,0:T(8,128)(2,1)S(1)}, bf16[3,96,1024]{2,1,0:T(8,128)(2,1)S(1)}, bf16[3,96,1024]{2,1,0:T(8,128)(2,1)S(1)}, bf16[3,96,1024]{2,1,0:T(8,128)(2,1)S(1)}, bf16[768,768]{1,0:T(8,128)(2,1)S(1)}) custom-call(bf16[384,1024]{1,0:T(8,128)(2,1)S(1)} %collective-permute-done.11.refs_0_, ...), custom_call_target="tpu_custom_call" | custom-call | flops 1024 | bytes 1024 | tf_op jit(solution)/shard_map/pallas_call | solution.py:145
  62.8 5.1 %shard_map.65 = (f32[384,1024]{1,0:T(8,128)S(1)}, bf16[384,1024]{1,0:T(8,128)(2,1)S(1)}, f32[384,1024]{1,0:T(8,128)S(1)}, bf16[384,1024]{1,0:T(8,128)(2,1)S(1)}) custom-call(bf16[384,768]{1,0:T(8,128)(2,1)S(1)} %get-tuple-element.51.refs_0_, bf16[384,768]{1,0:T(8,128)(2,1)S(1)} %get-tuple-element.52.refs_1_, bf16[768,768]{1,0:T(8,128)(2,1)S(1)} %get-tuple-element.56.refs_2_, ...), custom_call_target="tpu_custom_call" | custom-call | flops 1024 | bytes 1024 | tf_op jit(solution)/shard_map/pallas_call | solution.py:180
  68.0 3.4 %collective-permute-done.21 = bf16[3,192,1024]{2,1,0:T(8,128)(2,1)S(1)} collective-permute-done((bf16[3,192,1024]{2,1,0:T(8,128)(2,1)S(1)}, bf16[3,192,1024]{2,1,0:T(8,128)(2,1)S(1)}, u32[]{:S(2)}, u32[]{:S(2)}) %collective-permute-start.21) | collective-permute-done | bytes 1179680 | tf_op jit(solution)/shard_map/ppermute | solution.py:33
  73.7 2.5 %collective-permute-start.24 = (bf16[3,96,1024]{2,1,0:T(8,128)(2,1)S(1)}, bf16[3,96,1024]{2,1,0:T(8,128)(2,1)S(1)}, u32[]{:S(2)}, u32[]{:S(2)}) collective-permute-start(bf16[3,96,1024]{2,1,0:T(8,128)(2,1)S(1)} %add_convert_fusion.5), channel_id=1, source_target_pairs={{0,48},{1,17},{2,50},{3,19},{4,52},{5,21},{6,54},{7,23},{8,56},{9,... | collective-permute-start | bytes 1769480 | tf_op jit(solution)/shard_map/ppermute | solution.py:33
  77.6 4.0 %collective-permute-done.28 = bf16[3,96,1024]{2,1,0:T(8,128)(2,1)S(1)} collective-permute-done((bf16[3,96,1024]{2,1,0:T(8,128)(2,1)S(1)}, bf16[3,96,1024]{2,1,0:T(8,128)(2,1)S(1)}, u32[]{:S(2)}, u32[]{:S(2)}) %collective-permute-start.28) | collective-permute-done | bytes 589856 | tf_op jit(solution)/shard_map/ppermute | solution.py:33
  82.0 4.4 %collective-permute-start.31 = (bf16[3,24,1024]{2,1,0:T(8,128)(2,1)S(1)}, bf16[3,24,1024]{2,1,0:T(8,128)(2,1)S(1)}, u32[]{:S(2)}, u32[]{:S(2)}) collective-permute-start(bf16[3,24,1024]{2,1,0:T(8,128)(2,1)S(1)} %get-tuple-element.90), channel_id=1, source_target_pairs={{0,18},{1,115},{2,16},{3,113},{4,22},{5,119},{6,20},{7,117},{8,26}... | collective-permute-start | bytes 442376 | tf_op jit(solution)/shard_map/ppermute | solution.py:59
  86.6 3.1 %collective-permute-start.30 = (bf16[3,24,1024]{2,1,0:T(8,128)(2,1)S(1)}, bf16[3,24,1024]{2,1,0:T(8,128)(2,1)S(1)}, u32[]{:S(2)}, u32[]{:S(2)}) collective-permute-start(bf16[3,24,1024]{2,1,0:T(8,128)(2,1)S(1)} %get-tuple-element.91), channel_id=1, source_target_pairs={{0,2},{1,67},{2,0},{3,65},{4,6},{5,71},{6,4},{7,69},{8,10},{9,75},... | collective-permute-start | bytes 442376 | tf_op jit(solution)/shard_map/ppermute | solution.py:33
  90.2 2.9 %collective-permute-start.27 = (bf16[3,24,1024]{2,1,0:T(8,128)(2,1)S(1)}, bf16[3,24,1024]{2,1,0:T(8,128)(2,1)S(1)}, u32[]{:S(2)}, u32[]{:S(2)}) collective-permute-start(bf16[3,24,1024]{2,1,0:T(8,128)(2,1)S(1)} %get-tuple-element.87), channel_id=1, source_target_pairs={{0,18},{1,115},{2,16},{3,113},{4,22},{5,119},{6,20},{7,117},{8,26}... | collective-permute-start | bytes 442376 | tf_op jit(solution)/shard_map/ppermute | solution.py:59
  93.1 1.7 %collective-permute-start.26 = (bf16[3,24,1024]{2,1,0:T(8,128)(2,1)S(1)}, bf16[3,24,1024]{2,1,0:T(8,128)(2,1)S(1)}, u32[]{:S(2)}, u32[]{:S(2)}) collective-permute-start(bf16[3,24,1024]{2,1,0:T(8,128)(2,1)S(1)} %get-tuple-element.88), channel_id=1, source_target_pairs={{0,2},{1,67},{2,0},{3,65},{4,6},{5,71},{6,4},{7,69},{8,10},{9,75},... | collective-permute-start | bytes 442376 | tf_op jit(solution)/shard_map/ppermute | solution.py:33
  95.0 3.1 %collective-permute-start.32 = (bf16[3,24,1024]{2,1,0:T(8,128)(2,1)S(1)}, bf16[3,24,1024]{2,1,0:T(8,128)(2,1)S(1)}, u32[]{:S(2)}, u32[]{:S(2)}) collective-permute-start(bf16[3,24,1024]{2,1,0:T(8,128)(2,1)S(1)} %add_convert_fusion.6), channel_id=1, source_target_pairs={{0,12},{1,13},{2,14},{3,15},{4,8},{5,9},{6,10},{7,11},{8,4},{9,5},... | collective-permute-start | bytes 442376 | tf_op jit(solution)/shard_map/ppermute | solution.py:33
  99.4 2.0 %collective-permute-done.32 = bf16[3,24,1024]{2,1,0:T(8,128)(2,1)S(1)} collective-permute-done((bf16[3,24,1024]{2,1,0:T(8,128)(2,1)S(1)}, bf16[3,24,1024]{2,1,0:T(8,128)(2,1)S(1)}, u32[]{:S(2)}, u32[]{:S(2)}) %collective-permute-start.32) | collective-permute-done | bytes 147488 | tf_op jit(solution)/shard_map/ppermute | solution.py:33
  (67 shorter events, 27.1 us)
Async XLA Ops:
  0.6 23.9 %collective-permute-start.11 = (bf16[384,1024]{1,0:T(8,128)(2,1)}, bf16[384,1024]{1,0:T(8,128)(2,1)S(1)}, u32[]{:S(2)}, u32[]{:S(2)}) collective-permute-start(bf16[384,1024]{1,0:T(8,128)(2,1)} %refs_0_.5), channel_id=1, source_target_pairs={{0,4},{1,5},{2,6},{3,7},{4,0},{5,1},{6,2},{7,3},{8,12},{9,13},{10,... | collective-permute-start | bytes 2359304 | tf_op jit(solution)/shard_map/ppermute | solution.py:33
  11.0 7.2 %collective-permute-start.10 = (bf16[3,24,1024]{2,1,0:T(8,128)(2,1)S(1)}, bf16[3,24,1024]{2,1,0:T(8,128)(2,1)S(1)}, u32[]{:S(2)}, u32[]{:S(2)}) collective-permute-start(bf16[3,24,1024]{2,1,0:T(8,128)(2,1)S(1)} %collective-permute-done.5), channel_id=1, source_target_pairs={{0,18},{1,115},{2,16},{3,113},{4,22},{5,119},{6,20},{7,117},{8,26}... | collective-permute-start | bytes 442376 | tf_op jit(solution)/shard_map/ppermute | solution.py:59
  15.2 12.8 %collective-permute-start.6 = (bf16[3,96,1024]{2,1,0:T(8,128)(2,1)S(1)}, bf16[3,96,1024]{2,1,0:T(8,128)(2,1)S(1)}, u32[]{:S(2)}, u32[]{:S(2)}) collective-permute-start(bf16[3,96,1024]{2,1,0:T(8,128)(2,1)S(1)} %pad_maximum_fusion.refs_7_.refs_13_), channel_id=1, source_target_pairs={{0,48},{1,17},{2,50},{3,19},{4,52},{5,21},{6,54},{7,23},{8,56},{9,... | collective-permute-start | bytes 1769480 | tf_op jit(solution)/shard_map/ppermute | solution.py:33
  18.2 11.3 %collective-permute-start = (bf16[384,1024]{1,0:T(8,128)(2,1)S(1)}, bf16[384,1024]{1,0:T(8,128)(2,1)S(1)}, u32[]{:S(2)}, u32[]{:S(2)}) collective-permute-start(bf16[384,1024]{1,0:T(8,128)(2,1)S(1)} %copy-done), channel_id=1, source_target_pairs={{0,1},{1,0},{2,3},{3,2},{4,5},{5,4},{6,7},{7,6},{8,9},{9,8},{10,11... | collective-permute-start | bytes 2359304 | tf_op jit(solution)/shard_map/ppermute | solution.py:63
  18.7 11.3 %collective-permute-start.1 = (bf16[384,1024]{1,0:T(8,128)(2,1)S(1)}, bf16[384,1024]{1,0:T(8,128)(2,1)S(1)}, u32[]{:S(2)}, u32[]{:S(2)}) collective-permute-start(bf16[384,1024]{1,0:T(8,128)(2,1)S(1)} %copy-done.1), channel_id=1, source_target_pairs={{0,1},{1,0},{2,3},{3,2},{4,5},{5,4},{6,7},{7,6},{8,9},{9,8},{10,11... | collective-permute-start | bytes 2359304 | tf_op jit(solution)/shard_map/ppermute | solution.py:63
  24.6 10.0 %collective-permute-start.13 = (bf16[3,96,1024]{2,1,0:T(8,128)(2,1)S(1)}, bf16[3,96,1024]{2,1,0:T(8,128)(2,1)S(1)}, u32[]{:S(2)}, u32[]{:S(2)}) collective-permute-start(bf16[3,96,1024]{2,1,0:T(8,128)(2,1)S(1)} %pad_maximum_fusion.1.refs_5_.refs_11_), channel_id=1, source_target_pairs={{0,66},{1,3},{2,64},{3,1},{4,70},{5,7},{6,68},{7,5},{8,74},{9,11},... | collective-permute-start | bytes 1769480 | tf_op jit(solution)/shard_map/ppermute | solution.py:33
  26.2 18.0 %collective-permute-start.16 = (bf16[384,1024]{1,0:T(8,128)(2,1)S(1)}, bf16[384,1024]{1,0:T(8,128)(2,1)S(1)}, u32[]{:S(2)}, u32[]{:S(2)}) collective-permute-start(bf16[384,1024]{1,0:T(8,128)(2,1)S(1)} %copy-done.1), channel_id=1, source_target_pairs={{0,4},{1,5},{2,6},{3,7},{4,0},{5,1},{6,2},{7,3},{8,12},{9,13},{10,... | collective-permute-start | bytes 2359304 | tf_op jit(solution)/shard_map/ppermute | solution.py:33
  28.0 16.2 %collective-permute-start.7 = (bf16[3,96,1024]{2,1,0:T(8,128)(2,1)S(1)}, bf16[3,96,1024]{2,1,0:T(8,128)(2,1)S(1)}, u32[]{:S(2)}, u32[]{:S(2)}) collective-permute-start(bf16[3,96,1024]{2,1,0:T(8,128)(2,1)S(1)} %collective-permute-done.6.refs_6_.refs_12_), channel_id=1, source_target_pairs={{0,66},{1,3},{2,64},{3,1},{4,70},{5,7},{6,68},{7,5},{8,74},{9,11},... | collective-permute-start | bytes 1769480 | tf_op jit(solution)/shard_map/ppermute | solution.py:33
  29.5 17.7 %collective-permute-start.15 = (bf16[3,96,1024]{2,1,0:T(8,128)(2,1)S(1)}, bf16[3,96,1024]{2,1,0:T(8,128)(2,1)S(1)}, u32[]{:S(2)}, u32[]{:S(2)}) collective-permute-start(bf16[3,96,1024]{2,1,0:T(8,128)(2,1)S(1)} %pad_maximum_fusion.refs_7_.refs_13_), channel_id=1, source_target_pairs={{0,66},{1,3},{2,64},{3,1},{4,70},{5,7},{6,68},{7,5},{8,74},{9,11},... | collective-permute-start | bytes 1769480 | tf_op jit(solution)/shard_map/ppermute | solution.py:33
  30.0 14.6 %collective-permute-start.12 = (bf16[3,96,1024]{2,1,0:T(8,128)(2,1)S(1)}, bf16[3,96,1024]{2,1,0:T(8,128)(2,1)S(1)}, u32[]{:S(2)}, u32[]{:S(2)}) collective-permute-start(bf16[3,96,1024]{2,1,0:T(8,128)(2,1)S(1)} %pad_maximum_fusion.1.refs_5_.refs_11_), channel_id=1, source_target_pairs={{0,48},{1,17},{2,50},{3,19},{4,52},{5,21},{6,54},{7,23},{8,56},{9,... | collective-permute-start | bytes 1769480 | tf_op jit(solution)/shard_map/ppermute | solution.py:33
  34.5 14.9 %collective-permute-start.14 = (bf16[3,96,1024]{2,1,0:T(8,128)(2,1)S(1)}, bf16[3,96,1024]{2,1,0:T(8,128)(2,1)S(1)}, u32[]{:S(2)}, u32[]{:S(2)}) collective-permute-start(bf16[3,96,1024]{2,1,0:T(8,128)(2,1)S(1)} %collective-permute-done.13.refs_4_.refs_10_), channel_id=1, source_target_pairs={{0,48},{1,17},{2,50},{3,19},{4,52},{5,21},{6,54},{7,23},{8,56},{9,... | collective-permute-start | bytes 1769480 | tf_op jit(solution)/shard_map/ppermute | solution.py:33
  44.1 7.5 %collective-permute-start.17 = (bf16[384,1024]{1,0:T(8,128)(2,1)S(1)}, bf16[384,1024]{1,0:T(8,128)(2,1)S(1)}, u32[]{:S(2)}, u32[]{:S(2)}) collective-permute-start(bf16[384,1024]{1,0:T(8,128)(2,1)S(1)} %collective-permute-done.11.refs_0_), channel_id=1, source_target_pairs={{0,1},{1,0},{2,3},{3,2},{4,5},{5,4},{6,7},{7,6},{8,9},{9,8},{10,11... | collective-permute-start | bytes 2359304 | tf_op jit(solution)/shard_map/ppermute | solution.py:63
  44.1 7.5 %collective-permute-start.18 = (bf16[384,1024]{1,0:T(8,128)(2,1)S(1)}, bf16[384,1024]{1,0:T(8,128)(2,1)S(1)}, u32[]{:S(2)}, u32[]{:S(2)}) collective-permute-start(bf16[384,1024]{1,0:T(8,128)(2,1)S(1)} %collective-permute-done.16.refs_2_), channel_id=1, source_target_pairs={{0,1},{1,0},{2,3},{3,2},{4,5},{5,4},{6,7},{7,6},{8,9},{9,8},{10,11... | collective-permute-start | bytes 2359304 | tf_op jit(solution)/shard_map/ppermute | solution.py:63
  53.9 17.5 %collective-permute-start.21 = (bf16[3,192,1024]{2,1,0:T(8,128)(2,1)S(1)}, bf16[3,192,1024]{2,1,0:T(8,128)(2,1)S(1)}, u32[]{:S(2)}, u32[]{:S(2)}) collective-permute-start(bf16[3,192,1024]{2,1,0:T(8,128)(2,1)S(1)} %get-tuple-element.75), channel_id=1, source_target_pairs={{0,48},{1,17},{2,50},{3,19},{4,52},{5,21},{6,54},{7,23},{8,56},{9,... | collective-permute-start | bytes 3538952 | tf_op jit(solution)/shard_map/ppermute | solution.py:33
  57.0 16.5 %collective-permute-start.20 = (bf16[3,192,1024]{2,1,0:T(8,128)(2,1)S(1)}, bf16[3,192,1024]{2,1,0:T(8,128)(2,1)S(1)}, u32[]{:S(2)}, u32[]{:S(2)}) collective-permute-start(bf16[3,192,1024]{2,1,0:T(8,128)(2,1)S(1)} %get-tuple-element.74), channel_id=1, source_target_pairs={{0,66},{1,3},{2,64},{3,1},{4,70},{5,7},{6,68},{7,5},{8,74},{9,11},... | collective-permute-start | bytes 3538952 | tf_op jit(solution)/shard_map/ppermute | solution.py:33
  67.9 8.3 %collective-permute-start.22 = (bf16[384,1024]{1,0:T(8,128)(2,1)S(1)}, bf16[384,1024]{1,0:T(8,128)(2,1)S(1)}, u32[]{:S(2)}, u32[]{:S(2)}) collective-permute-start(bf16[384,1024]{1,0:T(8,128)(2,1)S(1)} %get-tuple-element.79), channel_id=1, source_target_pairs={{0,1},{1,0},{2,3},{3,2},{4,5},{5,4},{6,7},{7,6},{8,9},{9,8},{10,11... | collective-permute-start | bytes 2359304 | tf_op jit(solution)/shard_map/ppermute | solution.py:63
  71.6 10.0 %collective-permute-start.28 = (bf16[3,96,1024]{2,1,0:T(8,128)(2,1)S(1)}, bf16[3,96,1024]{2,1,0:T(8,128)(2,1)S(1)}, u32[]{:S(2)}, u32[]{:S(2)}) collective-permute-start(bf16[3,96,1024]{2,1,0:T(8,128)(2,1)S(1)} %add_convert_fusion.3), channel_id=1, source_target_pairs={{0,66},{1,3},{2,64},{3,1},{4,70},{5,7},{6,68},{7,5},{8,74},{9,11},... | collective-permute-start | bytes 1769480 | tf_op jit(solution)/shard_map/ppermute | solution.py:33
  73.2 21.8 %collective-permute-start.19 = (bf16[384,1024]{1,0:T(8,128)(2,1)S(1)}, bf16[384,1024]{1,0:T(8,128)(2,1)S(1)}, u32[]{:S(2)}, u32[]{:S(2)}) collective-permute-start(bf16[384,1024]{1,0:T(8,128)(2,1)S(1)} %get-tuple-element.73), channel_id=1, source_target_pairs={{0,1},{1,0},{2,3},{3,2},{4,5},{5,4},{6,7},{7,6},{8,9},{9,8},{10,11... | collective-permute-start | bytes 2359304 | tf_op jit(solution)/shard_map/ppermute | solution.py:63
  73.7 12.9 %collective-permute-start.24 = (bf16[3,96,1024]{2,1,0:T(8,128)(2,1)S(1)}, bf16[3,96,1024]{2,1,0:T(8,128)(2,1)S(1)}, u32[]{:S(2)}, u32[]{:S(2)}) collective-permute-start(bf16[3,96,1024]{2,1,0:T(8,128)(2,1)S(1)} %add_convert_fusion.5), channel_id=1, source_target_pairs={{0,48},{1,17},{2,50},{3,19},{4,52},{5,21},{6,54},{7,23},{8,56},{9,... | collective-permute-start | bytes 1769480 | tf_op jit(solution)/shard_map/ppermute | solution.py:33
  76.5 21.7 %collective-permute-start.23 = (bf16[384,1024]{1,0:T(8,128)(2,1)S(1)}, bf16[384,1024]{1,0:T(8,128)(2,1)S(1)}, u32[]{:S(2)}, u32[]{:S(2)}) collective-permute-start(bf16[384,1024]{1,0:T(8,128)(2,1)S(1)} %add_convert_fusion.1), channel_id=1, source_target_pairs={{0,4},{1,5},{2,6},{3,7},{4,0},{5,1},{6,2},{7,3},{8,12},{9,13},{10,... | collective-permute-start | bytes 2359304 | tf_op jit(solution)/shard_map/ppermute | solution.py:33
  81.9 8.2 %collective-permute-start.29 = (bf16[3,24,1024]{2,1,0:T(8,128)(2,1)S(1)}, bf16[3,24,1024]{2,1,0:T(8,128)(2,1)S(1)}, u32[]{:S(2)}, u32[]{:S(2)}) collective-permute-start(bf16[3,24,1024]{2,1,0:T(8,128)(2,1)S(1)} %get-tuple-element.89), channel_id=1, source_target_pairs={{0,16},{1,49},{2,18},{3,51},{4,20},{5,53},{6,22},{7,55},{8,24},{9,... | collective-permute-start | bytes 442376 | tf_op jit(solution)/shard_map/ppermute | solution.py:33
  82.0 8.2 %collective-permute-start.31 = (bf16[3,24,1024]{2,1,0:T(8,128)(2,1)S(1)}, bf16[3,24,1024]{2,1,0:T(8,128)(2,1)S(1)}, u32[]{:S(2)}, u32[]{:S(2)}) collective-permute-start(bf16[3,24,1024]{2,1,0:T(8,128)(2,1)S(1)} %get-tuple-element.90), channel_id=1, source_target_pairs={{0,18},{1,115},{2,16},{3,113},{4,22},{5,119},{6,20},{7,117},{8,26}... | collective-permute-start | bytes 442376 | tf_op jit(solution)/shard_map/ppermute | solution.py:59
  90.1 9.3 %collective-permute-start.25 = (bf16[3,24,1024]{2,1,0:T(8,128)(2,1)S(1)}, bf16[3,24,1024]{2,1,0:T(8,128)(2,1)S(1)}, u32[]{:S(2)}, u32[]{:S(2)}) collective-permute-start(bf16[3,24,1024]{2,1,0:T(8,128)(2,1)S(1)} %get-tuple-element.86), channel_id=1, source_target_pairs={{0,16},{1,49},{2,18},{3,51},{4,20},{5,53},{6,22},{7,55},{8,24},{9,... | collective-permute-start | bytes 442376 | tf_op jit(solution)/shard_map/ppermute | solution.py:33
  90.2 9.2 %collective-permute-start.27 = (bf16[3,24,1024]{2,1,0:T(8,128)(2,1)S(1)}, bf16[3,24,1024]{2,1,0:T(8,128)(2,1)S(1)}, u32[]{:S(2)}, u32[]{:S(2)}) collective-permute-start(bf16[3,24,1024]{2,1,0:T(8,128)(2,1)S(1)} %get-tuple-element.87), channel_id=1, source_target_pairs={{0,18},{1,115},{2,16},{3,113},{4,22},{5,119},{6,20},{7,117},{8,26}... | collective-permute-start | bytes 442376 | tf_op jit(solution)/shard_map/ppermute | solution.py:59
  (11 other events, 91.2 us)

commit v8 on v4

--- a/solution.py
+++ b/solution.py
@@ -49,14 +49,17 @@
     return swap(value, axis, lambda core: True)
 
 
-def swap_corner(value):
-    pairs = []
+def blocks_of_four():
+    groups = {}
     for device in range(DEVICES):
-        there = place(device)
-        for axis in (X, Y):
-            there[axis] = RING - 1 - there[axis] if there[3] == 1 else there[axis] ^ 1
-        pairs.append((device, index(*there)))
-    return lax.ppermute(value, AXES, pairs)
+        x, y, z, core = place(device)
+        key = z, core, (x + core) % RING // 2, (y + core) % RING // 2
+        groups.setdefault(key, []).append(device)
+    return list(groups.values())
+
+
+def trade(pieces):
+    return lax.all_to_all(pieces, AXES, 0, 0, axis_index_groups=blocks_of_four(), tiled=True)
 
 
 def swap_core(value):
@@ -72,14 +75,14 @@
 
 
 def gather_block(message):
-    return join(message, swap_first(message, Y), swap_first(message, X), swap_corner(message))
+    got = trade(jnp.broadcast_to(message[None], (4,) + message.shape))
+    return got.transpose(1, 0, 2, 3).reshape(message.shape[0], -1, message.shape[2])
 
 
 def reduce_block(block):
-    n = block.shape[1] // 4
-    own, along_y, along_x, corner = (block[:, i * n : (i + 1) * n] for i in range(4))
-    total = own.astype(F32) + swap_first(along_y, Y).astype(F32)
-    return total + swap_first(along_x, X).astype(F32) + swap_corner(corner).astype(F32)
+    mats, rows, width = block.shape
+    pieces = block.reshape(mats, 4, rows // 4, width).transpose(1, 0, 2, 3)
+    return jnp.sum(trade(pieces).astype(F32), axis=0)
 
 
 def halve(both, axis):

time: 103 us -> 130 us (1.26)
  waiting for transfers between devices: 24.5 us -> 41.7 us
  other arithmetic: 5.5 us -> 11.4 us
  local copies, waits for them, and re-layouts: 1.21 us -> 6.47 us
  starting transfers between devices: 48.1 us -> 45.5 us
    all_to_all x0 -> x4, starting transfers between devices: none -> 19.1 us  [trade(): lax.all_to_all(pieces, AXES, 0, 0, axis_index_groups=blocks_of_four(), ti...]
    ppermute x21 -> x13, starting transfers between devices: 40.2 us -> 22.4 us  [swap(): return lax.ppermute(value, AXES, pairs)]
    all_to_all x0 -> x4, waiting for transfers between devices: none -> 8.77 us  [trade(): lax.all_to_all(pieces, AXES, 0, 0, axis_index_groups=blocks_of_four(), ti...]
    ppermute x21 -> x13, waiting for transfers between devices: 23.2 us -> 30.7 us  [swap(): return lax.ppermute(value, AXES, pairs)]
    ppermute x4 -> x0, starting transfers between devices: 5.68 us -> none  [swap_corner(): return lax.ppermute(value, AXES, pairs)]
    broadcast_in_dim x0 -> x3, local copies, waits for them, and re-layouts: none -> 2.68 us  [the longest x2 1.8 us: gather_block(): got = trade(jnp.broadcast_to(message[None], (4,) + message.shape))]
    convert_element_type x1, other arithmetic: 0.25 us -> 2.36 us  [body(): z_part = swap_near((z_part + got[1].astype(F32)).astype(BF16), Z)]
    ppermute x5, starting transfers between devices: 2.24 us -> 4.1 us  [swap_core(): return lax.ppermute(value, AXES, [(d, d ^ 1) for d in range(DEVICES)])]
  transfers between devices with their start and end apart: 30 -> 22, of which waited for: 14 -> 11; matrix products, arithmetic and copies ran while one was open for 6% -> 11% of each run, Pallas kernels for 21% -> 17%
where the time goes in v8:
time: 130 us; the launch traced here: 128 us
  starting transfers between devices  45.5 us (35%)
  waiting for transfers between devices  41.7 us (32%)
  Pallas kernels  22.2 us (17%)
  other arithmetic  11.4 us (9%)
  local copies, waits for them, and re-layouts  6.47 us (5%)
    ppermute x13, waiting for transfers between devices, swap(): return lax.ppermute(value, AXES, pairs)  30.7 us
    ppermute x13, starting transfers between devices, swap(): return lax.ppermute(value, AXES, pairs)  22.4 us
    all_to_all x4, starting transfers between devices, trade(): lax.all_to_all(pieces, AXES, 0, 0, axis_index_groups=blocks_of_four(), ti...  19.1 us
    pallas_call x3, Pallas kernels, grads(): pl.pallas_call(kernel, out_shape=[jax.ShapeDtypeStruct(w.shape, BF16) for...  16 us
    all_to_all x4, waiting for transfers between devices, trade(): lax.all_to_all(pieces, AXES, 0, 0, axis_index_groups=blocks_of_four(), ti...  8.77 us
    pallas_call x1, Pallas kernels, input_parts(): pl.pallas_call(kernel, out_shape=[jax.ShapeDtypeStruct((group, width), F3...  6.21 us
    ppermute x5, starting transfers between devices, swap_core(): return lax.ppermute(value, AXES, [(d, d ^ 1) for d in range(DEVICES)])  4.1 us
  transfers between devices with their start and end apart: 22, of which 11 were waited for; matrix products, arithmetic and copies ran while one was open for 11% of the time, Pallas kernels for 17%

profile of v8, /device:TPU:2, one launch (start us, length us, event | category | flops | bytes accessed | tf_op | source)
XLA Modules:
  0.0 128.3 jit_solution(3479210562098067726)
XLA Ops:
  3.6 4.3 %all-to-all-start.1 = ((bf16[4,3,24,1024]{3,2,1,0:T(8,128)(2,1)}), bf16[4,3,24,1024]{3,2,1,0:T(8,128)(2,1)S(1)}, u32[]{:S(2)}, u32[]{:S(2)}) async-start(bf16[4,3,24,1024]{3,2,1,0:T(8,128)(2,1)} %broadcast_in_dim.8), calls=%async_computation.1 | async-start | bytes 1179648 | tf_op jit(solution)/shard_map/all_to_all | solution.py:62
  7.9 1.9 %collective-permute-start.2 = (bf16[384,1024]{1,0:T(8,128)(2,1)S(1)}, bf16[384,1024]{1,0:T(8,128)(2,1)S(1)}, u32[]{:S(2)}, u32[]{:S(2)}) collective-permute-start(bf16[384,1024]{1,0:T(8,128)(2,1)S(1)} %copy-done), channel_id=1, source_target_pairs={{0,4},{1,5},{2,6},{3,7},{4,0},{5,1},{6,2},{7,3},{8,12},{9,13},{10,... | collective-permute-start | bytes 2359304 | tf_op jit(solution)/shard_map/ppermute | solution.py:33
  9.8 2.5 %collective-permute-start.1 = (bf16[3,24,1024]{2,0,1:T(4,128)(2,1)S(1)}, bf16[3,24,1024]{2,0,1:T(4,128)(2,1)S(1)}, u32[]{:S(2)}, u32[]{:S(2)}) collective-permute-start(bf16[3,24,1024]{2,0,1:T(4,128)(2,1)S(1)} %pad_maximum_fusion.1), channel_id=1, source_target_pairs={{0,12},{1,13},{2,14},{3,15},{4,8},{5,9},{6,10},{7,11},{8,4},{9,5},... | collective-permute-start | bytes 442376 | tf_op jit(solution)/shard_map/ppermute | solution.py:33
  12.3 5.7 %collective-permute-done.1 = bf16[3,24,1024]{2,0,1:T(4,128)(2,1)S(1)} collective-permute-done((bf16[3,24,1024]{2,0,1:T(4,128)(2,1)S(1)}, bf16[3,24,1024]{2,0,1:T(4,128)(2,1)S(1)}, u32[]{:S(2)}, u32[]{:S(2)}) %collective-permute-start.1) | collective-permute-done | bytes 147488 | tf_op jit(solution)/shard_map/ppermute | solution.py:33
  19.0 3.5 %all-to-all-start = ((bf16[4,3,24,1024]{3,2,1,0:T(8,128)(2,1)}), bf16[4,3,24,1024]{3,2,1,0:T(8,128)(2,1)S(1)}, u32[]{:S(2)}, u32[]{:S(2)}) async-start(bf16[4,3,24,1024]{3,2,1,0:T(8,128)(2,1)} %broadcast_in_dim.7), calls=%async_computation | async-start | bytes 1179648 | tf_op jit(solution)/shard_map/all_to_all | solution.py:62
  23.3 3.7 %collective-permute-start.7 = (bf16[3,96,1024]{2,1,0:T(8,128)(2,1)}, bf16[3,96,1024]{2,1,0:T(8,128)(2,1)S(1)}, u32[]{:S(2)}, u32[]{:S(2)}) collective-permute-start(bf16[3,96,1024]{2,1,0:T(8,128)(2,1)} %bitcast.5), channel_id=1, source_target_pairs={{0,48},{1,17},{2,50},{3,19},{4,52},{5,21},{6,54},{7,23},{8,56},{9,... | collective-permute-start | bytes 1769480 | tf_op jit(solution)/shard_map/ppermute | solution.py:33
  28.9 2.9 %collective-permute-start.9 = (bf16[3,96,1024]{2,1,0:T(8,128)(2,1)S(1)}, bf16[3,96,1024]{2,1,0:T(8,128)(2,1)S(1)}, u32[]{:S(2)}, u32[]{:S(2)}) collective-permute-start(bf16[3,96,1024]{2,1,0:T(8,128)(2,1)S(1)} %bitcast.29), channel_id=1, source_target_pairs={{0,66},{1,3},{2,64},{3,1},{4,70},{5,7},{6,68},{7,5},{8,74},{9,11},... | collective-permute-start | bytes 1769480 | tf_op jit(solution)/shard_map/ppermute | solution.py:33
  31.8 3.6 %collective-permute-start = (bf16[384,1024]{1,0:T(8,128)(2,1)S(1)}, bf16[384,1024]{1,0:T(8,128)(2,1)S(1)}, u32[]{:S(2)}, u32[]{:S(2)}) collective-permute-start(bf16[384,1024]{1,0:T(8,128)(2,1)S(1)} %copy-done), channel_id=1, source_target_pairs={{0,1},{1,0},{2,3},{3,2},{4,5},{5,4},{6,7},{7,6},{8,9},{9,8},{10,11... | collective-permute-start | bytes 2359304 | tf_op jit(solution)/shard_map/ppermute | solution.py:66
  39.7 3.0 %collective-permute-start.10 = (bf16[3,192,1024]{2,1,0:T(8,128)(2,1)S(1)}, bf16[3,192,1024]{2,1,0:T(8,128)(2,1)S(1)}, u32[]{:S(2)}, u32[]{:S(2)}) collective-permute-start(bf16[3,192,1024]{2,1,0:T(8,128)(2,1)S(1)} %constant_dynamic-update-slice_fusion.refs_9_.refs_6_), channel_id=1, source_target_pairs={{0,48},{1,17},{2,50},{3,19},{4,52},{5,21},{6,54},{7,23},{8,56},{9,... | collective-permute-start | bytes 3538952 | tf_op jit(solution)/shard_map/ppermute | solution.py:33
  43.3 11.6 %collective-permute-done.5.refs_6_ = bf16[384,1024]{1,0:T(8,128)(2,1)S(1)} collective-permute-done((bf16[384,1024]{1,0:T(8,128)(2,1)S(1)}, bf16[384,1024]{1,0:T(8,128)(2,1)S(1)}, u32[]{:S(2)}, u32[]{:S(2)}) %collective-permute-start.5) | collective-permute-done | bytes 786464 | tf_op jit(solution)/shard_map/ppermute | solution.py:33
  54.8 2.3 %collective-permute-done.6.refs_7_ = bf16[384,1024]{1,0:T(8,128)(2,1)S(1)} collective-permute-done((bf16[384,1024]{1,0:T(8,128)(2,1)S(1)}, bf16[384,1024]{1,0:T(8,128)(2,1)S(1)}, u32[]{:S(2)}, u32[]{:S(2)}) %collective-permute-start.6) | collective-permute-done | bytes 786464 | tf_op jit(solution)/shard_map/ppermute | solution.py:66
  57.1 4.2 %shard_map.59 = (bf16[3,192,1024]{2,1,0:T(8,128)(2,1)S(1)}, bf16[384,1536]{1,0:T(8,128)(2,1)S(1)}) custom-call(bf16[384,1024]{1,0:T(8,128)(2,1)S(1)} %copy-done, bf16[384,1024]{1,0:T(8,128)(2,1)S(1)} %collective-permute-done.refs_1_, bf16[384,1024]{1,0:T(8,128)(2,1)S(1)} %collective-permute-done.2.refs_2_, ...), custom_call_target="tpu_custom_call" | custom-call | flops 1024 | bytes 1024 | tf_op jit(solution)/shard_map/pallas_call | solution.py:148
  61.3 2.0 %collective-permute-start.12 = (bf16[3,192,1024]{2,1,0:T(8,128)(2,1)S(1)}, bf16[3,192,1024]{2,1,0:T(8,128)(2,1)S(1)}, u32[]{:S(2)}, u32[]{:S(2)}) collective-permute-start(bf16[3,192,1024]{2,1,0:T(8,128)(2,1)S(1)} %get-tuple-element.35), channel_id=1, source_target_pairs={{0,66},{1,3},{2,64},{3,1},{4,70},{5,7},{6,68},{7,5},{8,74},{9,11},... | collective-permute-start | bytes 3538952 | tf_op jit(solution)/shard_map/ppermute | solution.py:33
  63.3 4.2 %shard_map.60 = (bf16[3,192,1024]{2,1,0:T(8,128)(2,1)S(1)}, bf16[384,1536]{1,0:T(8,128)(2,1)S(1)}) custom-call(bf16[384,1024]{1,0:T(8,128)(2,1)S(1)} %copy-done, bf16[384,1024]{1,0:T(8,128)(2,1)S(1)} %collective-permute-done.refs_1_, bf16[384,1024]{1,0:T(8,128)(2,1)S(1)} %collective-permute-done.2.refs_2_, ...), custom_call_target="tpu_custom_call" | custom-call | flops 1024 | bytes 1024 | tf_op jit(solution)/shard_map/pallas_call | solution.py:148
  67.8 7.7 %shard_map.61 = (bf16[3,192,1024]{2,1,0:T(8,128)(2,1)S(1)}, bf16[3,192,1024]{2,1,0:T(8,128)(2,1)S(1)}, bf16[768,1536]{1,0:T(8,128)(2,1)S(1)}) custom-call(bf16[384,1024]{1,0:T(8,128)(2,1)S(1)} %copy-done, bf16[384,1024]{1,0:T(8,128)(2,1)S(1)} %collective-permute-done.refs_1_, bf16[384,1024]{1,0:T(8,128)(2,1)S(1)} %collective-permute-done.2.refs_2_, ...), custom_call_target="tpu_custom_call" | custom-call | flops 1024 | bytes 1024 | tf_op jit(solution)/shard_map/pallas_call | solution.py:148
  75.5 6.2 %shard_map.62 = (f32[384,1024]{1,0:T(8,128)S(1)}, f32[384,1024]{1,0:T(8,128)S(1)}, bf16[2,384,1024]{2,1,0:T(8,128)(2,1)}) custom-call(bf16[384,1536]{1,0:T(8,128)(2,1)S(1)} %get-tuple-element.25.refs_0_, bf16[384,1536]{1,0:T(8,128)(2,1)S(1)} %get-tuple-element.28.refs_1_, bf16[768,1536]{1,0:T(8,128)(2,1)S(1)} %get-tuple-element.31.refs_2_, ...), custom_call_target="tpu_custom_call" | custom-call | flops 1024 | bytes 1024 | tf_op jit(solution)/shard_map/pallas_call | solution.py:187
  82.2 3.0 %collective-permute-done.13 = bf16[3,192,1024]{2,1,0:T(8,128)(2,1)S(1)} collective-permute-done((bf16[3,192,1024]{2,1,0:T(8,128)(2,1)S(1)}, bf16[3,192,1024]{2,1,0:T(8,128)(2,1)S(1)}, u32[]{:S(2)}, u32[]{:S(2)}) %collective-permute-start.13) | collective-permute-done | bytes 1179680 | tf_op jit(solution)/shard_map/ppermute | solution.py:33
  87.8 7.9 %collective-permute-done.14 = bf16[3,96,1024]{2,1,0:T(8,128)(2,1)S(1)} collective-permute-done((bf16[3,96,1024]{2,1,0:T(8,128)(2,1)S(1)}, bf16[3,96,1024]{2,1,0:T(8,128)(2,1)S(1)}, u32[]{:S(2)}, u32[]{:S(2)}) %collective-permute-start.14) | collective-permute-done | bytes 589856 | tf_op jit(solution)/shard_map/ppermute | solution.py:33
  96.8 7.3 %all-to-all-start.2 = ((bf16[4,3,24,1024]{3,2,1,0:T(8,128)(2,1)}), bf16[4,3,24,1024]{3,2,1,0:T(8,128)(2,1)}, u32[]{:S(2)}, u32[]{:S(2)}) async-start(bf16[4,3,24,1024]{3,2,1,0:T(8,128)(2,1)} %bitcast.31), calls=%async_computation.2 | async-start | bytes 1179648 | tf_op jit(solution)/shard_map/all_to_all | solution.py:62
  104.1 2.4 %fusion = bf16[384,1024]{1,0:T(8,128)(2,1)} fusion(f32[384,1024]{1,0:T(8,128)S(1)} %get-tuple-element.40, bf16[2,384,1024]{2,1,0:T(8,128)(2,1)} %collective-permute-done.11), kind=kLoop, calls=%fused_computation.3 | loop fusion | flops 1179648 | bytes 3145728 | tf_op jit(solution)/shard_map/convert_element_type | solution.py:229
  110.6 4.0 %all-to-all-start.3 = ((bf16[4,3,24,1024]{3,2,1,0:T(8,128)(2,1)}), bf16[4,3,24,1024]{3,2,1,0:T(8,128)(2,1)S(1)}, u32[]{:S(2)}, u32[]{:S(2)}) async-start(bf16[4,3,24,1024]{3,2,1,0:T(8,128)(2,1)} %bitcast.24), calls=%async_computation.3 | async-start | bytes 1179648 | tf_op jit(solution)/shard_map/all_to_all | solution.py:62
  115.8 5.2 %all-to-all-done.3 = bf16[4,3,24,1024]{3,2,1,0:T(8,128)(2,1)S(1)} async-done(((bf16[4,3,24,1024]{3,2,1,0:T(8,128)(2,1)}), bf16[4,3,24,1024]{3,2,1,0:T(8,128)(2,1)S(1)}, u32[]{:S(2)}, u32[]{:S(2)}) %all-to-all-start.3) | async-done | bytes 589856 | tf_op jit(solution)/shard_map/all_to_all | solution.py:62
  121.1 2.6 %collective-permute-start.17 = (bf16[3,24,1024]{2,1,0:T(8,128)(2,1)S(1)}, bf16[3,24,1024]{2,1,0:T(8,128)(2,1)S(1)}, u32[]{:S(2)}, u32[]{:S(2)}) collective-permute-start(bf16[3,24,1024]{2,1,0:T(8,128)(2,1)S(1)} %reduce_sum.21), channel_id=1, source_target_pairs={{0,12},{1,13},{2,14},{3,15},{4,8},{5,9},{6,10},{7,11},{8,4},{9,5},... | collective-permute-start | bytes 442376 | tf_op jit(solution)/shard_map/ppermute | solution.py:33
  123.7 2.4 %fusion.2 = bf16[384,1024]{1,0:T(8,128)(2,1)} fusion(f32[384,1024]{1,0:T(8,128)S(1)} %get-tuple-element.32, bf16[384,1024]{1,0:T(8,128)(2,1)S(1)} %collective-permute-done.15, bf16[2,384,1024]{2,1,0:T(8,128)(2,1)} %collective-permute-done.11), kind=kLoop, calls=%fused_computation.6 | loop fusion | flops 1966080 | bytes 3932160 | tf_op jit(solution)/shard_map/convert_element_type | solution.py:233
  (56 shorter events, 23.5 us)
Async XLA Ops:
  2.6 5.3 %copy-start = (bf16[384,1024]{1,0:T(8,128)(2,1)S(1)}, bf16[384,1024]{1,0:T(8,128)(2,1)}, u32[]{:S(2)}) copy-start(bf16[384,1024]{1,0:T(8,128)(2,1)} %refs_0_.5) | copy-start | bytes 2359300
  3.6 14.5 %all-to-all-start.1 = ((bf16[4,3,24,1024]{3,2,1,0:T(8,128)(2,1)}), bf16[4,3,24,1024]{3,2,1,0:T(8,128)(2,1)S(1)}, u32[]{:S(2)}, u32[]{:S(2)}) async-start(bf16[4,3,24,1024]{3,2,1,0:T(8,128)(2,1)} %broadcast_in_dim.8), calls=%async_computation.1 | async-start | bytes 1179648 | tf_op jit(solution)/shard_map/all_to_all | solution.py:62
  7.9 21.0 %collective-permute-start.2 = (bf16[384,1024]{1,0:T(8,128)(2,1)S(1)}, bf16[384,1024]{1,0:T(8,128)(2,1)S(1)}, u32[]{:S(2)}, u32[]{:S(2)}) collective-permute-start(bf16[384,1024]{1,0:T(8,128)(2,1)S(1)} %copy-done), channel_id=1, source_target_pairs={{0,4},{1,5},{2,6},{3,7},{4,0},{5,1},{6,2},{7,3},{8,12},{9,13},{10,... | collective-permute-start | bytes 2359304 | tf_op jit(solution)/shard_map/ppermute | solution.py:33
  9.8 8.2 %collective-permute-start.1 = (bf16[3,24,1024]{2,0,1:T(4,128)(2,1)S(1)}, bf16[3,24,1024]{2,0,1:T(4,128)(2,1)S(1)}, u32[]{:S(2)}, u32[]{:S(2)}) collective-permute-start(bf16[3,24,1024]{2,0,1:T(4,128)(2,1)S(1)} %pad_maximum_fusion.1), channel_id=1, source_target_pairs={{0,12},{1,13},{2,14},{3,15},{4,8},{5,9},{6,10},{7,11},{8,4},{9,5},... | collective-permute-start | bytes 442376 | tf_op jit(solution)/shard_map/ppermute | solution.py:33
  19.0 9.8 %all-to-all-start = ((bf16[4,3,24,1024]{3,2,1,0:T(8,128)(2,1)}), bf16[4,3,24,1024]{3,2,1,0:T(8,128)(2,1)S(1)}, u32[]{:S(2)}, u32[]{:S(2)}) async-start(bf16[4,3,24,1024]{3,2,1,0:T(8,128)(2,1)} %broadcast_in_dim.7), calls=%async_computation | async-start | bytes 1179648 | tf_op jit(solution)/shard_map/all_to_all | solution.py:62
  22.5 12.9 %copy-start.1 = (bf16[384,1024]{1,0:T(8,128)(2,1)S(1)}, bf16[384,1024]{1,0:T(8,128)(2,1)}, u32[]{:S(2)}) copy-start(bf16[384,1024]{1,0:T(8,128)(2,1)} %refs_4_.5) | copy-start | bytes 2359300
  23.3 13.4 %collective-permute-start.7 = (bf16[3,96,1024]{2,1,0:T(8,128)(2,1)}, bf16[3,96,1024]{2,1,0:T(8,128)(2,1)S(1)}, u32[]{:S(2)}, u32[]{:S(2)}) collective-permute-start(bf16[3,96,1024]{2,1,0:T(8,128)(2,1)} %bitcast.5), channel_id=1, source_target_pairs={{0,48},{1,17},{2,50},{3,19},{4,52},{5,21},{6,54},{7,23},{8,56},{9,... | collective-permute-start | bytes 1769480 | tf_op jit(solution)/shard_map/ppermute | solution.py:33
  28.9 10.8 %collective-permute-start.9 = (bf16[3,96,1024]{2,1,0:T(8,128)(2,1)S(1)}, bf16[3,96,1024]{2,1,0:T(8,128)(2,1)S(1)}, u32[]{:S(2)}, u32[]{:S(2)}) collective-permute-start(bf16[3,96,1024]{2,1,0:T(8,128)(2,1)S(1)} %bitcast.29), channel_id=1, source_target_pairs={{0,66},{1,3},{2,64},{3,1},{4,70},{5,7},{6,68},{7,5},{8,74},{9,11},... | collective-permute-start | bytes 1769480 | tf_op jit(solution)/shard_map/ppermute | solution.py:33
  31.8 11.4 %collective-permute-start = (bf16[384,1024]{1,0:T(8,128)(2,1)S(1)}, bf16[384,1024]{1,0:T(8,128)(2,1)S(1)}, u32[]{:S(2)}, u32[]{:S(2)}) collective-permute-start(bf16[384,1024]{1,0:T(8,128)(2,1)S(1)} %copy-done), channel_id=1, source_target_pairs={{0,1},{1,0},{2,3},{3,2},{4,5},{5,4},{6,7},{7,6},{8,9},{9,8},{10,11... | collective-permute-start | bytes 2359304 | tf_op jit(solution)/shard_map/ppermute | solution.py:66
  35.4 19.4 %collective-permute-start.5 = (bf16[384,1024]{1,0:T(8,128)(2,1)S(1)}, bf16[384,1024]{1,0:T(8,128)(2,1)S(1)}, u32[]{:S(2)}, u32[]{:S(2)}) collective-permute-start(bf16[384,1024]{1,0:T(8,128)(2,1)S(1)} %copy-done.1), channel_id=1, source_target_pairs={{0,4},{1,5},{2,6},{3,7},{4,0},{5,1},{6,2},{7,3},{8,12},{9,13},{10,... | collective-permute-start | bytes 2359304 | tf_op jit(solution)/shard_map/ppermute | solution.py:33
  37.9 17.0 %collective-permute-start.8 = (bf16[3,192,1024]{2,1,0:T(8,128)(2,1)S(1)}, bf16[3,192,1024]{2,1,0:T(8,128)(2,1)S(1)}, u32[]{:S(2)}, u32[]{:S(2)}) collective-permute-start(bf16[3,192,1024]{2,1,0:T(8,128)(2,1)S(1)} %pad_maximum_fusion.refs_8_.refs_5_), channel_id=1, source_target_pairs={{0,66},{1,3},{2,64},{3,1},{4,70},{5,7},{6,68},{7,5},{8,74},{9,11},... | collective-permute-start | bytes 3538952 | tf_op jit(solution)/shard_map/ppermute | solution.py:33
  39.7 23.6 %collective-permute-start.10 = (bf16[3,192,1024]{2,1,0:T(8,128)(2,1)S(1)}, bf16[3,192,1024]{2,1,0:T(8,128)(2,1)S(1)}, u32[]{:S(2)}, u32[]{:S(2)}) collective-permute-start(bf16[3,192,1024]{2,1,0:T(8,128)(2,1)S(1)} %constant_dynamic-update-slice_fusion.refs_9_.refs_6_), channel_id=1, source_target_pairs={{0,48},{1,17},{2,50},{3,19},{4,52},{5,21},{6,54},{7,23},{8,56},{9,... | collective-permute-start | bytes 3538952 | tf_op jit(solution)/shard_map/ppermute | solution.py:33
  42.7 12.1 %collective-permute-start.4 = (bf16[384,1024]{1,0:T(8,128)(2,1)S(1)}, bf16[384,1024]{1,0:T(8,128)(2,1)S(1)}, u32[]{:S(2)}, u32[]{:S(2)}) collective-permute-start(bf16[384,1024]{1,0:T(8,128)(2,1)S(1)} %copy-done.1), channel_id=1, source_target_pairs={{0,1},{1,0},{2,3},{3,2},{4,5},{5,4},{6,7},{7,6},{8,9},{9,8},{10,11... | collective-permute-start | bytes 2359304 | tf_op jit(solution)/shard_map/ppermute | solution.py:66
  43.2 11.7 %collective-permute-start.3 = (bf16[384,1024]{1,0:T(8,128)(2,1)S(1)}, bf16[384,1024]{1,0:T(8,128)(2,1)S(1)}, u32[]{:S(2)}, u32[]{:S(2)}) collective-permute-start(bf16[384,1024]{1,0:T(8,128)(2,1)S(1)} %collective-permute-done.2.refs_2_), channel_id=1, source_target_pairs={{0,1},{1,0},{2,3},{3,2},{4,5},{5,4},{6,7},{7,6},{8,9},{9,8},{10,11... | collective-permute-start | bytes 2359304 | tf_op jit(solution)/shard_map/ppermute | solution.py:66
  54.8 2.3 %collective-permute-start.6 = (bf16[384,1024]{1,0:T(8,128)(2,1)S(1)}, bf16[384,1024]{1,0:T(8,128)(2,1)S(1)}, u32[]{:S(2)}, u32[]{:S(2)}) collective-permute-start(bf16[384,1024]{1,0:T(8,128)(2,1)S(1)} %collective-permute-done.5.refs_6_), channel_id=1, source_target_pairs={{0,1},{1,0},{2,3},{3,2},{4,5},{5,4},{6,7},{7,6},{8,9},{9,8},{10,11... | collective-permute-start | bytes 2359304 | tf_op jit(solution)/shard_map/ppermute | solution.py:66
  61.3 20.4 %collective-permute-start.12 = (bf16[3,192,1024]{2,1,0:T(8,128)(2,1)S(1)}, bf16[3,192,1024]{2,1,0:T(8,128)(2,1)S(1)}, u32[]{:S(2)}, u32[]{:S(2)}) collective-permute-start(bf16[3,192,1024]{2,1,0:T(8,128)(2,1)S(1)} %get-tuple-element.35), channel_id=1, source_target_pairs={{0,66},{1,3},{2,64},{3,1},{4,70},{5,7},{6,68},{7,5},{8,74},{9,11},... | collective-permute-start | bytes 3538952 | tf_op jit(solution)/shard_map/ppermute | solution.py:33
  67.5 17.7 %collective-permute-start.13 = (bf16[3,192,1024]{2,1,0:T(8,128)(2,1)S(1)}, bf16[3,192,1024]{2,1,0:T(8,128)(2,1)S(1)}, u32[]{:S(2)}, u32[]{:S(2)}) collective-permute-start(bf16[3,192,1024]{2,1,0:T(8,128)(2,1)S(1)} %get-tuple-element.37), channel_id=1, source_target_pairs={{0,48},{1,17},{2,50},{3,19},{4,52},{5,21},{6,54},{7,23},{8,56},{9,... | collective-permute-start | bytes 3538952 | tf_op jit(solution)/shard_map/ppermute | solution.py:33
  81.7 22.4 %collective-permute-start.11 = (bf16[2,384,1024]{2,1,0:T(8,128)(2,1)}, bf16[2,384,1024]{2,1,0:T(8,128)(2,1)}, u32[]{:S(2)}, u32[]{:S(2)}) collective-permute-start(bf16[2,384,1024]{2,1,0:T(8,128)(2,1)} %get-tuple-element.33), channel_id=1, source_target_pairs={{0,1},{1,0},{2,3},{3,2},{4,5},{5,4},{6,7},{7,6},{8,9},{9,8},{10,11... | collective-permute-start | bytes 4718600 | tf_op jit(solution)/shard_map/ppermute | solution.py:66
  85.7 10.0 %collective-permute-start.14 = (bf16[3,96,1024]{2,1,0:T(8,128)(2,1)S(1)}, bf16[3,96,1024]{2,1,0:T(8,128)(2,1)S(1)}, u32[]{:S(2)}, u32[]{:S(2)}) collective-permute-start(bf16[3,96,1024]{2,1,0:T(8,128)(2,1)S(1)} %slice.20), channel_id=1, source_target_pairs={{0,66},{1,3},{2,64},{3,1},{4,70},{5,7},{6,68},{7,5},{8,74},{9,11},... | collective-permute-start | bytes 1769480 | tf_op jit(solution)/shard_map/ppermute | solution.py:33
  86.7 19.9 %collective-permute-start.16 = (bf16[3,96,1024]{2,1,0:T(8,128)(2,1)}, bf16[3,96,1024]{2,1,0:T(8,128)(2,1)}, u32[]{:S(2)}, u32[]{:S(2)}) collective-permute-start(bf16[3,96,1024]{2,1,0:T(8,128)(2,1)} %slice.23), channel_id=1, source_target_pairs={{0,48},{1,17},{2,50},{3,19},{4,52},{5,21},{6,54},{7,23},{8,56},{9,... | collective-permute-start | bytes 1769480 | tf_op jit(solution)/shard_map/ppermute | solution.py:33
  96.8 13.7 %all-to-all-start.2 = ((bf16[4,3,24,1024]{3,2,1,0:T(8,128)(2,1)}), bf16[4,3,24,1024]{3,2,1,0:T(8,128)(2,1)}, u32[]{:S(2)}, u32[]{:S(2)}) async-start(bf16[4,3,24,1024]{3,2,1,0:T(8,128)(2,1)} %bitcast.31), calls=%async_computation.2 | async-start | bytes 1179648 | tf_op jit(solution)/shard_map/all_to_all | solution.py:62
  106.4 14.6 %collective-permute-start.15 = (bf16[384,1024]{1,0:T(8,128)(2,1)}, bf16[384,1024]{1,0:T(8,128)(2,1)S(1)}, u32[]{:S(2)}, u32[]{:S(2)}) collective-permute-start(bf16[384,1024]{1,0:T(8,128)(2,1)} %fusion), channel_id=1, source_target_pairs={{0,4},{1,5},{2,6},{3,7},{4,0},{5,1},{6,2},{7,3},{8,12},{9,13},{10,... | collective-permute-start | bytes 2359304 | tf_op jit(solution)/shard_map/ppermute | solution.py:33
  110.6 10.4 %all-to-all-start.3 = ((bf16[4,3,24,1024]{3,2,1,0:T(8,128)(2,1)}), bf16[4,3,24,1024]{3,2,1,0:T(8,128)(2,1)S(1)}, u32[]{:S(2)}, u32[]{:S(2)}) async-start(bf16[4,3,24,1024]{3,2,1,0:T(8,128)(2,1)} %bitcast.24), calls=%async_computation.3 | async-start | bytes 1179648 | tf_op jit(solution)/shard_map/all_to_all | solution.py:62
  121.1 6.4 %collective-permute-start.17 = (bf16[3,24,1024]{2,1,0:T(8,128)(2,1)S(1)}, bf16[3,24,1024]{2,1,0:T(8,128)(2,1)S(1)}, u32[]{:S(2)}, u32[]{:S(2)}) collective-permute-start(bf16[3,24,1024]{2,1,0:T(8,128)(2,1)S(1)} %reduce_sum.21), channel_id=1, source_target_pairs={{0,12},{1,13},{2,14},{3,15},{4,8},{5,9},{6,10},{7,11},{8,4},{9,5},... | collective-permute-start | bytes 442376 | tf_op jit(solution)/shard_map/ppermute | solution.py:33
  (2 other events, 6.3 us)

commit v9 on v7

--- a/solution.py
+++ b/solution.py
@@ -78,8 +78,11 @@
 def reduce_block(block):
     n = block.shape[1] // 4
     own, along_y, along_x, corner = (block[:, i * n : (i + 1) * n] for i in range(4))
-    total = own.astype(F32) + swap_first(along_y, Y).astype(F32)
-    return total + swap_first(along_x, X).astype(F32) + swap_corner(corner).astype(F32)
+    return own, swap_first(along_y, Y), swap_first(along_x, X), swap_corner(corner)
+
+
+def added(terms):
+    return sum(term.astype(F32) for term in terms)
 
 
 def rows_of(refs, start, stop, cols=slice(None)):
@@ -195,36 +198,35 @@
     x_z = swap_near(activations, Z)
     message = jnp.concatenate([gate_up.transpose(1, 0, 2), down_proj[None]], axis=0)
     message = lax.optimization_barrier(message)
-    other = swap_wrap(message, Z)
-    block1 = gather_block(other)
-    o0, _ = lax.optimization_barrier((gather_block(message), other))
+    block1 = gather_block(swap_wrap(message, Z))
+    o0 = gather_block(message)
     block1, c_own = lax.optimization_barrier((block1, cotangent))
     c_z = swap_near(c_own, Z)
     o1, x_z = lax.optimization_barrier((block1, x_z))
-    n0, w0 = swap_second(o0, Y), swap_second(o0, X)
+    n0 = swap_second(o0, Y)
+    r0 = swap_second(join(o0, n0), X)
     n1 = swap_second(o1, X)
     w1 = swap_second(o1, Y)
-    f0, f1 = swap_second(n0, X), swap_second(n1, Y)
+    f1 = swap_second(n1, Y)
     xs, cs = [activations, swap_core(activations)], [cotangent, swap_core(cotangent)]
 
     near = [n1, o1, n0, o0]
     *g_near, a_near = grads(xs, cs, near, weight=3)
-    x_z, c_z, a_near = lax.optimization_barrier((x_z, c_z, a_near))
+    x_z, c_z, a_near, w1 = lax.optimization_barrier((x_z, c_z, a_near, w1))
     xs_z, cs_z = [x_z, swap_core(x_z)], [c_z, swap_core(c_z)]
-    f0, w1 = lax.optimization_barrier((f0, w1))
-    g_r0, a_r0 = grads(xs, cs, [w0, f0], joined=2, weight=0)
-    f1, a_r0 = lax.optimization_barrier((f1, a_r0))
-    g_r1, a_r1 = grads(xs, cs, [w1, f1], joined=2, weight=3)
+    f1, a_near = lax.optimization_barrier((f1, a_near))
+    g_r1, a_r1 = grads(xs, cs, [w1, f1], joined=2, weight=6)
 
     g_r1, a_r1_z = grads(xs_z, cs_z, [w1, f1], [g_r1], joined=2)
     back1 = swap_second(g_r1, Y)
-    f0, a_r1_z = lax.optimization_barrier((f0, a_r1_z))
-    g_r0, a_r0_z = grads(xs_z, cs_z, [w0, f0], [g_r0], joined=2)
+    r0, a_r1_z = lax.optimization_barrier((r0, a_r1_z))
+    g_r0, a_r0 = grads(xs + xs_z, cs + cs_z, [r0])
     back0 = swap_second(g_r0, X)
-    n1, a_r0_z = lax.optimization_barrier((n1, a_r0_z))
+    n1, a_r0 = lax.optimization_barrier((n1, a_r0))
     g_n1, g_o1, g_n0, g_o0, a_near_z = grads(xs_z, cs_z, [n1, o1, n0, o0], g_near)
-    parts = [a_r1, a_r0, a_near, a_r1_z, a_r0_z, a_near_z]
-    own, pair, z_part, z_pair = input_parts(parts, [w1, f1, w0, f0] + near)
+    n = a_r0.shape[1] // 2
+    parts = [a_r1, a_r0[:, :n], a_near, a_r1_z, a_r0[:, n:], a_near_z]
+    own, pair, z_part, z_pair = input_parts(parts, [w1, f1, r0] + near)
     z_got, got = swap_core(z_pair), swap_core(pair)
 
     n = g_n1.shape[1]
@@ -238,8 +240,9 @@
     def block_sum(own, back, near):
         return (own.astype(F32) + back.astype(F32) + near.astype(F32)).astype(BF16)
 
-    total1 = reduce_block(block_sum(g_o1, back1[:, :n], near1)).astype(BF16)
-    total0 = reduce_block(block_sum(g_o0, back0[:, :n], near0))
+    terms1 = reduce_block(block_sum(g_o1, back1[:, :n], near1))
+    total1 = added(terms1).astype(BF16)
+    total0 = added(reduce_block(block_sum(g_o0, back0[:, :n], near0)))
     grad_input = (mine + z_part.astype(F32)).astype(BF16)
     total = total0 + swap_wrap(total1, Z).astype(F32)
     return (grad_input, total.transpose(1, 0, 2))

time: 104 us -> 103 us (level); the launches traced: 102 us -> 102 us
  starting transfers between devices: 44.6 us -> 51.4 us
  waiting for transfers between devices: 29.4 us -> 22.9 us
    ppermute x23 -> x22, waiting for transfers between devices: 28.9 us -> 22.3 us  [swap(): return lax.ppermute(value, AXES, pairs)]
    ppermute x23 -> x22, starting transfers between devices: 33.5 us -> 39.8 us  [swap(): return lax.ppermute(value, AXES, pairs)]
    ppermute x6, starting transfers between devices: 0.6 us -> 2.4 us  [swap_core(): return lax.ppermute(value, AXES, [(d, d ^ 1) for d in range(DEVICES)])]
    ppermute x4, starting transfers between devices: 10.5 us -> 9.12 us  [swap_corner(): return lax.ppermute(value, AXES, pairs)]
    pallas_call x6 -> x5, Pallas kernels: 17 us -> 16.7 us  [grads(): pl.pallas_call(kernel, out_shape=[jax.ShapeDtypeStruct((3, joined * units...]
  transfers between devices with their start and end apart: 33 -> 32, of which waited for: 15 -> 15; matrix products, arithmetic and copies ran while one was open for 4% -> 5% of each run, Pallas kernels for 19% -> 21%
where the time goes in v9:
time: 103 us; the launch traced here: 102 us
  starting transfers between devices  51.4 us (50%)
  waiting for transfers between devices  22.9 us (22%)
  Pallas kernels  21.8 us (21%)
  other arithmetic  4.34 us (4%)
  local copies, waits for them, and re-layouts  1.14 us (1%)
    ppermute x22, starting transfers between devices, swap(): return lax.ppermute(value, AXES, pairs)  39.8 us
    ppermute x22, waiting for transfers between devices, swap(): return lax.ppermute(value, AXES, pairs)  22.3 us
    pallas_call x5, Pallas kernels, grads(): pl.pallas_call(kernel, out_shape=[jax.ShapeDtypeStruct((3, joined * units...  16.7 us
    ppermute x4, starting transfers between devices, swap_corner(): return lax.ppermute(value, AXES, pairs)  9.12 us
    pallas_call x1, Pallas kernels, input_parts(): pl.pallas_call(kernel, out_shape=[jax.ShapeDtypeStruct((group, width), ki...  5.06 us
    ppermute x6, starting transfers between devices, swap_core(): return lax.ppermute(value, AXES, [(d, d ^ 1) for d in range(DEVICES)])  2.4 us
  transfers between devices with their start and end apart: 32, of which 15 were waited for; matrix products, arithmetic and copies ran while one was open for 5% of the time, Pallas kernels for 21%

profile of v9, /device:TPU:2, one launch (start us, length us, event | category | flops | bytes accessed | tf_op | source)
XLA Modules:
  0.0 102.4 jit_solution(1241388945358462999)
XLA Ops:
  0.6 2.0 %collective-permute-start.6 = (bf16[384,1024]{1,0:T(8,128)(2,1)}, bf16[384,1024]{1,0:T(8,128)(2,1)S(1)}, u32[]{:S(2)}, u32[]{:S(2)}) collective-permute-start(bf16[384,1024]{1,0:T(8,128)(2,1)} %refs_0_.5), channel_id=1, source_target_pairs={{0,4},{1,5},{2,6},{3,7},{4,0},{5,1},{6,2},{7,3},{8,12},{9,13},{10,... | collective-permute-start | bytes 2359304 | tf_op jit(solution)/shard_map/ppermute | solution.py:33
  4.4 2.6 %collective-permute-start.2 = (bf16[3,24,1024]{2,1,0:T(8,128)(2,1)S(1)}, bf16[3,24,1024]{2,1,0:T(8,128)(2,1)S(1)}, u32[]{:S(2)}, u32[]{:S(2)}) collective-permute-start(bf16[3,24,1024]{2,1,0:T(8,128)(2,1)S(1)} %pad_maximum_fusion.2), channel_id=1, source_target_pairs={{0,12},{1,13},{2,14},{3,15},{4,8},{5,9},{6,10},{7,11},{8,4},{9,5},... | collective-permute-start | bytes 442376 | tf_op jit(solution)/shard_map/ppermute | solution.py:33
  15.3 3.0 %collective-permute-start.12 = (bf16[3,96,1024]{2,1,0:T(8,128)(2,1)S(1)}, bf16[3,96,1024]{2,1,0:T(8,128)(2,1)S(1)}, u32[]{:S(2)}, u32[]{:S(2)}) collective-permute-start(bf16[3,96,1024]{2,1,0:T(8,128)(2,1)S(1)} %pad_maximum_fusion.1.refs_7_.refs_12_), channel_id=1, source_target_pairs={{0,48},{1,17},{2,50},{3,19},{4,52},{5,21},{6,54},{7,23},{8,56},{9,... | collective-permute-start | bytes 1769480 | tf_op jit(solution)/shard_map/ppermute | solution.py:33
  23.7 2.8 %collective-permute-done.12.refs_6_.refs_11_ = bf16[3,96,1024]{2,1,0:T(8,128)(2,1)S(1)} collective-permute-done((bf16[3,96,1024]{2,1,0:T(8,128)(2,1)S(1)}, bf16[3,96,1024]{2,1,0:T(8,128)(2,1)S(1)}, u32[]{:S(2)}, u32[]{:S(2)}) %collective-permute-start.12) | collective-permute-done | bytes 589856 | tf_op jit(solution)/shard_map/ppermute | solution.py:33
  26.4 3.0 %collective-permute-start.13 = (bf16[3,96,1024]{2,1,0:T(8,128)(2,1)S(1)}, bf16[3,96,1024]{2,1,0:T(8,128)(2,1)S(1)}, u32[]{:S(2)}, u32[]{:S(2)}) collective-permute-start(bf16[3,96,1024]{2,1,0:T(8,128)(2,1)S(1)} %pad_maximum_fusion.refs_5_.refs_10_), channel_id=1, source_target_pairs={{0,48},{1,17},{2,50},{3,19},{4,52},{5,21},{6,54},{7,23},{8,56},{9,... | collective-permute-start | bytes 1769480 | tf_op jit(solution)/shard_map/ppermute | solution.py:33
  30.3 3.4 %collective-permute-start.14 = (bf16[3,96,1024]{2,1,0:T(8,128)(2,1)S(1)}, bf16[3,96,1024]{2,1,0:T(8,128)(2,1)S(1)}, u32[]{:S(2)}, u32[]{:S(2)}) collective-permute-start(bf16[3,96,1024]{2,1,0:T(8,128)(2,1)S(1)} %collective-permute-done.8.refs_4_.refs_9_), channel_id=1, source_target_pairs={{0,48},{1,17},{2,50},{3,19},{4,52},{5,21},{6,54},{7,23},{8,56},{9,... | collective-permute-start | bytes 1769480 | tf_op jit(solution)/shard_map/ppermute | solution.py:33
  33.7 1.9 %collective-permute-start.17 = (bf16[3,192,1024]{2,1,0:T(8,128)(2,1)S(1)}, bf16[3,192,1024]{2,1,0:T(8,128)(2,1)S(1)}, u32[]{:S(2)}, u32[]{:S(2)}) collective-permute-start(bf16[3,192,1024]{2,1,0:T(8,128)(2,1)S(1)} %constant_dynamic-update-slice_fusion), channel_id=1, source_target_pairs={{0,66},{1,3},{2,64},{3,1},{4,70},{5,7},{6,68},{7,5},{8,74},{9,11},... | collective-permute-start | bytes 3538952 | tf_op jit(solution)/shard_map/ppermute | solution.py:33
  35.6 4.0 %shard_map.59 = (bf16[3,96,1024]{2,1,0:T(8,128)(2,1)S(1)}, bf16[3,96,1024]{2,1,0:T(8,128)(2,1)S(1)}, bf16[3,96,1024]{2,1,0:T(8,128)(2,1)S(1)}, bf16[3,96,1024]{2,1,0:T(8,128)(2,1)S(1)}, bf16[768,768]{1,0:T(8,128)(2,1)S(1)}) custom-call(bf16[384,1024]{1,0:T(8,128)(2,1)S(1)} %copy-done, bf16[384,1024]{1,0:T(8,128)(2,1)S(1)} %collective-permute-done.refs_1_, ...), custom_call_target="tpu_custom_call" | custom-call | flops 3000001024 | bytes 1024 | tf_op jit(solution)/shard_map/pallas_call | solution.py:148
  39.6 2.1 %collective-permute-done.7.refs_2_.refs_6_ = bf16[384,1024]{1,0:T(8,128)(2,1)S(1)} collective-permute-done((bf16[384,1024]{1,0:T(8,128)(2,1)S(1)}, bf16[384,1024]{1,0:T(8,128)(2,1)S(1)}, u32[]{:S(2)}, u32[]{:S(2)}) %collective-permute-start.7) | collective-permute-done | bytes 786464 | tf_op jit(solution)/shard_map/ppermute | solution.py:33
  43.9 2.2 %shard_map.60 = (bf16[3,192,1024]{2,1,0:T(8,128)(2,1)S(1)}, bf16[384,768]{1,0:T(8,128)(2,1)S(1)}) custom-call(bf16[384,1024]{1,0:T(8,128)(2,1)S(1)} %copy-done, bf16[384,1024]{1,0:T(8,128)(2,1)S(1)} %collective-permute-done.refs_1_, bf16[384,1024]{1,0:T(8,128)(2,1)S(1)} %copy-done.1, bf16[384,1024]{1,0:T(8,128)(2,1)S(1)} %collective-permute-done.1.refs_3_.refs_5_, ...), custom_call_target="tpu_custom_call" | custom-call | flops 6000001024 | bytes 1024 | tf_op jit(solution)/shard_map/pallas_call | solution.py:148
  46.1 2.2 %shard_map.61 = (bf16[3,192,1024]{2,1,0:T(8,128)(2,1)S(1)}, bf16[384,768]{1,0:T(8,128)(2,1)S(1)}) custom-call(bf16[384,1024]{1,0:T(8,128)(2,1)S(1)} %collective-permute-done.6.refs_0_.refs_2_, bf16[384,1024]{1,0:T(8,128)(2,1)S(1)} %collective-permute-done.15.refs_1_.refs_3_, bf16[384,1024]{1,0:T(8,128)(2,1)S(1)} %collective-permute-done.7.refs_2_.refs_6_, ...), custom_call_target="tpu_custom_call" | custom-call | flops 1024 | bytes 1024 | tf_op jit(solution)/shard_map/pallas_call | solution.py:148
  48.3 3.2 %collective-permute-start.20 = (bf16[3,192,1024]{2,1,0:T(8,128)(2,1)S(1)}, bf16[3,192,1024]{2,1,0:T(8,128)(2,1)S(1)}, u32[]{:S(2)}, u32[]{:S(2)}) collective-permute-start(bf16[3,192,1024]{2,1,0:T(8,128)(2,1)S(1)} %get-tuple-element.67), channel_id=1, source_target_pairs={{0,48},{1,17},{2,50},{3,19},{4,52},{5,21},{6,54},{7,23},{8,56},{9,... | collective-permute-start | bytes 3538952 | tf_op jit(solution)/shard_map/ppermute | solution.py:33
  51.5 4.2 %shard_map.62 = (bf16[3,192,1024]{2,1,0:T(8,128)(2,1)S(1)}, bf16[384,1536]{1,0:T(8,128)(2,1)S(1)}) custom-call(bf16[384,1024]{1,0:T(8,128)(2,1)S(1)} %copy-done, bf16[384,1024]{1,0:T(8,128)(2,1)S(1)} %collective-permute-done.refs_1_, bf16[384,1024]{1,0:T(8,128)(2,1)S(1)} %collective-permute-done.6.refs_0_.refs_2_, ...), custom_call_target="tpu_custom_call" | custom-call | flops 1024 | bytes 1024 | tf_op jit(solution)/shard_map/pallas_call | solution.py:148
  57.3 4.1 %shard_map.63 = (bf16[3,96,1024]{2,1,0:T(8,128)(2,1)S(1)}, bf16[3,96,1024]{2,1,0:T(8,128)(2,1)S(1)}, bf16[3,96,1024]{2,1,0:T(8,128)(2,1)S(1)}, bf16[3,96,1024]{2,1,0:T(8,128)(2,1)S(1)}, bf16[768,768]{1,0:T(8,128)(2,1)S(1)}) custom-call(bf16[384,1024]{1,0:T(8,128)(2,1)S(1)} %collective-permute-done.6.refs_0_.refs_2_, ...), custom_call_target="tpu_custom_call" | custom-call | flops 1024 | bytes 1024 | tf_op jit(solution)/shard_map/pallas_call | solution.py:148
  61.5 5.1 %shard_map.64 = (f32[384,1024]{1,0:T(8,128)S(1)}, bf16[384,1024]{1,0:T(8,128)(2,1)S(1)}, f32[384,1024]{1,0:T(8,128)S(1)}, bf16[384,1024]{1,0:T(8,128)(2,1)S(1)}) custom-call(bf16[384,768]{1,0:T(8,128)(2,1)S(1)} %get-tuple-element.48.refs_0_, bf16[384,768]{1,0:T(8,128)(2,1)S(1)} %get-tuple-element.79.refs_1_, bf16[768,768]{1,0:T(8,128)(2,1)S(1)} %get-tuple-element.56.refs_2_, ...), custom_call_target="tpu_custom_call" | custom-call | flops 1024 | bytes 1024 | tf_op jit(solution)/shard_map/pallas_call | solution.py:183
  69.7 2.5 %collective-permute-done.19 = bf16[3,192,1024]{2,1,0:T(8,128)(2,1)S(1)} collective-permute-done((bf16[3,192,1024]{2,1,0:T(8,128)(2,1)S(1)}, bf16[3,192,1024]{2,1,0:T(8,128)(2,1)S(1)}, u32[]{:S(2)}, u32[]{:S(2)}) %collective-permute-start.19) | collective-permute-done | bytes 1179680 | tf_op jit(solution)/shard_map/ppermute | solution.py:33
  73.0 2.5 %collective-permute-start.22 = (bf16[384,1024]{1,0:T(8,128)(2,1)S(1)}, bf16[384,1024]{1,0:T(8,128)(2,1)S(1)}, u32[]{:S(2)}, u32[]{:S(2)}) collective-permute-start(bf16[384,1024]{1,0:T(8,128)(2,1)S(1)} %add_convert_fusion.1), channel_id=1, source_target_pairs={{0,4},{1,5},{2,6},{3,7},{4,0},{5,1},{6,2},{7,3},{8,12},{9,13},{10,... | collective-permute-start | bytes 2359304 | tf_op jit(solution)/shard_map/ppermute | solution.py:33
  75.5 3.0 %collective-permute-done.27 = bf16[3,96,1024]{2,1,0:T(8,128)(2,1)S(1)} collective-permute-done((bf16[3,96,1024]{2,1,0:T(8,128)(2,1)S(1)}, bf16[3,96,1024]{2,1,0:T(8,128)(2,1)S(1)}, u32[]{:S(2)}, u32[]{:S(2)}) %collective-permute-start.27) | collective-permute-done | bytes 589856 | tf_op jit(solution)/shard_map/ppermute | solution.py:33
  79.0 4.6 %collective-permute-start.30 = (bf16[3,24,1024]{2,1,0:T(8,128)(2,1)S(1)}, bf16[3,24,1024]{2,1,0:T(8,128)(2,1)S(1)}, u32[]{:S(2)}, u32[]{:S(2)}) collective-permute-start(bf16[3,24,1024]{2,1,0:T(8,128)(2,1)S(1)} %get-tuple-element.84), channel_id=1, source_target_pairs={{0,18},{1,115},{2,16},{3,113},{4,22},{5,119},{6,20},{7,117},{8,26}... | collective-permute-start | bytes 442376 | tf_op jit(solution)/shard_map/ppermute | solution.py:59
  83.6 3.2 %collective-permute-done.23 = bf16[3,96,1024]{2,1,0:T(8,128)(2,1)S(1)} collective-permute-done((bf16[3,96,1024]{2,1,0:T(8,128)(2,1)S(1)}, bf16[3,96,1024]{2,1,0:T(8,128)(2,1)S(1)}, u32[]{:S(2)}, u32[]{:S(2)}) %collective-permute-start.23) | collective-permute-done | bytes 589856 | tf_op jit(solution)/shard_map/ppermute | solution.py:33
  86.8 3.1 %collective-permute-start.29 = (bf16[3,24,1024]{2,1,0:T(8,128)(2,1)S(1)}, bf16[3,24,1024]{2,1,0:T(8,128)(2,1)S(1)}, u32[]{:S(2)}, u32[]{:S(2)}) collective-permute-start(bf16[3,24,1024]{2,1,0:T(8,128)(2,1)S(1)} %get-tuple-element.85), channel_id=1, source_target_pairs={{0,2},{1,67},{2,0},{3,65},{4,6},{5,71},{6,4},{7,69},{8,10},{9,75},... | collective-permute-start | bytes 442376 | tf_op jit(solution)/shard_map/ppermute | solution.py:33
  93.0 2.0 %collective-permute-start.25 = (bf16[3,24,1024]{2,1,0:T(8,128)(2,1)S(1)}, bf16[3,24,1024]{2,1,0:T(8,128)(2,1)S(1)}, u32[]{:S(2)}, u32[]{:S(2)}) collective-permute-start(bf16[3,24,1024]{2,1,0:T(8,128)(2,1)S(1)} %get-tuple-element.82), channel_id=1, source_target_pairs={{0,2},{1,67},{2,0},{3,65},{4,6},{5,71},{6,4},{7,69},{8,10},{9,75},... | collective-permute-start | bytes 442376 | tf_op jit(solution)/shard_map/ppermute | solution.py:33
  95.2 3.1 %collective-permute-start.31 = (bf16[3,24,1024]{2,1,0:T(8,128)(2,1)S(1)}, bf16[3,24,1024]{2,1,0:T(8,128)(2,1)S(1)}, u32[]{:S(2)}, u32[]{:S(2)}) collective-permute-start(bf16[3,24,1024]{2,1,0:T(8,128)(2,1)S(1)} %add_convert_fusion.6), channel_id=1, source_target_pairs={{0,12},{1,13},{2,14},{3,15},{4,8},{5,9},{6,10},{7,11},{8,4},{9,5},... | collective-permute-start | bytes 442376 | tf_op jit(solution)/shard_map/ppermute | solution.py:33
  99.5 2.1 %collective-permute-done.31 = bf16[3,24,1024]{2,1,0:T(8,128)(2,1)S(1)} collective-permute-done((bf16[3,24,1024]{2,1,0:T(8,128)(2,1)S(1)}, bf16[3,24,1024]{2,1,0:T(8,128)(2,1)S(1)}, u32[]{:S(2)}, u32[]{:S(2)}) %collective-permute-start.31) | collective-permute-done | bytes 147488 | tf_op jit(solution)/shard_map/ppermute | solution.py:33
  (70 shorter events, 29.6 us)
Async XLA Ops:
  0.6 19.7 %collective-permute-start.6 = (bf16[384,1024]{1,0:T(8,128)(2,1)}, bf16[384,1024]{1,0:T(8,128)(2,1)S(1)}, u32[]{:S(2)}, u32[]{:S(2)}) collective-permute-start(bf16[384,1024]{1,0:T(8,128)(2,1)} %refs_0_.5), channel_id=1, source_target_pairs={{0,4},{1,5},{2,6},{3,7},{4,0},{5,1},{6,2},{7,3},{8,12},{9,13},{10,... | collective-permute-start | bytes 2359304 | tf_op jit(solution)/shard_map/ppermute | solution.py:33
  4.4 6.6 %collective-permute-start.2 = (bf16[3,24,1024]{2,1,0:T(8,128)(2,1)S(1)}, bf16[3,24,1024]{2,1,0:T(8,128)(2,1)S(1)}, u32[]{:S(2)}, u32[]{:S(2)}) collective-permute-start(bf16[3,24,1024]{2,1,0:T(8,128)(2,1)S(1)} %pad_maximum_fusion.2), channel_id=1, source_target_pairs={{0,12},{1,13},{2,14},{3,15},{4,8},{5,9},{6,10},{7,11},{8,4},{9,5},... | collective-permute-start | bytes 442376 | tf_op jit(solution)/shard_map/ppermute | solution.py:33
  11.0 7.3 %collective-permute-start.5 = (bf16[3,24,1024]{2,1,0:T(8,128)(2,1)S(1)}, bf16[3,24,1024]{2,1,0:T(8,128)(2,1)S(1)}, u32[]{:S(2)}, u32[]{:S(2)}) collective-permute-start(bf16[3,24,1024]{2,1,0:T(8,128)(2,1)S(1)} %collective-permute-done.2), channel_id=1, source_target_pairs={{0,18},{1,115},{2,16},{3,113},{4,22},{5,119},{6,20},{7,117},{8,26}... | collective-permute-start | bytes 442376 | tf_op jit(solution)/shard_map/ppermute | solution.py:59
  15.3 11.2 %collective-permute-start.12 = (bf16[3,96,1024]{2,1,0:T(8,128)(2,1)S(1)}, bf16[3,96,1024]{2,1,0:T(8,128)(2,1)S(1)}, u32[]{:S(2)}, u32[]{:S(2)}) collective-permute-start(bf16[3,96,1024]{2,1,0:T(8,128)(2,1)S(1)} %pad_maximum_fusion.1.refs_7_.refs_12_), channel_id=1, source_target_pairs={{0,48},{1,17},{2,50},{3,19},{4,52},{5,21},{6,54},{7,23},{8,56},{9,... | collective-permute-start | bytes 1769480 | tf_op jit(solution)/shard_map/ppermute | solution.py:33
  18.3 15.4 %collective-permute-start = (bf16[384,1024]{1,0:T(8,128)(2,1)S(1)}, bf16[384,1024]{1,0:T(8,128)(2,1)S(1)}, u32[]{:S(2)}, u32[]{:S(2)}) collective-permute-start(bf16[384,1024]{1,0:T(8,128)(2,1)S(1)} %copy-done), channel_id=1, source_target_pairs={{0,1},{1,0},{2,3},{3,2},{4,5},{5,4},{6,7},{7,6},{8,9},{9,8},{10,11... | collective-permute-start | bytes 2359304 | tf_op jit(solution)/shard_map/ppermute | solution.py:63
  18.7 16.8 %collective-permute-start.1 = (bf16[384,1024]{1,0:T(8,128)(2,1)S(1)}, bf16[384,1024]{1,0:T(8,128)(2,1)S(1)}, u32[]{:S(2)}, u32[]{:S(2)}) collective-permute-start(bf16[384,1024]{1,0:T(8,128)(2,1)S(1)} %copy-done.1), channel_id=1, source_target_pairs={{0,1},{1,0},{2,3},{3,2},{4,5},{5,4},{6,7},{7,6},{8,9},{9,8},{10,11... | collective-permute-start | bytes 2359304 | tf_op jit(solution)/shard_map/ppermute | solution.py:63
  20.4 9.9 %collective-permute-start.8 = (bf16[3,96,1024]{2,1,0:T(8,128)(2,1)S(1)}, bf16[3,96,1024]{2,1,0:T(8,128)(2,1)S(1)}, u32[]{:S(2)}, u32[]{:S(2)}) collective-permute-start(bf16[3,96,1024]{2,1,0:T(8,128)(2,1)S(1)} %pad_maximum_fusion.refs_5_.refs_10_), channel_id=1, source_target_pairs={{0,66},{1,3},{2,64},{3,1},{4,70},{5,7},{6,68},{7,5},{8,74},{9,11},... | collective-permute-start | bytes 1769480 | tf_op jit(solution)/shard_map/ppermute | solution.py:33
  21.9 19.8 %collective-permute-start.7 = (bf16[384,1024]{1,0:T(8,128)(2,1)S(1)}, bf16[384,1024]{1,0:T(8,128)(2,1)S(1)}, u32[]{:S(2)}, u32[]{:S(2)}) collective-permute-start(bf16[384,1024]{1,0:T(8,128)(2,1)S(1)} %copy-done.1), channel_id=1, source_target_pairs={{0,4},{1,5},{2,6},{3,7},{4,0},{5,1},{6,2},{7,3},{8,12},{9,13},{10,... | collective-permute-start | bytes 2359304 | tf_op jit(solution)/shard_map/ppermute | solution.py:33
  26.4 15.2 %collective-permute-start.13 = (bf16[3,96,1024]{2,1,0:T(8,128)(2,1)S(1)}, bf16[3,96,1024]{2,1,0:T(8,128)(2,1)S(1)}, u32[]{:S(2)}, u32[]{:S(2)}) collective-permute-start(bf16[3,96,1024]{2,1,0:T(8,128)(2,1)S(1)} %pad_maximum_fusion.refs_5_.refs_10_), channel_id=1, source_target_pairs={{0,48},{1,17},{2,50},{3,19},{4,52},{5,21},{6,54},{7,23},{8,56},{9,... | collective-permute-start | bytes 1769480 | tf_op jit(solution)/shard_map/ppermute | solution.py:33
  30.3 13.6 %collective-permute-start.14 = (bf16[3,96,1024]{2,1,0:T(8,128)(2,1)S(1)}, bf16[3,96,1024]{2,1,0:T(8,128)(2,1)S(1)}, u32[]{:S(2)}, u32[]{:S(2)}) collective-permute-start(bf16[3,96,1024]{2,1,0:T(8,128)(2,1)S(1)} %collective-permute-done.8.refs_4_.refs_9_), channel_id=1, source_target_pairs={{0,48},{1,17},{2,50},{3,19},{4,52},{5,21},{6,54},{7,23},{8,56},{9,... | collective-permute-start | bytes 1769480 | tf_op jit(solution)/shard_map/ppermute | solution.py:33
  33.7 17.8 %collective-permute-start.17 = (bf16[3,192,1024]{2,1,0:T(8,128)(2,1)S(1)}, bf16[3,192,1024]{2,1,0:T(8,128)(2,1)S(1)}, u32[]{:S(2)}, u32[]{:S(2)}) collective-permute-start(bf16[3,192,1024]{2,1,0:T(8,128)(2,1)S(1)} %constant_dynamic-update-slice_fusion), channel_id=1, source_target_pairs={{0,66},{1,3},{2,64},{3,1},{4,70},{5,7},{6,68},{7,5},{8,74},{9,11},... | collective-permute-start | bytes 3538952 | tf_op jit(solution)/shard_map/ppermute | solution.py:33
  48.3 18.4 %collective-permute-start.20 = (bf16[3,192,1024]{2,1,0:T(8,128)(2,1)S(1)}, bf16[3,192,1024]{2,1,0:T(8,128)(2,1)S(1)}, u32[]{:S(2)}, u32[]{:S(2)}) collective-permute-start(bf16[3,192,1024]{2,1,0:T(8,128)(2,1)S(1)} %get-tuple-element.67), channel_id=1, source_target_pairs={{0,48},{1,17},{2,50},{3,19},{4,52},{5,21},{6,54},{7,23},{8,56},{9,... | collective-permute-start | bytes 3538952 | tf_op jit(solution)/shard_map/ppermute | solution.py:33
  55.7 16.5 %collective-permute-start.19 = (bf16[3,192,1024]{2,1,0:T(8,128)(2,1)S(1)}, bf16[3,192,1024]{2,1,0:T(8,128)(2,1)S(1)}, u32[]{:S(2)}, u32[]{:S(2)}) collective-permute-start(bf16[3,192,1024]{2,1,0:T(8,128)(2,1)S(1)} %get-tuple-element.66), channel_id=1, source_target_pairs={{0,66},{1,3},{2,64},{3,1},{4,70},{5,7},{6,68},{7,5},{8,74},{9,11},... | collective-permute-start | bytes 3538952 | tf_op jit(solution)/shard_map/ppermute | solution.py:33
  66.9 11.6 %collective-permute-start.27 = (bf16[3,96,1024]{2,1,0:T(8,128)(2,1)S(1)}, bf16[3,96,1024]{2,1,0:T(8,128)(2,1)S(1)}, u32[]{:S(2)}, u32[]{:S(2)}) collective-permute-start(bf16[3,96,1024]{2,1,0:T(8,128)(2,1)S(1)} %add_convert_fusion.3), channel_id=1, source_target_pairs={{0,66},{1,3},{2,64},{3,1},{4,70},{5,7},{6,68},{7,5},{8,74},{9,11},... | collective-permute-start | bytes 1769480 | tf_op jit(solution)/shard_map/ppermute | solution.py:33
  68.3 26.9 %collective-permute-start.18 = (bf16[384,1024]{1,0:T(8,128)(2,1)S(1)}, bf16[384,1024]{1,0:T(8,128)(2,1)S(1)}, u32[]{:S(2)}, u32[]{:S(2)}) collective-permute-start(bf16[384,1024]{1,0:T(8,128)(2,1)S(1)} %get-tuple-element.65), channel_id=1, source_target_pairs={{0,1},{1,0},{2,3},{3,2},{4,5},{5,4},{6,7},{7,6},{8,9},{9,8},{10,11... | collective-permute-start | bytes 2359304 | tf_op jit(solution)/shard_map/ppermute | solution.py:63
  72.5 14.3 %collective-permute-start.23 = (bf16[3,96,1024]{2,1,0:T(8,128)(2,1)S(1)}, bf16[3,96,1024]{2,1,0:T(8,128)(2,1)S(1)}, u32[]{:S(2)}, u32[]{:S(2)}) collective-permute-start(bf16[3,96,1024]{2,1,0:T(8,128)(2,1)S(1)} %add_convert_fusion.5), channel_id=1, source_target_pairs={{0,48},{1,17},{2,50},{3,19},{4,52},{5,21},{6,54},{7,23},{8,56},{9,... | collective-permute-start | bytes 1769480 | tf_op jit(solution)/shard_map/ppermute | solution.py:33
  73.0 25.2 %collective-permute-start.22 = (bf16[384,1024]{1,0:T(8,128)(2,1)S(1)}, bf16[384,1024]{1,0:T(8,128)(2,1)S(1)}, u32[]{:S(2)}, u32[]{:S(2)}) collective-permute-start(bf16[384,1024]{1,0:T(8,128)(2,1)S(1)} %add_convert_fusion.1), channel_id=1, source_target_pairs={{0,4},{1,5},{2,6},{3,7},{4,0},{5,1},{6,2},{7,3},{8,12},{9,13},{10,... | collective-permute-start | bytes 2359304 | tf_op jit(solution)/shard_map/ppermute | solution.py:33
  78.9 11.4 %collective-permute-start.28 = (bf16[3,24,1024]{2,1,0:T(8,128)(2,1)S(1)}, bf16[3,24,1024]{2,1,0:T(8,128)(2,1)S(1)}, u32[]{:S(2)}, u32[]{:S(2)}) collective-permute-start(bf16[3,24,1024]{2,1,0:T(8,128)(2,1)S(1)} %get-tuple-element.83), channel_id=1, source_target_pairs={{0,16},{1,49},{2,18},{3,51},{4,20},{5,53},{6,22},{7,55},{8,24},{9,... | collective-permute-start | bytes 442376 | tf_op jit(solution)/shard_map/ppermute | solution.py:33
  79.0 11.4 %collective-permute-start.30 = (bf16[3,24,1024]{2,1,0:T(8,128)(2,1)S(1)}, bf16[3,24,1024]{2,1,0:T(8,128)(2,1)S(1)}, u32[]{:S(2)}, u32[]{:S(2)}) collective-permute-start(bf16[3,24,1024]{2,1,0:T(8,128)(2,1)S(1)} %get-tuple-element.84), channel_id=1, source_target_pairs={{0,18},{1,115},{2,16},{3,113},{4,22},{5,119},{6,20},{7,117},{8,26}... | collective-permute-start | bytes 442376 | tf_op jit(solution)/shard_map/ppermute | solution.py:59
  86.8 6.3 %collective-permute-start.29 = (bf16[3,24,1024]{2,1,0:T(8,128)(2,1)S(1)}, bf16[3,24,1024]{2,1,0:T(8,128)(2,1)S(1)}, u32[]{:S(2)}, u32[]{:S(2)}) collective-permute-start(bf16[3,24,1024]{2,1,0:T(8,128)(2,1)S(1)} %get-tuple-element.85), channel_id=1, source_target_pairs={{0,2},{1,67},{2,0},{3,65},{4,6},{5,71},{6,4},{7,69},{8,10},{9,75},... | collective-permute-start | bytes 442376 | tf_op jit(solution)/shard_map/ppermute | solution.py:33
  90.3 9.2 %collective-permute-start.24 = (bf16[3,24,1024]{2,1,0:T(8,128)(2,1)S(1)}, bf16[3,24,1024]{2,1,0:T(8,128)(2,1)S(1)}, u32[]{:S(2)}, u32[]{:S(2)}) collective-permute-start(bf16[3,24,1024]{2,1,0:T(8,128)(2,1)S(1)} %get-tuple-element.80), channel_id=1, source_target_pairs={{0,16},{1,49},{2,18},{3,51},{4,20},{5,53},{6,22},{7,55},{8,24},{9,... | collective-permute-start | bytes 442376 | tf_op jit(solution)/shard_map/ppermute | solution.py:33
  90.4 9.1 %collective-permute-start.26 = (bf16[3,24,1024]{2,1,0:T(8,128)(2,1)S(1)}, bf16[3,24,1024]{2,1,0:T(8,128)(2,1)S(1)}, u32[]{:S(2)}, u32[]{:S(2)}) collective-permute-start(bf16[3,24,1024]{2,1,0:T(8,128)(2,1)S(1)} %get-tuple-element.81), channel_id=1, source_target_pairs={{0,18},{1,115},{2,16},{3,113},{4,22},{5,119},{6,20},{7,117},{8,26}... | collective-permute-start | bytes 442376 | tf_op jit(solution)/shard_map/ppermute | solution.py:59
  93.0 6.4 %collective-permute-start.25 = (bf16[3,24,1024]{2,1,0:T(8,128)(2,1)S(1)}, bf16[3,24,1024]{2,1,0:T(8,128)(2,1)S(1)}, u32[]{:S(2)}, u32[]{:S(2)}) collective-permute-start(bf16[3,24,1024]{2,1,0:T(8,128)(2,1)S(1)} %get-tuple-element.82), channel_id=1, source_target_pairs={{0,2},{1,67},{2,0},{3,65},{4,6},{5,71},{6,4},{7,69},{8,10},{9,75},... | collective-permute-start | bytes 442376 | tf_op jit(solution)/shard_map/ppermute | solution.py:33
  95.2 6.4 %collective-permute-start.31 = (bf16[3,24,1024]{2,1,0:T(8,128)(2,1)S(1)}, bf16[3,24,1024]{2,1,0:T(8,128)(2,1)S(1)}, u32[]{:S(2)}, u32[]{:S(2)}) collective-permute-start(bf16[3,24,1024]{2,1,0:T(8,128)(2,1)S(1)} %add_convert_fusion.6), channel_id=1, source_target_pairs={{0,12},{1,13},{2,14},{3,15},{4,8},{5,9},{6,10},{7,11},{8,4},{9,5},... | collective-permute-start | bytes 442376 | tf_op jit(solution)/shard_map/ppermute | solution.py:33
  (10 other events, 78.3 us)

commit v10 on v9

--- a/solution.py
+++ b/solution.py
@@ -194,18 +194,36 @@
     )(*parts, *ws)
 
 
+def stack_kernel(gate_up_ref, down_ref, out_ref):
+    both = gate_up_ref[...].astype(F32)
+    for m in range(2):
+        out_ref[m] = both[:, m].astype(BF16)
+    out_ref[2] = down_ref[...]
+
+
+def stack_rows(gate_up, down_proj):
+    vmem = pl.BlockSpec(memory_space=pltpu.VMEM)
+    rows, width = down_proj.shape
+    return pl.pallas_call(
+        stack_kernel,
+        out_shape=jax.ShapeDtypeStruct((3, rows, width), BF16),
+        in_specs=[vmem] * 2,
+        out_specs=vmem,
+    )(gate_up, down_proj)
+
+
 def body(activations, cotangent, gate_up, down_proj):
     x_z = swap_near(activations, Z)
-    message = jnp.concatenate([gate_up.transpose(1, 0, 2), down_proj[None]], axis=0)
-    message = lax.optimization_barrier(message)
+    message = stack_rows(gate_up, down_proj)
     block1 = gather_block(swap_wrap(message, Z))
     o0 = gather_block(message)
     block1, c_own = lax.optimization_barrier((block1, cotangent))
     c_z = swap_near(c_own, Z)
-    o1, x_z = lax.optimization_barrier((block1, x_z))
+    o1 = block1
     n0 = swap_second(o0, Y)
     r0 = swap_second(join(o0, n0), X)
     n1 = swap_second(o1, X)
+    o1, x_z = lax.optimization_barrier((o1, x_z))
     w1 = swap_second(o1, Y)
     f1 = swap_second(n1, Y)
     xs, cs = [activations, swap_core(activations)], [cotangent, swap_core(cotangent)]

time: 103 us -> 103 us (level)
  starting transfers between devices: 51.4 us -> 46.8 us
  waiting for transfers between devices: 22.9 us -> 26.6 us
  Pallas kernels: 21.8 us -> 23.6 us
    ppermute x22, waiting for transfers between devices: 22.3 us -> 26.1 us  [swap(): return lax.ppermute(value, AXES, pairs)]
    ppermute x22, starting transfers between devices: 39.8 us -> 36.6 us  [swap(): return lax.ppermute(value, AXES, pairs)]
    pallas_call x0 -> x1, Pallas kernels: none -> 1.81 us  [stack_rows(): pl.pallas_call(stack_kernel, out_shape=jax.ShapeDtypeStruct((3, rows, wid...]
  transfers between devices with their start and end apart: 32 -> 32, of which waited for: 15 -> 13; matrix products, arithmetic and copies ran while one was open for 5% -> 4% of each run, Pallas kernels for 21% -> 23%
where the time goes in v10:
time: 103 us
  starting transfers between devices  46.8 us (45%)
  waiting for transfers between devices  26.6 us (26%)
  Pallas kernels  23.6 us (23%)
  other arithmetic  4.43 us (4%)
    ppermute x22, starting transfers between devices, swap(): return lax.ppermute(value, AXES, pairs)  36.6 us
    ppermute x22, waiting for transfers between devices, swap(): return lax.ppermute(value, AXES, pairs)  26.1 us
    pallas_call x5, Pallas kernels, grads(): pl.pallas_call(kernel, out_shape=[jax.ShapeDtypeStruct((3, joined * units...  16.7 us
    ppermute x4, starting transfers between devices, swap_corner(): return lax.ppermute(value, AXES, pairs)  8.33 us
    pallas_call x1, Pallas kernels, input_parts(): pl.pallas_call(kernel, out_shape=[jax.ShapeDtypeStruct((group, width), ki...  5.06 us
  transfers between devices with their start and end apart: 32, of which 13 were waited for; matrix products, arithmetic and copies ran while one was open for 4% of the time, Pallas kernels for 23%

profile of v10, /device:TPU:2, one launch (start us, length us, event | category | flops | bytes accessed | tf_op | source)
XLA Modules:
  0.0 102.5 jit_solution(8903546039666019666)
XLA Ops:
  0.6 2.0 %collective-permute-start.6 = (bf16[384,1024]{1,0:T(8,128)(2,1)}, bf16[384,1024]{1,0:T(8,128)(2,1)S(1)}, u32[]{:S(2)}, u32[]{:S(2)}) collective-permute-start(bf16[384,1024]{1,0:T(8,128)(2,1)} %refs_0_.5), channel_id=1, source_target_pairs={{0,4},{1,5},{2,6},{3,7},{4,0},{5,1},{6,2},{7,3},{8,12},{9,13},{10,... | collective-permute-start | bytes 2359304 | tf_op jit(solution)/shard_map/ppermute | solution.py:33
  4.5 2.5 %collective-permute-start.2 = (bf16[3,24,1024]{2,1,0:T(8,128)(2,1)}, bf16[3,24,1024]{2,1,0:T(8,128)(2,1)S(1)}, u32[]{:S(2)}, u32[]{:S(2)}) collective-permute-start(bf16[3,24,1024]{2,1,0:T(8,128)(2,1)} %shard_map.59), channel_id=1, source_target_pairs={{0,12},{1,13},{2,14},{3,15},{4,8},{5,9},{6,10},{7,11},{8,4},{9,5},... | collective-permute-start | bytes 442376 | tf_op jit(solution)/shard_map/ppermute | solution.py:33
  16.4 3.1 %collective-permute-start.12 = (bf16[3,96,1024]{2,1,0:T(8,128)(2,1)S(1)}, bf16[3,96,1024]{2,1,0:T(8,128)(2,1)S(1)}, u32[]{:S(2)}, u32[]{:S(2)}) collective-permute-start(bf16[3,96,1024]{2,1,0:T(8,128)(2,1)S(1)} %pad_maximum_fusion.1.refs_7_.refs_12_), channel_id=1, source_target_pairs={{0,48},{1,17},{2,50},{3,19},{4,52},{5,21},{6,54},{7,23},{8,56},{9,... | collective-permute-start | bytes 1769480 | tf_op jit(solution)/shard_map/ppermute | solution.py:33
  22.7 4.8 %collective-permute-done.12.refs_6_.refs_11_ = bf16[3,96,1024]{2,1,0:T(8,128)(2,1)S(1)} collective-permute-done((bf16[3,96,1024]{2,1,0:T(8,128)(2,1)S(1)}, bf16[3,96,1024]{2,1,0:T(8,128)(2,1)S(1)}, u32[]{:S(2)}, u32[]{:S(2)}) %collective-permute-start.12) | collective-permute-done | bytes 589856 | tf_op jit(solution)/shard_map/ppermute | solution.py:33
  27.5 3.0 %collective-permute-start.13 = (bf16[3,96,1024]{2,1,0:T(8,128)(2,1)S(1)}, bf16[3,96,1024]{2,1,0:T(8,128)(2,1)S(1)}, u32[]{:S(2)}, u32[]{:S(2)}) collective-permute-start(bf16[3,96,1024]{2,1,0:T(8,128)(2,1)S(1)} %pad_maximum_fusion.refs_5_.refs_10_), channel_id=1, source_target_pairs={{0,48},{1,17},{2,50},{3,19},{4,52},{5,21},{6,54},{7,23},{8,56},{9,... | collective-permute-start | bytes 1769480 | tf_op jit(solution)/shard_map/ppermute | solution.py:33
  30.6 2.8 %collective-permute-start.14 = (bf16[3,96,1024]{2,1,0:T(8,128)(2,1)S(1)}, bf16[3,96,1024]{2,1,0:T(8,128)(2,1)S(1)}, u32[]{:S(2)}, u32[]{:S(2)}) collective-permute-start(bf16[3,96,1024]{2,1,0:T(8,128)(2,1)S(1)} %collective-permute-done.8.refs_4_.refs_9_), channel_id=1, source_target_pairs={{0,48},{1,17},{2,50},{3,19},{4,52},{5,21},{6,54},{7,23},{8,56},{9,... | collective-permute-start | bytes 1769480 | tf_op jit(solution)/shard_map/ppermute | solution.py:33
  33.5 2.1 %collective-permute-start.17 = (bf16[3,192,1024]{2,1,0:T(8,128)(2,1)S(1)}, bf16[3,192,1024]{2,1,0:T(8,128)(2,1)S(1)}, u32[]{:S(2)}, u32[]{:S(2)}) collective-permute-start(bf16[3,192,1024]{2,1,0:T(8,128)(2,1)S(1)} %constant_dynamic-update-slice_fusion), channel_id=1, source_target_pairs={{0,66},{1,3},{2,64},{3,1},{4,70},{5,7},{6,68},{7,5},{8,74},{9,11},... | collective-permute-start | bytes 3538952 | tf_op jit(solution)/shard_map/ppermute | solution.py:33
  35.6 4.0 %shard_map.60 = (bf16[3,96,1024]{2,1,0:T(8,128)(2,1)S(1)}, bf16[3,96,1024]{2,1,0:T(8,128)(2,1)S(1)}, bf16[3,96,1024]{2,1,0:T(8,128)(2,1)S(1)}, bf16[3,96,1024]{2,1,0:T(8,128)(2,1)S(1)}, bf16[768,768]{1,0:T(8,128)(2,1)S(1)}) custom-call(bf16[384,1024]{1,0:T(8,128)(2,1)S(1)} %copy-done, bf16[384,1024]{1,0:T(8,128)(2,1)S(1)} %collective-permute-done.refs_1_, ...), custom_call_target="tpu_custom_call" | custom-call | flops 3000001024 | bytes 1024 | tf_op jit(solution)/shard_map/pallas_call | solution.py:148
  39.6 2.2 %collective-permute-done.7.refs_2_.refs_6_ = bf16[384,1024]{1,0:T(8,128)(2,1)S(1)} collective-permute-done((bf16[384,1024]{1,0:T(8,128)(2,1)S(1)}, bf16[384,1024]{1,0:T(8,128)(2,1)S(1)}, u32[]{:S(2)}, u32[]{:S(2)}) %collective-permute-start.7) | collective-permute-done | bytes 786464 | tf_op jit(solution)/shard_map/ppermute | solution.py:33
  42.3 2.6 %collective-permute-done.14.refs_5_.refs_7_ = bf16[3,96,1024]{2,1,0:T(8,128)(2,1)S(1)} collective-permute-done((bf16[3,96,1024]{2,1,0:T(8,128)(2,1)S(1)}, bf16[3,96,1024]{2,1,0:T(8,128)(2,1)S(1)}, u32[]{:S(2)}, u32[]{:S(2)}) %collective-permute-start.14) | collective-permute-done | bytes 589856 | tf_op jit(solution)/shard_map/ppermute | solution.py:33
  45.0 2.2 %shard_map.61 = (bf16[3,192,1024]{2,1,0:T(8,128)(2,1)S(1)}, bf16[384,768]{1,0:T(8,128)(2,1)S(1)}) custom-call(bf16[384,1024]{1,0:T(8,128)(2,1)S(1)} %copy-done, bf16[384,1024]{1,0:T(8,128)(2,1)S(1)} %collective-permute-done.refs_1_, bf16[384,1024]{1,0:T(8,128)(2,1)S(1)} %copy-done.1, bf16[384,1024]{1,0:T(8,128)(2,1)S(1)} %collective-permute-done.1.refs_3_.refs_5_, ...), custom_call_target="tpu_custom_call" | custom-call | flops 6000001024 | bytes 1024 | tf_op jit(solution)/shard_map/pallas_call | solution.py:148
  47.2 2.2 %shard_map.62 = (bf16[3,192,1024]{2,1,0:T(8,128)(2,1)S(1)}, bf16[384,768]{1,0:T(8,128)(2,1)S(1)}) custom-call(bf16[384,1024]{1,0:T(8,128)(2,1)S(1)} %collective-permute-done.6.refs_0_.refs_2_, bf16[384,1024]{1,0:T(8,128)(2,1)S(1)} %collective-permute-done.15.refs_1_.refs_3_, bf16[384,1024]{1,0:T(8,128)(2,1)S(1)} %collective-permute-done.7.refs_2_.refs_6_, ...), custom_call_target="tpu_custom_call" | custom-call | flops 1024 | bytes 1024 | tf_op jit(solution)/shard_map/pallas_call | solution.py:148
  49.4 3.1 %collective-permute-start.20 = (bf16[3,192,1024]{2,1,0:T(8,128)(2,1)S(1)}, bf16[3,192,1024]{2,1,0:T(8,128)(2,1)S(1)}, u32[]{:S(2)}, u32[]{:S(2)}) collective-permute-start(bf16[3,192,1024]{2,1,0:T(8,128)(2,1)S(1)} %get-tuple-element.67), channel_id=1, source_target_pairs={{0,48},{1,17},{2,50},{3,19},{4,52},{5,21},{6,54},{7,23},{8,56},{9,... | collective-permute-start | bytes 3538952 | tf_op jit(solution)/shard_map/ppermute | solution.py:33
  52.5 4.2 %shard_map.63 = (bf16[3,192,1024]{2,1,0:T(8,128)(2,1)S(1)}, bf16[384,1536]{1,0:T(8,128)(2,1)S(1)}) custom-call(bf16[384,1024]{1,0:T(8,128)(2,1)S(1)} %copy-done, bf16[384,1024]{1,0:T(8,128)(2,1)S(1)} %collective-permute-done.refs_1_, bf16[384,1024]{1,0:T(8,128)(2,1)S(1)} %collective-permute-done.6.refs_0_.refs_2_, ...), custom_call_target="tpu_custom_call" | custom-call | flops 1024 | bytes 1024 | tf_op jit(solution)/shard_map/pallas_call | solution.py:148
  58.5 4.1 %shard_map.64 = (bf16[3,96,1024]{2,1,0:T(8,128)(2,1)S(1)}, bf16[3,96,1024]{2,1,0:T(8,128)(2,1)S(1)}, bf16[3,96,1024]{2,1,0:T(8,128)(2,1)S(1)}, bf16[3,96,1024]{2,1,0:T(8,128)(2,1)S(1)}, bf16[768,768]{1,0:T(8,128)(2,1)S(1)}) custom-call(bf16[384,1024]{1,0:T(8,128)(2,1)S(1)} %collective-permute-done.6.refs_0_.refs_2_, ...), custom_call_target="tpu_custom_call" | custom-call | flops 1024 | bytes 1024 | tf_op jit(solution)/shard_map/pallas_call | solution.py:148
  62.6 5.1 %shard_map.65 = (f32[384,1024]{1,0:T(8,128)S(1)}, bf16[384,1024]{1,0:T(8,128)(2,1)S(1)}, f32[384,1024]{1,0:T(8,128)S(1)}, bf16[384,1024]{1,0:T(8,128)(2,1)S(1)}) custom-call(bf16[384,768]{1,0:T(8,128)(2,1)S(1)} %get-tuple-element.48.refs_0_, bf16[384,768]{1,0:T(8,128)(2,1)S(1)} %get-tuple-element.79.refs_1_, bf16[768,768]{1,0:T(8,128)(2,1)S(1)} %get-tuple-element.56.refs_2_, ...), custom_call_target="tpu_custom_call" | custom-call | flops 1024 | bytes 1024 | tf_op jit(solution)/shard_map/pallas_call | solution.py:183
  70.1 3.0 %collective-permute-done.19 = bf16[3,192,1024]{2,1,0:T(8,128)(2,1)S(1)} collective-permute-done((bf16[3,192,1024]{2,1,0:T(8,128)(2,1)S(1)}, bf16[3,192,1024]{2,1,0:T(8,128)(2,1)S(1)}, u32[]{:S(2)}, u32[]{:S(2)}) %collective-permute-start.19) | collective-permute-done | bytes 1179680 | tf_op jit(solution)/shard_map/ppermute | solution.py:33
  74.1 2.5 %collective-permute-start.22 = (bf16[384,1024]{1,0:T(8,128)(2,1)S(1)}, bf16[384,1024]{1,0:T(8,128)(2,1)S(1)}, u32[]{:S(2)}, u32[]{:S(2)}) collective-permute-start(bf16[384,1024]{1,0:T(8,128)(2,1)S(1)} %add_convert_fusion.1), channel_id=1, source_target_pairs={{0,4},{1,5},{2,6},{3,7},{4,0},{5,1},{6,2},{7,3},{8,12},{9,13},{10,... | collective-permute-start | bytes 2359304 | tf_op jit(solution)/shard_map/ppermute | solution.py:33
  76.6 2.9 %collective-permute-done.27 = bf16[3,96,1024]{2,1,0:T(8,128)(2,1)S(1)} collective-permute-done((bf16[3,96,1024]{2,1,0:T(8,128)(2,1)S(1)}, bf16[3,96,1024]{2,1,0:T(8,128)(2,1)S(1)}, u32[]{:S(2)}, u32[]{:S(2)}) %collective-permute-start.27) | collective-permute-done | bytes 589856 | tf_op jit(solution)/shard_map/ppermute | solution.py:33
  79.9 3.8 %collective-permute-start.30 = (bf16[3,24,1024]{2,1,0:T(8,128)(2,1)S(1)}, bf16[3,24,1024]{2,1,0:T(8,128)(2,1)S(1)}, u32[]{:S(2)}, u32[]{:S(2)}) collective-permute-start(bf16[3,24,1024]{2,1,0:T(8,128)(2,1)S(1)} %get-tuple-element.84), channel_id=1, source_target_pairs={{0,18},{1,115},{2,16},{3,113},{4,22},{5,119},{6,20},{7,117},{8,26}... | collective-permute-start | bytes 442376 | tf_op jit(solution)/shard_map/ppermute | solution.py:59
  83.7 4.0 %collective-permute-done.23 = bf16[3,96,1024]{2,1,0:T(8,128)(2,1)S(1)} collective-permute-done((bf16[3,96,1024]{2,1,0:T(8,128)(2,1)S(1)}, bf16[3,96,1024]{2,1,0:T(8,128)(2,1)S(1)}, u32[]{:S(2)}, u32[]{:S(2)}) %collective-permute-start.23) | collective-permute-done | bytes 589856 | tf_op jit(solution)/shard_map/ppermute | solution.py:33
  87.7 2.3 %collective-permute-start.29 = (bf16[3,24,1024]{2,1,0:T(8,128)(2,1)S(1)}, bf16[3,24,1024]{2,1,0:T(8,128)(2,1)S(1)}, u32[]{:S(2)}, u32[]{:S(2)}) collective-permute-start(bf16[3,24,1024]{2,1,0:T(8,128)(2,1)S(1)} %get-tuple-element.85), channel_id=1, source_target_pairs={{0,2},{1,67},{2,0},{3,65},{4,6},{5,71},{6,4},{7,69},{8,10},{9,75},... | collective-permute-start | bytes 442376 | tf_op jit(solution)/shard_map/ppermute | solution.py:33
  93.2 2.0 %collective-permute-start.25 = (bf16[3,24,1024]{2,1,0:T(8,128)(2,1)S(1)}, bf16[3,24,1024]{2,1,0:T(8,128)(2,1)S(1)}, u32[]{:S(2)}, u32[]{:S(2)}) collective-permute-start(bf16[3,24,1024]{2,1,0:T(8,128)(2,1)S(1)} %get-tuple-element.82), channel_id=1, source_target_pairs={{0,2},{1,67},{2,0},{3,65},{4,6},{5,71},{6,4},{7,69},{8,10},{9,75},... | collective-permute-start | bytes 442376 | tf_op jit(solution)/shard_map/ppermute | solution.py:33
  98.7 3.0 %collective-permute-done.31 = bf16[3,24,1024]{2,1,0:T(8,128)(2,1)S(1)} collective-permute-done((bf16[3,24,1024]{2,1,0:T(8,128)(2,1)S(1)}, bf16[3,24,1024]{2,1,0:T(8,128)(2,1)S(1)}, u32[]{:S(2)}, u32[]{:S(2)}) %collective-permute-start.31) | collective-permute-done | bytes 147488 | tf_op jit(solution)/shard_map/ppermute | solution.py:33
  (71 shorter events, 28.1 us)
Async XLA Ops:
  0.6 21.0 %collective-permute-start.6 = (bf16[384,1024]{1,0:T(8,128)(2,1)}, bf16[384,1024]{1,0:T(8,128)(2,1)S(1)}, u32[]{:S(2)}, u32[]{:S(2)}) collective-permute-start(bf16[384,1024]{1,0:T(8,128)(2,1)} %refs_0_.5), channel_id=1, source_target_pairs={{0,4},{1,5},{2,6},{3,7},{4,0},{5,1},{6,2},{7,3},{8,12},{9,13},{10,... | collective-permute-start | bytes 2359304 | tf_op jit(solution)/shard_map/ppermute | solution.py:33
  4.5 6.7 %collective-permute-start.2 = (bf16[3,24,1024]{2,1,0:T(8,128)(2,1)}, bf16[3,24,1024]{2,1,0:T(8,128)(2,1)S(1)}, u32[]{:S(2)}, u32[]{:S(2)}) collective-permute-start(bf16[3,24,1024]{2,1,0:T(8,128)(2,1)} %shard_map.59), channel_id=1, source_target_pairs={{0,12},{1,13},{2,14},{3,15},{4,8},{5,9},{6,10},{7,11},{8,4},{9,5},... | collective-permute-start | bytes 442376 | tf_op jit(solution)/shard_map/ppermute | solution.py:33
  7.0 6.3 %collective-permute-start.11 = (bf16[3,24,1024]{2,1,0:T(8,128)(2,1)}, bf16[3,24,1024]{2,1,0:T(8,128)(2,1)S(1)}, u32[]{:S(2)}, u32[]{:S(2)}) collective-permute-start(bf16[3,24,1024]{2,1,0:T(8,128)(2,1)} %shard_map.59), channel_id=1, source_target_pairs={{0,18},{1,115},{2,16},{3,113},{4,22},{5,119},{6,20},{7,117},{8,26}... | collective-permute-start | bytes 442376 | tf_op jit(solution)/shard_map/ppermute | solution.py:59
  8.5 6.4 %collective-permute-start.10 = (bf16[3,24,1024]{2,1,0:T(8,128)(2,1)}, bf16[3,24,1024]{2,1,0:T(8,128)(2,1)S(1)}, u32[]{:S(2)}, u32[]{:S(2)}) collective-permute-start(bf16[3,24,1024]{2,1,0:T(8,128)(2,1)} %shard_map.59), channel_id=1, source_target_pairs={{0,2},{1,67},{2,0},{3,65},{4,6},{5,71},{6,4},{7,69},{8,10},{9,75},... | collective-permute-start | bytes 442376 | tf_op jit(solution)/shard_map/ppermute | solution.py:33
  11.2 8.2 %collective-permute-start.5 = (bf16[3,24,1024]{2,1,0:T(8,128)(2,1)S(1)}, bf16[3,24,1024]{2,1,0:T(8,128)(2,1)S(1)}, u32[]{:S(2)}, u32[]{:S(2)}) collective-permute-start(bf16[3,24,1024]{2,1,0:T(8,128)(2,1)S(1)} %collective-permute-done.2), channel_id=1, source_target_pairs={{0,18},{1,115},{2,16},{3,113},{4,22},{5,119},{6,20},{7,117},{8,26}... | collective-permute-start | bytes 442376 | tf_op jit(solution)/shard_map/ppermute | solution.py:59
  16.4 11.2 %collective-permute-start.12 = (bf16[3,96,1024]{2,1,0:T(8,128)(2,1)S(1)}, bf16[3,96,1024]{2,1,0:T(8,128)(2,1)S(1)}, u32[]{:S(2)}, u32[]{:S(2)}) collective-permute-start(bf16[3,96,1024]{2,1,0:T(8,128)(2,1)S(1)} %pad_maximum_fusion.1.refs_7_.refs_12_), channel_id=1, source_target_pairs={{0,48},{1,17},{2,50},{3,19},{4,52},{5,21},{6,54},{7,23},{8,56},{9,... | collective-permute-start | bytes 1769480 | tf_op jit(solution)/shard_map/ppermute | solution.py:33
  19.4 14.0 %collective-permute-start = (bf16[384,1024]{1,0:T(8,128)(2,1)S(1)}, bf16[384,1024]{1,0:T(8,128)(2,1)S(1)}, u32[]{:S(2)}, u32[]{:S(2)}) collective-permute-start(bf16[384,1024]{1,0:T(8,128)(2,1)S(1)} %copy-done), channel_id=1, source_target_pairs={{0,1},{1,0},{2,3},{3,2},{4,5},{5,4},{6,7},{7,6},{8,9},{9,8},{10,11... | collective-permute-start | bytes 2359304 | tf_op jit(solution)/shard_map/ppermute | solution.py:63
  19.4 16.1 %collective-permute-start.1 = (bf16[384,1024]{1,0:T(8,128)(2,1)}, bf16[384,1024]{1,0:T(8,128)(2,1)S(1)}, u32[]{:S(2)}, u32[]{:S(2)}) collective-permute-start(bf16[384,1024]{1,0:T(8,128)(2,1)} %refs_4_.1), channel_id=1, source_target_pairs={{0,1},{1,0},{2,3},{3,2},{4,5},{5,4},{6,7},{7,6},{8,9},{9,8},{10,11... | collective-permute-start | bytes 2359304 | tf_op jit(solution)/shard_map/ppermute | solution.py:63
  20.1 10.4 %collective-permute-start.8 = (bf16[3,96,1024]{2,1,0:T(8,128)(2,1)S(1)}, bf16[3,96,1024]{2,1,0:T(8,128)(2,1)S(1)}, u32[]{:S(2)}, u32[]{:S(2)}) collective-permute-start(bf16[3,96,1024]{2,1,0:T(8,128)(2,1)S(1)} %pad_maximum_fusion.refs_5_.refs_10_), channel_id=1, source_target_pairs={{0,66},{1,3},{2,64},{3,1},{4,70},{5,7},{6,68},{7,5},{8,74},{9,11},... | collective-permute-start | bytes 1769480 | tf_op jit(solution)/shard_map/ppermute | solution.py:33
  21.7 20.1 %collective-permute-start.7 = (bf16[384,1024]{1,0:T(8,128)(2,1)S(1)}, bf16[384,1024]{1,0:T(8,128)(2,1)S(1)}, u32[]{:S(2)}, u32[]{:S(2)}) collective-permute-start(bf16[384,1024]{1,0:T(8,128)(2,1)S(1)} %copy-done.1), channel_id=1, source_target_pairs={{0,4},{1,5},{2,6},{3,7},{4,0},{5,1},{6,2},{7,3},{8,12},{9,13},{10,... | collective-permute-start | bytes 2359304 | tf_op jit(solution)/shard_map/ppermute | solution.py:33
  27.5 14.3 %collective-permute-start.13 = (bf16[3,96,1024]{2,1,0:T(8,128)(2,1)S(1)}, bf16[3,96,1024]{2,1,0:T(8,128)(2,1)S(1)}, u32[]{:S(2)}, u32[]{:S(2)}) collective-permute-start(bf16[3,96,1024]{2,1,0:T(8,128)(2,1)S(1)} %pad_maximum_fusion.refs_5_.refs_10_), channel_id=1, source_target_pairs={{0,48},{1,17},{2,50},{3,19},{4,52},{5,21},{6,54},{7,23},{8,56},{9,... | collective-permute-start | bytes 1769480 | tf_op jit(solution)/shard_map/ppermute | solution.py:33
  30.6 14.4 %collective-permute-start.14 = (bf16[3,96,1024]{2,1,0:T(8,128)(2,1)S(1)}, bf16[3,96,1024]{2,1,0:T(8,128)(2,1)S(1)}, u32[]{:S(2)}, u32[]{:S(2)}) collective-permute-start(bf16[3,96,1024]{2,1,0:T(8,128)(2,1)S(1)} %collective-permute-done.8.refs_4_.refs_9_), channel_id=1, source_target_pairs={{0,48},{1,17},{2,50},{3,19},{4,52},{5,21},{6,54},{7,23},{8,56},{9,... | collective-permute-start | bytes 1769480 | tf_op jit(solution)/shard_map/ppermute | solution.py:33
  33.5 19.0 %collective-permute-start.17 = (bf16[3,192,1024]{2,1,0:T(8,128)(2,1)S(1)}, bf16[3,192,1024]{2,1,0:T(8,128)(2,1)S(1)}, u32[]{:S(2)}, u32[]{:S(2)}) collective-permute-start(bf16[3,192,1024]{2,1,0:T(8,128)(2,1)S(1)} %constant_dynamic-update-slice_fusion), channel_id=1, source_target_pairs={{0,66},{1,3},{2,64},{3,1},{4,70},{5,7},{6,68},{7,5},{8,74},{9,11},... | collective-permute-start | bytes 3538952 | tf_op jit(solution)/shard_map/ppermute | solution.py:33
  49.4 18.4 %collective-permute-start.20 = (bf16[3,192,1024]{2,1,0:T(8,128)(2,1)S(1)}, bf16[3,192,1024]{2,1,0:T(8,128)(2,1)S(1)}, u32[]{:S(2)}, u32[]{:S(2)}) collective-permute-start(bf16[3,192,1024]{2,1,0:T(8,128)(2,1)S(1)} %get-tuple-element.67), channel_id=1, source_target_pairs={{0,48},{1,17},{2,50},{3,19},{4,52},{5,21},{6,54},{7,23},{8,56},{9,... | collective-permute-start | bytes 3538952 | tf_op jit(solution)/shard_map/ppermute | solution.py:33
  56.7 16.5 %collective-permute-start.19 = (bf16[3,192,1024]{2,1,0:T(8,128)(2,1)S(1)}, bf16[3,192,1024]{2,1,0:T(8,128)(2,1)S(1)}, u32[]{:S(2)}, u32[]{:S(2)}) collective-permute-start(bf16[3,192,1024]{2,1,0:T(8,128)(2,1)S(1)} %get-tuple-element.66), channel_id=1, source_target_pairs={{0,66},{1,3},{2,64},{3,1},{4,70},{5,7},{6,68},{7,5},{8,74},{9,11},... | collective-permute-start | bytes 3538952 | tf_op jit(solution)/shard_map/ppermute | solution.py:33
  68.0 11.5 %collective-permute-start.27 = (bf16[3,96,1024]{2,1,0:T(8,128)(2,1)S(1)}, bf16[3,96,1024]{2,1,0:T(8,128)(2,1)S(1)}, u32[]{:S(2)}, u32[]{:S(2)}) collective-permute-start(bf16[3,96,1024]{2,1,0:T(8,128)(2,1)S(1)} %add_convert_fusion.3), channel_id=1, source_target_pairs={{0,66},{1,3},{2,64},{3,1},{4,70},{5,7},{6,68},{7,5},{8,74},{9,11},... | collective-permute-start | bytes 1769480 | tf_op jit(solution)/shard_map/ppermute | solution.py:33
  69.4 25.9 %collective-permute-start.18 = (bf16[384,1024]{1,0:T(8,128)(2,1)S(1)}, bf16[384,1024]{1,0:T(8,128)(2,1)S(1)}, u32[]{:S(2)}, u32[]{:S(2)}) collective-permute-start(bf16[384,1024]{1,0:T(8,128)(2,1)S(1)} %get-tuple-element.65), channel_id=1, source_target_pairs={{0,1},{1,0},{2,3},{3,2},{4,5},{5,4},{6,7},{7,6},{8,9},{9,8},{10,11... | collective-permute-start | bytes 2359304 | tf_op jit(solution)/shard_map/ppermute | solution.py:63
  73.4 14.3 %collective-permute-start.23 = (bf16[3,96,1024]{2,1,0:T(8,128)(2,1)S(1)}, bf16[3,96,1024]{2,1,0:T(8,128)(2,1)S(1)}, u32[]{:S(2)}, u32[]{:S(2)}) collective-permute-start(bf16[3,96,1024]{2,1,0:T(8,128)(2,1)S(1)} %add_convert_fusion.5), channel_id=1, source_target_pairs={{0,48},{1,17},{2,50},{3,19},{4,52},{5,21},{6,54},{7,23},{8,56},{9,... | collective-permute-start | bytes 1769480 | tf_op jit(solution)/shard_map/ppermute | solution.py:33
  74.1 22.5 %collective-permute-start.22 = (bf16[384,1024]{1,0:T(8,128)(2,1)S(1)}, bf16[384,1024]{1,0:T(8,128)(2,1)S(1)}, u32[]{:S(2)}, u32[]{:S(2)}) collective-permute-start(bf16[384,1024]{1,0:T(8,128)(2,1)S(1)} %add_convert_fusion.1), channel_id=1, source_target_pairs={{0,4},{1,5},{2,6},{3,7},{4,0},{5,1},{6,2},{7,3},{8,12},{9,13},{10,... | collective-permute-start | bytes 2359304 | tf_op jit(solution)/shard_map/ppermute | solution.py:33
  79.8 10.6 %collective-permute-start.28 = (bf16[3,24,1024]{2,1,0:T(8,128)(2,1)S(1)}, bf16[3,24,1024]{2,1,0:T(8,128)(2,1)S(1)}, u32[]{:S(2)}, u32[]{:S(2)}) collective-permute-start(bf16[3,24,1024]{2,1,0:T(8,128)(2,1)S(1)} %get-tuple-element.83), channel_id=1, source_target_pairs={{0,16},{1,49},{2,18},{3,51},{4,20},{5,53},{6,22},{7,55},{8,24},{9,... | collective-permute-start | bytes 442376 | tf_op jit(solution)/shard_map/ppermute | solution.py:33
  79.9 10.6 %collective-permute-start.30 = (bf16[3,24,1024]{2,1,0:T(8,128)(2,1)S(1)}, bf16[3,24,1024]{2,1,0:T(8,128)(2,1)S(1)}, u32[]{:S(2)}, u32[]{:S(2)}) collective-permute-start(bf16[3,24,1024]{2,1,0:T(8,128)(2,1)S(1)} %get-tuple-element.84), channel_id=1, source_target_pairs={{0,18},{1,115},{2,16},{3,113},{4,22},{5,119},{6,20},{7,117},{8,26}... | collective-permute-start | bytes 442376 | tf_op jit(solution)/shard_map/ppermute | solution.py:59
  90.4 7.5 %collective-permute-start.24 = (bf16[3,24,1024]{2,1,0:T(8,128)(2,1)S(1)}, bf16[3,24,1024]{2,1,0:T(8,128)(2,1)S(1)}, u32[]{:S(2)}, u32[]{:S(2)}) collective-permute-start(bf16[3,24,1024]{2,1,0:T(8,128)(2,1)S(1)} %get-tuple-element.80), channel_id=1, source_target_pairs={{0,16},{1,49},{2,18},{3,51},{4,20},{5,53},{6,22},{7,55},{8,24},{9,... | collective-permute-start | bytes 442376 | tf_op jit(solution)/shard_map/ppermute | solution.py:33
  90.5 7.4 %collective-permute-start.26 = (bf16[3,24,1024]{2,1,0:T(8,128)(2,1)S(1)}, bf16[3,24,1024]{2,1,0:T(8,128)(2,1)S(1)}, u32[]{:S(2)}, u32[]{:S(2)}) collective-permute-start(bf16[3,24,1024]{2,1,0:T(8,128)(2,1)S(1)} %get-tuple-element.81), channel_id=1, source_target_pairs={{0,18},{1,115},{2,16},{3,113},{4,22},{5,119},{6,20},{7,117},{8,26}... | collective-permute-start | bytes 442376 | tf_op jit(solution)/shard_map/ppermute | solution.py:59
  95.3 6.4 %collective-permute-start.31 = (bf16[3,24,1024]{2,1,0:T(8,128)(2,1)S(1)}, bf16[3,24,1024]{2,1,0:T(8,128)(2,1)S(1)}, u32[]{:S(2)}, u32[]{:S(2)}) collective-permute-start(bf16[3,24,1024]{2,1,0:T(8,128)(2,1)S(1)} %add_convert_fusion.6), channel_id=1, source_target_pairs={{0,12},{1,13},{2,14},{3,15},{4,8},{5,9},{6,10},{7,11},{8,4},{9,5},... | collective-permute-start | bytes 442376 | tf_op jit(solution)/shard_map/ppermute | solution.py:33
  (11 other events, 98.9 us)

commit v11 on v9

--- a/solution.py
+++ b/solution.py
@@ -33,12 +33,12 @@
     return lax.ppermute(value, AXES, pairs)
 
 
-def swap_first(value, axis):
-    return swap(value, axis, lambda core: core == 1)
-
-
-def swap_second(value, axis):
-    return swap(value, axis, lambda core: core == 0)
+def swap_first(value, axis, part):
+    return swap(value, axis, lambda core: (core + part) % 2 == 1)
+
+
+def swap_second(value, axis, part):
+    return swap(value, axis, lambda core: (core + part) % 2 == 0)
 
 
 def swap_near(value, axis):
@@ -49,12 +49,12 @@
     return swap(value, axis, lambda core: True)
 
 
-def swap_corner(value):
+def swap_corner(value, part):
     pairs = []
     for device in range(DEVICES):
         there = place(device)
         for axis in (X, Y):
-            there[axis] = RING - 1 - there[axis] if there[3] == 1 else there[axis] ^ 1
+            there[axis] = RING - 1 - there[axis] if (there[3] + part) % 2 == 1 else there[axis] ^ 1
         pairs.append((device, index(*there)))
     return lax.ppermute(value, AXES, pairs)
 
@@ -71,14 +71,16 @@
     return jnp.concatenate(blocks, axis=1)
 
 
-def gather_block(message):
-    return join(message, swap_first(message, Y), swap_first(message, X), swap_corner(message))
-
-
-def reduce_block(block):
+def gather_block(message, part):
+    return join(
+        message, swap_first(message, Y, part), swap_first(message, X, part), swap_corner(message, part)
+    )
+
+
+def reduce_block(block, part):
     n = block.shape[1] // 4
     own, along_y, along_x, corner = (block[:, i * n : (i + 1) * n] for i in range(4))
-    return own, swap_first(along_y, Y), swap_first(along_x, X), swap_corner(corner)
+    return own, swap_first(along_y, Y, part), swap_first(along_x, X, part), swap_corner(corner, part)
 
 
 def added(terms):
@@ -198,16 +200,17 @@
     x_z = swap_near(activations, Z)
     message = jnp.concatenate([gate_up.transpose(1, 0, 2), down_proj[None]], axis=0)
     message = lax.optimization_barrier(message)
-    block1 = gather_block(swap_wrap(message, Z))
-    o0 = gather_block(message)
+    block1 = gather_block(swap_wrap(message, Z), 1)
+    o0 = gather_block(message, 0)
     block1, c_own = lax.optimization_barrier((block1, cotangent))
     c_z = swap_near(c_own, Z)
-    o1, x_z = lax.optimization_barrier((block1, x_z))
-    n0 = swap_second(o0, Y)
-    r0 = swap_second(join(o0, n0), X)
-    n1 = swap_second(o1, X)
-    w1 = swap_second(o1, Y)
-    f1 = swap_second(n1, Y)
+    o1 = block1
+    n0 = swap_second(o0, Y, 0)
+    r0 = swap_second(join(o0, n0), X, 0)
+    n1 = swap_second(o1, X, 1)
+    o1, x_z = lax.optimization_barrier((o1, x_z))
+    w1 = swap_second(o1, Y, 1)
+    f1 = swap_second(n1, Y, 1)
     xs, cs = [activations, swap_core(activations)], [cotangent, swap_core(cotangent)]
 
     near = [n1, o1, n0, o0]
@@ -218,10 +221,10 @@
     g_r1, a_r1 = grads(xs, cs, [w1, f1], joined=2, weight=6)
 
     g_r1, a_r1_z = grads(xs_z, cs_z, [w1, f1], [g_r1], joined=2)
-    back1 = swap_second(g_r1, Y)
+    back1 = swap_second(g_r1, Y, 1)
     r0, a_r1_z = lax.optimization_barrier((r0, a_r1_z))
     g_r0, a_r0 = grads(xs + xs_z, cs + cs_z, [r0])
-    back0 = swap_second(g_r0, X)
+    back0 = swap_second(g_r0, X, 0)
     n1, a_r0 = lax.optimization_barrier((n1, a_r0))
     g_n1, g_o1, g_n0, g_o0, a_near_z = grads(xs_z, cs_z, [n1, o1, n0, o0], g_near)
     n = a_r0.shape[1] // 2
@@ -230,9 +233,9 @@
     z_got, got = swap_core(z_pair), swap_core(pair)
 
     n = g_n1.shape[1]
-    near1 = swap_second(add(g_n1, back1[:, n:]), X)
+    near1 = swap_second(add(g_n1, back1[:, n:]), X, 1)
     back0, back1 = lax.optimization_barrier((back0, back1))
-    near0 = swap_second(add(g_n0, back0[:, n:]), Y)
+    near0 = swap_second(add(g_n0, back0[:, n:]), Y, 0)
     back0, z_part = lax.optimization_barrier((back0, z_part))
     mine = own + got.astype(F32)
     z_part = swap_near((z_part + z_got.astype(F32)).astype(BF16), Z)
@@ -240,9 +243,9 @@
     def block_sum(own, back, near):
         return (own.astype(F32) + back.astype(F32) + near.astype(F32)).astype(BF16)
 
-    terms1 = reduce_block(block_sum(g_o1, back1[:, :n], near1))
+    terms1 = reduce_block(block_sum(g_o1, back1[:, :n], near1), 1)
     total1 = added(terms1).astype(BF16)
-    total0 = added(reduce_block(block_sum(g_o0, back0[:, :n], near0)))
+    total0 = added(reduce_block(block_sum(g_o0, back0[:, :n], near0), 0))
     grad_input = (mine + z_part.astype(F32)).astype(BF16)
     total = total0 + swap_wrap(total1, Z).astype(F32)
     return (grad_input, total.transpose(1, 0, 2))

time: 103 us -> 105 us (1.019)
  waiting for transfers between devices: 22.9 us -> 36.1 us
  starting transfers between devices: 51.4 us -> 39.2 us
    ppermute x22, waiting for transfers between devices: 22.3 us -> 36.1 us  [swap(): return lax.ppermute(value, AXES, pairs)]
    ppermute x22, starting transfers between devices: 39.8 us -> 30.1 us  [swap(): return lax.ppermute(value, AXES, pairs)]
    ppermute x6, starting transfers between devices: 2.4 us -> 0.79 us  [swap_core(): return lax.ppermute(value, AXES, [(d, d ^ 1) for d in range(DEVICES)])]
  transfers between devices with their start and end apart: 32 -> 32, of which waited for: 15 -> 14; matrix products, arithmetic and copies ran while one was open for 5% -> 5% of each run, Pallas kernels for 21% -> 21%
where the time goes in v11:
time: 105 us; the launch traced here: 103 us
  starting transfers between devices  39.2 us (37%)
  waiting for transfers between devices  36.1 us (34%)
  Pallas kernels  21.8 us (21%)
  other arithmetic  4.33 us (4%)
  local copies, waits for them, and re-layouts  1.14 us (1%)
    ppermute x22, waiting for transfers between devices, swap(): return lax.ppermute(value, AXES, pairs)  36.1 us
    ppermute x22, starting transfers between devices, swap(): return lax.ppermute(value, AXES, pairs)  30.1 us
    pallas_call x5, Pallas kernels, grads(): pl.pallas_call(kernel, out_shape=[jax.ShapeDtypeStruct((3, joined * units...  16.7 us
    ppermute x4, starting transfers between devices, swap_corner(): return lax.ppermute(value, AXES, pairs)  8.22 us
    pallas_call x1, Pallas kernels, input_parts(): pl.pallas_call(kernel, out_shape=[jax.ShapeDtypeStruct((group, width), ki...  5.06 us
  transfers between devices with their start and end apart: 32, of which 14 were waited for; matrix products, arithmetic and copies ran while one was open for 5% of the time, Pallas kernels for 21%

profile of v11, /device:TPU:2, one launch (start us, length us, event | category | flops | bytes accessed | tf_op | source)
XLA Modules:
  0.0 103.4 jit_solution(323560686722012451)
XLA Ops:
  0.6 2.0 %collective-permute-start.6 = (bf16[384,1024]{1,0:T(8,128)(2,1)}, bf16[384,1024]{1,0:T(8,128)(2,1)S(1)}, u32[]{:S(2)}, u32[]{:S(2)}) collective-permute-start(bf16[384,1024]{1,0:T(8,128)(2,1)} %refs_0_.5), channel_id=1, source_target_pairs={{0,4},{1,5},{2,6},{3,7},{4,0},{5,1},{6,2},{7,3},{8,12},{9,13},{10,... | collective-permute-start | bytes 2359304 | tf_op jit(solution)/shard_map/ppermute | solution.py:33
  4.4 2.6 %collective-permute-start.2 = (bf16[3,24,1024]{2,1,0:T(8,128)(2,1)S(1)}, bf16[3,24,1024]{2,1,0:T(8,128)(2,1)S(1)}, u32[]{:S(2)}, u32[]{:S(2)}) collective-permute-start(bf16[3,24,1024]{2,1,0:T(8,128)(2,1)S(1)} %pad_maximum_fusion.2), channel_id=1, source_target_pairs={{0,12},{1,13},{2,14},{3,15},{4,8},{5,9},{6,10},{7,11},{8,4},{9,5},... | collective-permute-start | bytes 442376 | tf_op jit(solution)/shard_map/ppermute | solution.py:33
  11.0 3.9 %collective-permute-start.5 = (bf16[3,24,1024]{2,1,0:T(8,128)(2,1)S(1)}, bf16[3,24,1024]{2,1,0:T(8,128)(2,1)S(1)}, u32[]{:S(2)}, u32[]{:S(2)}) collective-permute-start(bf16[3,24,1024]{2,1,0:T(8,128)(2,1)S(1)} %collective-permute-done.2), channel_id=1, source_target_pairs={{0,114},{1,19},{2,112},{3,17},{4,118},{5,23},{6,116},{7,21},{8,122... | collective-permute-start | bytes 442376 | tf_op jit(solution)/shard_map/ppermute | solution.py:59
  16.1 1.8 %collective-permute-start.3 = (bf16[3,24,1024]{2,1,0:T(8,128)(2,1)S(1)}, bf16[3,24,1024]{2,1,0:T(8,128)(2,1)S(1)}, u32[]{:S(2)}, u32[]{:S(2)}) collective-permute-start(bf16[3,24,1024]{2,1,0:T(8,128)(2,1)S(1)} %collective-permute-done.2), channel_id=1, source_target_pairs={{0,48},{1,17},{2,50},{3,19},{4,52},{5,21},{6,54},{7,23},{8,56},{9,... | collective-permute-start | bytes 442376 | tf_op jit(solution)/shard_map/ppermute | solution.py:33
  20.2 2.3 %collective-permute-done.3 = bf16[3,24,1024]{2,1,0:T(8,128)(2,1)S(1)} collective-permute-done((bf16[3,24,1024]{2,1,0:T(8,128)(2,1)S(1)}, bf16[3,24,1024]{2,1,0:T(8,128)(2,1)S(1)}, u32[]{:S(2)}, u32[]{:S(2)}) %collective-permute-start.3) | collective-permute-done | bytes 147488 | tf_op jit(solution)/shard_map/ppermute | solution.py:33
  24.3 4.8 %collective-permute-done.12.refs_6_.refs_11_ = bf16[3,96,1024]{2,1,0:T(8,128)(2,1)S(1)} collective-permute-done((bf16[3,96,1024]{2,1,0:T(8,128)(2,1)S(1)}, bf16[3,96,1024]{2,1,0:T(8,128)(2,1)S(1)}, u32[]{:S(2)}, u32[]{:S(2)}) %collective-permute-start.12) | collective-permute-done | bytes 589856 | tf_op jit(solution)/shard_map/ppermute | solution.py:33
  29.2 3.3 %collective-permute-done.8.refs_4_.refs_9_ = bf16[3,96,1024]{2,1,0:T(8,128)(2,1)S(1)} collective-permute-done((bf16[3,96,1024]{2,1,0:T(8,128)(2,1)S(1)}, bf16[3,96,1024]{2,1,0:T(8,128)(2,1)S(1)}, u32[]{:S(2)}, u32[]{:S(2)}) %collective-permute-start.8) | collective-permute-done | bytes 589856 | tf_op jit(solution)/shard_map/ppermute | solution.py:33
  33.8 4.0 %shard_map.59 = (bf16[3,96,1024]{2,1,0:T(8,128)(2,1)S(1)}, bf16[3,96,1024]{2,1,0:T(8,128)(2,1)S(1)}, bf16[3,96,1024]{2,1,0:T(8,128)(2,1)S(1)}, bf16[3,96,1024]{2,1,0:T(8,128)(2,1)S(1)}, bf16[768,768]{1,0:T(8,128)(2,1)S(1)}) custom-call(bf16[384,1024]{1,0:T(8,128)(2,1)S(1)} %copy-done, bf16[384,1024]{1,0:T(8,128)(2,1)S(1)} %collective-permute-done.refs_1_, ...), custom_call_target="tpu_custom_call" | custom-call | flops 3000001024 | bytes 1024 | tf_op jit(solution)/shard_map/pallas_call | solution.py:150
  37.9 3.6 %collective-permute-done.7.refs_2_.refs_6_ = bf16[384,1024]{1,0:T(8,128)(2,1)S(1)} collective-permute-done((bf16[384,1024]{1,0:T(8,128)(2,1)S(1)}, bf16[384,1024]{1,0:T(8,128)(2,1)S(1)}, u32[]{:S(2)}, u32[]{:S(2)}) %collective-permute-start.7) | collective-permute-done | bytes 786464 | tf_op jit(solution)/shard_map/ppermute | solution.py:33
  42.0 3.3 %collective-permute-done.14.refs_5_.refs_7_ = bf16[3,96,1024]{2,1,0:T(8,128)(2,1)S(1)} collective-permute-done((bf16[3,96,1024]{2,1,0:T(8,128)(2,1)S(1)}, bf16[3,96,1024]{2,1,0:T(8,128)(2,1)S(1)}, u32[]{:S(2)}, u32[]{:S(2)}) %collective-permute-start.14) | collective-permute-done | bytes 589856 | tf_op jit(solution)/shard_map/ppermute | solution.py:33
  45.3 2.2 %shard_map.60 = (bf16[3,192,1024]{2,1,0:T(8,128)(2,1)S(1)}, bf16[384,768]{1,0:T(8,128)(2,1)S(1)}) custom-call(bf16[384,1024]{1,0:T(8,128)(2,1)S(1)} %copy-done, bf16[384,1024]{1,0:T(8,128)(2,1)S(1)} %collective-permute-done.refs_1_, bf16[384,1024]{1,0:T(8,128)(2,1)S(1)} %copy-done.1, bf16[384,1024]{1,0:T(8,128)(2,1)S(1)} %collective-permute-done.1.refs_3_.refs_5_, ...), custom_call_target="tpu_custom_call" | custom-call | flops 6000001024 | bytes 1024 | tf_op jit(solution)/shard_map/pallas_call | solution.py:150
  47.6 2.2 %shard_map.61 = (bf16[3,192,1024]{2,1,0:T(8,128)(2,1)S(1)}, bf16[384,768]{1,0:T(8,128)(2,1)S(1)}) custom-call(bf16[384,1024]{1,0:T(8,128)(2,1)S(1)} %collective-permute-done.6.refs_0_.refs_2_, bf16[384,1024]{1,0:T(8,128)(2,1)S(1)} %collective-permute-done.15.refs_1_.refs_3_, bf16[384,1024]{1,0:T(8,128)(2,1)S(1)} %collective-permute-done.7.refs_2_.refs_6_, ...), custom_call_target="tpu_custom_call" | custom-call | flops 1024 | bytes 1024 | tf_op jit(solution)/shard_map/pallas_call | solution.py:150
  49.9 4.2 %shard_map.62 = (bf16[3,192,1024]{2,1,0:T(8,128)(2,1)S(1)}, bf16[384,1536]{1,0:T(8,128)(2,1)S(1)}) custom-call(bf16[384,1024]{1,0:T(8,128)(2,1)S(1)} %copy-done, bf16[384,1024]{1,0:T(8,128)(2,1)S(1)} %collective-permute-done.refs_1_, bf16[384,1024]{1,0:T(8,128)(2,1)S(1)} %collective-permute-done.6.refs_0_.refs_2_, ...), custom_call_target="tpu_custom_call" | custom-call | flops 1024 | bytes 1024 | tf_op jit(solution)/shard_map/pallas_call | solution.py:150
  55.3 4.1 %shard_map.63 = (bf16[3,96,1024]{2,1,0:T(8,128)(2,1)S(1)}, bf16[3,96,1024]{2,1,0:T(8,128)(2,1)S(1)}, bf16[3,96,1024]{2,1,0:T(8,128)(2,1)S(1)}, bf16[3,96,1024]{2,1,0:T(8,128)(2,1)S(1)}, bf16[768,768]{1,0:T(8,128)(2,1)S(1)}) custom-call(bf16[384,1024]{1,0:T(8,128)(2,1)S(1)} %collective-permute-done.6.refs_0_.refs_2_, ...), custom_call_target="tpu_custom_call" | custom-call | flops 1024 | bytes 1024 | tf_op jit(solution)/shard_map/pallas_call | solution.py:150
  59.4 5.1 %shard_map.64 = (f32[384,1024]{1,0:T(8,128)S(1)}, bf16[384,1024]{1,0:T(8,128)(2,1)S(1)}, f32[384,1024]{1,0:T(8,128)S(1)}, bf16[384,1024]{1,0:T(8,128)(2,1)S(1)}) custom-call(bf16[384,768]{1,0:T(8,128)(2,1)S(1)} %get-tuple-element.48.refs_0_, bf16[384,768]{1,0:T(8,128)(2,1)S(1)} %get-tuple-element.79.refs_1_, bf16[768,768]{1,0:T(8,128)(2,1)S(1)} %get-tuple-element.56.refs_2_, ...), custom_call_target="tpu_custom_call" | custom-call | flops 1024 | bytes 1024 | tf_op jit(solution)/shard_map/pallas_call | solution.py:185
  66.3 1.7 %collective-permute-start.27 = (bf16[3,96,1024]{2,1,0:T(8,128)(2,1)S(1)}, bf16[3,96,1024]{2,1,0:T(8,128)(2,1)S(1)}, u32[]{:S(2)}, u32[]{:S(2)}) collective-permute-start(bf16[3,96,1024]{2,1,0:T(8,128)(2,1)S(1)} %add_convert_fusion.3), channel_id=1, source_target_pairs={{0,2},{1,67},{2,0},{3,65},{4,6},{5,71},{6,4},{7,69},{8,10},{9,75},... | collective-permute-start | bytes 1769480 | tf_op jit(solution)/shard_map/ppermute | solution.py:33
  68.0 5.1 %collective-permute-done.19 = bf16[3,192,1024]{2,1,0:T(8,128)(2,1)S(1)} collective-permute-done((bf16[3,192,1024]{2,1,0:T(8,128)(2,1)S(1)}, bf16[3,192,1024]{2,1,0:T(8,128)(2,1)S(1)}, u32[]{:S(2)}, u32[]{:S(2)}) %collective-permute-start.19) | collective-permute-done | bytes 1179680 | tf_op jit(solution)/shard_map/ppermute | solution.py:33
  76.6 2.3 %collective-permute-start.28 = (bf16[3,24,1024]{2,1,0:T(8,128)(2,1)S(1)}, bf16[3,24,1024]{2,1,0:T(8,128)(2,1)S(1)}, u32[]{:S(2)}, u32[]{:S(2)}) collective-permute-start(bf16[3,24,1024]{2,1,0:T(8,128)(2,1)S(1)} %get-tuple-element.83), channel_id=1, source_target_pairs={{0,48},{1,17},{2,50},{3,19},{4,52},{5,21},{6,54},{7,23},{8,56},{9,... | collective-permute-start | bytes 442376 | tf_op jit(solution)/shard_map/ppermute | solution.py:33
  78.9 2.1 %collective-permute-start.30 = (bf16[3,24,1024]{2,1,0:T(8,128)(2,1)S(1)}, bf16[3,24,1024]{2,1,0:T(8,128)(2,1)S(1)}, u32[]{:S(2)}, u32[]{:S(2)}) collective-permute-start(bf16[3,24,1024]{2,1,0:T(8,128)(2,1)S(1)} %get-tuple-element.84), channel_id=1, source_target_pairs={{0,114},{1,19},{2,112},{3,17},{4,118},{5,23},{6,116},{7,21},{8,122... | collective-permute-start | bytes 442376 | tf_op jit(solution)/shard_map/ppermute | solution.py:59
  81.0 3.5 %collective-permute-done.23 = bf16[3,96,1024]{2,1,0:T(8,128)(2,1)S(1)} collective-permute-done((bf16[3,96,1024]{2,1,0:T(8,128)(2,1)S(1)}, bf16[3,96,1024]{2,1,0:T(8,128)(2,1)S(1)}, u32[]{:S(2)}, u32[]{:S(2)}) %collective-permute-start.23) | collective-permute-done | bytes 589856 | tf_op jit(solution)/shard_map/ppermute | solution.py:33
  85.5 4.8 %collective-permute-done.28 = bf16[3,24,1024]{2,1,0:T(8,128)(2,1)S(1)} collective-permute-done((bf16[3,24,1024]{2,1,0:T(8,128)(2,1)S(1)}, bf16[3,24,1024]{2,1,0:T(8,128)(2,1)S(1)}, u32[]{:S(2)}, u32[]{:S(2)}) %collective-permute-start.28) | collective-permute-done | bytes 147488 | tf_op jit(solution)/shard_map/ppermute | solution.py:33
  92.3 1.9 %collective-permute-start.25 = (bf16[3,24,1024]{2,1,0:T(8,128)(2,1)S(1)}, bf16[3,24,1024]{2,1,0:T(8,128)(2,1)S(1)}, u32[]{:S(2)}, u32[]{:S(2)}) collective-permute-start(bf16[3,24,1024]{2,1,0:T(8,128)(2,1)S(1)} %get-tuple-element.82), channel_id=1, source_target_pairs={{0,2},{1,67},{2,0},{3,65},{4,6},{5,71},{6,4},{7,69},{8,10},{9,75},... | collective-permute-start | bytes 442376 | tf_op jit(solution)/shard_map/ppermute | solution.py:33
  94.2 5.3 %collective-permute-start.31 = (bf16[3,24,1024]{2,1,0:T(8,128)(2,1)S(1)}, bf16[3,24,1024]{2,1,0:T(8,128)(2,1)S(1)}, u32[]{:S(2)}, u32[]{:S(2)}) collective-permute-start(bf16[3,24,1024]{2,1,0:T(8,128)(2,1)S(1)} %add_convert_fusion.6), channel_id=1, source_target_pairs={{0,12},{1,13},{2,14},{3,15},{4,8},{5,9},{6,10},{7,11},{8,4},{9,5},... | collective-permute-start | bytes 442376 | tf_op jit(solution)/shard_map/ppermute | solution.py:33
  100.8 1.9 %collective-permute-done.31 = bf16[3,24,1024]{2,1,0:T(8,128)(2,1)S(1)} collective-permute-done((bf16[3,24,1024]{2,1,0:T(8,128)(2,1)S(1)}, bf16[3,24,1024]{2,1,0:T(8,128)(2,1)S(1)}, u32[]{:S(2)}, u32[]{:S(2)}) %collective-permute-start.31) | collective-permute-done | bytes 147488 | tf_op jit(solution)/shard_map/ppermute | solution.py:33
  (70 shorter events, 24.6 us)
Async XLA Ops:
  0.6 23.0 %collective-permute-start.6 = (bf16[384,1024]{1,0:T(8,128)(2,1)}, bf16[384,1024]{1,0:T(8,128)(2,1)S(1)}, u32[]{:S(2)}, u32[]{:S(2)}) collective-permute-start(bf16[384,1024]{1,0:T(8,128)(2,1)} %refs_0_.5), channel_id=1, source_target_pairs={{0,4},{1,5},{2,6},{3,7},{4,0},{5,1},{6,2},{7,3},{8,12},{9,13},{10,... | collective-permute-start | bytes 2359304 | tf_op jit(solution)/shard_map/ppermute | solution.py:33
  7.0 7.9 %collective-permute-start.11 = (bf16[3,24,1024]{2,1,0:T(8,128)(2,1)S(1)}, bf16[3,24,1024]{2,1,0:T(8,128)(2,1)S(1)}, u32[]{:S(2)}, u32[]{:S(2)}) collective-permute-start(bf16[3,24,1024]{2,1,0:T(8,128)(2,1)S(1)} %pad_maximum_fusion.2), channel_id=1, source_target_pairs={{0,18},{1,115},{2,16},{3,113},{4,22},{5,119},{6,20},{7,117},{8,26}... | collective-permute-start | bytes 442376 | tf_op jit(solution)/shard_map/ppermute | solution.py:59
  11.0 8.5 %collective-permute-start.5 = (bf16[3,24,1024]{2,1,0:T(8,128)(2,1)S(1)}, bf16[3,24,1024]{2,1,0:T(8,128)(2,1)S(1)}, u32[]{:S(2)}, u32[]{:S(2)}) collective-permute-start(bf16[3,24,1024]{2,1,0:T(8,128)(2,1)S(1)} %collective-permute-done.2), channel_id=1, source_target_pairs={{0,114},{1,19},{2,112},{3,17},{4,118},{5,23},{6,116},{7,21},{8,122... | collective-permute-start | bytes 442376 | tf_op jit(solution)/shard_map/ppermute | solution.py:59
  17.9 11.2 %collective-permute-start.12 = (bf16[3,96,1024]{2,1,0:T(8,128)(2,1)S(1)}, bf16[3,96,1024]{2,1,0:T(8,128)(2,1)S(1)}, u32[]{:S(2)}, u32[]{:S(2)}) collective-permute-start(bf16[3,96,1024]{2,1,0:T(8,128)(2,1)S(1)} %pad_maximum_fusion.1.refs_7_.refs_12_), channel_id=1, source_target_pairs={{0,48},{1,17},{2,50},{3,19},{4,52},{5,21},{6,54},{7,23},{8,56},{9,... | collective-permute-start | bytes 1769480 | tf_op jit(solution)/shard_map/ppermute | solution.py:33
  19.5 13.0 %collective-permute-start = (bf16[384,1024]{1,0:T(8,128)(2,1)S(1)}, bf16[384,1024]{1,0:T(8,128)(2,1)S(1)}, u32[]{:S(2)}, u32[]{:S(2)}) collective-permute-start(bf16[384,1024]{1,0:T(8,128)(2,1)S(1)} %copy-done), channel_id=1, source_target_pairs={{0,1},{1,0},{2,3},{3,2},{4,5},{5,4},{6,7},{7,6},{8,9},{9,8},{10,11... | collective-permute-start | bytes 2359304 | tf_op jit(solution)/shard_map/ppermute | solution.py:63
  20.2 13.7 %collective-permute-start.1 = (bf16[384,1024]{1,0:T(8,128)(2,1)S(1)}, bf16[384,1024]{1,0:T(8,128)(2,1)S(1)}, u32[]{:S(2)}, u32[]{:S(2)}) collective-permute-start(bf16[384,1024]{1,0:T(8,128)(2,1)S(1)} %copy-done.1), channel_id=1, source_target_pairs={{0,1},{1,0},{2,3},{3,2},{4,5},{5,4},{6,7},{7,6},{8,9},{9,8},{10,11... | collective-permute-start | bytes 2359304 | tf_op jit(solution)/shard_map/ppermute | solution.py:63
  22.5 10.0 %collective-permute-start.8 = (bf16[3,96,1024]{2,1,0:T(8,128)(2,1)S(1)}, bf16[3,96,1024]{2,1,0:T(8,128)(2,1)S(1)}, u32[]{:S(2)}, u32[]{:S(2)}) collective-permute-start(bf16[3,96,1024]{2,1,0:T(8,128)(2,1)S(1)} %pad_maximum_fusion.refs_5_.refs_10_), channel_id=1, source_target_pairs={{0,2},{1,67},{2,0},{3,65},{4,6},{5,71},{6,4},{7,69},{8,10},{9,75},... | collective-permute-start | bytes 1769480 | tf_op jit(solution)/shard_map/ppermute | solution.py:33
  23.7 17.8 %collective-permute-start.7 = (bf16[384,1024]{1,0:T(8,128)(2,1)S(1)}, bf16[384,1024]{1,0:T(8,128)(2,1)S(1)}, u32[]{:S(2)}, u32[]{:S(2)}) collective-permute-start(bf16[384,1024]{1,0:T(8,128)(2,1)S(1)} %copy-done.1), channel_id=1, source_target_pairs={{0,4},{1,5},{2,6},{3,7},{4,0},{5,1},{6,2},{7,3},{8,12},{9,13},{10,... | collective-permute-start | bytes 2359304 | tf_op jit(solution)/shard_map/ppermute | solution.py:33
  29.1 12.3 %collective-permute-start.13 = (bf16[3,96,1024]{2,1,0:T(8,128)(2,1)S(1)}, bf16[3,96,1024]{2,1,0:T(8,128)(2,1)S(1)}, u32[]{:S(2)}, u32[]{:S(2)}) collective-permute-start(bf16[3,96,1024]{2,1,0:T(8,128)(2,1)S(1)} %pad_maximum_fusion.refs_5_.refs_10_), channel_id=1, source_target_pairs={{0,16},{1,49},{2,18},{3,51},{4,20},{5,53},{6,22},{7,55},{8,24},{9,... | collective-permute-start | bytes 1769480 | tf_op jit(solution)/shard_map/ppermute | solution.py:33
  32.5 12.8 %collective-permute-start.14 = (bf16[3,96,1024]{2,1,0:T(8,128)(2,1)S(1)}, bf16[3,96,1024]{2,1,0:T(8,128)(2,1)S(1)}, u32[]{:S(2)}, u32[]{:S(2)}) collective-permute-start(bf16[3,96,1024]{2,1,0:T(8,128)(2,1)S(1)} %collective-permute-done.8.refs_4_.refs_9_), channel_id=1, source_target_pairs={{0,16},{1,49},{2,18},{3,51},{4,20},{5,53},{6,22},{7,55},{8,24},{9,... | collective-permute-start | bytes 1769480 | tf_op jit(solution)/shard_map/ppermute | solution.py:33
  32.6 17.3 %collective-permute-start.17 = (bf16[3,192,1024]{2,1,0:T(8,128)(2,1)S(1)}, bf16[3,192,1024]{2,1,0:T(8,128)(2,1)S(1)}, u32[]{:S(2)}, u32[]{:S(2)}) collective-permute-start(bf16[3,192,1024]{2,1,0:T(8,128)(2,1)S(1)} %constant_dynamic-update-slice_fusion), channel_id=1, source_target_pairs={{0,66},{1,3},{2,64},{3,1},{4,70},{5,7},{6,68},{7,5},{8,74},{9,11},... | collective-permute-start | bytes 3538952 | tf_op jit(solution)/shard_map/ppermute | solution.py:33
  49.8 16.3 %collective-permute-start.20 = (bf16[3,192,1024]{2,1,0:T(8,128)(2,1)S(1)}, bf16[3,192,1024]{2,1,0:T(8,128)(2,1)S(1)}, u32[]{:S(2)}, u32[]{:S(2)}) collective-permute-start(bf16[3,192,1024]{2,1,0:T(8,128)(2,1)S(1)} %get-tuple-element.67), channel_id=1, source_target_pairs={{0,16},{1,49},{2,18},{3,51},{4,20},{5,53},{6,22},{7,55},{8,24},{9,... | collective-permute-start | bytes 3538952 | tf_op jit(solution)/shard_map/ppermute | solution.py:33
  54.1 19.0 %collective-permute-start.19 = (bf16[3,192,1024]{2,1,0:T(8,128)(2,1)S(1)}, bf16[3,192,1024]{2,1,0:T(8,128)(2,1)S(1)}, u32[]{:S(2)}, u32[]{:S(2)}) collective-permute-start(bf16[3,192,1024]{2,1,0:T(8,128)(2,1)S(1)} %get-tuple-element.66), channel_id=1, source_target_pairs={{0,66},{1,3},{2,64},{3,1},{4,70},{5,7},{6,68},{7,5},{8,74},{9,11},... | collective-permute-start | bytes 3538952 | tf_op jit(solution)/shard_map/ppermute | solution.py:33
  64.5 9.9 %collective-permute-start.21 = (bf16[384,1024]{1,0:T(8,128)(2,1)S(1)}, bf16[384,1024]{1,0:T(8,128)(2,1)S(1)}, u32[]{:S(2)}, u32[]{:S(2)}) collective-permute-start(bf16[384,1024]{1,0:T(8,128)(2,1)S(1)} %get-tuple-element.71), channel_id=1, source_target_pairs={{0,1},{1,0},{2,3},{3,2},{4,5},{5,4},{6,7},{7,6},{8,9},{9,8},{10,11... | collective-permute-start | bytes 2359304 | tf_op jit(solution)/shard_map/ppermute | solution.py:63
  66.3 10.0 %collective-permute-start.27 = (bf16[3,96,1024]{2,1,0:T(8,128)(2,1)S(1)}, bf16[3,96,1024]{2,1,0:T(8,128)(2,1)S(1)}, u32[]{:S(2)}, u32[]{:S(2)}) collective-permute-start(bf16[3,96,1024]{2,1,0:T(8,128)(2,1)S(1)} %add_convert_fusion.3), channel_id=1, source_target_pairs={{0,2},{1,67},{2,0},{3,65},{4,6},{5,71},{6,4},{7,69},{8,10},{9,75},... | collective-permute-start | bytes 1769480 | tf_op jit(solution)/shard_map/ppermute | solution.py:33
  68.0 26.2 %collective-permute-start.18 = (bf16[384,1024]{1,0:T(8,128)(2,1)S(1)}, bf16[384,1024]{1,0:T(8,128)(2,1)S(1)}, u32[]{:S(2)}, u32[]{:S(2)}) collective-permute-start(bf16[384,1024]{1,0:T(8,128)(2,1)S(1)} %get-tuple-element.65), channel_id=1, source_target_pairs={{0,1},{1,0},{2,3},{3,2},{4,5},{5,4},{6,7},{7,6},{8,9},{9,8},{10,11... | collective-permute-start | bytes 2359304 | tf_op jit(solution)/shard_map/ppermute | solution.py:63
  73.3 11.2 %collective-permute-start.23 = (bf16[3,96,1024]{2,1,0:T(8,128)(2,1)S(1)}, bf16[3,96,1024]{2,1,0:T(8,128)(2,1)S(1)}, u32[]{:S(2)}, u32[]{:S(2)}) collective-permute-start(bf16[3,96,1024]{2,1,0:T(8,128)(2,1)S(1)} %add_convert_fusion.5), channel_id=1, source_target_pairs={{0,48},{1,17},{2,50},{3,19},{4,52},{5,21},{6,54},{7,23},{8,56},{9,... | collective-permute-start | bytes 1769480 | tf_op jit(solution)/shard_map/ppermute | solution.py:33
  74.7 24.8 %collective-permute-start.22 = (bf16[384,1024]{1,0:T(8,128)(2,1)S(1)}, bf16[384,1024]{1,0:T(8,128)(2,1)S(1)}, u32[]{:S(2)}, u32[]{:S(2)}) collective-permute-start(bf16[384,1024]{1,0:T(8,128)(2,1)S(1)} %add_convert_fusion.1), channel_id=1, source_target_pairs={{0,4},{1,5},{2,6},{3,7},{4,0},{5,1},{6,2},{7,3},{8,12},{9,13},{10,... | collective-permute-start | bytes 2359304 | tf_op jit(solution)/shard_map/ppermute | solution.py:33
  76.6 13.7 %collective-permute-start.28 = (bf16[3,24,1024]{2,1,0:T(8,128)(2,1)S(1)}, bf16[3,24,1024]{2,1,0:T(8,128)(2,1)S(1)}, u32[]{:S(2)}, u32[]{:S(2)}) collective-permute-start(bf16[3,24,1024]{2,1,0:T(8,128)(2,1)S(1)} %get-tuple-element.83), channel_id=1, source_target_pairs={{0,48},{1,17},{2,50},{3,19},{4,52},{5,21},{6,54},{7,23},{8,56},{9,... | collective-permute-start | bytes 442376 | tf_op jit(solution)/shard_map/ppermute | solution.py:33
  78.9 12.7 %collective-permute-start.30 = (bf16[3,24,1024]{2,1,0:T(8,128)(2,1)S(1)}, bf16[3,24,1024]{2,1,0:T(8,128)(2,1)S(1)}, u32[]{:S(2)}, u32[]{:S(2)}) collective-permute-start(bf16[3,24,1024]{2,1,0:T(8,128)(2,1)S(1)} %get-tuple-element.84), channel_id=1, source_target_pairs={{0,114},{1,19},{2,112},{3,17},{4,118},{5,23},{6,116},{7,21},{8,122... | collective-permute-start | bytes 442376 | tf_op jit(solution)/shard_map/ppermute | solution.py:59
  90.3 10.5 %collective-permute-start.24 = (bf16[3,24,1024]{2,1,0:T(8,128)(2,1)S(1)}, bf16[3,24,1024]{2,1,0:T(8,128)(2,1)S(1)}, u32[]{:S(2)}, u32[]{:S(2)}) collective-permute-start(bf16[3,24,1024]{2,1,0:T(8,128)(2,1)S(1)} %get-tuple-element.80), channel_id=1, source_target_pairs={{0,16},{1,49},{2,18},{3,51},{4,20},{5,53},{6,22},{7,55},{8,24},{9,... | collective-permute-start | bytes 442376 | tf_op jit(solution)/shard_map/ppermute | solution.py:33
  91.6 9.1 %collective-permute-start.26 = (bf16[3,24,1024]{2,1,0:T(8,128)(2,1)S(1)}, bf16[3,24,1024]{2,1,0:T(8,128)(2,1)S(1)}, u32[]{:S(2)}, u32[]{:S(2)}) collective-permute-start(bf16[3,24,1024]{2,1,0:T(8,128)(2,1)S(1)} %get-tuple-element.81), channel_id=1, source_target_pairs={{0,18},{1,115},{2,16},{3,113},{4,22},{5,119},{6,20},{7,117},{8,26}... | collective-permute-start | bytes 442376 | tf_op jit(solution)/shard_map/ppermute | solution.py:59
  92.3 8.5 %collective-permute-start.25 = (bf16[3,24,1024]{2,1,0:T(8,128)(2,1)S(1)}, bf16[3,24,1024]{2,1,0:T(8,128)(2,1)S(1)}, u32[]{:S(2)}, u32[]{:S(2)}) collective-permute-start(bf16[3,24,1024]{2,1,0:T(8,128)(2,1)S(1)} %get-tuple-element.82), channel_id=1, source_target_pairs={{0,2},{1,67},{2,0},{3,65},{4,6},{5,71},{6,4},{7,69},{8,10},{9,75},... | collective-permute-start | bytes 442376 | tf_op jit(solution)/shard_map/ppermute | solution.py:33
  94.2 8.4 %collective-permute-start.31 = (bf16[3,24,1024]{2,1,0:T(8,128)(2,1)S(1)}, bf16[3,24,1024]{2,1,0:T(8,128)(2,1)S(1)}, u32[]{:S(2)}, u32[]{:S(2)}) collective-permute-start(bf16[3,24,1024]{2,1,0:T(8,128)(2,1)S(1)} %add_convert_fusion.6), channel_id=1, source_target_pairs={{0,12},{1,13},{2,14},{3,15},{4,8},{5,9},{6,10},{7,11},{8,4},{9,5},... | collective-permute-start | bytes 442376 | tf_op jit(solution)/shard_map/ppermute | solution.py:33
  (10 other events, 92.0 us)

commit v12 on v4

--- a/solution.py
+++ b/solution.py
@@ -82,9 +82,8 @@
     return total + swap_first(along_x, X).astype(F32) + swap_corner(corner).astype(F32)
 
 
-def halve(both, axis):
-    n = both.shape[1] // 2
-    return add(both[:, :n], swap_second(both[:, n:], axis))
+def summed(own, back, near):
+    return (own.astype(F32) + back.astype(F32) + near.astype(F32)).astype(BF16)
 
 
 def rows_of(refs, start, stop, cols=slice(None)):
@@ -200,13 +199,15 @@
 def body(activations, cotangent, gate_up, down_proj):
     x_z = swap_near(activations, Z)
     message = jnp.concatenate([gate_up.transpose(1, 0, 2), down_proj[None]], axis=0)
+    message = lax.optimization_barrier(message)
     other = swap_wrap(message, Z)
     block0 = gather_block(message)
     block1 = gather_block(other)
-    block1, x_z, c_own = lax.optimization_barrier((block1, x_z, cotangent))
+    block1, c_own = lax.optimization_barrier((block1, cotangent))
+    gated, x_z = lax.optimization_barrier((block1, x_z))
     c_z = swap_near(c_own, Z)
     j0 = join(block0, swap_second(block0, Y))
-    j1 = join(block1, swap_second(block1, X))
+    j1 = join(block1, swap_second(gated, X))
     r0, r1 = swap_second(j0, X), swap_second(j1, Y)
     xs = [activations, swap_core(activations), x_z, swap_core(x_z)]
     cs = [cotangent, swap_core(cotangent), c_z, swap_core(c_z)]
@@ -220,15 +221,15 @@
 
     own, z_part, pair = input_parts([a_r0, a_r1, a_j], [r0, r1, j0, j1])
     got = swap_core(pair)
-    near0, near1 = add(g_j0, back0), add(g_j1, back1)
-    near0, near1, z_part = lax.optimization_barrier((near0, near1, z_part))
+    n = back0.shape[1] // 2
+    give0, give1 = add(g_j0[:, n:], back0[:, n:]), add(g_j1[:, n:], back1[:, n:])
+    give0, give1, z_part = lax.optimization_barrier((give0, give1, z_part))
     mine = own + got[0].astype(F32)
     z_part = swap_near((z_part + got[1].astype(F32)).astype(BF16), Z)
 
-    total1 = reduce_block(halve(near1, X)).astype(BF16)
-    total1, z_part = lax.optimization_barrier((total1, z_part))
+    total1 = reduce_block(summed(g_j1[:, :n], back1[:, :n], swap_second(give1, X))).astype(BF16)
     grad_input = (mine + z_part.astype(F32)).astype(BF16)
-    total0 = reduce_block(halve(near0, Y))
+    total0 = reduce_block(summed(g_j0[:, :n], back0[:, :n], swap_second(give0, Y)))
     total = total0 + swap_wrap(total1, Z).astype(F32)
     return (grad_input, total.transpose(1, 0, 2))
 

time: 103 us -> 104 us (level)
  waiting for transfers between devices: 24.5 us -> 26.8 us
  other arithmetic: 5.5 us -> 4.34 us
    ppermute x4, starting transfers between devices: 5.68 us -> 11.8 us  [swap_corner(): return lax.ppermute(value, AXES, pairs)]
    ppermute x21, starting transfers between devices: 40.2 us -> 35.8 us  [swap(): return lax.ppermute(value, AXES, pairs)]
    ppermute x5, waiting for transfers between devices: 0.6 us -> 2.28 us  [swap_core(): return lax.ppermute(value, AXES, [(d, d ^ 1) for d in range(DEVICES)])]
    ppermute x5, starting transfers between devices: 2.24 us -> 0.68 us  [swap_core(): return lax.ppermute(value, AXES, [(d, d ^ 1) for d in range(DEVICES)])]
  transfers between devices with their start and end apart: 30 -> 30, of which waited for: 14 -> 14; matrix products, arithmetic and copies ran while one was open for 6% -> 4% of each run, Pallas kernels for 21% -> 21%
where the time goes in v12:
time: 104 us; the launch traced here: 103 us
  starting transfers between devices  48.3 us (46%)
  waiting for transfers between devices  26.8 us (26%)
  Pallas kernels  21.1 us (20%)
  other arithmetic  4.34 us (4%)
  local copies, waits for them, and re-layouts  1.15 us (1%)
    ppermute x21, starting transfers between devices, swap(): return lax.ppermute(value, AXES, pairs)  35.8 us
    ppermute x21, waiting for transfers between devices, swap(): return lax.ppermute(value, AXES, pairs)  24 us
    pallas_call x3, Pallas kernels, grads(): pl.pallas_call(kernel, out_shape=[jax.ShapeDtypeStruct(w.shape, BF16) for...  16 us
    ppermute x4, starting transfers between devices, swap_corner(): return lax.ppermute(value, AXES, pairs)  11.8 us
    pallas_call x1, Pallas kernels, input_parts(): pl.pallas_call(kernel, out_shape=[jax.ShapeDtypeStruct((group, width), F3...  5.05 us
    ppermute x5, waiting for transfers between devices, swap_core(): return lax.ppermute(value, AXES, [(d, d ^ 1) for d in range(DEVICES)])  2.28 us
  transfers between devices with their start and end apart: 30, of which 14 were waited for; matrix products, arithmetic and copies ran while one was open for 4% of the time, Pallas kernels for 21%

profile of v12, /device:TPU:2, one launch (start us, length us, event | category | flops | bytes accessed | tf_op | source)
XLA Modules:
  0.0 102.5 jit_solution(15519187414436151773)
XLA Ops:
  0.6 2.0 %collective-permute-start.5 = (bf16[384,1024]{1,0:T(8,128)(2,1)}, bf16[384,1024]{1,0:T(8,128)(2,1)S(1)}, u32[]{:S(2)}, u32[]{:S(2)}) collective-permute-start(bf16[384,1024]{1,0:T(8,128)(2,1)} %refs_0_.5), channel_id=1, source_target_pairs={{0,4},{1,5},{2,6},{3,7},{4,0},{5,1},{6,2},{7,3},{8,12},{9,13},{10,... | collective-permute-start | bytes 2359304 | tf_op jit(solution)/shard_map/ppermute | solution.py:33
  4.4 2.6 %collective-permute-start.1 = (bf16[3,24,1024]{2,1,0:T(8,128)(2,1)S(1)}, bf16[3,24,1024]{2,1,0:T(8,128)(2,1)S(1)}, u32[]{:S(2)}, u32[]{:S(2)}) collective-permute-start(bf16[3,24,1024]{2,1,0:T(8,128)(2,1)S(1)} %pad_maximum_fusion.2), channel_id=1, source_target_pairs={{0,12},{1,13},{2,14},{3,15},{4,8},{5,9},{6,10},{7,11},{8,4},{9,5},... | collective-permute-start | bytes 442376 | tf_op jit(solution)/shard_map/ppermute | solution.py:33
  7.0 1.5 %collective-permute-start.12 = (bf16[3,24,1024]{2,1,0:T(8,128)(2,1)S(1)}, bf16[3,24,1024]{2,1,0:T(8,128)(2,1)S(1)}, u32[]{:S(2)}, u32[]{:S(2)}) collective-permute-start(bf16[3,24,1024]{2,1,0:T(8,128)(2,1)S(1)} %pad_maximum_fusion.2), channel_id=1, source_target_pairs={{0,18},{1,115},{2,16},{3,113},{4,22},{5,119},{6,20},{7,117},{8,26}... | collective-permute-start | bytes 442376 | tf_op jit(solution)/shard_map/ppermute | solution.py:59
  11.0 1.5 %collective-permute-start.4 = (bf16[3,24,1024]{2,1,0:T(8,128)(2,1)S(1)}, bf16[3,24,1024]{2,1,0:T(8,128)(2,1)S(1)}, u32[]{:S(2)}, u32[]{:S(2)}) collective-permute-start(bf16[3,24,1024]{2,1,0:T(8,128)(2,1)S(1)} %collective-permute-done.1), channel_id=1, source_target_pairs={{0,18},{1,115},{2,16},{3,113},{4,22},{5,119},{6,20},{7,117},{8,26}... | collective-permute-start | bytes 442376 | tf_op jit(solution)/shard_map/ppermute | solution.py:59
  15.3 3.1 %collective-permute-start.13 = (bf16[3,96,1024]{2,1,0:T(8,128)(2,1)S(1)}, bf16[3,96,1024]{2,1,0:T(8,128)(2,1)S(1)}, u32[]{:S(2)}, u32[]{:S(2)}) collective-permute-start(bf16[3,96,1024]{2,1,0:T(8,128)(2,1)S(1)} %pad_maximum_fusion.1), channel_id=1, source_target_pairs={{0,48},{1,17},{2,50},{3,19},{4,52},{5,21},{6,54},{7,23},{8,56},{9,... | collective-permute-start | bytes 1769480 | tf_op jit(solution)/shard_map/ppermute | solution.py:33
  22.7 3.7 %collective-permute-done.13 = bf16[3,96,1024]{2,1,0:T(8,128)(2,1)S(1)} collective-permute-done((bf16[3,96,1024]{2,1,0:T(8,128)(2,1)S(1)}, bf16[3,96,1024]{2,1,0:T(8,128)(2,1)S(1)}, u32[]{:S(2)}, u32[]{:S(2)}) %collective-permute-start.13) | collective-permute-done | bytes 589856 | tf_op jit(solution)/shard_map/ppermute | solution.py:33
  26.5 2.2 %collective-permute-start.14 = (bf16[3,192,1024]{2,1,0:T(8,128)(2,1)S(1)}, bf16[3,192,1024]{2,1,0:T(8,128)(2,1)S(1)}, u32[]{:S(2)}, u32[]{:S(2)}) collective-permute-start(bf16[3,192,1024]{2,1,0:T(8,128)(2,1)S(1)} %constant_dynamic-update-slice_fusion.refs_8_.refs_5_), channel_id=1, source_target_pairs={{0,66},{1,3},{2,64},{3,1},{4,70},{5,7},{6,68},{7,5},{8,74},{9,11},... | collective-permute-start | bytes 3538952 | tf_op jit(solution)/shard_map/ppermute | solution.py:33
  28.7 2.3 %collective-permute-done.15 = bf16[3,96,1024]{2,1,0:T(8,128)(2,1)S(1)} collective-permute-done((bf16[3,96,1024]{2,1,0:T(8,128)(2,1)S(1)}, bf16[3,96,1024]{2,1,0:T(8,128)(2,1)S(1)}, u32[]{:S(2)}, u32[]{:S(2)}) %collective-permute-start.15) | collective-permute-done | bytes 589856 | tf_op jit(solution)/shard_map/ppermute | solution.py:33
  31.1 3.7 %collective-permute-start.16 = (bf16[3,192,1024]{2,1,0:T(8,128)(2,1)S(1)}, bf16[3,192,1024]{2,1,0:T(8,128)(2,1)S(1)}, u32[]{:S(2)}, u32[]{:S(2)}) collective-permute-start(bf16[3,192,1024]{2,1,0:T(8,128)(2,1)S(1)} %constant_dynamic-update-slice_fusion.5.refs_9_.refs_6_), channel_id=1, source_target_pairs={{0,48},{1,17},{2,50},{3,19},{4,52},{5,21},{6,54},{7,23},{8,56},{9,... | collective-permute-start | bytes 3538952 | tf_op jit(solution)/shard_map/ppermute | solution.py:33
  35.3 4.1 %collective-permute-done.8.refs_6_ = bf16[384,1024]{1,0:T(8,128)(2,1)S(1)} collective-permute-done((bf16[384,1024]{1,0:T(8,128)(2,1)S(1)}, bf16[384,1024]{1,0:T(8,128)(2,1)S(1)}, u32[]{:S(2)}, u32[]{:S(2)}) %collective-permute-start.8) | collective-permute-done | bytes 786464 | tf_op jit(solution)/shard_map/ppermute | solution.py:33
  39.4 2.3 %collective-permute-done.9.refs_7_ = bf16[384,1024]{1,0:T(8,128)(2,1)S(1)} collective-permute-done((bf16[384,1024]{1,0:T(8,128)(2,1)S(1)}, bf16[384,1024]{1,0:T(8,128)(2,1)S(1)}, u32[]{:S(2)}, u32[]{:S(2)}) %collective-permute-start.9) | collective-permute-done | bytes 786464 | tf_op jit(solution)/shard_map/ppermute | solution.py:63
  41.7 2.0 %collective-permute-done.14.refs_8_.refs_3_ = bf16[3,192,1024]{2,1,0:T(8,128)(2,1)S(1)} collective-permute-done((bf16[3,192,1024]{2,1,0:T(8,128)(2,1)S(1)}, bf16[3,192,1024]{2,1,0:T(8,128)(2,1)S(1)}, u32[]{:S(2)}, u32[]{:S(2)}) %collective-permute-start.14) | collective-permute-done | bytes 1179680 | tf_op jit(solution)/shard_map/ppermute | solution.py:33
  43.7 4.2 %shard_map.59 = (bf16[3,192,1024]{2,1,0:T(8,128)(2,1)S(1)}, bf16[384,1536]{1,0:T(8,128)(2,1)S(1)}) custom-call(bf16[384,1024]{1,0:T(8,128)(2,1)S(1)} %copy-done, bf16[384,1024]{1,0:T(8,128)(2,1)S(1)} %collective-permute-done.refs_1_, bf16[384,1024]{1,0:T(8,128)(2,1)S(1)} %collective-permute-done.5.refs_2_, ...), custom_call_target="tpu_custom_call" | custom-call | flops 1024 | bytes 1024 | tf_op jit(solution)/shard_map/pallas_call | solution.py:144
  47.9 1.8 %collective-permute-start.18 = (bf16[3,192,1024]{2,1,0:T(8,128)(2,1)S(1)}, bf16[3,192,1024]{2,1,0:T(8,128)(2,1)S(1)}, u32[]{:S(2)}, u32[]{:S(2)}) collective-permute-start(bf16[3,192,1024]{2,1,0:T(8,128)(2,1)S(1)} %get-tuple-element.35), channel_id=1, source_target_pairs={{0,66},{1,3},{2,64},{3,1},{4,70},{5,7},{6,68},{7,5},{8,74},{9,11},... | collective-permute-start | bytes 3538952 | tf_op jit(solution)/shard_map/ppermute | solution.py:33
  49.6 4.2 %shard_map.60 = (bf16[3,192,1024]{2,1,0:T(8,128)(2,1)S(1)}, bf16[384,1536]{1,0:T(8,128)(2,1)S(1)}) custom-call(bf16[384,1024]{1,0:T(8,128)(2,1)S(1)} %copy-done, bf16[384,1024]{1,0:T(8,128)(2,1)S(1)} %collective-permute-done.refs_1_, bf16[384,1024]{1,0:T(8,128)(2,1)S(1)} %collective-permute-done.5.refs_2_, ...), custom_call_target="tpu_custom_call" | custom-call | flops 1024 | bytes 1024 | tf_op jit(solution)/shard_map/pallas_call | solution.py:144
  53.8 4.1 %collective-permute-start.19 = (bf16[3,192,1024]{2,1,0:T(8,128)(2,1)S(1)}, bf16[3,192,1024]{2,1,0:T(8,128)(2,1)S(1)}, u32[]{:S(2)}, u32[]{:S(2)}) collective-permute-start(bf16[3,192,1024]{2,1,0:T(8,128)(2,1)S(1)} %get-tuple-element.37), channel_id=1, source_target_pairs={{0,48},{1,17},{2,50},{3,19},{4,52},{5,21},{6,54},{7,23},{8,56},{9,... | collective-permute-start | bytes 3538952 | tf_op jit(solution)/shard_map/ppermute | solution.py:33
  57.9 7.7 %shard_map.61 = (bf16[3,192,1024]{2,1,0:T(8,128)(2,1)S(1)}, bf16[3,192,1024]{2,1,0:T(8,128)(2,1)S(1)}, bf16[768,1536]{1,0:T(8,128)(2,1)S(1)}) custom-call(bf16[384,1024]{1,0:T(8,128)(2,1)S(1)} %copy-done, bf16[384,1024]{1,0:T(8,128)(2,1)S(1)} %collective-permute-done.refs_1_, bf16[384,1024]{1,0:T(8,128)(2,1)S(1)} %collective-permute-done.5.refs_2_, ...), custom_call_target="tpu_custom_call" | custom-call | flops 1024 | bytes 1024 | tf_op jit(solution)/shard_map/pallas_call | solution.py:144
  65.5 5.1 %shard_map.62 = (f32[384,1024]{1,0:T(8,128)S(1)}, f32[384,1024]{1,0:T(8,128)S(1)}, bf16[2,384,1024]{2,1,0:T(8,128)(2,1)S(1)}) custom-call(bf16[384,1536]{1,0:T(8,128)(2,1)S(1)} %get-tuple-element.25.refs_0_, bf16[384,1536]{1,0:T(8,128)(2,1)S(1)} %get-tuple-element.28.refs_1_, bf16[768,1536]{1,0:T(8,128)(2,1)S(1)} %get-tuple-element.31.refs_2_, ...), custom_call_target="tpu_custom_call" | custom-call | flops 1024 | bytes 1024 | tf_op jit(solution)/shard_map/pallas_call | solution.py:183
  72.8 3.2 %collective-permute-start.21 = (bf16[3,96,1024]{2,1,0:T(8,128)(2,1)S(1)}, bf16[3,96,1024]{2,1,0:T(8,128)(2,1)S(1)}, u32[]{:S(2)}, u32[]{:S(2)}) collective-permute-start(bf16[3,96,1024]{2,1,0:T(8,128)(2,1)S(1)} %add_convert_fusion.3), channel_id=1, source_target_pairs={{0,48},{1,17},{2,50},{3,19},{4,52},{5,21},{6,54},{7,23},{8,56},{9,... | collective-permute-start | bytes 1769480 | tf_op jit(solution)/shard_map/ppermute | solution.py:33
  77.3 4.9 %collective-permute-done.25 = bf16[3,96,1024]{2,1,0:T(8,128)(2,1)S(1)} collective-permute-done((bf16[3,96,1024]{2,1,0:T(8,128)(2,1)S(1)}, bf16[3,96,1024]{2,1,0:T(8,128)(2,1)S(1)}, u32[]{:S(2)}, u32[]{:S(2)}) %collective-permute-start.25) | collective-permute-done | bytes 589856 | tf_op jit(solution)/shard_map/ppermute | solution.py:33
  83.3 5.4 %collective-permute-start.28 = (bf16[3,24,1024]{2,1,0:T(8,128)(2,1)S(1)}, bf16[3,24,1024]{2,1,0:T(8,128)(2,1)S(1)}, u32[]{:S(2)}, u32[]{:S(2)}) collective-permute-start(bf16[3,24,1024]{2,1,0:T(8,128)(2,1)S(1)} %get-tuple-element.46), channel_id=1, source_target_pairs={{0,18},{1,115},{2,16},{3,113},{4,22},{5,119},{6,20},{7,117},{8,26}... | collective-permute-start | bytes 442376 | tf_op jit(solution)/shard_map/ppermute | solution.py:59
  89.7 3.3 %collective-permute-start.24 = (bf16[3,24,1024]{2,1,0:T(8,128)(2,1)S(1)}, bf16[3,24,1024]{2,1,0:T(8,128)(2,1)S(1)}, u32[]{:S(2)}, u32[]{:S(2)}) collective-permute-start(bf16[3,24,1024]{2,1,0:T(8,128)(2,1)S(1)} %get-tuple-element.43), channel_id=1, source_target_pairs={{0,18},{1,115},{2,16},{3,113},{4,22},{5,119},{6,20},{7,117},{8,26}... | collective-permute-start | bytes 442376 | tf_op jit(solution)/shard_map/ppermute | solution.py:59
  94.0 3.1 %collective-permute-start.29 = (bf16[3,24,1024]{2,1,0:T(8,128)(2,1)S(1)}, bf16[3,24,1024]{2,1,0:T(8,128)(2,1)S(1)}, u32[]{:S(2)}, u32[]{:S(2)}) collective-permute-start(bf16[3,24,1024]{2,1,0:T(8,128)(2,1)S(1)} %add_convert_fusion.4), channel_id=1, source_target_pairs={{0,12},{1,13},{2,14},{3,15},{4,8},{5,9},{6,10},{7,11},{8,4},{9,5},... | collective-permute-start | bytes 442376 | tf_op jit(solution)/shard_map/ppermute | solution.py:33
  98.7 1.8 %collective-permute-done.29 = bf16[3,24,1024]{2,1,0:T(8,128)(2,1)S(1)} collective-permute-done((bf16[3,24,1024]{2,1,0:T(8,128)(2,1)S(1)}, bf16[3,24,1024]{2,1,0:T(8,128)(2,1)S(1)}, u32[]{:S(2)}, u32[]{:S(2)}) %collective-permute-start.29) | collective-permute-done | bytes 147488 | tf_op jit(solution)/shard_map/ppermute | solution.py:33
  (65 shorter events, 21.9 us)
Async XLA Ops:
  0.6 20.5 %collective-permute-start.5 = (bf16[384,1024]{1,0:T(8,128)(2,1)}, bf16[384,1024]{1,0:T(8,128)(2,1)S(1)}, u32[]{:S(2)}, u32[]{:S(2)}) collective-permute-start(bf16[384,1024]{1,0:T(8,128)(2,1)} %refs_0_.5), channel_id=1, source_target_pairs={{0,4},{1,5},{2,6},{3,7},{4,0},{5,1},{6,2},{7,3},{8,12},{9,13},{10,... | collective-permute-start | bytes 2359304 | tf_op jit(solution)/shard_map/ppermute | solution.py:33
  4.4 6.6 %collective-permute-start.1 = (bf16[3,24,1024]{2,1,0:T(8,128)(2,1)S(1)}, bf16[3,24,1024]{2,1,0:T(8,128)(2,1)S(1)}, u32[]{:S(2)}, u32[]{:S(2)}) collective-permute-start(bf16[3,24,1024]{2,1,0:T(8,128)(2,1)S(1)} %pad_maximum_fusion.2), channel_id=1, source_target_pairs={{0,12},{1,13},{2,14},{3,15},{4,8},{5,9},{6,10},{7,11},{8,4},{9,5},... | collective-permute-start | bytes 442376 | tf_op jit(solution)/shard_map/ppermute | solution.py:33
  7.0 6.0 %collective-permute-start.12 = (bf16[3,24,1024]{2,1,0:T(8,128)(2,1)S(1)}, bf16[3,24,1024]{2,1,0:T(8,128)(2,1)S(1)}, u32[]{:S(2)}, u32[]{:S(2)}) collective-permute-start(bf16[3,24,1024]{2,1,0:T(8,128)(2,1)S(1)} %pad_maximum_fusion.2), channel_id=1, source_target_pairs={{0,18},{1,115},{2,16},{3,113},{4,22},{5,119},{6,20},{7,117},{8,26}... | collective-permute-start | bytes 442376 | tf_op jit(solution)/shard_map/ppermute | solution.py:59
  8.5 6.2 %collective-permute-start.11 = (bf16[3,24,1024]{2,1,0:T(8,128)(2,1)S(1)}, bf16[3,24,1024]{2,1,0:T(8,128)(2,1)S(1)}, u32[]{:S(2)}, u32[]{:S(2)}) collective-permute-start(bf16[3,24,1024]{2,1,0:T(8,128)(2,1)S(1)} %pad_maximum_fusion.2), channel_id=1, source_target_pairs={{0,2},{1,67},{2,0},{3,65},{4,6},{5,71},{6,4},{7,69},{8,10},{9,75},... | collective-permute-start | bytes 442376 | tf_op jit(solution)/shard_map/ppermute | solution.py:33
  11.0 7.4 %collective-permute-start.4 = (bf16[3,24,1024]{2,1,0:T(8,128)(2,1)S(1)}, bf16[3,24,1024]{2,1,0:T(8,128)(2,1)S(1)}, u32[]{:S(2)}, u32[]{:S(2)}) collective-permute-start(bf16[3,24,1024]{2,1,0:T(8,128)(2,1)S(1)} %collective-permute-done.1), channel_id=1, source_target_pairs={{0,18},{1,115},{2,16},{3,113},{4,22},{5,119},{6,20},{7,117},{8,26}... | collective-permute-start | bytes 442376 | tf_op jit(solution)/shard_map/ppermute | solution.py:59
  13.0 5.7 %collective-permute-start.3 = (bf16[3,24,1024]{2,1,0:T(8,128)(2,1)S(1)}, bf16[3,24,1024]{2,1,0:T(8,128)(2,1)S(1)}, u32[]{:S(2)}, u32[]{:S(2)}) collective-permute-start(bf16[3,24,1024]{2,1,0:T(8,128)(2,1)S(1)} %collective-permute-done.1), channel_id=1, source_target_pairs={{0,2},{1,67},{2,0},{3,65},{4,6},{5,71},{6,4},{7,69},{8,10},{9,75},... | collective-permute-start | bytes 442376 | tf_op jit(solution)/shard_map/ppermute | solution.py:33
  15.3 11.2 %collective-permute-start.13 = (bf16[3,96,1024]{2,1,0:T(8,128)(2,1)S(1)}, bf16[3,96,1024]{2,1,0:T(8,128)(2,1)S(1)}, u32[]{:S(2)}, u32[]{:S(2)}) collective-permute-start(bf16[3,96,1024]{2,1,0:T(8,128)(2,1)S(1)} %pad_maximum_fusion.1), channel_id=1, source_target_pairs={{0,48},{1,17},{2,50},{3,19},{4,52},{5,21},{6,54},{7,23},{8,56},{9,... | collective-permute-start | bytes 1769480 | tf_op jit(solution)/shard_map/ppermute | solution.py:33
  18.3 16.4 %collective-permute-start = (bf16[384,1024]{1,0:T(8,128)(2,1)S(1)}, bf16[384,1024]{1,0:T(8,128)(2,1)S(1)}, u32[]{:S(2)}, u32[]{:S(2)}) collective-permute-start(bf16[384,1024]{1,0:T(8,128)(2,1)S(1)} %copy-done), channel_id=1, source_target_pairs={{0,1},{1,0},{2,3},{3,2},{4,5},{5,4},{6,7},{7,6},{8,9},{9,8},{10,11... | collective-permute-start | bytes 2359304 | tf_op jit(solution)/shard_map/ppermute | solution.py:63
  19.9 19.5 %collective-permute-start.8 = (bf16[384,1024]{1,0:T(8,128)(2,1)S(1)}, bf16[384,1024]{1,0:T(8,128)(2,1)S(1)}, u32[]{:S(2)}, u32[]{:S(2)}) collective-permute-start(bf16[384,1024]{1,0:T(8,128)(2,1)S(1)} %copy-done.1), channel_id=1, source_target_pairs={{0,4},{1,5},{2,6},{3,7},{4,0},{5,1},{6,2},{7,3},{8,12},{9,13},{10,... | collective-permute-start | bytes 2359304 | tf_op jit(solution)/shard_map/ppermute | solution.py:33
  21.1 9.9 %collective-permute-start.15 = (bf16[3,96,1024]{2,1,0:T(8,128)(2,1)S(1)}, bf16[3,96,1024]{2,1,0:T(8,128)(2,1)S(1)}, u32[]{:S(2)}, u32[]{:S(2)}) collective-permute-start(bf16[3,96,1024]{2,1,0:T(8,128)(2,1)S(1)} %pad_maximum_fusion), channel_id=1, source_target_pairs={{0,66},{1,3},{2,64},{3,1},{4,70},{5,7},{6,68},{7,5},{8,74},{9,11},... | collective-permute-start | bytes 1769480 | tf_op jit(solution)/shard_map/ppermute | solution.py:33
  26.5 17.2 %collective-permute-start.14 = (bf16[3,192,1024]{2,1,0:T(8,128)(2,1)S(1)}, bf16[3,192,1024]{2,1,0:T(8,128)(2,1)S(1)}, u32[]{:S(2)}, u32[]{:S(2)}) collective-permute-start(bf16[3,192,1024]{2,1,0:T(8,128)(2,1)S(1)} %constant_dynamic-update-slice_fusion.refs_8_.refs_5_), channel_id=1, source_target_pairs={{0,66},{1,3},{2,64},{3,1},{4,70},{5,7},{6,68},{7,5},{8,74},{9,11},... | collective-permute-start | bytes 3538952 | tf_op jit(solution)/shard_map/ppermute | solution.py:33
  31.1 18.5 %collective-permute-start.16 = (bf16[3,192,1024]{2,1,0:T(8,128)(2,1)S(1)}, bf16[3,192,1024]{2,1,0:T(8,128)(2,1)S(1)}, u32[]{:S(2)}, u32[]{:S(2)}) collective-permute-start(bf16[3,192,1024]{2,1,0:T(8,128)(2,1)S(1)} %constant_dynamic-update-slice_fusion.5.refs_9_.refs_6_), channel_id=1, source_target_pairs={{0,48},{1,17},{2,50},{3,19},{4,52},{5,21},{6,54},{7,23},{8,56},{9,... | collective-permute-start | bytes 3538952 | tf_op jit(solution)/shard_map/ppermute | solution.py:33
  47.9 22.8 %collective-permute-start.18 = (bf16[3,192,1024]{2,1,0:T(8,128)(2,1)S(1)}, bf16[3,192,1024]{2,1,0:T(8,128)(2,1)S(1)}, u32[]{:S(2)}, u32[]{:S(2)}) collective-permute-start(bf16[3,192,1024]{2,1,0:T(8,128)(2,1)S(1)} %get-tuple-element.35), channel_id=1, source_target_pairs={{0,66},{1,3},{2,64},{3,1},{4,70},{5,7},{6,68},{7,5},{8,74},{9,11},... | collective-permute-start | bytes 3538952 | tf_op jit(solution)/shard_map/ppermute | solution.py:33
  53.8 18.2 %collective-permute-start.19 = (bf16[3,192,1024]{2,1,0:T(8,128)(2,1)S(1)}, bf16[3,192,1024]{2,1,0:T(8,128)(2,1)S(1)}, u32[]{:S(2)}, u32[]{:S(2)}) collective-permute-start(bf16[3,192,1024]{2,1,0:T(8,128)(2,1)S(1)} %get-tuple-element.37), channel_id=1, source_target_pairs={{0,48},{1,17},{2,50},{3,19},{4,52},{5,21},{6,54},{7,23},{8,56},{9,... | collective-permute-start | bytes 3538952 | tf_op jit(solution)/shard_map/ppermute | solution.py:33
  70.6 5.4 %collective-permute-start.17 = (bf16[2,384,1024]{2,1,0:T(8,128)(2,1)S(1)}, bf16[2,384,1024]{2,1,0:T(8,128)(2,1)S(1)}, u32[]{:S(2)}, u32[]{:S(2)}) collective-permute-start(bf16[2,384,1024]{2,1,0:T(8,128)(2,1)S(1)} %get-tuple-element.33), channel_id=1, source_target_pairs={{0,1},{1,0},{2,3},{3,2},{4,5},{5,4},{6,7},{7,6},{8,9},{9,8},{10,11... | collective-permute-start | bytes 4718600 | tf_op jit(solution)/shard_map/ppermute | solution.py:63
  72.3 10.0 %collective-permute-start.25 = (bf16[3,96,1024]{2,1,0:T(8,128)(2,1)S(1)}, bf16[3,96,1024]{2,1,0:T(8,128)(2,1)S(1)}, u32[]{:S(2)}, u32[]{:S(2)}) collective-permute-start(bf16[3,96,1024]{2,1,0:T(8,128)(2,1)S(1)} %add_convert_fusion.2), channel_id=1, source_target_pairs={{0,66},{1,3},{2,64},{3,1},{4,70},{5,7},{6,68},{7,5},{8,74},{9,11},... | collective-permute-start | bytes 1769480 | tf_op jit(solution)/shard_map/ppermute | solution.py:33
  72.8 15.9 %collective-permute-start.21 = (bf16[3,96,1024]{2,1,0:T(8,128)(2,1)S(1)}, bf16[3,96,1024]{2,1,0:T(8,128)(2,1)S(1)}, u32[]{:S(2)}, u32[]{:S(2)}) collective-permute-start(bf16[3,96,1024]{2,1,0:T(8,128)(2,1)S(1)} %add_convert_fusion.3), channel_id=1, source_target_pairs={{0,48},{1,17},{2,50},{3,19},{4,52},{5,21},{6,54},{7,23},{8,56},{9,... | collective-permute-start | bytes 1769480 | tf_op jit(solution)/shard_map/ppermute | solution.py:33
  76.3 25.0 %collective-permute-start.20 = (bf16[384,1024]{1,0:T(8,128)(2,1)S(1)}, bf16[384,1024]{1,0:T(8,128)(2,1)S(1)}, u32[]{:S(2)}, u32[]{:S(2)}) collective-permute-start(bf16[384,1024]{1,0:T(8,128)(2,1)S(1)} %fusion), channel_id=1, source_target_pairs={{0,4},{1,5},{2,6},{3,7},{4,0},{5,1},{6,2},{7,3},{8,12},{9,13},{10,... | collective-permute-start | bytes 2359304 | tf_op jit(solution)/shard_map/ppermute | solution.py:33
  82.6 7.1 %collective-permute-start.26 = (bf16[3,24,1024]{2,1,0:T(8,128)(2,1)S(1)}, bf16[3,24,1024]{2,1,0:T(8,128)(2,1)S(1)}, u32[]{:S(2)}, u32[]{:S(2)}) collective-permute-start(bf16[3,24,1024]{2,1,0:T(8,128)(2,1)S(1)} %get-tuple-element.45), channel_id=1, source_target_pairs={{0,16},{1,49},{2,18},{3,51},{4,20},{5,53},{6,22},{7,55},{8,24},{9,... | collective-permute-start | bytes 442376 | tf_op jit(solution)/shard_map/ppermute | solution.py:33
  83.3 9.7 %collective-permute-start.28 = (bf16[3,24,1024]{2,1,0:T(8,128)(2,1)S(1)}, bf16[3,24,1024]{2,1,0:T(8,128)(2,1)S(1)}, u32[]{:S(2)}, u32[]{:S(2)}) collective-permute-start(bf16[3,24,1024]{2,1,0:T(8,128)(2,1)S(1)} %get-tuple-element.46), channel_id=1, source_target_pairs={{0,18},{1,115},{2,16},{3,113},{4,22},{5,119},{6,20},{7,117},{8,26}... | collective-permute-start | bytes 442376 | tf_op jit(solution)/shard_map/ppermute | solution.py:59
  89.1 8.1 %collective-permute-start.22 = (bf16[3,24,1024]{2,1,0:T(8,128)(2,1)S(1)}, bf16[3,24,1024]{2,1,0:T(8,128)(2,1)S(1)}, u32[]{:S(2)}, u32[]{:S(2)}) collective-permute-start(bf16[3,24,1024]{2,1,0:T(8,128)(2,1)S(1)} %get-tuple-element.42), channel_id=1, source_target_pairs={{0,16},{1,49},{2,18},{3,51},{4,20},{5,53},{6,22},{7,55},{8,24},{9,... | collective-permute-start | bytes 442376 | tf_op jit(solution)/shard_map/ppermute | solution.py:33
  89.7 7.5 %collective-permute-start.24 = (bf16[3,24,1024]{2,1,0:T(8,128)(2,1)S(1)}, bf16[3,24,1024]{2,1,0:T(8,128)(2,1)S(1)}, u32[]{:S(2)}, u32[]{:S(2)}) collective-permute-start(bf16[3,24,1024]{2,1,0:T(8,128)(2,1)S(1)} %get-tuple-element.43), channel_id=1, source_target_pairs={{0,18},{1,115},{2,16},{3,113},{4,22},{5,119},{6,20},{7,117},{8,26}... | collective-permute-start | bytes 442376 | tf_op jit(solution)/shard_map/ppermute | solution.py:59
  93.0 5.7 %collective-permute-start.23 = (bf16[3,24,1024]{2,1,0:T(8,128)(2,1)S(1)}, bf16[3,24,1024]{2,1,0:T(8,128)(2,1)S(1)}, u32[]{:S(2)}, u32[]{:S(2)}) collective-permute-start(bf16[3,24,1024]{2,1,0:T(8,128)(2,1)S(1)} %get-tuple-element.44), channel_id=1, source_target_pairs={{0,2},{1,67},{2,0},{3,65},{4,6},{5,71},{6,4},{7,69},{8,10},{9,75},... | collective-permute-start | bytes 442376 | tf_op jit(solution)/shard_map/ppermute | solution.py:33
  94.0 6.4 %collective-permute-start.29 = (bf16[3,24,1024]{2,1,0:T(8,128)(2,1)S(1)}, bf16[3,24,1024]{2,1,0:T(8,128)(2,1)S(1)}, u32[]{:S(2)}, u32[]{:S(2)}) collective-permute-start(bf16[3,24,1024]{2,1,0:T(8,128)(2,1)S(1)} %add_convert_fusion.4), channel_id=1, source_target_pairs={{0,12},{1,13},{2,14},{3,15},{4,8},{5,9},{6,10},{7,11},{8,4},{9,5},... | collective-permute-start | bytes 442376 | tf_op jit(solution)/shard_map/ppermute | solution.py:33
  (8 other events, 60.4 us)

commit v13 on v9

--- a/solution.py
+++ b/solution.py
@@ -202,10 +202,11 @@
     o0 = gather_block(message)
     block1, c_own = lax.optimization_barrier((block1, cotangent))
     c_z = swap_near(c_own, Z)
-    o1, x_z = lax.optimization_barrier((block1, x_z))
+    o1 = block1
     n0 = swap_second(o0, Y)
     r0 = swap_second(join(o0, n0), X)
     n1 = swap_second(o1, X)
+    o1, x_z = lax.optimization_barrier((o1, x_z))
     w1 = swap_second(o1, Y)
     f1 = swap_second(n1, Y)
     xs, cs = [activations, swap_core(activations)], [cotangent, swap_core(cotangent)]

time: 103 us -> 103 us (level)
  starting transfers between devices: 51.4 us -> 49.7 us
  waiting for transfers between devices: 22.9 us -> 24.5 us
    ppermute x22, starting transfers between devices: 39.8 us -> 37.9 us  [swap(): return lax.ppermute(value, AXES, pairs)]
    ppermute x22, waiting for transfers between devices: 22.3 us -> 24 us  [swap(): return lax.ppermute(value, AXES, pairs)]
where the time goes in v13:
time: 103 us; the launch traced here: 102 us
  starting transfers between devices  49.7 us (48%)
  waiting for transfers between devices  24.5 us (24%)
  Pallas kernels  21.8 us (21%)
  other arithmetic  4.34 us (4%)
  local copies, waits for them, and re-layouts  1.14 us (1%)
    ppermute x22, starting transfers between devices, swap(): return lax.ppermute(value, AXES, pairs)  37.9 us
    ppermute x22, waiting for transfers between devices, swap(): return lax.ppermute(value, AXES, pairs)  24 us
    pallas_call x5, Pallas kernels, grads(): pl.pallas_call(kernel, out_shape=[jax.ShapeDtypeStruct((3, joined * units...  16.7 us
    ppermute x4, starting transfers between devices, swap_corner(): return lax.ppermute(value, AXES, pairs)  9.14 us
    pallas_call x1, Pallas kernels, input_parts(): pl.pallas_call(kernel, out_shape=[jax.ShapeDtypeStruct((group, width), ki...  5.06 us
    ppermute x6, starting transfers between devices, swap_core(): return lax.ppermute(value, AXES, [(d, d ^ 1) for d in range(DEVICES)])  2.61 us
  transfers between devices with their start and end apart: 32, of which 15 were waited for; matrix products, arithmetic and copies ran while one was open for 5% of the time, Pallas kernels for 21%

profile of v13, /device:TPU:2, one launch (start us, length us, event | category | flops | bytes accessed | tf_op | source)
XLA Modules:
  0.0 102.4 jit_solution(17170061087350398491)
XLA Ops:
  0.6 2.0 %collective-permute-start.6 = (bf16[384,1024]{1,0:T(8,128)(2,1)}, bf16[384,1024]{1,0:T(8,128)(2,1)S(1)}, u32[]{:S(2)}, u32[]{:S(2)}) collective-permute-start(bf16[384,1024]{1,0:T(8,128)(2,1)} %refs_0_.5), channel_id=1, source_target_pairs={{0,4},{1,5},{2,6},{3,7},{4,0},{5,1},{6,2},{7,3},{8,12},{9,13},{10,... | collective-permute-start | bytes 2359304 | tf_op jit(solution)/shard_map/ppermute | solution.py:33
  4.4 2.6 %collective-permute-start.2 = (bf16[3,24,1024]{2,1,0:T(8,128)(2,1)S(1)}, bf16[3,24,1024]{2,1,0:T(8,128)(2,1)S(1)}, u32[]{:S(2)}, u32[]{:S(2)}) collective-permute-start(bf16[3,24,1024]{2,1,0:T(8,128)(2,1)S(1)} %pad_maximum_fusion.2), channel_id=1, source_target_pairs={{0,12},{1,13},{2,14},{3,15},{4,8},{5,9},{6,10},{7,11},{8,4},{9,5},... | collective-permute-start | bytes 442376 | tf_op jit(solution)/shard_map/ppermute | solution.py:33
  15.3 3.0 %collective-permute-start.12 = (bf16[3,96,1024]{2,1,0:T(8,128)(2,1)S(1)}, bf16[3,96,1024]{2,1,0:T(8,128)(2,1)S(1)}, u32[]{:S(2)}, u32[]{:S(2)}) collective-permute-start(bf16[3,96,1024]{2,1,0:T(8,128)(2,1)S(1)} %pad_maximum_fusion.1.refs_7_.refs_12_), channel_id=1, source_target_pairs={{0,48},{1,17},{2,50},{3,19},{4,52},{5,21},{6,54},{7,23},{8,56},{9,... | collective-permute-start | bytes 1769480 | tf_op jit(solution)/shard_map/ppermute | solution.py:33
  22.7 3.8 %collective-permute-done.12.refs_6_.refs_11_ = bf16[3,96,1024]{2,1,0:T(8,128)(2,1)S(1)} collective-permute-done((bf16[3,96,1024]{2,1,0:T(8,128)(2,1)S(1)}, bf16[3,96,1024]{2,1,0:T(8,128)(2,1)S(1)}, u32[]{:S(2)}, u32[]{:S(2)}) %collective-permute-start.12) | collective-permute-done | bytes 589856 | tf_op jit(solution)/shard_map/ppermute | solution.py:33
  26.4 3.0 %collective-permute-start.13 = (bf16[3,96,1024]{2,1,0:T(8,128)(2,1)S(1)}, bf16[3,96,1024]{2,1,0:T(8,128)(2,1)S(1)}, u32[]{:S(2)}, u32[]{:S(2)}) collective-permute-start(bf16[3,96,1024]{2,1,0:T(8,128)(2,1)S(1)} %pad_maximum_fusion.refs_5_.refs_10_), channel_id=1, source_target_pairs={{0,48},{1,17},{2,50},{3,19},{4,52},{5,21},{6,54},{7,23},{8,56},{9,... | collective-permute-start | bytes 1769480 | tf_op jit(solution)/shard_map/ppermute | solution.py:33
  29.9 3.8 %collective-permute-start.14 = (bf16[3,96,1024]{2,1,0:T(8,128)(2,1)S(1)}, bf16[3,96,1024]{2,1,0:T(8,128)(2,1)S(1)}, u32[]{:S(2)}, u32[]{:S(2)}) collective-permute-start(bf16[3,96,1024]{2,1,0:T(8,128)(2,1)S(1)} %collective-permute-done.8.refs_4_.refs_9_), channel_id=1, source_target_pairs={{0,48},{1,17},{2,50},{3,19},{4,52},{5,21},{6,54},{7,23},{8,56},{9,... | collective-permute-start | bytes 1769480 | tf_op jit(solution)/shard_map/ppermute | solution.py:33
  33.7 1.9 %collective-permute-start.17 = (bf16[3,192,1024]{2,1,0:T(8,128)(2,1)S(1)}, bf16[3,192,1024]{2,1,0:T(8,128)(2,1)S(1)}, u32[]{:S(2)}, u32[]{:S(2)}) collective-permute-start(bf16[3,192,1024]{2,1,0:T(8,128)(2,1)S(1)} %constant_dynamic-update-slice_fusion), channel_id=1, source_target_pairs={{0,66},{1,3},{2,64},{3,1},{4,70},{5,7},{6,68},{7,5},{8,74},{9,11},... | collective-permute-start | bytes 3538952 | tf_op jit(solution)/shard_map/ppermute | solution.py:33
  35.6 4.0 %shard_map.59 = (bf16[3,96,1024]{2,1,0:T(8,128)(2,1)S(1)}, bf16[3,96,1024]{2,1,0:T(8,128)(2,1)S(1)}, bf16[3,96,1024]{2,1,0:T(8,128)(2,1)S(1)}, bf16[3,96,1024]{2,1,0:T(8,128)(2,1)S(1)}, bf16[768,768]{1,0:T(8,128)(2,1)S(1)}) custom-call(bf16[384,1024]{1,0:T(8,128)(2,1)S(1)} %copy-done, bf16[384,1024]{1,0:T(8,128)(2,1)S(1)} %collective-permute-done.refs_1_, ...), custom_call_target="tpu_custom_call" | custom-call | flops 3000001024 | bytes 1024 | tf_op jit(solution)/shard_map/pallas_call | solution.py:148
  42.0 1.8 %collective-permute-done.14.refs_5_.refs_7_ = bf16[3,96,1024]{2,1,0:T(8,128)(2,1)S(1)} collective-permute-done((bf16[3,96,1024]{2,1,0:T(8,128)(2,1)S(1)}, bf16[3,96,1024]{2,1,0:T(8,128)(2,1)S(1)}, u32[]{:S(2)}, u32[]{:S(2)}) %collective-permute-start.14) | collective-permute-done | bytes 589856 | tf_op jit(solution)/shard_map/ppermute | solution.py:33
  43.9 2.2 %shard_map.60 = (bf16[3,192,1024]{2,1,0:T(8,128)(2,1)S(1)}, bf16[384,768]{1,0:T(8,128)(2,1)S(1)}) custom-call(bf16[384,1024]{1,0:T(8,128)(2,1)S(1)} %copy-done, bf16[384,1024]{1,0:T(8,128)(2,1)S(1)} %collective-permute-done.refs_1_, bf16[384,1024]{1,0:T(8,128)(2,1)S(1)} %copy-done.1, bf16[384,1024]{1,0:T(8,128)(2,1)S(1)} %collective-permute-done.1.refs_3_.refs_5_, ...), custom_call_target="tpu_custom_call" | custom-call | flops 6000001024 | bytes 1024 | tf_op jit(solution)/shard_map/pallas_call | solution.py:148
  46.1 2.2 %shard_map.61 = (bf16[3,192,1024]{2,1,0:T(8,128)(2,1)S(1)}, bf16[384,768]{1,0:T(8,128)(2,1)S(1)}) custom-call(bf16[384,1024]{1,0:T(8,128)(2,1)S(1)} %collective-permute-done.6.refs_0_.refs_2_, bf16[384,1024]{1,0:T(8,128)(2,1)S(1)} %collective-permute-done.15.refs_1_.refs_3_, bf16[384,1024]{1,0:T(8,128)(2,1)S(1)} %collective-permute-done.7.refs_2_.refs_6_, ...), custom_call_target="tpu_custom_call" | custom-call | flops 1024 | bytes 1024 | tf_op jit(solution)/shard_map/pallas_call | solution.py:148
  48.3 3.2 %collective-permute-start.20 = (bf16[3,192,1024]{2,1,0:T(8,128)(2,1)S(1)}, bf16[3,192,1024]{2,1,0:T(8,128)(2,1)S(1)}, u32[]{:S(2)}, u32[]{:S(2)}) collective-permute-start(bf16[3,192,1024]{2,1,0:T(8,128)(2,1)S(1)} %get-tuple-element.67), channel_id=1, source_target_pairs={{0,48},{1,17},{2,50},{3,19},{4,52},{5,21},{6,54},{7,23},{8,56},{9,... | collective-permute-start | bytes 3538952 | tf_op jit(solution)/shard_map/ppermute | solution.py:33
  51.5 4.2 %shard_map.62 = (bf16[3,192,1024]{2,1,0:T(8,128)(2,1)S(1)}, bf16[384,1536]{1,0:T(8,128)(2,1)S(1)}) custom-call(bf16[384,1024]{1,0:T(8,128)(2,1)S(1)} %copy-done, bf16[384,1024]{1,0:T(8,128)(2,1)S(1)} %collective-permute-done.refs_1_, bf16[384,1024]{1,0:T(8,128)(2,1)S(1)} %collective-permute-done.6.refs_0_.refs_2_, ...), custom_call_target="tpu_custom_call" | custom-call | flops 1024 | bytes 1024 | tf_op jit(solution)/shard_map/pallas_call | solution.py:148
  55.7 1.6 %collective-permute-start.19 = (bf16[3,192,1024]{2,1,0:T(8,128)(2,1)S(1)}, bf16[3,192,1024]{2,1,0:T(8,128)(2,1)S(1)}, u32[]{:S(2)}, u32[]{:S(2)}) collective-permute-start(bf16[3,192,1024]{2,1,0:T(8,128)(2,1)S(1)} %get-tuple-element.66), channel_id=1, source_target_pairs={{0,66},{1,3},{2,64},{3,1},{4,70},{5,7},{6,68},{7,5},{8,74},{9,11},... | collective-permute-start | bytes 3538952 | tf_op jit(solution)/shard_map/ppermute | solution.py:33
  57.3 4.1 %shard_map.63 = (bf16[3,96,1024]{2,1,0:T(8,128)(2,1)S(1)}, bf16[3,96,1024]{2,1,0:T(8,128)(2,1)S(1)}, bf16[3,96,1024]{2,1,0:T(8,128)(2,1)S(1)}, bf16[3,96,1024]{2,1,0:T(8,128)(2,1)S(1)}, bf16[768,768]{1,0:T(8,128)(2,1)S(1)}) custom-call(bf16[384,1024]{1,0:T(8,128)(2,1)S(1)} %collective-permute-done.6.refs_0_.refs_2_, ...), custom_call_target="tpu_custom_call" | custom-call | flops 1024 | bytes 1024 | tf_op jit(solution)/shard_map/pallas_call | solution.py:148
  61.5 5.1 %shard_map.64 = (f32[384,1024]{1,0:T(8,128)S(1)}, bf16[384,1024]{1,0:T(8,128)(2,1)S(1)}, f32[384,1024]{1,0:T(8,128)S(1)}, bf16[384,1024]{1,0:T(8,128)(2,1)S(1)}) custom-call(bf16[384,768]{1,0:T(8,128)(2,1)S(1)} %get-tuple-element.48.refs_0_, bf16[384,768]{1,0:T(8,128)(2,1)S(1)} %get-tuple-element.79.refs_1_, bf16[768,768]{1,0:T(8,128)(2,1)S(1)} %get-tuple-element.56.refs_2_, ...), custom_call_target="tpu_custom_call" | custom-call | flops 1024 | bytes 1024 | tf_op jit(solution)/shard_map/pallas_call | solution.py:183
  69.4 2.8 %collective-permute-done.19 = bf16[3,192,1024]{2,1,0:T(8,128)(2,1)S(1)} collective-permute-done((bf16[3,192,1024]{2,1,0:T(8,128)(2,1)S(1)}, bf16[3,192,1024]{2,1,0:T(8,128)(2,1)S(1)}, u32[]{:S(2)}, u32[]{:S(2)}) %collective-permute-start.19) | collective-permute-done | bytes 1179680 | tf_op jit(solution)/shard_map/ppermute | solution.py:33
  73.0 2.5 %collective-permute-start.22 = (bf16[384,1024]{1,0:T(8,128)(2,1)S(1)}, bf16[384,1024]{1,0:T(8,128)(2,1)S(1)}, u32[]{:S(2)}, u32[]{:S(2)}) collective-permute-start(bf16[384,1024]{1,0:T(8,128)(2,1)S(1)} %add_convert_fusion.1), channel_id=1, source_target_pairs={{0,4},{1,5},{2,6},{3,7},{4,0},{5,1},{6,2},{7,3},{8,12},{9,13},{10,... | collective-permute-start | bytes 2359304 | tf_op jit(solution)/shard_map/ppermute | solution.py:33
  75.5 3.0 %collective-permute-done.27 = bf16[3,96,1024]{2,1,0:T(8,128)(2,1)S(1)} collective-permute-done((bf16[3,96,1024]{2,1,0:T(8,128)(2,1)S(1)}, bf16[3,96,1024]{2,1,0:T(8,128)(2,1)S(1)}, u32[]{:S(2)}, u32[]{:S(2)}) %collective-permute-start.27) | collective-permute-done | bytes 589856 | tf_op jit(solution)/shard_map/ppermute | solution.py:33
  79.0 4.6 %collective-permute-start.30 = (bf16[3,24,1024]{2,1,0:T(8,128)(2,1)S(1)}, bf16[3,24,1024]{2,1,0:T(8,128)(2,1)S(1)}, u32[]{:S(2)}, u32[]{:S(2)}) collective-permute-start(bf16[3,24,1024]{2,1,0:T(8,128)(2,1)S(1)} %get-tuple-element.84), channel_id=1, source_target_pairs={{0,18},{1,115},{2,16},{3,113},{4,22},{5,119},{6,20},{7,117},{8,26}... | collective-permute-start | bytes 442376 | tf_op jit(solution)/shard_map/ppermute | solution.py:59
  83.6 3.2 %collective-permute-done.23 = bf16[3,96,1024]{2,1,0:T(8,128)(2,1)S(1)} collective-permute-done((bf16[3,96,1024]{2,1,0:T(8,128)(2,1)S(1)}, bf16[3,96,1024]{2,1,0:T(8,128)(2,1)S(1)}, u32[]{:S(2)}, u32[]{:S(2)}) %collective-permute-start.23) | collective-permute-done | bytes 589856 | tf_op jit(solution)/shard_map/ppermute | solution.py:33
  86.8 3.1 %collective-permute-start.29 = (bf16[3,24,1024]{2,1,0:T(8,128)(2,1)S(1)}, bf16[3,24,1024]{2,1,0:T(8,128)(2,1)S(1)}, u32[]{:S(2)}, u32[]{:S(2)}) collective-permute-start(bf16[3,24,1024]{2,1,0:T(8,128)(2,1)S(1)} %get-tuple-element.85), channel_id=1, source_target_pairs={{0,2},{1,67},{2,0},{3,65},{4,6},{5,71},{6,4},{7,69},{8,10},{9,75},... | collective-permute-start | bytes 442376 | tf_op jit(solution)/shard_map/ppermute | solution.py:33
  93.0 2.0 %collective-permute-start.25 = (bf16[3,24,1024]{2,1,0:T(8,128)(2,1)S(1)}, bf16[3,24,1024]{2,1,0:T(8,128)(2,1)S(1)}, u32[]{:S(2)}, u32[]{:S(2)}) collective-permute-start(bf16[3,24,1024]{2,1,0:T(8,128)(2,1)S(1)} %get-tuple-element.82), channel_id=1, source_target_pairs={{0,2},{1,67},{2,0},{3,65},{4,6},{5,71},{6,4},{7,69},{8,10},{9,75},... | collective-permute-start | bytes 442376 | tf_op jit(solution)/shard_map/ppermute | solution.py:33
  98.6 3.0 %collective-permute-done.31 = bf16[3,24,1024]{2,1,0:T(8,128)(2,1)S(1)} collective-permute-done((bf16[3,24,1024]{2,1,0:T(8,128)(2,1)S(1)}, bf16[3,24,1024]{2,1,0:T(8,128)(2,1)S(1)}, u32[]{:S(2)}, u32[]{:S(2)}) %collective-permute-start.31) | collective-permute-done | bytes 147488 | tf_op jit(solution)/shard_map/ppermute | solution.py:33
  (70 shorter events, 28.7 us)
Async XLA Ops:
  0.6 20.8 %collective-permute-start.6 = (bf16[384,1024]{1,0:T(8,128)(2,1)}, bf16[384,1024]{1,0:T(8,128)(2,1)S(1)}, u32[]{:S(2)}, u32[]{:S(2)}) collective-permute-start(bf16[384,1024]{1,0:T(8,128)(2,1)} %refs_0_.5), channel_id=1, source_target_pairs={{0,4},{1,5},{2,6},{3,7},{4,0},{5,1},{6,2},{7,3},{8,12},{9,13},{10,... | collective-permute-start | bytes 2359304 | tf_op jit(solution)/shard_map/ppermute | solution.py:33
  4.4 6.6 %collective-permute-start.2 = (bf16[3,24,1024]{2,1,0:T(8,128)(2,1)S(1)}, bf16[3,24,1024]{2,1,0:T(8,128)(2,1)S(1)}, u32[]{:S(2)}, u32[]{:S(2)}) collective-permute-start(bf16[3,24,1024]{2,1,0:T(8,128)(2,1)S(1)} %pad_maximum_fusion.2), channel_id=1, source_target_pairs={{0,12},{1,13},{2,14},{3,15},{4,8},{5,9},{6,10},{7,11},{8,4},{9,5},... | collective-permute-start | bytes 442376 | tf_op jit(solution)/shard_map/ppermute | solution.py:33
  8.5 6.2 %collective-permute-start.10 = (bf16[3,24,1024]{2,1,0:T(8,128)(2,1)S(1)}, bf16[3,24,1024]{2,1,0:T(8,128)(2,1)S(1)}, u32[]{:S(2)}, u32[]{:S(2)}) collective-permute-start(bf16[3,24,1024]{2,1,0:T(8,128)(2,1)S(1)} %pad_maximum_fusion.2), channel_id=1, source_target_pairs={{0,2},{1,67},{2,0},{3,65},{4,6},{5,71},{6,4},{7,69},{8,10},{9,75},... | collective-permute-start | bytes 442376 | tf_op jit(solution)/shard_map/ppermute | solution.py:33
  11.0 7.3 %collective-permute-start.5 = (bf16[3,24,1024]{2,1,0:T(8,128)(2,1)S(1)}, bf16[3,24,1024]{2,1,0:T(8,128)(2,1)S(1)}, u32[]{:S(2)}, u32[]{:S(2)}) collective-permute-start(bf16[3,24,1024]{2,1,0:T(8,128)(2,1)S(1)} %collective-permute-done.2), channel_id=1, source_target_pairs={{0,18},{1,115},{2,16},{3,113},{4,22},{5,119},{6,20},{7,117},{8,26}... | collective-permute-start | bytes 442376 | tf_op jit(solution)/shard_map/ppermute | solution.py:59
  15.3 11.2 %collective-permute-start.12 = (bf16[3,96,1024]{2,1,0:T(8,128)(2,1)S(1)}, bf16[3,96,1024]{2,1,0:T(8,128)(2,1)S(1)}, u32[]{:S(2)}, u32[]{:S(2)}) collective-permute-start(bf16[3,96,1024]{2,1,0:T(8,128)(2,1)S(1)} %pad_maximum_fusion.1.refs_7_.refs_12_), channel_id=1, source_target_pairs={{0,48},{1,17},{2,50},{3,19},{4,52},{5,21},{6,54},{7,23},{8,56},{9,... | collective-permute-start | bytes 1769480 | tf_op jit(solution)/shard_map/ppermute | solution.py:33
  18.3 15.4 %collective-permute-start = (bf16[384,1024]{1,0:T(8,128)(2,1)S(1)}, bf16[384,1024]{1,0:T(8,128)(2,1)S(1)}, u32[]{:S(2)}, u32[]{:S(2)}) collective-permute-start(bf16[384,1024]{1,0:T(8,128)(2,1)S(1)} %copy-done), channel_id=1, source_target_pairs={{0,1},{1,0},{2,3},{3,2},{4,5},{5,4},{6,7},{7,6},{8,9},{9,8},{10,11... | collective-permute-start | bytes 2359304 | tf_op jit(solution)/shard_map/ppermute | solution.py:63
  18.7 16.8 %collective-permute-start.1 = (bf16[384,1024]{1,0:T(8,128)(2,1)S(1)}, bf16[384,1024]{1,0:T(8,128)(2,1)S(1)}, u32[]{:S(2)}, u32[]{:S(2)}) collective-permute-start(bf16[384,1024]{1,0:T(8,128)(2,1)S(1)} %copy-done.1), channel_id=1, source_target_pairs={{0,1},{1,0},{2,3},{3,2},{4,5},{5,4},{6,7},{7,6},{8,9},{9,8},{10,11... | collective-permute-start | bytes 2359304 | tf_op jit(solution)/shard_map/ppermute | solution.py:63
  19.9 10.0 %collective-permute-start.8 = (bf16[3,96,1024]{2,1,0:T(8,128)(2,1)S(1)}, bf16[3,96,1024]{2,1,0:T(8,128)(2,1)S(1)}, u32[]{:S(2)}, u32[]{:S(2)}) collective-permute-start(bf16[3,96,1024]{2,1,0:T(8,128)(2,1)S(1)} %pad_maximum_fusion.refs_5_.refs_10_), channel_id=1, source_target_pairs={{0,66},{1,3},{2,64},{3,1},{4,70},{5,7},{6,68},{7,5},{8,74},{9,11},... | collective-permute-start | bytes 1769480 | tf_op jit(solution)/shard_map/ppermute | solution.py:33
  21.5 19.3 %collective-permute-start.7 = (bf16[384,1024]{1,0:T(8,128)(2,1)S(1)}, bf16[384,1024]{1,0:T(8,128)(2,1)S(1)}, u32[]{:S(2)}, u32[]{:S(2)}) collective-permute-start(bf16[384,1024]{1,0:T(8,128)(2,1)S(1)} %copy-done.1), channel_id=1, source_target_pairs={{0,4},{1,5},{2,6},{3,7},{4,0},{5,1},{6,2},{7,3},{8,12},{9,13},{10,... | collective-permute-start | bytes 2359304 | tf_op jit(solution)/shard_map/ppermute | solution.py:33
  26.4 14.4 %collective-permute-start.13 = (bf16[3,96,1024]{2,1,0:T(8,128)(2,1)S(1)}, bf16[3,96,1024]{2,1,0:T(8,128)(2,1)S(1)}, u32[]{:S(2)}, u32[]{:S(2)}) collective-permute-start(bf16[3,96,1024]{2,1,0:T(8,128)(2,1)S(1)} %pad_maximum_fusion.refs_5_.refs_10_), channel_id=1, source_target_pairs={{0,48},{1,17},{2,50},{3,19},{4,52},{5,21},{6,54},{7,23},{8,56},{9,... | collective-permute-start | bytes 1769480 | tf_op jit(solution)/shard_map/ppermute | solution.py:33
  29.9 14.0 %collective-permute-start.14 = (bf16[3,96,1024]{2,1,0:T(8,128)(2,1)S(1)}, bf16[3,96,1024]{2,1,0:T(8,128)(2,1)S(1)}, u32[]{:S(2)}, u32[]{:S(2)}) collective-permute-start(bf16[3,96,1024]{2,1,0:T(8,128)(2,1)S(1)} %collective-permute-done.8.refs_4_.refs_9_), channel_id=1, source_target_pairs={{0,48},{1,17},{2,50},{3,19},{4,52},{5,21},{6,54},{7,23},{8,56},{9,... | collective-permute-start | bytes 1769480 | tf_op jit(solution)/shard_map/ppermute | solution.py:33
  33.7 17.8 %collective-permute-start.17 = (bf16[3,192,1024]{2,1,0:T(8,128)(2,1)S(1)}, bf16[3,192,1024]{2,1,0:T(8,128)(2,1)S(1)}, u32[]{:S(2)}, u32[]{:S(2)}) collective-permute-start(bf16[3,192,1024]{2,1,0:T(8,128)(2,1)S(1)} %constant_dynamic-update-slice_fusion), channel_id=1, source_target_pairs={{0,66},{1,3},{2,64},{3,1},{4,70},{5,7},{6,68},{7,5},{8,74},{9,11},... | collective-permute-start | bytes 3538952 | tf_op jit(solution)/shard_map/ppermute | solution.py:33
  48.3 18.4 %collective-permute-start.20 = (bf16[3,192,1024]{2,1,0:T(8,128)(2,1)S(1)}, bf16[3,192,1024]{2,1,0:T(8,128)(2,1)S(1)}, u32[]{:S(2)}, u32[]{:S(2)}) collective-permute-start(bf16[3,192,1024]{2,1,0:T(8,128)(2,1)S(1)} %get-tuple-element.67), channel_id=1, source_target_pairs={{0,48},{1,17},{2,50},{3,19},{4,52},{5,21},{6,54},{7,23},{8,56},{9,... | collective-permute-start | bytes 3538952 | tf_op jit(solution)/shard_map/ppermute | solution.py:33
  55.7 16.5 %collective-permute-start.19 = (bf16[3,192,1024]{2,1,0:T(8,128)(2,1)S(1)}, bf16[3,192,1024]{2,1,0:T(8,128)(2,1)S(1)}, u32[]{:S(2)}, u32[]{:S(2)}) collective-permute-start(bf16[3,192,1024]{2,1,0:T(8,128)(2,1)S(1)} %get-tuple-element.66), channel_id=1, source_target_pairs={{0,66},{1,3},{2,64},{3,1},{4,70},{5,7},{6,68},{7,5},{8,74},{9,11},... | collective-permute-start | bytes 3538952 | tf_op jit(solution)/shard_map/ppermute | solution.py:33
  66.9 11.6 %collective-permute-start.27 = (bf16[3,96,1024]{2,1,0:T(8,128)(2,1)S(1)}, bf16[3,96,1024]{2,1,0:T(8,128)(2,1)S(1)}, u32[]{:S(2)}, u32[]{:S(2)}) collective-permute-start(bf16[3,96,1024]{2,1,0:T(8,128)(2,1)S(1)} %add_convert_fusion.3), channel_id=1, source_target_pairs={{0,66},{1,3},{2,64},{3,1},{4,70},{5,7},{6,68},{7,5},{8,74},{9,11},... | collective-permute-start | bytes 1769480 | tf_op jit(solution)/shard_map/ppermute | solution.py:33
  68.3 26.9 %collective-permute-start.18 = (bf16[384,1024]{1,0:T(8,128)(2,1)S(1)}, bf16[384,1024]{1,0:T(8,128)(2,1)S(1)}, u32[]{:S(2)}, u32[]{:S(2)}) collective-permute-start(bf16[384,1024]{1,0:T(8,128)(2,1)S(1)} %get-tuple-element.65), channel_id=1, source_target_pairs={{0,1},{1,0},{2,3},{3,2},{4,5},{5,4},{6,7},{7,6},{8,9},{9,8},{10,11... | collective-permute-start | bytes 2359304 | tf_op jit(solution)/shard_map/ppermute | solution.py:63
  72.4 14.3 %collective-permute-start.23 = (bf16[3,96,1024]{2,1,0:T(8,128)(2,1)S(1)}, bf16[3,96,1024]{2,1,0:T(8,128)(2,1)S(1)}, u32[]{:S(2)}, u32[]{:S(2)}) collective-permute-start(bf16[3,96,1024]{2,1,0:T(8,128)(2,1)S(1)} %add_convert_fusion.5), channel_id=1, source_target_pairs={{0,48},{1,17},{2,50},{3,19},{4,52},{5,21},{6,54},{7,23},{8,56},{9,... | collective-permute-start | bytes 1769480 | tf_op jit(solution)/shard_map/ppermute | solution.py:33
  73.0 23.4 %collective-permute-start.22 = (bf16[384,1024]{1,0:T(8,128)(2,1)S(1)}, bf16[384,1024]{1,0:T(8,128)(2,1)S(1)}, u32[]{:S(2)}, u32[]{:S(2)}) collective-permute-start(bf16[384,1024]{1,0:T(8,128)(2,1)S(1)} %add_convert_fusion.1), channel_id=1, source_target_pairs={{0,4},{1,5},{2,6},{3,7},{4,0},{5,1},{6,2},{7,3},{8,12},{9,13},{10,... | collective-permute-start | bytes 2359304 | tf_op jit(solution)/shard_map/ppermute | solution.py:33
  78.9 11.4 %collective-permute-start.28 = (bf16[3,24,1024]{2,1,0:T(8,128)(2,1)S(1)}, bf16[3,24,1024]{2,1,0:T(8,128)(2,1)S(1)}, u32[]{:S(2)}, u32[]{:S(2)}) collective-permute-start(bf16[3,24,1024]{2,1,0:T(8,128)(2,1)S(1)} %get-tuple-element.83), channel_id=1, source_target_pairs={{0,16},{1,49},{2,18},{3,51},{4,20},{5,53},{6,22},{7,55},{8,24},{9,... | collective-permute-start | bytes 442376 | tf_op jit(solution)/shard_map/ppermute | solution.py:33
  79.0 11.4 %collective-permute-start.30 = (bf16[3,24,1024]{2,1,0:T(8,128)(2,1)S(1)}, bf16[3,24,1024]{2,1,0:T(8,128)(2,1)S(1)}, u32[]{:S(2)}, u32[]{:S(2)}) collective-permute-start(bf16[3,24,1024]{2,1,0:T(8,128)(2,1)S(1)} %get-tuple-element.84), channel_id=1, source_target_pairs={{0,18},{1,115},{2,16},{3,113},{4,22},{5,119},{6,20},{7,117},{8,26}... | collective-permute-start | bytes 442376 | tf_op jit(solution)/shard_map/ppermute | solution.py:59
  86.8 6.3 %collective-permute-start.29 = (bf16[3,24,1024]{2,1,0:T(8,128)(2,1)S(1)}, bf16[3,24,1024]{2,1,0:T(8,128)(2,1)S(1)}, u32[]{:S(2)}, u32[]{:S(2)}) collective-permute-start(bf16[3,24,1024]{2,1,0:T(8,128)(2,1)S(1)} %get-tuple-element.85), channel_id=1, source_target_pairs={{0,2},{1,67},{2,0},{3,65},{4,6},{5,71},{6,4},{7,69},{8,10},{9,75},... | collective-permute-start | bytes 442376 | tf_op jit(solution)/shard_map/ppermute | solution.py:33
  90.3 7.4 %collective-permute-start.24 = (bf16[3,24,1024]{2,1,0:T(8,128)(2,1)S(1)}, bf16[3,24,1024]{2,1,0:T(8,128)(2,1)S(1)}, u32[]{:S(2)}, u32[]{:S(2)}) collective-permute-start(bf16[3,24,1024]{2,1,0:T(8,128)(2,1)S(1)} %get-tuple-element.80), channel_id=1, source_target_pairs={{0,16},{1,49},{2,18},{3,51},{4,20},{5,53},{6,22},{7,55},{8,24},{9,... | collective-permute-start | bytes 442376 | tf_op jit(solution)/shard_map/ppermute | solution.py:33
  90.4 7.3 %collective-permute-start.26 = (bf16[3,24,1024]{2,1,0:T(8,128)(2,1)S(1)}, bf16[3,24,1024]{2,1,0:T(8,128)(2,1)S(1)}, u32[]{:S(2)}, u32[]{:S(2)}) collective-permute-start(bf16[3,24,1024]{2,1,0:T(8,128)(2,1)S(1)} %get-tuple-element.81), channel_id=1, source_target_pairs={{0,18},{1,115},{2,16},{3,113},{4,22},{5,119},{6,20},{7,117},{8,26}... | collective-permute-start | bytes 442376 | tf_op jit(solution)/shard_map/ppermute | solution.py:59
  95.2 6.4 %collective-permute-start.31 = (bf16[3,24,1024]{2,1,0:T(8,128)(2,1)S(1)}, bf16[3,24,1024]{2,1,0:T(8,128)(2,1)S(1)}, u32[]{:S(2)}, u32[]{:S(2)}) collective-permute-start(bf16[3,24,1024]{2,1,0:T(8,128)(2,1)S(1)} %add_convert_fusion.6), channel_id=1, source_target_pairs={{0,12},{1,13},{2,14},{3,15},{4,8},{5,9},{6,10},{7,11},{8,4},{9,5},... | collective-permute-start | bytes 442376 | tf_op jit(solution)/shard_map/ppermute | solution.py:33
  (10 other events, 78.9 us)
